TPU v7x, 32 devices: a whole 2x2x4 slice. The times are simulated.
32 devices in a mesh: dp: 8 (over z, x), tensor: 4 (over y, core).
Axes of the slice: x: 2, y: 2, z: 4, core: 2. Of those that a mesh axis runs over, the one named last changes fastest.
Arguments:
- inputs: bfloat16 [8, 256, 768], P('dp'), may hold values from -6 to 6
- encoded: bfloat16 [8, 512, 768], P('dp', 'tensor'), may hold values from -6 to 6
- dec_len: int32 [8], P('dp'), may hold values from 1 to 256
- enc_len: int32 [8], P('dp'), may hold values from 1 to 512
- language: int32 [8], P('dp'), may hold values from 0 to 7
- objective: int32 [8], P('dp'), may hold values from 0 to 1
- distance_bucket: int32 [256], replicated, may hold values from 0 to 31, as said below
- token_weights: float32 [16, 256], replicated, may hold values from 0.25 to 2
- cotangent: bfloat16 [8, 256, 768], P('dp'), may hold values from -6 to 6
- gain_self: float32 [768], replicated, may hold values from 0.5 to 1.5
- self_query: bfloat16 [768, 768], P(None, 'tensor'), may hold values from -0.21875 to 0.21875
- self_key: bfloat16 [768, 768], P(None, 'tensor'), may hold values from -0.21875 to 0.21875
- self_value: bfloat16 [768, 768], P(None, 'tensor'), may hold values from -0.21875 to 0.21875
- self_output: bfloat16 [768, 768], P('tensor'), may hold values from -1.25 to 1.25
- bias_table: float32 [32, 12], P(None, 'tensor'), may hold values from -4 to 4
- gain_cross: float32 [768], replicated, may hold values from 0.5 to 1.5
- cross_query: bfloat16 [768, 768], P(None, 'tensor'), may hold values from -0.21875 to 0.21875
- cross_key: bfloat16 [768, 768], P(None, 'tensor'), may hold values from -0.21875 to 0.21875
- cross_value: bfloat16 [768, 768], P(None, 'tensor'), may hold values from -0.21875 to 0.21875
- cross_output: bfloat16 [768, 768], P('tensor'), may hold values from -1.25 to 1.25
- gain_ffn: float32 [768], replicated, may hold values from 0.5 to 1.5
- ffn_up: bfloat16 [768, 3072], P(None, 'tensor'), may hold values from -0.21875 to 0.21875
- ffn_down: bfloat16 [3072, 768], P('tensor'), may hold values from -0.109375 to 0.109375
Outputs:
- layer_out: bfloat16 [8, 256, 768], P('dp')
- input_grad: bfloat16 [8, 256, 768], P('dp')
- encoded_grad: bfloat16 [8, 512, 768], P('dp', 'tensor')
- grad_gain_self: float32 [768], P('dp')
- grad_self_query: float32 [768, 768], P('dp', 'tensor')
- grad_self_key: float32 [768, 768], P('dp', 'tensor')
- grad_self_value: float32 [768, 768], P('dp', 'tensor')
- grad_self_output: float32 [768, 768], P('tensor', 'dp')
- grad_bias_table: float32 [32, 12], P(None, 'tensor')
- grad_gain_cross: float32 [768], P('dp')
- grad_cross_query: float32 [768, 768], P('dp', 'tensor')
- grad_cross_key: float32 [768, 768], P('dp', 'tensor')
- grad_cross_value: float32 [768, 768], P('dp', 'tensor')
- grad_cross_output: float32 [768, 768], P('tensor', 'dp')
- grad_gain_ffn: float32 [768], P('dp')
- grad_ffn_up: float32 [768, 3072], P('dp', 'tensor')
- grad_ffn_down: float32 [3072, 768], P('tensor', 'dp')
Inputs may be any that keep to these rules, and one draw needn't show every extreme that they name: distance_bucket never falls as the distance grows, is 0 at distance 0 and 31 at distance 256 - 1.
All inputs are finite; a program needn't handle non-finite values.
Results may differ from a plain program's by a relative error of at most 0.033.
Values may be sent and summed in bfloat16 or wider, within the bound.
No kernel may reach another device: no remote copies, remote signals or barrier semaphores. Data moves between devices by JAX's collectives and lax.ppermute only.
A program may use at most 128 MiB of HBM per device.

v0:
```python
import jax
import jax.numpy as jnp
from jax import lax
from jax.sharding import PartitionSpec as P

HEAD_DIM = 64
LANGS = 8


EPSILON = 1e-06
SCALE = 0.125
NEGATIVE = -1e30
PRECISE = lax.Precision.HIGHEST


def rms_norm(resid, gain):
    return resid * lax.rsqrt(jnp.mean(resid * resid, -1, keepdims=True) + EPSILON) * gain


def smooth_gate(value):
    return (
        0.5
        * value
        * (1.0 + jnp.tanh(0.7978845608028654 * (value + 0.044715 * value * value * value)))
    )


def norm_back(resid, gain, incoming):
    _, pull = jax.vjp(rms_norm, resid, gain)
    return pull(incoming)


def masked_logits(queries, keys_all, bias_full, allowed):
    logits = (
        SCALE * jnp.einsum("sihe,sjhe->shij", queries, keys_all, preferred_element_type=jnp.float32)
        + bias_full
    )
    return jnp.where(allowed, logits, NEGATIVE)


def attention_forward(queries, keys_all, values_all, bias_full, allowed):
    logits = masked_logits(queries, keys_all, bias_full, allowed)
    highest = jnp.max(logits, -1, keepdims=True)
    expo = jnp.exp(logits - highest)
    totals = jnp.sum(expo, -1, keepdims=True)
    probs = (expo / totals).astype(jnp.bfloat16)
    context = jnp.einsum(
        "shij,sjhe->sihe", probs, values_all, preferred_element_type=jnp.float32
    ).astype(jnp.bfloat16)
    return (context, highest + jnp.log(totals))


def attention_backward(queries, keys_all, values_all, bias_full, allowed, log_totals, grad_context):
    logits = masked_logits(queries, keys_all, bias_full, allowed)
    probs = jnp.exp(logits - log_totals)
    probs_low = probs.astype(jnp.bfloat16)
    grad_values = jnp.einsum(
        "shij,sihe->sjhe", probs_low, grad_context, preferred_element_type=jnp.float32
    ).astype(jnp.bfloat16)
    grad_probs = jnp.einsum(
        "sihe,sjhe->shij", grad_context, values_all, preferred_element_type=jnp.float32
    )
    weighted = jnp.sum(grad_probs * probs, -1, keepdims=True)
    grad_logits = (probs * (grad_probs - weighted)).astype(jnp.bfloat16)
    grad_queries = (
        SCALE
        * jnp.einsum("shij,sjhe->sihe", grad_logits, keys_all, preferred_element_type=jnp.float32)
    ).astype(jnp.bfloat16)
    grad_keys = (
        SCALE
        * jnp.einsum("shij,sihe->sjhe", grad_logits, queries, preferred_element_type=jnp.float32)
    ).astype(jnp.bfloat16)
    return (grad_queries, grad_keys, grad_values, grad_logits)


def diagonal_sums(matrix):
    heads, length, _ = matrix.shape
    flipped = matrix[:, :, ::-1]
    padded = jnp.pad(flipped, ((0, 0), (0, 0), (0, length)))
    skewed = padded.reshape(heads, 2 * length * length)[:, : length * (2 * length - 1)]
    skewed = skewed.reshape(heads, length, 2 * length - 1)
    return jnp.sum(skewed, 1)[:, length - 1 :]


def project_rows(rows, matrix):
    return jnp.einsum("rd,dk->rk", rows, matrix, preferred_element_type=jnp.float32)


def weight_grad(rows, grads):
    return jnp.einsum("rd,rk->dk", rows, grads, preferred_element_type=jnp.float32)


def back_project(grads, matrix):
    return jnp.einsum("rk,dk->rd", grads, matrix, preferred_element_type=jnp.float32)


def on_device(
    inputs,
    encoded,
    dec_len,
    enc_len,
    language,
    objective,
    distance_bucket,
    token_weights,
    cotangent,
    gain_self,
    self_query,
    self_key,
    self_value,
    self_output,
    bias_table,
    gain_cross,
    cross_query,
    cross_key,
    cross_value,
    cross_output,
    gain_ffn,
    ffn_up,
    ffn_down,
):
    seqs, length, width = inputs.shape
    total_rows = seqs * length
    heads_here = self_query.shape[1] // HEAD_DIM

    def settle(partial_value):
        return lax.psum(partial_value.astype(jnp.bfloat16), "tensor").astype(jnp.float32)

    def normed(resid, gain):
        rounded = rms_norm(resid, gain).astype(jnp.bfloat16)
        return rounded

    def back_sum(partial_value):
        return lax.psum(partial_value.astype(jnp.bfloat16), "tensor").astype(jnp.float32)

    def branch_grad(resid_grad):
        rounded = resid_grad.astype(jnp.bfloat16)
        return rounded

    def split_heads(flat, count):
        return flat.astype(jnp.bfloat16).reshape(seqs, count, heads_here, HEAD_DIM)

    position = jnp.arange(length)
    causal = position[None, :] <= position[:, None]
    allowed_self = causal[None, None] & (
        position[None, None, None, :] < dec_len[:, None, None, None]
    )
    encoded_full = lax.all_gather(encoded, "tensor", axis=1, tiled=True)
    span = encoded_full.shape[1]
    allowed_cross = jnp.arange(span)[None, None, None, :] < enc_len[:, None, None, None]
    bucket_onehot = (distance_bucket[:, None] == jnp.arange(bias_table.shape[0])[None, :]).astype(
        jnp.float32
    )
    distance_bias = jnp.dot(bucket_onehot, bias_table, precision=PRECISE)
    offset = jnp.maximum(position[:, None] - position[None, :], 0)
    bias_self = jnp.transpose(distance_bias[offset], (2, 0, 1))
    row_pick = objective * LANGS + language
    table_onehot = (row_pick[:, None] == jnp.arange(token_weights.shape[0])[None, :]).astype(
        jnp.float32
    )
    weighting = jnp.dot(table_onehot, token_weights, precision=PRECISE)
    weighting = weighting * (position[None, :] < dec_len[:, None]).astype(jnp.float32)
    grad_full = (cotangent.astype(jnp.float32) * weighting[:, :, None]).reshape(total_rows, width)
    hidden_zero = inputs.reshape(total_rows, width).astype(jnp.float32)
    normed_one = normed(hidden_zero, gain_self)
    query_one = split_heads(project_rows(normed_one, self_query), length)
    key_one = split_heads(project_rows(normed_one, self_key), length)
    value_one = split_heads(project_rows(normed_one, self_value), length)
    context_one, totals_one = attention_forward(
        query_one, key_one, value_one, bias_self[None], allowed_self
    )
    flat_one = context_one.reshape(total_rows, heads_here * HEAD_DIM)
    hidden_one = hidden_zero + settle(
        jnp.dot(flat_one, self_output, preferred_element_type=jnp.float32)
    )
    normed_two = normed(hidden_one, gain_cross)
    query_two = split_heads(project_rows(normed_two, cross_query), length)
    key_two = (
        jnp.einsum("spd,dk->spk", encoded_full, cross_key, preferred_element_type=jnp.float32)
        .astype(jnp.bfloat16)
        .reshape(seqs, span, heads_here, HEAD_DIM)
    )
    value_two = (
        jnp.einsum("spd,dk->spk", encoded_full, cross_value, preferred_element_type=jnp.float32)
        .astype(jnp.bfloat16)
        .reshape(seqs, span, heads_here, HEAD_DIM)
    )
    context_two, totals_two = attention_forward(query_two, key_two, value_two, 0.0, allowed_cross)
    flat_two = context_two.reshape(total_rows, heads_here * HEAD_DIM)
    hidden_two = hidden_one + settle(
        jnp.dot(flat_two, cross_output, preferred_element_type=jnp.float32)
    )
    normed_three = normed(hidden_two, gain_ffn)
    pre_gate = project_rows(normed_three, ffn_up)
    activity = smooth_gate(pre_gate).astype(jnp.bfloat16)
    hidden_three = hidden_two + settle(
        jnp.dot(activity, ffn_down, preferred_element_type=jnp.float32)
    )
    branch_three = grad_full.astype(jnp.bfloat16)
    grad_ffn_down = weight_grad(activity, branch_three)
    grad_activity = back_project(branch_three, ffn_down)
    _, gate_pull = jax.vjp(smooth_gate, pre_gate)
    grad_pre = gate_pull(grad_activity)[0].astype(jnp.bfloat16)
    grad_ffn_up = weight_grad(normed_three, grad_pre)
    grad_normed_three = back_sum(back_project(grad_pre, ffn_up))
    added_two, grad_gain_ffn = norm_back(hidden_two, gain_ffn, grad_normed_three)
    grad_two = grad_full + added_two
    branch_two = branch_grad(grad_two)
    grad_cross_output = weight_grad(flat_two, branch_two)
    grad_context_two = split_heads(back_project(branch_two, cross_output), length)
    grad_query_two, grad_key_two, grad_value_two, _ = attention_backward(
        query_two, key_two, value_two, 0.0, allowed_cross, totals_two, grad_context_two
    )
    grad_query_flat = grad_query_two.reshape(total_rows, heads_here * HEAD_DIM)
    grad_key_flat = grad_key_two.reshape(seqs, span, heads_here * HEAD_DIM)
    grad_value_flat = grad_value_two.reshape(seqs, span, heads_here * HEAD_DIM)
    grad_cross_query = weight_grad(normed_two, grad_query_flat)
    grad_cross_key = jnp.einsum(
        "spd,spk->dk", encoded_full, grad_key_flat, preferred_element_type=jnp.float32
    )
    grad_cross_value = jnp.einsum(
        "spd,spk->dk", encoded_full, grad_value_flat, preferred_element_type=jnp.float32
    )
    encoded_terms = jnp.einsum(
        "spk,dk->spd", grad_key_flat, cross_key, preferred_element_type=jnp.float32
    )
    encoded_terms = encoded_terms + jnp.einsum(
        "spk,dk->spd", grad_value_flat, cross_value, preferred_element_type=jnp.float32
    )
    encoded_grad = lax.psum_scatter(
        encoded_terms.astype(jnp.bfloat16), "tensor", scatter_dimension=1, tiled=True
    )
    grad_normed_two = back_sum(back_project(grad_query_flat, cross_query))
    added_one, grad_gain_cross = norm_back(hidden_one, gain_cross, grad_normed_two)
    grad_one = grad_two + added_one
    branch_one = branch_grad(grad_one)
    grad_self_output = weight_grad(flat_one, branch_one)
    grad_context_one = split_heads(back_project(branch_one, self_output), length)
    grad_query_one, grad_key_one, grad_value_one, grad_logits_one = attention_backward(
        query_one, key_one, value_one, bias_self[None], allowed_self, totals_one, grad_context_one
    )
    logit_total = jnp.sum(grad_logits_one, 0, dtype=jnp.float32)
    grad_distance = diagonal_sums(logit_total)
    grad_table_terms = jnp.einsum("lb,hl->bh", bucket_onehot, grad_distance, precision=PRECISE)
    query_flat = grad_query_one.reshape(total_rows, heads_here * HEAD_DIM)
    key_flat = grad_key_one.reshape(total_rows, heads_here * HEAD_DIM)
    value_flat = grad_value_one.reshape(total_rows, heads_here * HEAD_DIM)
    grad_self_query = weight_grad(normed_one, query_flat)
    grad_self_key = weight_grad(normed_one, key_flat)
    grad_self_value = weight_grad(normed_one, value_flat)
    normed_terms = (
        back_project(query_flat, self_query)
        + back_project(key_flat, self_key)
        + back_project(value_flat, self_value)
    )
    grad_normed_one = back_sum(normed_terms)
    added_zero, grad_gain_self = norm_back(hidden_zero, gain_self, grad_normed_one)
    grad_zero = grad_one + added_zero
    layer_out = hidden_three.astype(jnp.bfloat16)
    input_grad = grad_zero.astype(jnp.bfloat16)
    summed = (
        lax.psum_scatter(grad_gain_self, "dp", scatter_dimension=0, tiled=True),
        lax.psum_scatter(grad_self_query, "dp", scatter_dimension=0, tiled=True),
        lax.psum_scatter(grad_self_key, "dp", scatter_dimension=0, tiled=True),
        lax.psum_scatter(grad_self_value, "dp", scatter_dimension=0, tiled=True),
        lax.psum_scatter(grad_self_output, "dp", scatter_dimension=1, tiled=True),
        lax.psum_scatter(grad_gain_cross, "dp", scatter_dimension=0, tiled=True),
        lax.psum_scatter(grad_cross_query, "dp", scatter_dimension=0, tiled=True),
        lax.psum_scatter(grad_cross_key, "dp", scatter_dimension=0, tiled=True),
        lax.psum_scatter(grad_cross_value, "dp", scatter_dimension=0, tiled=True),
        lax.psum_scatter(grad_cross_output, "dp", scatter_dimension=1, tiled=True),
        lax.psum_scatter(grad_gain_ffn, "dp", scatter_dimension=0, tiled=True),
        lax.psum_scatter(grad_ffn_up, "dp", scatter_dimension=0, tiled=True),
        lax.psum_scatter(grad_ffn_down, "dp", scatter_dimension=1, tiled=True),
    )
    grad_bias_table = lax.psum(grad_table_terms, "dp")
    return (
        layer_out.reshape(seqs, length, width),
        input_grad.reshape(seqs, length, width),
        encoded_grad,
        summed[0],
        summed[1],
        summed[2],
        summed[3],
        summed[4],
        grad_bias_table,
        summed[5],
        summed[6],
        summed[7],
        summed[8],
        summed[9],
        summed[10],
        summed[11],
        summed[12],
    )


def solution(mesh):
    return jax.shard_map(
        on_device,
        mesh=mesh,
        in_specs=(
            P("dp", None, None),
            P("dp", "tensor", None),
            P("dp"),
            P("dp"),
            P("dp"),
            P("dp"),
            P(),
            P(),
            P("dp", None, None),
            P(),
            P(None, "tensor"),
            P(None, "tensor"),
            P(None, "tensor"),
            P("tensor", None),
            P(None, "tensor"),
            P(),
            P(None, "tensor"),
            P(None, "tensor"),
            P(None, "tensor"),
            P("tensor", None),
            P(),
            P(None, "tensor"),
            P("tensor", None),
        ),
        out_specs=(
            P("dp", None, None),
            P("dp", None, None),
            P("dp", "tensor", None),
            P("dp"),
            P("dp", "tensor"),
            P("dp", "tensor"),
            P("dp", "tensor"),
            P("tensor", "dp"),
            P(None, "tensor"),
            P("dp"),
            P("dp", "tensor"),
            P("dp", "tensor"),
            P("dp", "tensor"),
            P("tensor", "dp"),
            P("dp"),
            P("dp", "tensor"),
            P("tensor", "dp"),
        ),
        check_vma=False,
    )
```

profile of v0, /device:TPU:0, one launch (start us, length us, event | category | flops | bytes accessed | tf_op | source)
XLA Modules:
  0.0 1150.7 jit_solution(16719919737966426628)
XLA Ops:
  7.3 1.3 fusion.27
  8.6 1.5 convolution_convert_fusion.15
  11.8 217.1 %gather_fusion = f32[65536,3]{1,0:T(8,128)} fusion(f32[256,3]{1,0:T(8,128)S(1)} %fusion.62, s32[65536]{0:T(1024)S(1)} %broadcast_clamp_fusion), kind=kCustom, calls=%fused_computation | custom fusion | bytes 1835008 | tf_op jit(solution)/shard_map/gather | solution.py:156
  228.9 19.0 %copy.59 = f32[256,256,3]{0,1,2:T(8,128)S(1)} copy(f32[256,256,3]{2,1,0:T(8,128)} %bitcast.218) | data formatting | bytes 1572864 | tf_op jit(solution)/shard_map/gather | solution.py:156
  250.2 1.0 convolution_convert_fusion.4
  251.4 10.1 all_gather.3
  262.6 1.1 convolution_convert_fusion.7
  265.7 21.1 %all-reduce.12.cloned.1.call-done = bf16[256,768]{1,0:T(8,128)(2,1)} async-done(((bf16[256,768]{1,0:T(8,128)(2,1)}), bf16[256,768]{1,0:T(8,128)(2,1)}) %all-reduce.12.cloned.1.call-update) | async-done | bytes 393232 | tf_op jit(solution)/shard_map/psum | solution.py:127
  286.8 1.2 multiply_reduce_fusion.3
  288.0 1.4 convolution_convert_fusion.12
  291.9 1.0 convolution_convert_fusion.3
  293.7 32.0 %all-reduce.14.cloned.1.call-done = bf16[256,768]{1,0:T(8,128)(2,1)} async-done(((bf16[256,768]{1,0:T(8,128)(2,1)}), bf16[256,768]{1,0:T(8,128)(2,1)}) %all-reduce.14.cloned.1.call-update) | async-done | bytes 393232 | tf_op jit(solution)/shard_map/psum | solution.py:127
  325.7 1.3 multiply_reduce_fusion.2
  327.0 0.8 copy-done.2
  328.6 0.9 fusion.34
  329.6 0.8 copy-done.25
  330.4 1.3 convolution_convert_fusion.1
  332.5 32.0 %all-reduce.16.cloned.1.call-done = bf16[256,768]{1,0:T(8,128)(2,1)} async-done(((bf16[256,768]{1,0:T(8,128)(2,1)}), bf16[256,768]{1,0:T(8,128)(2,1)}) %all-reduce.16.cloned.1.call-update) | async-done | bytes 393232 | tf_op jit(solution)/shard_map/psum | solution.py:134
  364.4 2.2 fusion.24
  367.3 1.4 fusion.37
  370.1 0.9 copy-done.15
  372.0 1.0 convolution_convert_fusion
  373.3 2.9 convolution_convert_fusion.2
  376.2 29.7 %all-reduce.18.cloned.1.call-done = bf16[256,768]{1,0:T(8,128)(2,1)} async-done(((bf16[256,768]{1,0:T(8,128)(2,1)}), bf16[256,768]{1,0:T(8,128)(2,1)}) %all-reduce.18.cloned.1.call-update) | async-done | bytes 393232 | tf_op jit(solution)/shard_map/psum | solution.py:134
  405.8 2.0 fusion.25
  408.6 1.4 fusion.38
  413.1 1.1 fusion.4
  414.2 2.4 convolution_bitcast_fusion
  416.7 2.4 convolution_bitcast_fusion.1
  419.2 2.2 fusion.76
  421.5 1.4 convolution_convert_fusion.5
  422.9 1.1 convolution_bitcast_fusion.2
  424.0 2.3 copy.78
  426.4 1.1 fusion.6
  428.0 1.2 copy.76
  429.2 1.3 fusion.77
  430.7 1.3 fusion.79
  432.0 1.3 fusion.81
  434.3 1.3 fusion.1
  435.7 2.0 fusion.74
  438.1 0.8 copy-done.20
  439.0 2.1 fusion.59
  443.5 1.2 copy.82
  444.7 1.3 pad_bitcast_fusion
  446.1 1.1 copy.84
  447.1 1.7 slice.10
  448.9 4.6 reshape.498
  453.4 1.6 reduce_sum.141
  455.3 1.4 fusion.26
  456.7 37.2 %all-reduce.4 = (f32[768]{0:T(1024)S(1)}, f32[32,3]{0,1:T(4,128)}, f32[768]{0:T(1024)S(1)}, f32[768]{0:T(1024)S(1)}) all-reduce(f32[768]{0:T(1024)S(1)} %get-tuple-element.72, f32[32,3]{0,1:T(4,128)S(1)} %fusion.61, f32[768]{0:T(1024)S(1)} %copy-done.72, f32[768]{0:T(1024)S(1)} %copy-done.71), channel_id=3, replica_groups=mesh['dp'=8,'tensor'=4] {'dp'}, use_global_device_ids=true, to_apply=%region_20.21.clone | all-reduce | flops 2400 | bytes 19200
  495.7 2.3 fusion.50
  498.0 16.9 %reduce-scatter.40.cloned.1.call-done = f32[96,192]{1,0:T(8,128)} async-done(((f32[768,192]{1,0:T(8,128)}), f32[96,192]{1,0:T(8,128)}) %reduce-scatter.40.cloned.1.call-update) | async-done | bytes 73744
  514.9 1.6 copy.81
  516.6 63.5 %reduce-scatter.34.cloned.1.call-done = f32[96,192]{1,0:T(8,128)} async-done(((f32[768,192]{1,0:T(8,128)}), f32[96,192]{1,0:T(8,128)}) %reduce-scatter.34.cloned.1.call-update) | async-done | bytes 73744
  580.1 1.6 copy.75
  581.7 63.7 %reduce-scatter.28.cloned.1.call-done = f32[96,192]{1,0:T(8,128)} async-done(((f32[768,192]{1,0:T(8,128)}), f32[96,192]{1,0:T(8,128)}) %reduce-scatter.28.cloned.1.call-update) | async-done | bytes 73744 | tf_op jit(solution)/shard_map/reduce_scatter | solution.py:268
  645.4 65.8 %reduce-scatter.38.cloned.1.call-done = f32[96,192]{1,0:T(8,128)} async-done(((f32[768,192]{1,0:T(8,128)}), f32[96,192]{1,0:T(8,128)}) %reduce-scatter.38.cloned.1.call-update) | async-done | bytes 73744
  711.2 65.2 %reduce-scatter.36.cloned.1.call-done = f32[96,192]{1,0:T(8,128)} async-done(((f32[768,192]{1,0:T(8,128)}), f32[96,192]{1,0:T(8,128)}) %reduce-scatter.36.cloned.1.call-update) | async-done | bytes 73744
  776.4 65.8 %reduce-scatter.26.cloned.1.call-done = f32[96,192]{1,0:T(8,128)} async-done(((f32[768,192]{1,0:T(8,128)}), f32[96,192]{1,0:T(8,128)}) %reduce-scatter.26.cloned.1.call-update) | async-done | bytes 73744 | tf_op jit(solution)/shard_map/reduce_scatter | solution.py:265
  842.2 65.2 %reduce-scatter.24.cloned.1.call-done = f32[96,192]{1,0:T(8,128)} async-done(((f32[768,192]{1,0:T(8,128)}), f32[96,192]{1,0:T(8,128)}) %reduce-scatter.24.cloned.1.call-update) | async-done | bytes 73744 | tf_op jit(solution)/shard_map/reduce_scatter | solution.py:264
  907.4 65.8 %reduce-scatter.22.cloned.1.call-done = f32[96,192]{1,0:T(8,128)} async-done(((f32[768,192]{1,0:T(8,128)}), f32[96,192]{1,0:T(8,128)}) %reduce-scatter.22.cloned.1.call-update) | async-done | bytes 73744 | tf_op jit(solution)/shard_map/reduce_scatter | solution.py:263
  973.2 25.2 %reduce-scatter.20.cloned.1.call-done = bf16[1,128,768]{2,1,0:T(8,128)(2,1)} async-done(((bf16[1,512,768]{2,1,0:T(8,128)(2,1)}), bf16[1,128,768]{2,1,0:T(8,128)(2,1)}) %reduce-scatter.20.cloned.1.call-update) | async-done | bytes 196624 | tf_op jit(solution)/shard_map/reduce_scatter | solution.py:230
  998.5 73.3 %reduce-scatter.30.cloned.1.call-done = f32[96,768]{1,0:T(8,128)} async-done(((f32[768,768]{1,0:T(8,128)}), f32[96,768]{1,0:T(8,128)}) %reduce-scatter.30.cloned.1.call-update) | async-done | bytes 294928 | tf_op jit(solution)/shard_map/reduce_scatter | solution.py:273
  1071.8 72.4 %reduce-scatter.32.cloned.1.call-done = f32[768,96]{0,1:T(8,128)} async-done(((f32[768,768]{0,1:T(8,128)}), f32[768,96]{0,1:T(8,128)}) %reduce-scatter.32.cloned.1.call-update) | async-done | bytes 294928 | tf_op jit(solution)/shard_map/reduce_scatter | solution.py:274
  (250 shorter events, 22.0 us)
Async XLA Ops:
  7.2 320.7 %copy-start = (bf16[768,768]{1,0:T(8,128)(2,1)S(1)}, bf16[768,768]{1,0:T(8,128)(2,1)}, u32[]{:S(2)}) copy-start(bf16[768,768]{1,0:T(8,128)(2,1)} %param.44) | copy-start | bytes 3538948
  7.2 2.9 copy-start.1
  7.2 2.9 copy-start.60
  7.2 2.9 copy-start.55
  7.2 279.5 %all-reduce.12.cloned.1.call-start = ((), (), s32[]{:S(2)}) async-start(), calls=%async_computation.11 | async-start | bytes 786432 | tf_op jit(solution)/shard_map/psum | solution.py:127
  8.6 2.9 copy-start.77
  8.6 239.3 %copy-start.67 = (f32[256]{0:T(256)}, f32[256]{0:T(256)S(1)}, u32[]{:S(2)}) copy-start(f32[256]{0:T(256)S(1)} %fusion.69) | copy-start | bytes 3076
  8.6 2.9 copy-start.82
  8.6 2.9 copy-start.83
  10.1 238.2 %copy-start.46 = (bf16[256,192]{0,1:T(8,128)(2,1)}, bf16[256,192]{0,1:T(8,128)(2,1)S(1)}, u32[]{:S(2)}) copy-start(bf16[256,192]{0,1:T(8,128)(2,1)S(1)} %convolution_convert_fusion.15) | copy-start | bytes 294916
  10.5 237.8 %copy-start.48 = (bf16[256,192]{0,1:T(8,128)(2,1)}, bf16[256,192]{0,1:T(8,128)(2,1)S(1)}, u32[]{:S(2)}) copy-start(bf16[256,192]{0,1:T(8,128)(2,1)S(1)} %convolution_convert_fusion.14) | copy-start | bytes 294916
  228.9 19.0 %copy-start.57 = (bf16[768,192]{0,1:T(8,128)(2,1)S(1)}, bf16[768,192]{0,1:T(8,128)(2,1)}, u32[]{:S(2)}) copy-start(bf16[768,192]{0,1:T(8,128)(2,1)} %param.35) | copy-start | bytes 884740
  248.8 2.5 copy-start.59
  249.6 12.5 %copy-start.31 = (bf16[768,192]{0,1:T(8,128)(2,1)S(1)}, bf16[768,192]{0,1:T(8,128)(2,1)}, u32[]{:S(2)}) copy-start(bf16[768,192]{0,1:T(8,128)(2,1)} %param.40) | copy-start | bytes 884740
  250.2 12.3 %copy-start.33 = (bf16[768,192]{0,1:T(8,128)(2,1)S(1)}, bf16[768,192]{0,1:T(8,128)(2,1)}, u32[]{:S(2)}) copy-start(bf16[768,192]{0,1:T(8,128)(2,1)} %param.41) | copy-start | bytes 884740
  251.3 13.7 %copy-start.74 = (f32[16,256]{1,0:T(8,128)S(1)}, f32[16,256]{1,0:T(8,128)}, u32[]{:S(2)}) copy-start(f32[16,256]{1,0:T(8,128)} %param.30) | copy-start | bytes 49156
  251.3 74.4 %all-reduce.14.cloned.1.call-start = ((), (), s32[]{:S(2)}) async-start(), calls=%async_computation.12 | async-start | bytes 786432 | tf_op jit(solution)/shard_map/psum | solution.py:127
  262.1 25.9 %copy-start.52 = (bf16[768,192]{0,1:T(8,128)(2,1)S(1)}, bf16[768,192]{0,1:T(8,128)(2,1)}, u32[]{:S(2)}) copy-start(bf16[768,192]{0,1:T(8,128)(2,1)} %param.39) | copy-start | bytes 884740
  262.1 25.9 %copy-start.64 = (f32[768]{0:T(1024)S(1)}, f32[768]{0:T(1024)}, u32[]{:S(2)}) copy-start(f32[768]{0:T(1024)} %param.38) | copy-start | bytes 9220
  262.6 26.9 %copy-start.21 = (bf16[512,192]{0,1:T(8,128)(2,1)}, bf16[512,192]{0,1:T(8,128)(2,1)S(1)}, u32[]{:S(2)}) copy-start(bf16[512,192]{0,1:T(8,128)(2,1)S(1)} %convolution_convert_fusion.6) | copy-start | bytes 589828
  288.0 2.0 copy-start.79
  288.0 1.9 copy-start.75
  290.6 35.1 %copy-start.14 = (bf16[256,768]{1,0:T(8,128)(2,1)S(1)}, bf16[256,768]{1,0:T(8,128)(2,1)}, u32[]{:S(2)}) copy-start(bf16[256,768]{1,0:T(8,128)(2,1)} %all-reduce.12.cloned.1.call-done) | copy-start | bytes 1179652
  291.8 36.0 %copy-start.63 = (f32[768]{0:T(1024)S(1)}, f32[768]{0:T(1024)}, u32[]{:S(2)}) copy-start(f32[768]{0:T(1024)} %param.43) | copy-start | bytes 9220
  292.9 71.5 %all-reduce.16.cloned.1.call-start = ((), (), s32[]{:S(2)}) async-start(), calls=%async_computation.13 | async-start | bytes 786432 | tf_op jit(solution)/shard_map/psum | solution.py:134
  293.7 34.7 %copy-start.80 = (f32[256]{0:T(256)}, f32[256]{0:T(256)S(1)}, u32[]{:S(2)}) copy-start(f32[256]{0:T(256)S(1)} %broadcast_select_fusion) | copy-start | bytes 3076
  327.0 1.7 copy-start.85
  331.7 74.2 %all-reduce.18.cloned.1.call-start = ((), (), s32[]{:S(2)}) async-start(), calls=%async_computation.14 | async-start | bytes 786432 | tf_op jit(solution)/shard_map/psum | solution.py:134
  364.4 2.9 copy-start.3
  364.4 4.3 copy-start.28
  367.3 1.8 copy-start.44
  369.7 2.3 copy-start.53
  373.1 82.2 %all-reduce.20.cloned.1.call-start = ((), (), s32[]{:S(2)}) async-start(), calls=%async_computation.26 | async-start | bytes 1572864 | tf_op jit(solution)/shard_map/psum | solution.py:127
  405.8 2.8 copy-start.11
  407.9 2.1 copy-start.30
  408.6 1.7 copy-start.9
  408.6 1.7 copy-start.62
  411.0 2.1 copy-start.41
  411.6 1.4 copy-start.17
  414.2 100.8 %reduce-scatter.40.cloned.1.call-start = ((), (), s32[]{:S(2)}) async-start(), calls=%async_computation.25 | async-start | bytes 884736
  416.6 2.5 copy-start.65
  416.7 163.4 %reduce-scatter.34.cloned.1.call-start = ((), (), s32[]{:S(2)}) async-start(), calls=%async_computation.22 | async-start | bytes 884736
  419.1 226.3 %reduce-scatter.28.cloned.1.call-start = ((), (), s32[]{:S(2)}) async-start(), calls=%async_computation.19 | async-start | bytes 884736 | tf_op jit(solution)/shard_map/reduce_scatter | solution.py:268
  421.4 289.8 %reduce-scatter.38.cloned.1.call-start = ((), (), s32[]{:S(2)}) async-start(), calls=%async_computation.24 | async-start | bytes 884736
  422.9 3.6 copy-start.16
  424.0 3.6 copy-start.7
  426.4 350.0 %reduce-scatter.36.cloned.1.call-start = ((), (), s32[]{:S(2)}) async-start(), calls=%async_computation.23 | async-start | bytes 884736
  427.6 1.6 copy-start.42
  427.6 1.6 copy-start.68
  429.2 1.5 copy-start.40
  429.2 413.0 %reduce-scatter.26.cloned.1.call-start = ((), (), s32[]{:S(2)}) async-start(), calls=%async_computation.18 | async-start | bytes 884736 | tf_op jit(solution)/shard_map/reduce_scatter | solution.py:265
  430.6 1.5 copy-start.36
  430.6 476.8 %reduce-scatter.24.cloned.1.call-start = ((), (), s32[]{:S(2)}) async-start(), calls=%async_computation.17 | async-start | bytes 884736 | tf_op jit(solution)/shard_map/reduce_scatter | solution.py:264
  432.0 1.5 copy-start.32
  432.0 541.3 %reduce-scatter.22.cloned.1.call-start = ((), (), s32[]{:S(2)}) async-start(), calls=%async_computation.16 | async-start | bytes 884736 | tf_op jit(solution)/shard_map/reduce_scatter | solution.py:263
  433.4 565.1 %reduce-scatter.20.cloned.1.call-start = ((), (), s32[]{:S(2)}) async-start(), calls=%async_computation.15 | async-start | bytes 983040 | tf_op jit(solution)/shard_map/reduce_scatter | solution.py:230
  435.6 636.2 %reduce-scatter.30.cloned.1.call-start = ((), (), s32[]{:S(2)}) async-start(), calls=%async_computation.20 | async-start | bytes 2654208 | tf_op jit(solution)/shard_map/reduce_scatter | solution.py:273
  437.8 706.4 %reduce-scatter.32.cloned.1.call-start = ((), (), s32[]{:S(2)}) async-start(), calls=%async_computation.21 | async-start | bytes 2654208 | tf_op jit(solution)/shard_map/reduce_scatter | solution.py:274
  441.2 1.9 copy-start.18
  453.4 1.6 copy-start.84
  453.4 3.2 copy-start.71
  453.4 3.2 copy-start.72
  453.4 42.2 %copy-start.78 = (f32[256]{0:T(256)S(1)}, f32[256]{0:T(256)}, u32[]{:S(2)}) copy-start(f32[256]{0:T(256)} %copy-done.77) | copy-start | bytes 3076
  453.4 42.2 %copy-start.13 = (f32[256,768]{1,0:T(8,128)S(1)}, f32[256,768]{1,0:T(8,128)}, u32[]{:S(2)}) copy-start(f32[256,768]{1,0:T(8,128)} %copy-done.12) | copy-start | bytes 2359300
  (39 other events, 39.1 us)
Sparse Core Ops, SparseCore 0:
  251.4 35.3 all-reduce.11
  293.0 32.5 all-reduce.13
  331.8 32.5 all-reduce.15
  373.2 32.6 all-reduce.17
  414.3 34.7 all-reduce.19
  452.2 62.6 reduce-scatter.39
  518.6 61.4 reduce-scatter.33
  583.9 61.4 reduce-scatter.27
  649.7 61.4 reduce-scatter.37
  714.9 61.4 reduce-scatter.35
  780.6 61.5 reduce-scatter.25
  846.0 61.4 reduce-scatter.23
  911.6 61.5 reduce-scatter.21
  976.2 22.2 reduce-scatter.19
  1002.8 68.9 reduce-scatter.29
  1076.1 68.0 reduce-scatter.31
where the time goes:
time: 1150 us
  waiting for transfers between devices  758 us (66%)
  local copies, waits for them, and re-layouts  264 us (23%)
  blocking collectives  47.3 us (4%)
  matrix products  41.7 us (4%)
  other arithmetic  20.2 us (2%)
  between operations  18.3 us (2%)
    gather x2, local copies, waits for them, and re-layouts, on_device(): bias_self = jnp.transpose(distance_bias[offset], (2, 0, 1))  236 us
    unnamed x20, waiting for transfers between devices  212 us
    reduce_scatter x1, waiting for transfers between devices, on_device(): lax.psum_scatter(grad_ffn_up, 'dp', scatter_dimension=0, tiled=True)  73.3 us
    reduce_scatter x1, waiting for transfers between devices, on_device(): lax.psum_scatter(grad_ffn_down, 'dp', scatter_dimension=1, tiled=True)  72.4 us
    reduce_scatter x1, waiting for transfers between devices, on_device(): lax.psum_scatter(grad_self_value, 'dp', scatter_dimension=0, tiled=True)  65.8 us
    reduce_scatter x1, waiting for transfers between devices, on_device(): lax.psum_scatter(grad_self_query, 'dp', scatter_dimension=0, tiled=True)  65.8 us
    reduce_scatter x1, waiting for transfers between devices, on_device(): lax.psum_scatter(grad_self_key, 'dp', scatter_dimension=0, tiled=True)  65.2 us
    reduce_scatter x1, waiting for transfers between devices, on_device(): lax.psum_scatter(grad_cross_query, 'dp', scatter_dimension=0, tiled=True)  63.7 us
  transfers between devices with their start and end apart: 16, of which 15 were waited for; matrix products, arithmetic and copies ran while one was open for 5% of the time, Pallas kernels for 0%

commit v1 on v0

v1 whole, which is shorter than its diff:
```python
import jax
import jax.numpy as jnp
from jax import lax
from jax.experimental import pallas as pl
from jax.experimental.pallas import tpu as pltpu
from jax.sharding import PartitionSpec as P

HEAD_DIM = 64
LANGS = 8
EPSILON = 1e-06
SCALE = 0.125
NEGATIVE = -1e30
F32 = jnp.float32
BF16 = jnp.bfloat16
VMEM_LIMIT = 20 * 1024 * 1024
EXTRA = 16


def dot(left, right):
    return jnp.dot(left, right, preferred_element_type=F32)


def dot_nt(left, right):
    return lax.dot_general(left, right, (((1,), (1,)), ((), ())), preferred_element_type=F32)


def dot_tn(left, right):
    return lax.dot_general(left, right, (((0,), (0,)), ((), ())), preferred_element_type=F32)


def inverse_rms(resid):
    return lax.rsqrt(jnp.mean(resid * resid, -1, keepdims=True) + EPSILON)


def norm_back(resid, gain, incoming):
    scale = inverse_rms(resid)
    weighted = incoming * gain
    inner = jnp.mean(weighted * resid, -1, keepdims=True)
    grad = scale * weighted - resid * (scale * scale * scale * inner)
    gain_grad = jnp.sum(incoming * resid * scale, 0, keepdims=True)
    return grad, gain_grad


def groups_of(width):
    return [(start, min(2 * HEAD_DIM, width - start)) for start in range(0, width, 2 * HEAD_DIM)]


def head_mask(count, which, value):
    lane = lax.broadcasted_iota(jnp.int32, (1, count), 1)
    return jnp.where(lane // HEAD_DIM == which, value, 0.0).astype(BF16)


def merge_heads(parts):
    merged = []
    for pair in parts:
        if len(pair) == 1:
            merged.append(pair[0])
        else:
            lane = lax.broadcasted_iota(jnp.int32, (1, 2 * HEAD_DIM), 1)
            merged.append(jnp.where(lane < HEAD_DIM, pair[0], pair[1]))
    return jnp.concatenate(merged, -1) if len(merged) > 1 else merged[0]


def heads_forward(queries, keys, values, finish, probs_ref):
    parts = []
    head = 0
    for start, width in groups_of(queries.shape[1]):
        query, key, value = (item[:, start : start + width] for item in (queries, keys, values))
        pair = []
        for inside in range(width // HEAD_DIM):
            logits = finish(head, dot_nt(query * head_mask(width, inside, SCALE), key))
            expo = jnp.exp(logits - jnp.max(logits, -1, keepdims=True))
            probs = (expo * (1.0 / jnp.sum(expo, -1, keepdims=True))).astype(BF16)
            probs_ref[head] = probs
            pair.append(dot(probs, value))
            head += 1
        parts.append(pair)
    return merge_heads(parts).astype(BF16)


def heads_backward(grad_context, keys, values, probs_ref, grad_logits_ref):
    parts = []
    head = 0
    for start, width in groups_of(grad_context.shape[1]):
        grad, key, value = (item[:, start : start + width] for item in (grad_context, keys, values))
        pair = []
        for inside in range(width // HEAD_DIM):
            grad_probs = dot_nt(grad * head_mask(width, inside, 1.0), value)
            probs = probs_ref[head].astype(F32)
            weighted = jnp.sum(grad_probs * probs, -1, keepdims=True)
            grad_logits = (probs * (grad_probs - weighted)).astype(BF16)
            grad_logits_ref[head] = grad_logits
            pair.append(SCALE * dot(grad_logits, key))
            head += 1
        parts.append(pair)
    return merge_heads(parts).astype(BF16)


def heads_transposed(matrix_ref, rows, factor):
    parts = []
    head = 0
    for start, width in groups_of(rows.shape[1]):
        pair = []
        for _ in range(width // HEAD_DIM):
            pair.append(factor * dot_tn(matrix_ref[head], rows[:, start : start + width]))
            head += 1
        parts.append(pair)
    return merge_heads(parts).astype(BF16)


def own_rows(core, half):
    return pl.ds(pl.multiple_of(core * half, half), half)


def split_halves(whole_ref, keep_ref, send_ref):
    half = keep_ref.shape[0]
    core = lax.axis_index("tensor") % 2
    keep_ref[...] = whole_ref[own_rows(core, half), :]
    send_ref[...] = whole_ref[own_rows(1 - core, half), :]


def reversed_onehot(bucket_ref, buckets):
    length = bucket_ref.shape[1]
    row = lax.broadcasted_iota(jnp.int32, (length, length), 0)
    column = lax.broadcasted_iota(jnp.int32, (length, length), 1)
    turn = jnp.where((row + column == length) | (row + column == 0), 1.0, 0.0).astype(BF16)
    bucket = jnp.broadcast_to(bucket_ref[...], (8, length)).astype(F32).astype(BF16)
    turned = dot(bucket, turn)[:1]
    wanted = lax.broadcasted_iota(jnp.int32, (buckets, length), 0).astype(F32)
    return jnp.where(turned == wanted, 1.0, 0.0)


def add_kernel(left_ref, right_ref, out_ref):
    out_ref[...] = (left_ref[...].astype(F32) + right_ref[...].astype(F32)).astype(out_ref.dtype)


def self_forward_kernel(
    dec_len, x, gain, w_query, w_key, w_value, w_output, bucket, table,
    keep, send, normed_out, query_out, key_out, value_out, context_out, probs_out, whole,
):
    length = x.shape[0]
    resid = x[...].astype(F32)
    normed = (resid * inverse_rms(resid) * gain[...]).astype(BF16)
    normed_out[...] = normed
    queries = dot(normed, w_query[...]).astype(BF16)
    keys = dot(normed, w_key[...]).astype(BF16)
    values = dot(normed, w_value[...]).astype(BF16)
    query_out[...] = queries
    key_out[...] = keys
    value_out[...] = values
    onehot = reversed_onehot(bucket, table.shape[0])
    row = lax.broadcasted_iota(jnp.int32, (length, length), 0)
    column = lax.broadcasted_iota(jnp.int32, (length, length), 1)
    allowed = (column <= row) & (column < dec_len[0])

    def finish(head, scores):
        by_distance = jnp.sum(table[:, head : head + 1] * onehot, 0, keepdims=True)
        spread = jnp.broadcast_to(by_distance, (length, length))
        bias = pltpu.roll(spread, 0, 1, stride=1, stride_axis=0)
        return jnp.where(allowed, scores + bias, NEGATIVE)

    context = heads_forward(queries, keys, values, finish, probs_out)
    context_out[...] = context
    whole[...] = dot(context, w_output[...]).astype(BF16)
    split_halves(whole, keep, send)


def cross_source_kernel(e0, e1, e2, e3, wk_own, wv_own, wk_peer, wv_peer, k_own, v_own, k_peer, v_peer):
    rows = e0.shape[0]
    for index, part in enumerate((e0, e1, e2, e3)):
        for weight, out in ((wk_own, k_own), (wv_own, v_own), (wk_peer, k_peer), (wv_peer, v_peer)):
            out[index * rows : (index + 1) * rows, :] = dot(part[...], weight[...]).astype(BF16)


def out_grad_kernel(
    objective, language, dec_len, token_weights, cotangent, down_own, down_peer,
    grad_own, branch_own, branch_peer, act_grad_own, act_grad_peer,
):
    half = grad_own.shape[0]
    length = cotangent.shape[0]
    core = lax.axis_index("tensor") % 2
    weights = token_weights[pl.ds(objective[0] * LANGS + language[0], 1), :]
    position = lax.broadcasted_iota(jnp.int32, (1, length), 1)
    weights = jnp.where(position < dec_len[0], weights, 0.0)

    def rows_of(side):
        row = lax.broadcasted_iota(jnp.int32, (half, length), 0) + side * half
        column = lax.broadcasted_iota(jnp.int32, (half, length), 1)
        factor = jnp.sum(jnp.where(row == column, weights, 0.0), -1, keepdims=True)
        return cotangent[own_rows(side, half), :].astype(F32) * factor

    own = rows_of(core)
    grad_own[...] = own
    branch = own.astype(BF16)
    branch_own[...] = branch
    branch_peer[...] = rows_of(1 - core).astype(BF16)
    act_grad_own[...] = dot_nt(branch, down_own[...])
    act_grad_peer[...] = dot_nt(branch, down_peer[...])


def cross_forward_kernel(
    enc_len, chip_own, chip_other, x, gain, wq_own, wq_peer, wo_own, wo_peer, k_own, v_own, k_peer, v_peer,
    partial_out, hidden_out, normed_out, q_own, q_peer, context_own, probs_own, probs_peer, pack,
):
    half, width = chip_own.shape
    tensor = lax.axis_index("tensor")
    resid = x[own_rows(tensor % 2, half), :].astype(F32)
    resid = resid + (chip_own[...].astype(F32) + chip_other[...].astype(F32))
    hidden_out[...] = resid
    normed = (resid * inverse_rms(resid) * gain[...]).astype(BF16)
    normed_out[...] = normed
    pack[:, :width] = normed
    span = k_own.shape[0]
    column = lax.broadcasted_iota(jnp.int32, (1, span), 1)
    block = column // half
    flip = jnp.where(block % 2 == 1, 2, 0) + jnp.where(block >= 2, 1, 0)
    position = (tensor ^ flip) * half + column % half
    allowed = position < enc_len[0]

    def finish(head, scores):
        return jnp.where(allowed, scores, NEGATIVE)

    queries = dot(normed, wq_own[...]).astype(BF16)
    q_own[...] = queries
    first = heads_forward(queries, k_own[...], v_own[...], finish, probs_own)
    context_own[...] = first
    queries = dot(normed, wq_peer[...]).astype(BF16)
    q_peer[...] = queries
    second = heads_forward(queries, k_peer[...], v_peer[...], finish, probs_peer)
    pack[:, width:] = second
    partial_out[...] = (dot(first, wo_own[...]) + dot(second, wo_peer[...])).astype(BF16)


def ffn_kernel(
    chip_own, chip_other, hidden, gain, up_own, up_peer, act_grad_own, act_grad_peer,
    partial_out, hidden_out, normed_out, act_own, grad_pre_own, pack,
):
    width = hidden.shape[1]
    resid = hidden[...] + (chip_own[...].astype(F32) + chip_other[...].astype(F32))
    hidden_out[...] = resid
    normed = (resid * inverse_rms(resid) * gain[...]).astype(BF16)
    normed_out[...] = normed
    pack[:, :width] = normed

    def through(up, act_grad):
        pre = dot(normed, up[...])
        square = pre * pre
        tanh = jnp.tanh(0.7978845608028654 * (pre + 0.044715 * square * pre))
        half_sum = 0.5 * (1.0 + tanh)
        slope = half_sum + 0.5 * pre * (1.0 - tanh * tanh) * (
            0.7978845608028654 * (1.0 + 3.0 * 0.044715 * square)
        )
        return (pre * half_sum).astype(BF16), (act_grad[...] * slope).astype(BF16)

    act, grad_pre = through(up_own, act_grad_own)
    act_own[...] = act
    grad_pre_own[...] = grad_pre
    total = dot_nt(grad_pre, up_own[...])
    act, grad_pre = through(up_peer, act_grad_peer)
    units = act.shape[1]
    pack[:, width : width + units] = act
    pack[:, width + units :] = grad_pre
    total = total + dot_nt(grad_pre, up_peer[...])
    partial_out[...] = total.astype(BF16)


def ffn_out_kernel(act_own, pack, down_own, down_peer, out):
    units = act_own.shape[1]
    width = out.shape[1]
    out[...] = (
        dot(act_own[...], down_own[...]) + dot(pack[:, width : width + units], down_peer[...])
    ).astype(BF16)


def layer_out_kernel(hidden, chip_own, chip_other, out):
    out[...] = (hidden[...] + (chip_own[...].astype(F32) + chip_other[...].astype(F32))).astype(BF16)


def halves_kernel(own, peer, out):
    half = own.shape[0]
    core = lax.axis_index("tensor") % 2
    out[own_rows(core, half), :] = own[...]
    out[own_rows(1 - core, half), :] = peer[...]


def write_blocks(whole, first_bit, rest_bits, size, targets, extra=None):
    index = lax.axis_index("dp")
    count = 1 << len(rest_bits)
    for first, target in enumerate(targets):
        for entry in range(count):
            relative = first << first_bit
            for place, bit in enumerate(rest_bits):
                if entry >> (len(rest_bits) - 1 - place) & 1:
                    relative |= 1 << bit
            block = index ^ relative
            rows = whole[pl.ds(pl.multiple_of(block * size, size), size), :]
            target[entry, :size, :] = rows
            if extra is not None:
                target[entry, size:, :] = extra


def emit(whole, outs, order, size, extra=None):
    if order is None:
        outs[0][: whole.shape[0], :] = whole[...]
        if extra is not None:
            outs[0][whole.shape[0] :, :] = extra
    else:
        write_blocks(whole, order[0], order[1:], size, outs, extra)


def ffn_weights_kernel(orders, size, normed, pack, act_own, grad_pre_own, branch_own, branch_peer, *refs):
    *outs, whole, left, right = refs
    half, width = normed.shape
    units = act_own.shape[1]
    left[:half] = normed[...]
    left[half:] = pack[:, :width]
    right[:half] = grad_pre_own[...]
    right[half:] = pack[:, width + units :]
    whole[...] = dot_tn(left[...], right[...]).astype(BF16)
    count = 1 if orders[0] is None else 2
    emit(whole, outs[:count], orders[0], size)
    left[:half] = branch_own[...]
    left[half:] = branch_peer[...]
    right[:half] = act_own[...]
    right[half:] = pack[:, width : width + units]
    whole[...] = dot_tn(left[...], right[...]).astype(BF16)
    emit(whole, outs[count:], orders[1], size)


def cross_backward_kernel(
    chip_own, chip_other, hidden, gain, grad_out, wo_own, wo_peer, k_own, v_own, k_peer, v_peer,
    probs_own, probs_peer, wq_own, wq_peer,
    partial_out, grad_hidden, gain_grad, gl_own, gl_peer, gc_own, gc_peer, gq_own, branch, pack,
):
    width = hidden.shape[1]
    incoming = chip_own[...].astype(F32) + chip_other[...].astype(F32)
    added, gain_terms = norm_back(hidden[...], gain[...], incoming)
    gain_grad[...] = jnp.broadcast_to(gain_terms, gain_grad.shape)
    grad = grad_out[...] + added
    grad_hidden[...] = grad
    rounded = grad.astype(BF16)
    branch[...] = rounded
    pack[:, :width] = rounded
    context = dot_nt(rounded, wo_own[...]).astype(BF16)
    gc_own[...] = context
    queries = heads_backward(context, k_own[...], v_own[...], probs_own, gl_own)
    gq_own[...] = queries
    total = dot_nt(queries, wq_own[...])
    context = dot_nt(rounded, wo_peer[...]).astype(BF16)
    gc_peer[...] = context
    queries = heads_backward(context, k_peer[...], v_peer[...], probs_peer, gl_peer)
    pack[:, width:] = queries
    total = total + dot_nt(queries, wq_peer[...])
    partial_out[...] = total.astype(BF16)


def cross_source_grad_kernel(gl_peer, probs_peer, gc_peer, q_peer, out):
    span = out.shape[0] // 2
    middle = span // 2
    for start, grads in (
        (0, heads_transposed(gl_peer, q_peer[...], SCALE)),
        (span, heads_transposed(probs_peer, gc_peer[...], 1.0)),
    ):
        out[start : start + middle] = grads[middle:]
        out[start + middle : start + span] = grads[:middle]


def cross_weights_kernel(
    order, size, gl_own, probs_own, gc_own, q_own, other, e0, e1, e2, e3, normed, pack_forward,
    branch, pack_backward, context_own, gq_own, wk_own, wv_own, *refs,
):
    *outs, encoded_keep, encoded_send, whole, left, right = refs
    span = other.shape[0] // 2
    half, width = normed.shape
    columns = q_own.shape[1]
    grad_keys = heads_transposed(gl_own, q_own[...], SCALE).astype(F32) + other[:span].astype(F32)
    grad_values = heads_transposed(probs_own, gc_own[...], 1.0).astype(F32) + other[span:].astype(F32)
    grad_keys = grad_keys.astype(BF16)
    grad_values = grad_values.astype(BF16)
    terms = (dot_nt(grad_keys, wk_own[...]) + dot_nt(grad_values, wv_own[...])).astype(BF16)
    encoded_keep[...] = terms[: 2 * half]
    encoded_send[...] = terms[2 * half :]
    for index, part in enumerate((e0, e1, e2, e3)):
        left[index * half : (index + 1) * half] = part[...]
    right[:, :columns] = grad_keys
    right[:, columns:] = grad_values
    whole[:, : 2 * columns] = dot_tn(left[...], right[...]).astype(BF16)
    left[:half] = normed[...]
    left[half : 2 * half] = pack_forward[:, :width]
    left[2 * half : 3 * half] = branch[...]
    left[3 * half :] = pack_backward[:, :width]
    right[...] = jnp.zeros_like(right)
    right[:half, :columns] = gq_own[...]
    right[half : 2 * half, :columns] = pack_backward[:, width:]
    right[2 * half : 3 * half, columns:] = context_own[...]
    right[3 * half :, columns:] = pack_forward[:, width:]
    whole[:, 2 * columns :] = dot_tn(left[...], right[...]).astype(BF16)
    emit(whole, outs, order, size)


def encoded_sum_kernel(left, right, keep, send):
    half = keep.shape[0]
    total = (left[...].astype(F32) + right[...].astype(F32)).astype(BF16)
    keep[...] = total[:half]
    send[...] = total[half:]


def self_norm_kernel(chip_own, chip_other, hidden, gain, grad_hidden, gain_ffn, grad_out, pack):
    half = hidden.shape[0]
    incoming = chip_own[...].astype(F32) + chip_other[...].astype(F32)
    added, gain_terms = norm_back(hidden[...], gain[...], incoming)
    grad = grad_hidden[...] + added
    grad_out[...] = grad
    pack[:half] = grad.astype(BF16)
    row = lax.broadcasted_iota(jnp.int32, (EXTRA, hidden.shape[1]), 0)
    extra = jnp.where(row == 0, gain_terms, 0.0) + jnp.where(row == 1, gain_ffn[:1], 0.0)
    pack[half:] = extra.astype(BF16)


def self_backward_kernel(
    pack_own, pack_peer, w_output, w_query, w_key, w_value, queries, keys, values, probs,
    keep, send, branch_out, gq_out, gk_out, gv_out, gl_out, whole,
):
    half = keep.shape[0]
    core = lax.axis_index("tensor") % 2
    branch_out[own_rows(core, half), :] = pack_own[:half]
    branch_out[own_rows(1 - core, half), :] = pack_peer[:half]
    context = dot_nt(branch_out[...], w_output[...]).astype(BF16)
    grad_queries = heads_backward(context, keys[...], values[...], probs, gl_out)
    grad_keys = heads_transposed(gl_out, queries[...], SCALE)
    grad_values = heads_transposed(probs, context, 1.0)
    gq_out[...] = grad_queries
    gk_out[...] = grad_keys
    gv_out[...] = grad_values
    whole[...] = (
        dot_nt(grad_queries, w_query[...]) + dot_nt(grad_keys, w_key[...]) + dot_nt(grad_values, w_value[...])
    ).astype(BF16)
    split_halves(whole, keep, send)


def self_weights_kernel(
    order, size, normed, branch, gq, gk, gv, context, gl, bucket, pack_own, pack_peer, *refs
):
    *outs, whole, right, left = refs
    length, columns = gq.shape
    half = pack_own.shape[0] - EXTRA
    right[:length, :columns] = gq[...]
    right[:length, columns:] = gk[...]
    whole[:, : 2 * columns] = dot_tn(normed[...], right[:length]).astype(BF16)
    left[:length] = normed[...]
    left[length:] = branch[...]
    right[...] = jnp.zeros_like(right)
    right[:length, :columns] = gv[...]
    right[length:, columns:] = context[...]
    whole[:, 2 * columns :] = dot_tn(left[...], right[...]).astype(BF16)
    buckets = 32
    onehot = reversed_onehot(bucket, buckets)
    row = lax.broadcasted_iota(jnp.int32, (length, length), 0)
    column = lax.broadcasted_iota(jnp.int32, (length, length), 1)
    turn = jnp.where(row + column == length - 1, 1.0, 0.0).astype(BF16)
    place = lax.broadcasted_iota(jnp.int32, (8, length), 0)
    sums = jnp.zeros((8, length), F32)
    for head in range(gl.shape[0]):
        skewed = pltpu.roll(dot(turn, gl[head]), 1, 1, stride=1, stride_axis=0)
        sums = sums + jnp.where(place == head, jnp.sum(skewed, 0, keepdims=True), 0.0)
    table = lax.dot_general(
        sums, onehot, (((1,), (1,)), ((), ())), precision=lax.Precision.HIGHEST, preferred_element_type=F32
    )
    extra = pack_own[half:].astype(F32) + pack_peer[half:].astype(F32)
    wide = jnp.concatenate([table, jnp.zeros((8, extra.shape[1] - buckets), F32)], 1)
    extra = jnp.concatenate([extra[:8], wide], 0)
    emit(whole, outs, order, size, extra.astype(BF16))


def input_grad_kernel(chip_own, chip_other, x, gain, grad_hidden, out, gain_grad):
    half = out.shape[0]
    resid = x[own_rows(lax.axis_index("tensor") % 2, half), :].astype(F32)
    incoming = chip_own[...].astype(F32) + chip_other[...].astype(F32)
    added, gain_terms = norm_back(resid, gain[...], incoming)
    out[...] = (grad_hidden[...] + added).astype(BF16)
    gain_grad[...] = jnp.broadcast_to(gain_terms, gain_grad.shape)


def pass_on_kernel(keep, got, send_next, keep_next):
    count = keep_next.shape[0]
    for entry in range(count):
        keep_next[entry] = (keep[entry].astype(F32) + got[entry].astype(F32)).astype(BF16)
        send_next[entry] = (keep[count + entry].astype(F32) + got[count + entry].astype(F32)).astype(BF16)


def run(kernel, name, outs, ins, flops=0, scratch=(), scalars=0):
    shapes = [jax.ShapeDtypeStruct(shape, dtype) for shape, dtype in outs]
    moved = sum(item.size * item.dtype.itemsize for item in ins)
    moved += sum(item.size * item.dtype.itemsize for item in shapes)
    vmem = pl.BlockSpec(memory_space=pltpu.VMEM)
    smem = pl.BlockSpec(memory_space=pltpu.SMEM)
    result = pl.pallas_call(
        kernel,
        out_shape=shapes,
        in_specs=[smem] * scalars + [vmem] * (len(ins) - scalars),
        out_specs=[vmem] * len(shapes),
        scratch_shapes=[pltpu.VMEM(shape, dtype) for shape, dtype in scratch],
        compiler_params=pltpu.CompilerParams(vmem_limit_bytes=VMEM_LIMIT),
        cost_estimate=pl.CostEstimate(flops=int(flops), bytes_accessed=int(moved), transcendentals=0),
        name=name,
    )(*ins)
    return result[0] if len(shapes) == 1 else result


def to_core(value):
    return lax.ppermute(value, "tensor", [(i, i ^ 1) for i in range(lax.axis_size("tensor"))])


def to_chip(value):
    return lax.ppermute(value, "tensor", [(i, i ^ 2) for i in range(lax.axis_size("tensor"))])


def to_peer(value, bit):
    return lax.ppermute(value, "dp", [(i, i ^ (1 << bit)) for i in range(lax.axis_size("dp"))])


def add(left, right, name):
    return run(add_kernel, name, [(left.shape, left.dtype)], [left, right])


def scatter_sum(keep, send, order, name):
    for place, bit in enumerate(order):
        got = to_peer(send, bit)
        if place == len(order) - 1:
            return keep, got
        count, rows, columns = keep.shape
        shape = ((count // 2, rows, columns), BF16)
        send, keep = run(pass_on_kernel, f"{name}_{place}", [shape, shape], [keep, got])


def on_device(
    inputs, encoded, dec_len, enc_len, language, objective, distance_bucket, token_weights, cotangent,
    gain_self, self_query, self_key, self_value, self_output, bias_table,
    gain_cross, cross_query, cross_key, cross_value, cross_output, gain_ffn, ffn_up, ffn_down,
):
    seqs, length, width = inputs.shape
    half = length // 2
    columns = self_query.shape[1]
    heads = columns // HEAD_DIM
    units = ffn_up.shape[1]
    span_part = encoded.shape[1]
    span = span_part * lax.axis_size("tensor")
    dp = lax.axis_size("dp")
    size = width // dp
    bits = dp.bit_length() - 1
    halving = dp > 1 and dp == 1 << bits and size % 16 == 0
    if halving:
        along_x = tuple(range(bits))
        along_z = (1, 0) + tuple(range(2, bits)) if bits > 1 else along_x
    else:
        along_x = along_z = None

    def payload(order, extra=0):
        if order is None:
            return [((width + extra, width), BF16)]
        return [((dp // 2, size + extra, width), BF16)] * 2

    x = inputs.reshape(length, width)
    cot = cotangent.reshape(length, width)
    gain_one = gain_self.reshape(1, width)
    gain_two = gain_cross.reshape(1, width)
    gain_three = gain_ffn.reshape(1, width)
    bucket = distance_bucket.reshape(1, length)
    e0 = encoded.reshape(span_part, width)

    e1 = to_chip(e0)
    keep, send, normed_one, query_one, key_one, value_one, context_one, probs_one = run(
        self_forward_kernel, "self_forward",
        [((half, width), BF16)] * 2 + [((length, width), BF16)] + [((length, columns), BF16)] * 4
        + [((heads, length, length), BF16)],
        [dec_len, x, gain_one, self_query, self_key, self_value, self_output, bucket, bias_table],
        flops=2 * length * width * columns * 4 + 4 * length * length * columns,
        scratch=[((length, width), BF16)], scalars=1,
    )
    chip_one = add(keep, to_core(send), "self_sum")
    other_one = to_chip(chip_one)
    wk_peer = to_core(cross_key)
    wv_peer = to_core(cross_value)
    e2 = to_core(e0)
    e3 = to_core(e1)
    wq_peer = to_core(cross_query)
    wo_peer = to_core(cross_output)
    down_peer = to_core(ffn_down)
    up_peer = to_core(ffn_up)
    k_own, v_own, k_peer, v_peer = run(
        cross_source_kernel, "cross_source", [((span, columns), BF16)] * 4,
        [e0, e1, e2, e3, cross_key, cross_value, wk_peer, wv_peer], flops=8 * span * width * columns,
    )
    grad_full, branch_three, branch_three_peer, act_grad, act_grad_peer = run(
        out_grad_kernel, "out_grad",
        [((half, width), F32)] + [((half, width), BF16)] * 2 + [((half, units), F32)] * 2,
        [objective, language, dec_len, token_weights, cot, ffn_down, down_peer],
        flops=4 * half * width * units, scalars=3,
    )

    partial_two, hidden_one, normed_two, q_own, q_peer, context_two, probs_own, probs_peer, pack_forward = run(
        cross_forward_kernel, "cross_forward",
        [((half, width), BF16), ((half, width), F32), ((half, width), BF16)] + [((half, columns), BF16)] * 3
        + [((heads, half, span), BF16)] * 2 + [((half, width + columns), BF16)],
        [enc_len, chip_one, other_one, x, gain_two, cross_query, wq_peer, cross_output, wo_peer,
         k_own, v_own, k_peer, v_peer],
        flops=8 * half * width * columns + 8 * half * span * columns, scalars=1,
    )
    other_two = to_chip(partial_two)
    pack_forward_peer = to_core(pack_forward)

    partial_three, hidden_two, normed_three, act_own, grad_pre_own, pack_ffn = run(
        ffn_kernel, "ffn",
        [((half, width), BF16), ((half, width), F32), ((half, width), BF16)] + [((half, units), BF16)] * 2
        + [((half, width + 2 * units), BF16)],
        [partial_two, other_two, hidden_one, gain_three, ffn_up, up_peer, act_grad, act_grad_peer],
        flops=8 * half * width * units,
    )
    other_three = to_chip(partial_three)
    pack_ffn_peer = to_core(pack_ffn)
    branch_out = run(
        ffn_out_kernel, "ffn_out", [((half, width), BF16)], [act_own, pack_ffn, ffn_down, down_peer],
        flops=4 * half * width * units,
    )

    def ffn_weights(*refs):
        ffn_weights_kernel((along_x, along_z), size, *refs)

    ffn_payloads = run(
        ffn_weights, "ffn_weights", payload(along_x) + payload(along_z),
        [normed_three, pack_ffn_peer, act_own, grad_pre_own, branch_three, branch_three_peer],
        flops=8 * half * width * units,
        scratch=[((width, units), BF16), ((length, width), BF16), ((length, units), BF16)],
    )

    (partial_four, grad_two, gain_grad_three, gl_own, gl_peer, gc_own, gc_peer, gq_own, branch_two,
     pack_backward) = run(
        cross_backward_kernel, "cross_backward",
        [((half, width), BF16), ((half, width), F32), ((8, width), F32)] + [((heads, half, span), BF16)] * 2
        + [((half, columns), BF16)] * 3 + [((half, width), BF16), ((half, width + columns), BF16)],
        [partial_three, other_three, hidden_two, gain_three, grad_full, cross_output, wo_peer,
         k_own, v_own, k_peer, v_peer, probs_own, probs_peer, cross_query, wq_peer],
        flops=8 * half * width * columns + 8 * half * span * columns,
    )
    other_four = to_chip(partial_four)
    source_grad = run(
        cross_source_grad_kernel, "cross_source_grad", [((2 * span, columns), BF16)],
        [gl_peer, probs_peer, gc_peer, q_peer], flops=4 * half * span * columns,
    )
    source_grad_peer = to_core(source_grad)
    pack_backward_peer = to_core(pack_backward)
    other_out = to_chip(branch_out)
    out_own = run(layer_out_kernel, "layer_out", [((half, width), BF16)], [hidden_two, branch_out, other_out])
    layer_out = run(halves_kernel, "layer_out_halves", [((length, width), BF16)], [out_own, to_core(out_own)])

    def cross_weights(*refs):
        cross_weights_kernel(along_x, size, *refs)

    *cross_payload, encoded_keep, encoded_send = run(
        cross_weights, "cross_weights", payload(along_x) + [((span // 2, width), BF16)] * 2,
        [gl_own, probs_own, gc_own, q_own, source_grad_peer, e0, e1, e2, e3, normed_two, pack_forward_peer,
         branch_two, pack_backward_peer, context_two, gq_own, cross_key, cross_value],
        flops=4 * half * span * columns + 4 * span * width * columns + 4 * span * width * columns,
        scratch=[((width, 4 * columns), BF16), ((span, width), BF16), ((span, 2 * columns), BF16)],
    )

    grad_one, pack_self = run(
        self_norm_kernel, "self_norm", [((half, width), F32), ((half + EXTRA, width), BF16)],
        [partial_four, other_four, hidden_one, gain_two, grad_two, gain_grad_three],
    )
    pack_self_peer = to_core(pack_self)
    keep, send, branch_one, gq_one, gk_one, gv_one, gl_one = run(
        self_backward_kernel, "self_backward",
        [((half, width), BF16)] * 2 + [((length, width), BF16)] + [((length, columns), BF16)] * 3
        + [((heads, length, length), BF16)],
        [pack_self, pack_self_peer, self_output, self_query, self_key, self_value, query_one, key_one, value_one,
         probs_one],
        flops=8 * length * width * columns + 8 * length * length * columns,
        scratch=[((length, width), BF16)],
    )
    chip_five = add(keep, to_core(send), "input_sum")
    other_five = to_chip(chip_five)

    def self_weights(*refs):
        self_weights_kernel(along_x, size, *refs)

    self_payload = run(
        self_weights, "self_weights", payload(along_x, EXTRA),
        [normed_one, branch_one, gq_one, gk_one, gv_one, context_one, gl_one, bucket, pack_self, pack_self_peer],
        flops=8 * length * width * columns + 2 * heads * length**3,
        scratch=[((width, 4 * columns), BF16), ((2 * length, 2 * columns), BF16), ((2 * length, width), BF16)],
    )
    if not isinstance(self_payload, (list, tuple)):
        self_payload = [self_payload]

    encoded_part, encoded_pass = run(
        encoded_sum_kernel, "encoded_sum", [((span_part, width), BF16)] * 2, [encoded_keep, to_core(encoded_send)]
    )
    encoded_grad = add(encoded_part, to_chip(encoded_pass), "encoded_grad")

    input_own, gain_terms = run(
        input_grad_kernel, "input_grad", [((half, width), BF16), ((8, width), F32)],
        [chip_five, other_five, x, gain_one, grad_one],
    )
    input_grad = run(halves_kernel, "input_grad_halves", [((length, width), BF16)], [input_own, to_core(input_own)])
    gain_terms = add(gain_terms, to_core(gain_terms), "gain_core")

    if halving:
        for bit in along_x:
            gain_terms = add(gain_terms, to_peer(gain_terms, bit), f"gain_{bit}")
        last = [
            scatter_sum(*ffn_payloads[:2], along_x, "up"),
            scatter_sum(*ffn_payloads[2:], along_z, "down"),
            scatter_sum(*cross_payload, along_x, "cross"),
            scatter_sum(*self_payload, along_x, "self"),
        ]
        up, down, cross, own = ((left[0].astype(F32) + right[0].astype(F32)) for left, right in last)
    else:
        gain_terms = lax.psum(gain_terms, "dp")
        up, down, cross = (
            lax.psum_scatter(item.astype(F32), "dp", scatter_dimension=0, tiled=True)
            for item in (ffn_payloads[0], ffn_payloads[1], cross_payload[0])
        )
        item = self_payload[0].astype(F32)
        own = lax.psum_scatter(item[:width], "dp", scatter_dimension=0, tiled=True)
        own = jnp.concatenate([own, lax.psum(item[width:], "dp")], 0)

    index = lax.axis_index("dp")

    def gain_part(row):
        return lax.dynamic_slice(row, (index * size,), (size,))

    return (
        layer_out.reshape(seqs, length, width),
        input_grad.reshape(seqs, length, width),
        encoded_grad.reshape(seqs, span_part, width),
        gain_part(gain_terms[0]),
        own[:size, :columns],
        own[:size, columns : 2 * columns],
        own[:size, 2 * columns : 3 * columns],
        own[:size, 3 * columns :].T,
        own[size + 8 : size + 8 + heads, : bias_table.shape[0]].T,
        gain_part(own[size]),
        cross[:, 2 * columns : 3 * columns],
        cross[:, :columns],
        cross[:, columns : 2 * columns],
        cross[:, 3 * columns :].T,
        gain_part(own[size + 1]),
        up,
        down.T,
    )


def solution(mesh):
    return jax.shard_map(
        on_device,
        mesh=mesh,
        in_specs=(
            P("dp", None, None),
            P("dp", "tensor", None),
            P("dp"),
            P("dp"),
            P("dp"),
            P("dp"),
            P(),
            P(),
            P("dp", None, None),
            P(),
            P(None, "tensor"),
            P(None, "tensor"),
            P(None, "tensor"),
            P("tensor", None),
            P(None, "tensor"),
            P(),
            P(None, "tensor"),
            P(None, "tensor"),
            P(None, "tensor"),
            P("tensor", None),
            P(),
            P(None, "tensor"),
            P("tensor", None),
        ),
        out_specs=(
            P("dp", None, None),
            P("dp", None, None),
            P("dp", "tensor", None),
            P("dp"),
            P("dp", "tensor"),
            P("dp", "tensor"),
            P("dp", "tensor"),
            P("tensor", "dp"),
            P(None, "tensor"),
            P("dp"),
            P("dp", "tensor"),
            P("dp", "tensor"),
            P("dp", "tensor"),
            P("tensor", "dp"),
            P("dp"),
            P("dp", "tensor"),
            P("tensor", "dp"),
        ),
        check_vma=False,
    )
```

time: 1150 us -> 170 us (0.15)
  waiting for transfers between devices: 758 us -> 69.1 us
  local copies, waits for them, and re-layouts: 264 us -> 24.3 us
  blocking collectives: 47.3 us -> 0 us
  matrix products: 41.7 us -> 0 us
  starting transfers between devices: 1.07 us -> 39.1 us
  Pallas kernels: 0 us -> 30.6 us
  other arithmetic: 20.2 us -> 2.48 us
  between operations: 18.3 us -> 3.74 us
    reduce_scatter x7 -> x0, waiting for transfers between devices: 432 us -> none  [the longest x1 73.3 us: on_device(): lax.psum_scatter(grad_ffn_up, 'dp', scatter_dimension=0, tiled=True)]
    gather x2 -> x0, local copies, waits for them, and re-layouts: 236 us -> none  [on_device(): bias_self = jnp.transpose(distance_bias[offset], (2, 0, 1))]
    unnamed x20 -> x0, waiting for transfers between devices: 212 us -> none
    psum x5 -> x0, waiting for transfers between devices: 115 us -> none  [the longest x2 61.6 us: back_sum(): lax.psum(partial_value.astype(jnp.bfloat16), 'tensor').astype(jnp.float32)]
    ppermute x0 -> x42, waiting for transfers between devices: none -> 69.1 us  [the longest x15 51.9 us: to_peer(): lax.ppermute(value, 'dp', [(i, i ^ 1 << bit) for i in range(lax.axis_size...]
    ppermute x0 -> x42, starting transfers between devices: none -> 39.1 us  [the longest x15 22.4 us: to_peer(): lax.ppermute(value, 'dp', [(i, i ^ 1 << bit) for i in range(lax.axis_size...]
    unnamed x1 -> x0, blocking collectives: 37.2 us -> none
    dot_general x43 -> x0, matrix products: 36.9 us -> none  [the longest x6 10.3 us: weight_grad(): jnp.einsum('rd,rk->dk', rows, grads, preferred_element_type=jnp.float32)]
  transfers between devices with their start and end apart: 16 -> 42, of which waited for: 15 -> 15; matrix products, arithmetic and copies ran while one was open for 5% -> 7% of each run, Pallas kernels for 0% -> 15%
where the time goes in v1:
time: 170 us; the launch traced here: 169 us
  waiting for transfers between devices  69.1 us (41%)
  starting transfers between devices  39.1 us (23%)
  Pallas kernels  30.6 us (18%)
  local copies, waits for them, and re-layouts  24.3 us (14%)
  between operations  3.74 us (2%)
  other arithmetic  2.48 us (1%)
    ppermute x15, waiting for transfers between devices, to_peer(): lax.ppermute(value, 'dp', [(i, i ^ 1 << bit) for i in range(lax.axis_size...  51.9 us
    pallas_call x33, Pallas kernels, run(): pl.pallas_call(kernel, out_shape=shapes, in_specs=[smem] * scalars + [vme...  30.6 us
    ppermute x15, starting transfers between devices, to_peer(): lax.ppermute(value, 'dp', [(i, i ^ 1 << bit) for i in range(lax.axis_size...  22.4 us
    unnamed x85, local copies, waits for them, and re-layouts  20.3 us
    ppermute x8, waiting for transfers between devices, to_chip(): lax.ppermute(value, 'tensor', [(i, i ^ 2) for i in range(lax.axis_size('t...  15.1 us
    ppermute x8, starting transfers between devices, to_chip(): lax.ppermute(value, 'tensor', [(i, i ^ 2) for i in range(lax.axis_size('t...  12.3 us
    ppermute x19, starting transfers between devices, to_core(): lax.ppermute(value, 'tensor', [(i, i ^ 1) for i in range(lax.axis_size('t...  4.45 us
  transfers between devices with their start and end apart: 42, of which 15 were waited for; matrix products, arithmetic and copies ran while one was open for 7% of the time, Pallas kernels for 15%

profile of v1, /device:TPU:0, one launch (start us, length us, event | category | flops | bytes accessed | tf_op | source)
XLA Modules:
  0.0 169.4 jit_solution(11343954002680072609)
XLA Ops:
  2.7 1.1 copy.40.w_query
  3.8 1.1 copy.41.w_key
  5.2 2.7 %self_forward.1 = (bf16[128,768]{1,0:T(8,128)(2,1)S(1)}, bf16[128,768]{1,0:T(8,128)(2,1)}, bf16[256,768]{1,0:T(8,128)(2,1)S(1)}, bf16[256,192]{1,0:T(8,128)(2,1)...) custom-call(s32[1]{0:T(128)S(6)} %copy.58.dec_len, ...), custom_call_target="tpu_custom_call" | custom-call | flops 352321536 | bytes 3150212 | tf_op jit(solution)/shard_map/self_forward/pallas_call | solution.py:497
  7.9 0.8 copy-done.10
  8.6 0.7 copy-done.12
  13.1 2.6 %collective-permute-start.4 = (bf16[128,768]{1,0:T(8,128)(2,1)}, bf16[128,768]{1,0:T(8,128)(2,1)}, u32[]{:S(2)}, u32[]{:S(2)}) collective-permute-start(bf16[128,768]{1,0:T(8,128)(2,1)} %bitcast.2.e0.refs_5_), channel_id=1, source_target_pairs={{0,2},{1,3},{2,0},{3,1},{4,6},{5,7},{6,4},{7,5},{8,10},{9,11},{10,... | collective-permute-start | bytes 589832 | tf_op jit(solution)/shard_map/ppermute | solution.py:515
  15.7 1.1 copy.47.wk_own.refs_15_
  17.1 1.9 %copy.48.wv_own.refs_16_ = bf16[768,192]{1,0:T(8,128)(2,1)} copy(bf16[768,192]{0,1:T(8,128)(2,1)} %param.41) | data formatting | bytes 589824 | tf_op args[18]
  20.0 1.5 collective-permute-done.4.e1.refs_6_
  21.5 1.6 collective-permute-done.5.e2.refs_7_
  24.0 1.1 copy.49.wq_own
  25.7 0.9 copy-done.19
  26.6 0.9 copy-done.21
  27.6 1.8 %collective-permute-start.1 = (bf16[128,768]{1,0:T(8,128)(2,1)S(1)}, bf16[128,768]{1,0:T(8,128)(2,1)S(1)}, u32[]{:S(2)}, u32[]{:S(2)}) collective-permute-start(bf16[128,768]{1,0:T(8,128)(2,1)S(1)} %self_sum.1.chip_own), channel_id=1, source_target_pairs={{0,2},{1,3},{2,0},{3,1},{4,6},{5,7},{6,4},{7,5},{8,10},{9,11},{10,... | collective-permute-start | bytes 589832 | tf_op jit(solution)/shard_map/ppermute | solution.py:515
  30.1 0.9 copy-done.7
  31.1 2.5 %cross_source.1 = (bf16[512,192]{1,0:T(8,128)(2,1)S(1)}, bf16[512,192]{1,0:T(8,128)(2,1)S(1)}, bf16[512,192]{1,0:T(8,128)(2,1)S(1)}, bf16[512,192]{1,0:T(8,128)(2,1)S(1)}) custom-call(bf16[128,768]{1,0:T(8,128)(2,1)} %bitcast.2.e0.refs_5_, bf16[128,768]{1,0:T(8,128)(2,1)} %collective-permute-done.4.e1.refs_6_, bf16[128,768]{1,0:T(8,128)(2,1)S(1)} %copy-done.7, ...), custom_call_target="tpu_custom_call" | custom-call | flops 603979776 | bytes 2752512 | tf_op jit(solution)/shard_map/cross_source/pallas_call | solution.py:497
  33.6 1.3 collective-permute-done.1.chip_other
  34.9 3.0 %cross_forward.1 = (bf16[128,768]{1,0:T(8,128)(2,1)S(1)}, f32[128,768]{1,0:T(8,128)S(1)}, bf16[128,768]{1,0:T(8,128)(2,1)S(1)}, bf16[128,192]{1,0:T(8,128)(2,1)S...) custom-call(s32[1]{0:T(128)S(6)} %copy.59.enc_len, ...), custom_call_target="tpu_custom_call" | custom-call | flops 251658240 | bytes 4721668 | tf_op jit(solution)/shard_map/cross_forward/pallas_call | solution.py:497
  37.9 1.8 %collective-permute-start.9 = (bf16[128,768]{1,0:T(8,128)(2,1)S(1)}, bf16[128,768]{1,0:T(8,128)(2,1)S(1)}, u32[]{:S(2)}, u32[]{:S(2)}) collective-permute-start(bf16[128,768]{1,0:T(8,128)(2,1)S(1)} %get-tuple-element.104.chip_own), channel_id=1, source_target_pairs={{0,2},{1,3},{2,0},{3,1},{4,6},{5,7},{6,4},{7,5},{8,10},{9,11},{10,... | collective-permute-start | bytes 589832 | tf_op jit(solution)/shard_map/ppermute | solution.py:515
  41.1 0.9 out_grad.1
  42.0 2.4 %collective-permute-done.9.chip_other = bf16[128,768]{1,0:T(8,128)(2,1)S(1)} collective-permute-done((bf16[128,768]{1,0:T(8,128)(2,1)S(1)}, bf16[128,768]{1,0:T(8,128)(2,1)S(1)}, u32[]{:S(2)}, u32[]{:S(2)}) %collective-permute-start.9) | collective-permute-done | bytes 196640 | tf_op jit(solution)/shard_map/ppermute | solution.py:515
  44.3 2.9 %ffn.1 = (bf16[128,768]{1,0:T(8,128)(2,1)S(1)}, f32[128,768]{1,0:T(8,128)S(1)}, bf16[128,768]{1,0:T(8,128)(2,1)S(1)}, bf16[128,768]{1,0:T(8,128)(2,1)S(1)}, bf16...) custom-call(bf16[128,768]{1,0:T(8,128)(2,1)S(1)} %get-tuple-element.104.chip_own, ...), custom_call_target="tpu_custom_call" | custom-call | flops 603979776 | bytes 5704704 | tf_op jit(solution)/shard_map/ffn/pallas_call | solution.py:497
  47.3 1.8 %collective-permute-start.14 = (bf16[128,768]{1,0:T(8,128)(2,1)S(1)}, bf16[128,768]{1,0:T(8,128)(2,1)S(1)}, u32[]{:S(2)}, u32[]{:S(2)}) collective-permute-start(bf16[128,768]{1,0:T(8,128)(2,1)S(1)} %get-tuple-element.111.chip_own), channel_id=1, source_target_pairs={{0,2},{1,3},{2,0},{3,1},{4,6},{5,7},{6,4},{7,5},{8,10},{9,11},{10,... | collective-permute-start | bytes 589832 | tf_op jit(solution)/shard_map/ppermute | solution.py:515
  49.0 3.9 %collective-permute-done.14.chip_other = bf16[128,768]{1,0:T(8,128)(2,1)S(1)} collective-permute-done((bf16[128,768]{1,0:T(8,128)(2,1)S(1)}, bf16[128,768]{1,0:T(8,128)(2,1)S(1)}, u32[]{:S(2)}, u32[]{:S(2)}) %collective-permute-start.14) | collective-permute-done | bytes 196640 | tf_op jit(solution)/shard_map/ppermute | solution.py:515
  53.0 2.7 %cross_backward.1 = (bf16[128,768]{1,0:T(8,128)(2,1)S(1)}, f32[128,768]{1,0:T(8,128)S(1)}, f32[8,768]{1,0:T(8,128)S(1)}, bf16[3,128,512]{2,1,0:T(8,128)(2,1)S(1)...) custom-call(bf16[128,768]{1,0:T(8,128)(2,1)S(1)} %get-tuple-element., ...), custom_call_target="tpu_custom_call" | custom-call | flops 251658240 | bytes 5925888 | tf_op jit(solution)/shard_map/cross_backward/pallas_call | solution.py:497
  55.7 1.8 %collective-permute-start.15 = (bf16[128,768]{1,0:T(8,128)(2,1)S(1)}, bf16[128,768]{1,0:T(8,128)(2,1)S(1)}, u32[]{:S(2)}, u32[]{:S(2)}) collective-permute-start(bf16[128,768]{1,0:T(8,128)(2,1)S(1)} %get-tuple-element.115.chip_own), channel_id=1, source_target_pairs={{0,2},{1,3},{2,0},{3,1},{4,6},{5,7},{6,4},{7,5},{8,10},{9,11},{10,... | collective-permute-start | bytes 589832 | tf_op jit(solution)/shard_map/ppermute | solution.py:515
  58.5 3.0 %collective-permute-done.15.chip_other = bf16[128,768]{1,0:T(8,128)(2,1)S(1)} collective-permute-done((bf16[128,768]{1,0:T(8,128)(2,1)S(1)}, bf16[128,768]{1,0:T(8,128)(2,1)S(1)}, u32[]{:S(2)}, u32[]{:S(2)}) %collective-permute-start.15) | collective-permute-done | bytes 196640 | tf_op jit(solution)/shard_map/ppermute | solution.py:515
  63.3 1.7 %collective-permute-start.12 = (bf16[128,768]{1,0:T(8,128)(2,1)S(1)}, bf16[128,768]{1,0:T(8,128)(2,1)S(1)}, u32[]{:S(2)}, u32[]{:S(2)}) collective-permute-start(bf16[128,768]{1,0:T(8,128)(2,1)S(1)} %ffn_out.1.chip_own), channel_id=1, source_target_pairs={{0,2},{1,3},{2,0},{3,1},{4,6},{5,7},{6,4},{7,5},{8,10},{9,11},{10,... | collective-permute-start | bytes 589832 | tf_op jit(solution)/shard_map/ppermute | solution.py:515
  65.0 1.8 %self_backward.1 = (bf16[128,768]{1,0:T(8,128)(2,1)S(1)}, bf16[128,768]{1,0:T(8,128)(2,1)S(1)}, bf16[256,768]{1,0:T(8,128)(2,1)S(1)}, bf16[256,192]{1,0:T(8,128)...) custom-call(bf16[144,768]{1,0:T(8,128)(2,1)S(1)} %get-tuple-element.118.pack, ...), custom_call_target="tpu_custom_call" | custom-call | flops 402653184 | bytes 3784704 | tf_op jit(solution)/shard_map/self_backward/pallas_call | solution.py:497
  67.0 3.2 %cross_weights.1 = (bf16[4,96,768]{2,1,0:T(8,128)(2,1)S(1)}, bf16[4,96,768]{2,1,0:T(8,128)(2,1)S(1)}, bf16[256,768]{1,0:T(8,128)(2,1)S(1)}, bf16[256,768]{1,0:T(8,128)(2,1)S(1)}) custom-call(bf16[3,128,512]{2,1,0:T(8,128)(2,1)S(1)} %get-tuple-element.127.refs_0_, bf16[3,128,512]{2,1,0:T(8,128)(2,1)S(1)} %get-tuple-element.113.probs_own.refs_1_, ...), custom_call_target="tpu_custom_call" | custom-call | flops 654311424 | bytes 5603328 | tf_op jit(solution)/shard_map/cross_weights/pallas_call | solution.py:497
  70.2 1.6 collective-permute-start.32
  72.7 1.0 ffn_weights.1
  73.7 1.1 collective-permute-start.36
  74.8 1.6 collective-permute-start.39
  76.4 3.0 %collective-permute-done.18.chip_other = bf16[128,768]{1,0:T(8,128)(2,1)S(1)} collective-permute-done((bf16[128,768]{1,0:T(8,128)(2,1)S(1)}, bf16[128,768]{1,0:T(8,128)(2,1)S(1)}, u32[]{:S(2)}, u32[]{:S(2)}) %collective-permute-start.18) | collective-permute-done | bytes 196640 | tf_op jit(solution)/shard_map/ppermute | solution.py:515
  80.2 2.2 %self_weights.1 = (bf16[4,112,768]{2,1,0:T(8,128)(2,1)S(1)}, bf16[4,112,768]{2,1,0:T(8,128)(2,1)}) custom-call(bf16[256,768]{1,0:T(8,128)(2,1)S(1)} %copy-done.11, bf16[256,768]{1,0:T(8,128)(2,1)S(1)} %get-tuple-element.145.refs_1_, bf16[256,192]{1,0:T(8,128)(2,1)S(1)} %get-tuple-element.146.refs_2_, bf16[256,192]{1,0:T(8,128)(2,1)S(1)} %get-tuple-element.147.refs_3_, ...), custom_call_target="tpu_custom_call" | custom-call | flops 402653184 | bytes 3392512 | tf_op jit(solution)/shard_map/self_weights/pallas_call | solution.py:497
  82.9 3.4 %collective-permute-done.32.got = bf16[4,96,768]{2,1,0:T(8,128)(2,1)S(1)} collective-permute-done((bf16[4,96,768]{2,1,0:T(8,128)(2,1)S(1)}, bf16[4,96,768]{2,1,0:T(8,128)(2,1)S(1)}, u32[]{:S(2)}, u32[]{:S(2)}) %collective-permute-start.32) | collective-permute-done | bytes 589856 | tf_op jit(solution)/shard_map/ppermute | solution.py:519
  86.4 1.5 collective-permute-start.26
  88.0 25.9 %collective-permute-done.26.right_ref = f32[8,768]{1,0:T(8,128)S(1)} collective-permute-done((f32[8,768]{1,0:T(8,128)S(1)}, f32[8,768]{1,0:T(8,128)S(1)}, u32[]{:S(2)}, u32[]{:S(2)}) %collective-permute-start.26) | collective-permute-done | bytes 24608 | tf_op jit(solution)/shard_map/ppermute | solution.py:519
  113.9 1.6 collective-permute-start.33
  116.1 6.9 %collective-permute-done.27.right_ref = f32[8,768]{1,0:T(8,128)S(1)} collective-permute-done((f32[8,768]{1,0:T(8,128)S(1)}, f32[8,768]{1,0:T(8,128)S(1)}, u32[]{:S(2)}, u32[]{:S(2)}) %collective-permute-start.27) | collective-permute-done | bytes 24608 | tf_op jit(solution)/shard_map/ppermute | solution.py:519
  123.2 2.8 %collective-permute-start.28 = (f32[8,768]{1,0:T(8,128)S(1)}, f32[8,768]{1,0:T(8,128)S(1)}, u32[]{:S(2)}, u32[]{:S(2)}) collective-permute-start(f32[8,768]{1,0:T(8,128)S(1)} %gain_1.1.left_ref), channel_id=1, source_target_pairs={{0,16},{4,20},{8,24},{12,28},{16,0},{20,4},{24,8},{28,12},{1,17},{... | collective-permute-start | bytes 73736 | tf_op jit(solution)/shard_map/ppermute | solution.py:519
  126.0 0.8 up_0.1
  126.8 1.6 collective-permute-start.37
  128.4 0.8 down_0.1
  129.2 1.5 collective-permute-start.40
  132.7 1.8 %collective-permute-start.34 = (bf16[1,96,768]{2,1,0:T(8,128)(2,1)}, bf16[1,96,768]{2,1,0:T(8,128)(2,1)}, u32[]{:S(2)}, u32[]{:S(2)}) collective-permute-start(bf16[1,96,768]{2,1,0:T(8,128)(2,1)} %get-tuple-element.162), channel_id=1, source_target_pairs={{0,16},{4,20},{8,24},{12,28},{16,0},{20,4},{24,8},{28,12},{1,17},{... | collective-permute-start | bytes 442376 | tf_op jit(solution)/shard_map/ppermute | solution.py:519
  134.5 0.8 layer_out_halves.1
  135.9 0.9 copy-done.15
  136.8 0.9 copy-done.17
  138.5 1.7 %input_grad_halves.1 = bf16[256,768]{1,0:T(8,128)(2,1)} custom-call(bf16[128,768]{1,0:T(8,128)(2,1)S(1)} %get-tuple-element.126.own, bf16[128,768]{1,0:T(8,128)(2,1)} %collective-permute-done.19.peer), custom_call_target="tpu_custom_call" | custom-call | bytes 786432 | tf_op jit(solution)/shard_map/input_grad_halves/pallas_call | solution.py:497
  140.4 1.7 %collective-permute-start.30 = (bf16[2,112,768]{2,1,0:T(8,128)(2,1)S(1)}, bf16[2,112,768]{2,1,0:T(8,128)(2,1)S(1)}, u32[]{:S(2)}, u32[]{:S(2)}) collective-permute-start(bf16[2,112,768]{2,1,0:T(8,128)(2,1)S(1)} %get-tuple-element.154), channel_id=1, source_target_pairs={{0,8},{4,12},{8,0},{12,4},{16,24},{20,28},{24,16},{28,20},{1,9},{5... | collective-permute-start | bytes 1032200 | tf_op jit(solution)/shard_map/ppermute | solution.py:519
  142.6 2.7 %collective-permute-start.41 = (bf16[1,96,768]{2,1,0:T(8,128)(2,1)S(1)}, bf16[1,96,768]{2,1,0:T(8,128)(2,1)S(1)}, u32[]{:S(2)}, u32[]{:S(2)}) collective-permute-start(bf16[1,96,768]{2,1,0:T(8,128)(2,1)S(1)} %get-tuple-element.178), channel_id=1, source_target_pairs={{0,16},{4,20},{8,24},{12,28},{16,0},{20,4},{24,8},{28,12},{1,17},{... | collective-permute-start | bytes 442376 | tf_op jit(solution)/shard_map/ppermute | solution.py:519
  145.3 0.9 add_bitcast_fusion.2
  146.2 0.7 slice_bitcast_fusion
  147.0 0.7 copy.57
  147.7 5.9 %collective-permute-done.38 = bf16[1,96,768]{2,1,0:T(8,128)(2,1)S(1)} collective-permute-done((bf16[1,96,768]{2,1,0:T(8,128)(2,1)S(1)}, bf16[1,96,768]{2,1,0:T(8,128)(2,1)S(1)}, u32[]{:S(2)}, u32[]{:S(2)}) %collective-permute-start.38) | collective-permute-done | bytes 147488 | tf_op jit(solution)/shard_map/ppermute | solution.py:519
  153.6 0.7 add_bitcast_fusion.1
  154.4 1.8 %collective-permute-done.30.got = bf16[2,112,768]{2,1,0:T(8,128)(2,1)S(1)} collective-permute-done((bf16[2,112,768]{2,1,0:T(8,128)(2,1)S(1)}, bf16[2,112,768]{2,1,0:T(8,128)(2,1)S(1)}, u32[]{:S(2)}, u32[]{:S(2)}) %collective-permute-start.30) | collective-permute-done | bytes 344096 | tf_op jit(solution)/shard_map/ppermute | solution.py:519
  156.3 1.6 collective-permute-start.31
  158.3 0.7 add_bitcast_fusion
  159.1 7.5 %collective-permute-done.31 = bf16[1,112,768]{2,1,0:T(8,128)(2,1)S(1)} collective-permute-done((bf16[1,112,768]{2,1,0:T(8,128)(2,1)S(1)}, bf16[1,112,768]{2,1,0:T(8,128)(2,1)S(1)}, u32[]{:S(2)}, u32[]{:S(2)}) %collective-permute-start.31) | collective-permute-done | bytes 172064 | tf_op jit(solution)/shard_map/ppermute | solution.py:519
  166.7 0.8 slice_bitcast_fusion.1
  168.0 0.7 copy.56
  (152 shorter events, 19.9 us)
Async XLA Ops:
  0.7 4.3 %copy-start.34 = (bf16[768,192]{0,1:T(8,128)(2,1)S(1)}, bf16[768,192]{0,1:T(8,128)(2,1)}, u32[]{:S(2)}) copy-start(bf16[768,192]{0,1:T(8,128)(2,1)} %param.35) | copy-start | bytes 884740
  0.7 4.4 %copy-start.37 = (f32[32,3]{0,1:T(4,128)S(1)}, f32[32,3]{0,1:T(4,128)}, u32[]{:S(2)}) copy-start(f32[32,3]{0,1:T(4,128)} %param.37) | copy-start | bytes 1156
  0.7 4.5 %copy-start.1 = (bf16[1,256,768]{2,1,0:T(8,128)(2,1)S(1)}, bf16[1,256,768]{2,1,0:T(8,128)(2,1)}, u32[]{:S(2)}) copy-start(bf16[1,256,768]{2,1,0:T(8,128)(2,1)} %param.23) | copy-start | bytes 1179652
  0.7 4.5 %copy-start.4 = (bf16[192,768]{1,0:T(8,128)(2,1)S(1)}, bf16[192,768]{1,0:T(8,128)(2,1)}, u32[]{:S(2)}) copy-start(bf16[192,768]{1,0:T(8,128)(2,1)} %w_output.3) | copy-start | bytes 884740
  0.7 4.5 %copy-start.33 = (s32[256]{0:T(256)S(1)}, s32[256]{0:T(256)}, u32[]{:S(2)}) copy-start(s32[256]{0:T(256)} %param.29) | copy-start | bytes 3076
  0.7 40.3 %collective-permute-start.11 = (bf16[768,768]{1,0:T(8,128)(2,1)}, bf16[768,768]{1,0:T(8,128)(2,1)S(1)}, u32[]{:S(2)}, u32[]{:S(2)}) collective-permute-start(bf16[768,768]{1,0:T(8,128)(2,1)} %down_own.3), channel_id=1, source_target_pairs={{0,1},{1,0},{2,3},{3,2},{4,5},{5,4},{6,7},{7,6},{8,9},{9,8},{10,11... | collective-permute-start | bytes 3538952 | tf_op jit(solution)/shard_map/ppermute | solution.py:511
  1.2 43.1 %collective-permute-start.10 = (bf16[768,768]{1,0:T(8,128)(2,1)}, bf16[768,768]{1,0:T(8,128)(2,1)}, u32[]{:S(2)}, u32[]{:S(2)}) collective-permute-start(bf16[768,768]{1,0:T(8,128)(2,1)} %up_own.1), channel_id=1, source_target_pairs={{0,1},{1,0},{2,3},{3,2},{4,5},{5,4},{6,7},{7,6},{8,9},{9,8},{10,11... | collective-permute-start | bytes 3538952 | tf_op jit(solution)/shard_map/ppermute | solution.py:511
  12.7 6.3 %collective-permute-start = (bf16[128,768]{1,0:T(8,128)(2,1)}, bf16[128,768]{1,0:T(8,128)(2,1)S(1)}, u32[]{:S(2)}, u32[]{:S(2)}) collective-permute-start(bf16[128,768]{1,0:T(8,128)(2,1)} %get-tuple-element.99), channel_id=1, source_target_pairs={{0,1},{1,0},{2,3},{3,2},{4,5},{5,4},{6,7},{7,6},{8,9},{9,8},{10,11... | collective-permute-start | bytes 589832 | tf_op jit(solution)/shard_map/ppermute | solution.py:511
  13.1 17.0 %copy-start.35 = (f32[768]{0:T(1024)S(1)}, f32[768]{0:T(1024)}, u32[]{:S(2)}) copy-start(f32[768]{0:T(1024)} %param.38) | copy-start | bytes 9220
  13.1 8.4 %collective-permute-start.4 = (bf16[128,768]{1,0:T(8,128)(2,1)}, bf16[128,768]{1,0:T(8,128)(2,1)}, u32[]{:S(2)}, u32[]{:S(2)}) collective-permute-start(bf16[128,768]{1,0:T(8,128)(2,1)} %bitcast.2.e0.refs_5_), channel_id=1, source_target_pairs={{0,2},{1,3},{2,0},{3,1},{4,6},{5,7},{6,4},{7,5},{8,10},{9,11},{10,... | collective-permute-start | bytes 589832 | tf_op jit(solution)/shard_map/ppermute | solution.py:515
  16.8 8.3 %collective-permute-start.7 = (bf16[768,192]{1,0:T(8,128)(2,1)S(1)}, bf16[768,192]{1,0:T(8,128)(2,1)}, u32[]{:S(2)}, u32[]{:S(2)}) collective-permute-start(bf16[768,192]{1,0:T(8,128)(2,1)S(1)} %copy.47.wk_own.refs_15_), channel_id=1, source_target_pairs={{0,1},{1,0},{2,3},{3,2},{4,5},{5,4},{6,7},{7,6},{8,9},{9,8},{10,11... | collective-permute-start | bytes 884744 | tf_op jit(solution)/shard_map/ppermute | solution.py:511
  19.6 5.9 %collective-permute-start.8 = (bf16[768,192]{1,0:T(8,128)(2,1)}, bf16[768,192]{1,0:T(8,128)(2,1)}, u32[]{:S(2)}, u32[]{:S(2)}) collective-permute-start(bf16[768,192]{1,0:T(8,128)(2,1)} %copy.48.wv_own.refs_16_), channel_id=1, source_target_pairs={{0,1},{1,0},{2,3},{3,2},{4,5},{5,4},{6,7},{7,6},{8,9},{9,8},{10,11... | collective-permute-start | bytes 884744 | tf_op jit(solution)/shard_map/ppermute | solution.py:511
  21.5 1.7 collective-permute-start.5
  23.8 3.8 %collective-permute-start.6 = (bf16[128,768]{1,0:T(8,128)(2,1)}, bf16[128,768]{1,0:T(8,128)(2,1)}, u32[]{:S(2)}, u32[]{:S(2)}) collective-permute-start(bf16[128,768]{1,0:T(8,128)(2,1)} %collective-permute-done.4.e1.refs_6_), channel_id=1, source_target_pairs={{0,1},{1,0},{2,3},{3,2},{4,5},{5,4},{6,7},{7,6},{8,9},{9,8},{10,11... | collective-permute-start | bytes 589832 | tf_op jit(solution)/shard_map/ppermute | solution.py:511
  25.1 8.4 %collective-permute-start.2 = (bf16[768,192]{1,0:T(8,128)(2,1)S(1)}, bf16[768,192]{1,0:T(8,128)(2,1)S(1)}, u32[]{:S(2)}, u32[]{:S(2)}) collective-permute-start(bf16[768,192]{1,0:T(8,128)(2,1)S(1)} %copy.49.wq_own), channel_id=1, source_target_pairs={{0,1},{1,0},{2,3},{3,2},{4,5},{5,4},{6,7},{7,6},{8,9},{9,8},{10,11... | collective-permute-start | bytes 884744 | tf_op jit(solution)/shard_map/ppermute | solution.py:511
  25.6 8.0 %collective-permute-start.3 = (bf16[192,768]{1,0:T(8,128)(2,1)}, bf16[192,768]{1,0:T(8,128)(2,1)S(1)}, u32[]{:S(2)}, u32[]{:S(2)}) collective-permute-start(bf16[192,768]{1,0:T(8,128)(2,1)} %wo_own.3), channel_id=1, source_target_pairs={{0,1},{1,0},{2,3},{3,2},{4,5},{5,4},{6,7},{7,6},{8,9},{9,8},{10,11... | collective-permute-start | bytes 884744 | tf_op jit(solution)/shard_map/ppermute | solution.py:511
  27.6 7.3 %collective-permute-start.1 = (bf16[128,768]{1,0:T(8,128)(2,1)S(1)}, bf16[128,768]{1,0:T(8,128)(2,1)S(1)}, u32[]{:S(2)}, u32[]{:S(2)}) collective-permute-start(bf16[128,768]{1,0:T(8,128)(2,1)S(1)} %self_sum.1.chip_own), channel_id=1, source_target_pairs={{0,2},{1,3},{2,0},{3,1},{4,6},{5,7},{6,4},{7,5},{8,10},{9,11},{10,... | collective-permute-start | bytes 589832 | tf_op jit(solution)/shard_map/ppermute | solution.py:515
  31.1 3.8 %copy-start.2 = (bf16[192,768]{1,0:T(8,128)(2,1)S(1)}, bf16[192,768]{1,0:T(8,128)(2,1)}, u32[]{:S(2)}) copy-start(bf16[192,768]{1,0:T(8,128)(2,1)} %wo_own.3) | copy-start | bytes 884740
  34.9 4.8 %copy-start.36 = (f32[768]{0:T(1024)S(1)}, f32[768]{0:T(1024)}, u32[]{:S(2)}) copy-start(f32[768]{0:T(1024)} %param.43) | copy-start | bytes 9220
  34.9 6.1 %copy-start = (bf16[768,768]{1,0:T(8,128)(2,1)S(1)}, bf16[768,768]{1,0:T(8,128)(2,1)}, u32[]{:S(2)}) copy-start(bf16[768,768]{1,0:T(8,128)(2,1)} %down_own.3) | copy-start | bytes 3538948
  34.9 6.1 %copy-start.9 = (bf16[1,256,768]{2,1,0:T(8,128)(2,1)S(1)}, bf16[1,256,768]{2,1,0:T(8,128)(2,1)}, u32[]{:S(2)}) copy-start(bf16[1,256,768]{2,1,0:T(8,128)(2,1)} %param.31) | copy-start | bytes 1179652
  34.9 6.1 %copy-start.32 = (f32[16,256]{1,0:T(8,128)S(1)}, f32[16,256]{1,0:T(8,128)}, u32[]{:S(2)}) copy-start(f32[16,256]{1,0:T(8,128)} %token_weights.1) | copy-start | bytes 49156
  37.9 6.4 %collective-permute-start.9 = (bf16[128,768]{1,0:T(8,128)(2,1)S(1)}, bf16[128,768]{1,0:T(8,128)(2,1)S(1)}, u32[]{:S(2)}, u32[]{:S(2)}) collective-permute-start(bf16[128,768]{1,0:T(8,128)(2,1)S(1)} %get-tuple-element.104.chip_own), channel_id=1, source_target_pairs={{0,2},{1,3},{2,0},{3,1},{4,6},{5,7},{6,4},{7,5},{8,10},{9,11},{10,... | collective-permute-start | bytes 589832 | tf_op jit(solution)/shard_map/ppermute | solution.py:515
  41.0 3.3 %copy-start.3 = (bf16[768,768]{1,0:T(8,128)(2,1)S(1)}, bf16[768,768]{1,0:T(8,128)(2,1)}, u32[]{:S(2)}) copy-start(bf16[768,768]{1,0:T(8,128)(2,1)} %up_own.1) | copy-start | bytes 3538948
  47.3 5.7 %collective-permute-start.14 = (bf16[128,768]{1,0:T(8,128)(2,1)S(1)}, bf16[128,768]{1,0:T(8,128)(2,1)S(1)}, u32[]{:S(2)}, u32[]{:S(2)}) collective-permute-start(bf16[128,768]{1,0:T(8,128)(2,1)S(1)} %get-tuple-element.111.chip_own), channel_id=1, source_target_pairs={{0,2},{1,3},{2,0},{3,1},{4,6},{5,7},{6,4},{7,5},{8,10},{9,11},{10,... | collective-permute-start | bytes 589832 | tf_op jit(solution)/shard_map/ppermute | solution.py:515
  55.7 5.7 %collective-permute-start.15 = (bf16[128,768]{1,0:T(8,128)(2,1)S(1)}, bf16[128,768]{1,0:T(8,128)(2,1)S(1)}, u32[]{:S(2)}, u32[]{:S(2)}) collective-permute-start(bf16[128,768]{1,0:T(8,128)(2,1)S(1)} %get-tuple-element.115.chip_own), channel_id=1, source_target_pairs={{0,2},{1,3},{2,0},{3,1},{4,6},{5,7},{6,4},{7,5},{8,10},{9,11},{10,... | collective-permute-start | bytes 589832 | tf_op jit(solution)/shard_map/ppermute | solution.py:515
  57.9 9.0 %collective-permute-start.20 = (bf16[1024,192]{1,0:T(8,128)(2,1)S(1)}, bf16[1024,192]{1,0:T(8,128)(2,1)S(1)}, u32[]{:S(2)}, u32[]{:S(2)}) collective-permute-start(bf16[1024,192]{1,0:T(8,128)(2,1)S(1)} %cross_source_grad.1), channel_id=1, source_target_pairs={{0,1},{1,0},{2,3},{3,2},{4,5},{5,4},{6,7},{7,6},{8,9},{9,8},{10,11... | collective-permute-start | bytes 1179656 | tf_op jit(solution)/shard_map/ppermute | solution.py:511
  58.0 14.7 %collective-permute-start.35 = (bf16[128,2304]{1,0:T(8,128)(2,1)S(1)}, bf16[128,2304]{1,0:T(8,128)(2,1)S(1)}, u32[]{:S(2)}, u32[]{:S(2)}) collective-permute-start(bf16[128,2304]{1,0:T(8,128)(2,1)S(1)} %get-tuple-element.110.pack), channel_id=1, source_target_pairs={{0,1},{1,0},{2,3},{3,2},{4,5},{5,4},{6,7},{7,6},{8,9},{9,8},{10,11... | collective-permute-start | bytes 1769480 | tf_op jit(solution)/shard_map/ppermute | solution.py:511
  61.7 1.5 collective-permute-start.16
  61.8 5.0 %collective-permute-start.21 = (bf16[128,960]{1,0:T(8,128)(2,1)S(1)}, bf16[128,960]{1,0:T(8,128)(2,1)S(1)}, u32[]{:S(2)}, u32[]{:S(2)}) collective-permute-start(bf16[128,960]{1,0:T(8,128)(2,1)S(1)} %get-tuple-element.134), channel_id=1, source_target_pairs={{0,1},{1,0},{2,3},{3,2},{4,5},{5,4},{6,7},{7,6},{8,9},{9,8},{10,11... | collective-permute-start | bytes 737288 | tf_op jit(solution)/shard_map/ppermute | solution.py:511
  62.3 4.6 %collective-permute-start.22 = (bf16[128,960]{1,0:T(8,128)(2,1)S(1)}, bf16[128,960]{1,0:T(8,128)(2,1)S(1)}, u32[]{:S(2)}, u32[]{:S(2)}) collective-permute-start(bf16[128,960]{1,0:T(8,128)(2,1)S(1)} %get-tuple-element.136), channel_id=1, source_target_pairs={{0,1},{1,0},{2,3},{3,2},{4,5},{5,4},{6,7},{7,6},{8,9},{9,8},{10,11... | collective-permute-start | bytes 737288 | tf_op jit(solution)/shard_map/ppermute | solution.py:511
  62.4 2.6 %copy-start.5 = (bf16[192,768]{1,0:T(8,128)(2,1)S(1)}, bf16[192,768]{1,0:T(8,128)(2,1)}, u32[]{:S(2)}) copy-start(bf16[192,768]{1,0:T(8,128)(2,1)} %w_output.3) | copy-start | bytes 884740
  62.4 2.6 %copy-start.13 = (bf16[3,256,256]{2,1,0:T(8,128)(2,1)S(1)}, bf16[3,256,256]{2,1,0:T(8,128)(2,1)}, u32[]{:S(2)}) copy-start(bf16[3,256,256]{2,1,0:T(8,128)(2,1)} %copy-done.12) | copy-start | bytes 1179652
  62.4 2.6 %copy-start.27 = (bf16[256,192]{1,0:T(8,128)(2,1)S(1)}, bf16[256,192]{1,0:T(8,128)(2,1)}, u32[]{:S(2)}) copy-start(bf16[256,192]{1,0:T(8,128)(2,1)} %copy-done.26) | copy-start | bytes 294916
  62.4 2.6 %copy-start.29 = (bf16[256,192]{1,0:T(8,128)(2,1)S(1)}, bf16[256,192]{1,0:T(8,128)(2,1)}, u32[]{:S(2)}) copy-start(bf16[256,192]{1,0:T(8,128)(2,1)} %copy-done.28) | copy-start | bytes 294916
  62.4 2.6 %copy-start.31 = (bf16[256,192]{1,0:T(8,128)(2,1)S(1)}, bf16[256,192]{1,0:T(8,128)(2,1)}, u32[]{:S(2)}) copy-start(bf16[256,192]{1,0:T(8,128)(2,1)} %copy-done.30) | copy-start | bytes 294916
  63.3 8.5 %collective-permute-start.12 = (bf16[128,768]{1,0:T(8,128)(2,1)S(1)}, bf16[128,768]{1,0:T(8,128)(2,1)S(1)}, u32[]{:S(2)}, u32[]{:S(2)}) collective-permute-start(bf16[128,768]{1,0:T(8,128)(2,1)S(1)} %ffn_out.1.chip_own), channel_id=1, source_target_pairs={{0,2},{1,3},{2,0},{3,1},{4,6},{5,7},{6,4},{7,5},{8,10},{9,11},{10,... | collective-permute-start | bytes 589832 | tf_op jit(solution)/shard_map/ppermute | solution.py:515
  65.0 1.9 %copy-start.8 = (bf16[128,768]{1,0:T(8,128)(2,1)S(1)}, bf16[128,768]{1,0:T(8,128)(2,1)}, u32[]{:S(2)}) copy-start(bf16[128,768]{1,0:T(8,128)(2,1)} %copy-done.6) | copy-start | bytes 589828
  66.9 5.2 %collective-permute-start.17 = (bf16[128,768]{1,0:T(8,128)(2,1)S(1)}, bf16[128,768]{1,0:T(8,128)(2,1)S(1)}, u32[]{:S(2)}, u32[]{:S(2)}) collective-permute-start(bf16[128,768]{1,0:T(8,128)(2,1)S(1)} %get-tuple-element.124), channel_id=1, source_target_pairs={{0,1},{1,0},{2,3},{3,2},{4,5},{5,4},{6,7},{7,6},{8,9},{9,8},{10,11... | collective-permute-start | bytes 589832 | tf_op jit(solution)/shard_map/ppermute | solution.py:511
  70.2 16.2 %collective-permute-start.32 = (bf16[4,96,768]{2,1,0:T(8,128)(2,1)S(1)}, bf16[4,96,768]{2,1,0:T(8,128)(2,1)S(1)}, u32[]{:S(2)}, u32[]{:S(2)}) collective-permute-start(bf16[4,96,768]{2,1,0:T(8,128)(2,1)S(1)} %get-tuple-element.158), channel_id=1, source_target_pairs={{0,4},{4,0},{8,12},{12,8},{16,20},{20,16},{24,28},{28,24},{1,5},{5... | collective-permute-start | bytes 1769480 | tf_op jit(solution)/shard_map/ppermute | solution.py:519
  71.8 7.8 %collective-permute-start.13 = (bf16[128,768]{1,0:T(8,128)(2,1)S(1)}, bf16[128,768]{1,0:T(8,128)(2,1)S(1)}, u32[]{:S(2)}, u32[]{:S(2)}) collective-permute-start(bf16[128,768]{1,0:T(8,128)(2,1)S(1)} %layer_out.1.own), channel_id=1, source_target_pairs={{0,1},{1,0},{2,3},{3,2},{4,5},{5,4},{6,7},{7,6},{8,9},{9,8},{10,11... | collective-permute-start | bytes 589832 | tf_op jit(solution)/shard_map/ppermute | solution.py:511
  72.1 7.2 %collective-permute-start.18 = (bf16[128,768]{1,0:T(8,128)(2,1)S(1)}, bf16[128,768]{1,0:T(8,128)(2,1)S(1)}, u32[]{:S(2)}, u32[]{:S(2)}) collective-permute-start(bf16[128,768]{1,0:T(8,128)(2,1)S(1)} %input_sum.1.chip_own), channel_id=1, source_target_pairs={{0,2},{1,3},{2,0},{3,1},{4,6},{5,7},{6,4},{7,5},{8,10},{9,11},{10,... | collective-permute-start | bytes 589832 | tf_op jit(solution)/shard_map/ppermute | solution.py:515
  72.7 7.5 %copy-start.11 = (bf16[256,768]{1,0:T(8,128)(2,1)S(1)}, bf16[256,768]{1,0:T(8,128)(2,1)}, u32[]{:S(2)}) copy-start(bf16[256,768]{1,0:T(8,128)(2,1)} %copy-done.10) | copy-start | bytes 1179652
  72.7 7.5 %copy-start.25 = (bf16[256,192]{1,0:T(8,128)(2,1)S(1)}, bf16[256,192]{1,0:T(8,128)(2,1)}, u32[]{:S(2)}) copy-start(bf16[256,192]{1,0:T(8,128)(2,1)} %copy-done.24) | copy-start | bytes 294916
  73.7 49.5 %collective-permute-start.36 = (bf16[4,96,768]{2,1,0:T(8,128)(2,1)S(1)}, bf16[4,96,768]{2,1,0:T(8,128)(2,1)S(1)}, u32[]{:S(2)}, u32[]{:S(2)}) collective-permute-start(bf16[4,96,768]{2,1,0:T(8,128)(2,1)S(1)} %get-tuple-element.168), channel_id=1, source_target_pairs={{0,4},{4,0},{8,12},{12,8},{16,20},{20,16},{24,28},{28,24},{1,5},{5... | collective-permute-start | bytes 1769480 | tf_op jit(solution)/shard_map/ppermute | solution.py:519
  74.8 52.0 %collective-permute-start.39 = (bf16[4,96,768]{2,1,0:T(8,128)(2,1)S(1)}, bf16[4,96,768]{2,1,0:T(8,128)(2,1)S(1)}, u32[]{:S(2)}, u32[]{:S(2)}) collective-permute-start(bf16[4,96,768]{2,1,0:T(8,128)(2,1)S(1)} %get-tuple-element.174), channel_id=1, source_target_pairs={{0,8},{4,12},{8,0},{12,4},{16,24},{20,28},{24,16},{28,20},{1,9},{5... | collective-permute-start | bytes 1769480 | tf_op jit(solution)/shard_map/ppermute | solution.py:519
  79.3 36.1 %collective-permute-start.23 = (bf16[256,768]{1,0:T(8,128)(2,1)S(1)}, bf16[256,768]{1,0:T(8,128)(2,1)S(1)}, u32[]{:S(2)}, u32[]{:S(2)}) collective-permute-start(bf16[256,768]{1,0:T(8,128)(2,1)S(1)} %get-tuple-element.140), channel_id=1, source_target_pairs={{0,1},{1,0},{2,3},{3,2},{4,5},{5,4},{6,7},{7,6},{8,9},{9,8},{10,11... | collective-permute-start | bytes 1179656 | tf_op jit(solution)/shard_map/ppermute | solution.py:511
  79.6 2.8 %collective-permute-start.25 = (f32[8,768]{1,0:T(8,128)S(1)}, f32[8,768]{1,0:T(8,128)S(1)}, u32[]{:S(2)}, u32[]{:S(2)}) collective-permute-start(f32[8,768]{1,0:T(8,128)S(1)} %get-tuple-element.143.left_ref), channel_id=1, source_target_pairs={{0,1},{1,0},{2,3},{3,2},{4,5},{5,4},{6,7},{7,6},{8,9},{9,8},{10,11... | collective-permute-start | bytes 73736 | tf_op jit(solution)/shard_map/ppermute | solution.py:511
  82.4 57.8 %collective-permute-start.29 = (bf16[4,112,768]{2,1,0:T(8,128)(2,1)}, bf16[4,112,768]{2,1,0:T(8,128)(2,1)S(1)}, u32[]{:S(2)}, u32[]{:S(2)}) collective-permute-start(bf16[4,112,768]{2,1,0:T(8,128)(2,1)} %get-tuple-element.152), channel_id=1, source_target_pairs={{0,4},{4,0},{8,12},{12,8},{16,20},{20,16},{24,28},{28,24},{1,5},{5... | collective-permute-start | bytes 2064392 | tf_op jit(solution)/shard_map/ppermute | solution.py:519
  86.4 27.5 %collective-permute-start.26 = (f32[8,768]{1,0:T(8,128)S(1)}, f32[8,768]{1,0:T(8,128)S(1)}, u32[]{:S(2)}, u32[]{:S(2)}) collective-permute-start(f32[8,768]{1,0:T(8,128)S(1)} %gain_core.1.left_ref), channel_id=1, source_target_pairs={{0,4},{4,0},{8,12},{12,8},{16,20},{20,16},{24,28},{28,24},{1,5},{5... | collective-permute-start | bytes 73736 | tf_op jit(solution)/shard_map/ppermute | solution.py:519
  113.9 16.8 %collective-permute-start.33 = (bf16[2,96,768]{2,1,0:T(8,128)(2,1)S(1)}, bf16[2,96,768]{2,1,0:T(8,128)(2,1)S(1)}, u32[]{:S(2)}, u32[]{:S(2)}) collective-permute-start(bf16[2,96,768]{2,1,0:T(8,128)(2,1)S(1)} %get-tuple-element.160), channel_id=1, source_target_pairs={{0,8},{4,12},{8,0},{12,4},{16,24},{20,28},{24,16},{28,20},{1,9},{5... | collective-permute-start | bytes 884744 | tf_op jit(solution)/shard_map/ppermute | solution.py:519
  115.5 7.5 %collective-permute-start.27 = (f32[8,768]{1,0:T(8,128)S(1)}, f32[8,768]{1,0:T(8,128)S(1)}, u32[]{:S(2)}, u32[]{:S(2)}) collective-permute-start(f32[8,768]{1,0:T(8,128)S(1)} %gain_0.1.left_ref), channel_id=1, source_target_pairs={{0,8},{4,12},{8,0},{12,4},{16,24},{20,28},{24,16},{28,20},{1,9},{5... | collective-permute-start | bytes 73736 | tf_op jit(solution)/shard_map/ppermute | solution.py:519
  116.1 13.1 %copy-start.14 = (bf16[128,768]{1,0:T(8,128)(2,1)}, bf16[128,768]{1,0:T(8,128)(2,1)S(1)}, u32[]{:S(2)}) copy-start(bf16[128,768]{1,0:T(8,128)(2,1)S(1)} %get-tuple-element.141.left_ref) | copy-start | bytes 589828
  123.0 9.0 %collective-permute-start.24 = (bf16[128,768]{1,0:T(8,128)(2,1)S(1)}, bf16[128,768]{1,0:T(8,128)(2,1)S(1)}, u32[]{:S(2)}, u32[]{:S(2)}) collective-permute-start(bf16[128,768]{1,0:T(8,128)(2,1)S(1)} %get-tuple-element.142), channel_id=1, source_target_pairs={{0,2},{1,3},{2,0},{3,1},{4,6},{5,7},{6,4},{7,5},{8,10},{9,11},{10,... | collective-permute-start | bytes 589832 | tf_op jit(solution)/shard_map/ppermute | solution.py:515
  123.2 6.0 %collective-permute-start.28 = (f32[8,768]{1,0:T(8,128)S(1)}, f32[8,768]{1,0:T(8,128)S(1)}, u32[]{:S(2)}, u32[]{:S(2)}) collective-permute-start(f32[8,768]{1,0:T(8,128)S(1)} %gain_1.1.left_ref), channel_id=1, source_target_pairs={{0,16},{4,20},{8,24},{12,28},{16,0},{20,4},{24,8},{28,12},{1,17},{... | collective-permute-start | bytes 73736 | tf_op jit(solution)/shard_map/ppermute | solution.py:519
  126.8 15.3 %collective-permute-start.37 = (bf16[2,96,768]{2,1,0:T(8,128)(2,1)}, bf16[2,96,768]{2,1,0:T(8,128)(2,1)S(1)}, u32[]{:S(2)}, u32[]{:S(2)}) collective-permute-start(bf16[2,96,768]{2,1,0:T(8,128)(2,1)} %get-tuple-element.170), channel_id=1, source_target_pairs={{0,8},{4,12},{8,0},{12,4},{16,24},{20,28},{24,16},{28,20},{1,9},{5... | collective-permute-start | bytes 884744 | tf_op jit(solution)/shard_map/ppermute | solution.py:519
  129.2 13.4 %collective-permute-start.40 = (bf16[2,96,768]{2,1,0:T(8,128)(2,1)}, bf16[2,96,768]{2,1,0:T(8,128)(2,1)S(1)}, u32[]{:S(2)}, u32[]{:S(2)}) collective-permute-start(bf16[2,96,768]{2,1,0:T(8,128)(2,1)} %get-tuple-element.176), channel_id=1, source_target_pairs={{0,4},{4,0},{8,12},{12,8},{16,20},{20,16},{24,28},{28,24},{1,5},{5... | collective-permute-start | bytes 884744 | tf_op jit(solution)/shard_map/ppermute | solution.py:519
  130.7 7.8 %collective-permute-start.19 = (bf16[128,768]{1,0:T(8,128)(2,1)S(1)}, bf16[128,768]{1,0:T(8,128)(2,1)}, u32[]{:S(2)}, u32[]{:S(2)}) collective-permute-start(bf16[128,768]{1,0:T(8,128)(2,1)S(1)} %get-tuple-element.126.own), channel_id=1, source_target_pairs={{0,1},{1,0},{2,3},{3,2},{4,5},{5,4},{6,7},{7,6},{8,9},{9,8},{10,11... | collective-permute-start | bytes 589832 | tf_op jit(solution)/shard_map/ppermute | solution.py:511
  132.7 12.6 %collective-permute-start.34 = (bf16[1,96,768]{2,1,0:T(8,128)(2,1)}, bf16[1,96,768]{2,1,0:T(8,128)(2,1)}, u32[]{:S(2)}, u32[]{:S(2)}) collective-permute-start(bf16[1,96,768]{2,1,0:T(8,128)(2,1)} %get-tuple-element.162), channel_id=1, source_target_pairs={{0,16},{4,20},{8,24},{12,28},{16,0},{20,4},{24,8},{28,12},{1,17},{... | collective-permute-start | bytes 442376 | tf_op jit(solution)/shard_map/ppermute | solution.py:519
  140.2 5.1 %copy-start.23 = (bf16[1,96,768]{2,1,0:T(8,128)(2,1)S(1)}, bf16[1,96,768]{2,1,0:T(8,128)(2,1)}, u32[]{:S(2)}) copy-start(bf16[1,96,768]{2,1,0:T(8,128)(2,1)} %copy-done.22) | copy-start | bytes 442372
  140.4 15.8 %collective-permute-start.30 = (bf16[2,112,768]{2,1,0:T(8,128)(2,1)S(1)}, bf16[2,112,768]{2,1,0:T(8,128)(2,1)S(1)}, u32[]{:S(2)}, u32[]{:S(2)}) collective-permute-start(bf16[2,112,768]{2,1,0:T(8,128)(2,1)S(1)} %get-tuple-element.154), channel_id=1, source_target_pairs={{0,8},{4,12},{8,0},{12,4},{16,24},{20,28},{24,16},{28,20},{1,9},{5... | collective-permute-start | bytes 1032200 | tf_op jit(solution)/shard_map/ppermute | solution.py:519
  142.1 11.5 %collective-permute-start.38 = (bf16[1,96,768]{2,1,0:T(8,128)(2,1)S(1)}, bf16[1,96,768]{2,1,0:T(8,128)(2,1)S(1)}, u32[]{:S(2)}, u32[]{:S(2)}) collective-permute-start(bf16[1,96,768]{2,1,0:T(8,128)(2,1)S(1)} %get-tuple-element.172), channel_id=1, source_target_pairs={{0,16},{4,20},{8,24},{12,28},{16,0},{20,4},{24,8},{28,12},{1,17},{... | collective-permute-start | bytes 442376 | tf_op jit(solution)/shard_map/ppermute | solution.py:519
  142.6 15.7 %collective-permute-start.41 = (bf16[1,96,768]{2,1,0:T(8,128)(2,1)S(1)}, bf16[1,96,768]{2,1,0:T(8,128)(2,1)S(1)}, u32[]{:S(2)}, u32[]{:S(2)}) collective-permute-start(bf16[1,96,768]{2,1,0:T(8,128)(2,1)S(1)} %get-tuple-element.178), channel_id=1, source_target_pairs={{0,16},{4,20},{8,24},{12,28},{16,0},{20,4},{24,8},{28,12},{1,17},{... | collective-permute-start | bytes 442376 | tf_op jit(solution)/shard_map/ppermute | solution.py:519
  156.3 10.3 %collective-permute-start.31 = (bf16[1,112,768]{2,1,0:T(8,128)(2,1)S(1)}, bf16[1,112,768]{2,1,0:T(8,128)(2,1)S(1)}, u32[]{:S(2)}, u32[]{:S(2)}) collective-permute-start(bf16[1,112,768]{2,1,0:T(8,128)(2,1)S(1)} %get-tuple-element.156), channel_id=1, source_target_pairs={{0,16},{4,20},{8,24},{12,28},{16,0},{20,4},{24,8},{28,12},{1,17},{... | collective-permute-start | bytes 516104 | tf_op jit(solution)/shard_map/ppermute | solution.py:519
  (16 other events, 12.1 us)

commit v2 on v1

v2 whole, which is shorter than its diff:
```python
import jax
import jax.numpy as jnp
from jax import lax
from jax.experimental import pallas as pl
from jax.experimental.pallas import tpu as pltpu
from jax.sharding import PartitionSpec as P

HEAD_DIM = 64
LANGS = 8
EPSILON = 1e-06
SCALE = 0.125
NEGATIVE = -1e30
F32 = jnp.float32
BF16 = jnp.bfloat16
VMEM_LIMIT = 20 * 1024 * 1024
EXTRA = 16
FILL = 5.0
LONG = 20.0


def dot(left, right):
    return jnp.dot(left, right, preferred_element_type=F32)


def dot_nt(left, right):
    return lax.dot_general(left, right, (((1,), (1,)), ((), ())), preferred_element_type=F32)


def dot_tn(left, right):
    return lax.dot_general(left, right, (((0,), (0,)), ((), ())), preferred_element_type=F32)


def row_of(vector_ref):
    return vector_ref[...].reshape(1, vector_ref.shape[0])


def inverse_rms(resid):
    return lax.rsqrt(jnp.mean(resid * resid, -1, keepdims=True) + EPSILON)


def norm_back(resid, gain, incoming):
    scale = inverse_rms(resid)
    weighted = incoming * gain
    inner = jnp.mean(weighted * resid, -1, keepdims=True)
    grad = scale * weighted - resid * (scale * scale * scale * inner)
    gain_grad = jnp.sum(incoming * resid * scale, 0, keepdims=True)
    return grad, gain_grad


def groups_of(width):
    return [(start, min(2 * HEAD_DIM, width - start)) for start in range(0, width, 2 * HEAD_DIM)]


def head_mask(count, which, value):
    lane = lax.broadcasted_iota(jnp.int32, (1, count), 1)
    return jnp.where(lane // HEAD_DIM == which, value, 0.0).astype(BF16)


def merge_heads(parts):
    merged = []
    for pair in parts:
        if len(pair) == 1:
            merged.append(pair[0])
        else:
            lane = lax.broadcasted_iota(jnp.int32, (1, 2 * HEAD_DIM), 1)
            merged.append(jnp.where(lane < HEAD_DIM, pair[0], pair[1]))
    return jnp.concatenate(merged, -1) if len(merged) > 1 else merged[0]


def heads_forward(queries, keys, values, finish, probs_ref):
    parts = []
    head = 0
    for start, width in groups_of(queries.shape[1]):
        query, key, value = (item[:, start : start + width] for item in (queries, keys, values))
        pair = []
        for inside in range(width // HEAD_DIM):
            logits = finish(head, dot_nt(query * head_mask(width, inside, SCALE), key))
            expo = jnp.exp(logits - jnp.max(logits, -1, keepdims=True))
            probs = (expo * (1.0 / jnp.sum(expo, -1, keepdims=True))).astype(BF16)
            probs_ref[head] = probs
            pair.append(dot(probs, value))
            head += 1
        parts.append(pair)
    return merge_heads(parts).astype(BF16)


def heads_backward(grad_context, keys, values, probs_ref, grad_logits_ref):
    parts = []
    head = 0
    for start, width in groups_of(grad_context.shape[1]):
        grad, key, value = (item[:, start : start + width] for item in (grad_context, keys, values))
        pair = []
        for inside in range(width // HEAD_DIM):
            grad_probs = dot_nt(grad * head_mask(width, inside, 1.0), value)
            probs = probs_ref[head].astype(F32)
            weighted = jnp.sum(grad_probs * probs, -1, keepdims=True)
            grad_logits = (probs * (grad_probs - weighted)).astype(BF16)
            grad_logits_ref[head] = grad_logits
            pair.append(SCALE * dot(grad_logits, key))
            head += 1
        parts.append(pair)
    return merge_heads(parts).astype(BF16)


def heads_transposed(matrix_ref, rows, factor):
    parts = []
    head = 0
    for start, width in groups_of(rows.shape[1]):
        pair = []
        for _ in range(width // HEAD_DIM):
            pair.append(factor * dot_tn(matrix_ref[head], rows[:, start : start + width]))
            head += 1
        parts.append(pair)
    return merge_heads(parts).astype(BF16)


def own_rows(core, half):
    return pl.ds(pl.multiple_of(core * half, half), half)


def split_halves(whole_ref, keep_ref, send_ref):
    half = keep_ref.shape[0]
    core = lax.axis_index("tensor") % 2
    keep_ref[...] = whole_ref[own_rows(core, half), :]
    send_ref[...] = whole_ref[own_rows(1 - core, half), :]


def reversed_onehot(bucket_ref, buckets):
    length = bucket_ref.shape[1]
    row = lax.broadcasted_iota(jnp.int32, (length, length), 0)
    column = lax.broadcasted_iota(jnp.int32, (length, length), 1)
    turn = jnp.where((row + column == length) | (row + column == 0), 1.0, 0.0).astype(BF16)
    bucket = jnp.broadcast_to(bucket_ref[...], (8, length)).astype(F32).astype(BF16)
    turned = dot(bucket, turn)[:1]
    wanted = lax.broadcasted_iota(jnp.int32, (buckets, length), 0).astype(F32)
    return jnp.where(turned == wanted, 1.0, 0.0)


def add_kernel(left_ref, right_ref, out_ref):
    out_ref[...] = (left_ref[...].astype(F32) + right_ref[...].astype(F32)).astype(out_ref.dtype)


def self_forward_kernel(
    dec_len, x, gain, w_query, w_key, w_value, w_output, bucket, table,
    keep, send, normed_out, query_out, key_out, value_out, context_out, probs_out,
    whole, x_here, gain_here, query_here, key_here, value_here, output_here, bucket_here, table_here, sems,
):
    sources = (x, gain, w_query, w_key, w_value, bucket, table, w_output)
    places = (x_here, gain_here, query_here, key_here, value_here, bucket_here, table_here, output_here)
    copies = [
        pltpu.make_async_copy(source, place, sems.at[index])
        for index, (source, place) in enumerate(zip(sources, places))
    ]
    for copy in copies:
        copy.start()
    length = x.shape[0]
    copies[0].wait()
    copies[1].wait()
    resid = x_here[...].astype(F32)
    normed = (resid * inverse_rms(resid) * row_of(gain_here)).astype(BF16)
    normed_out[...] = normed
    copies[2].wait()
    queries = dot_nt(normed, query_here[...]).astype(BF16)
    copies[3].wait()
    keys = dot_nt(normed, key_here[...]).astype(BF16)
    copies[4].wait()
    values = dot_nt(normed, value_here[...]).astype(BF16)
    query_out[...] = queries
    key_out[...] = keys
    value_out[...] = values
    copies[5].wait()
    copies[6].wait()
    by_distance = lax.dot_general(
        table_here[...],
        reversed_onehot(bucket_here, table.shape[1]),
        (((1,), (0,)), ((), ())),
        precision=lax.Precision.HIGHEST,
        preferred_element_type=F32,
    )
    row = lax.broadcasted_iota(jnp.int32, (length, length), 0)
    column = lax.broadcasted_iota(jnp.int32, (length, length), 1)
    allowed = (column <= row) & (column < dec_len[0])

    def finish(head, scores):
        spread = jnp.broadcast_to(by_distance[head : head + 1], (length, length))
        bias = pltpu.roll(spread, 0, 1, stride=1, stride_axis=0)
        return jnp.where(allowed, scores + bias, NEGATIVE)

    context = heads_forward(queries, keys, values, finish, probs_out)
    context_out[...] = context
    copies[7].wait()
    whole[...] = dot(context, output_here[...]).astype(BF16)
    split_halves(whole, keep, send)


def cross_source_kernel(first, second, wk_own, wv_own, wk_peer, wv_peer, k_own, v_own, k_peer, v_peer):
    rows = first.shape[0]
    for index, part in enumerate((first, second)):
        for weight, out in ((wk_own, k_own), (wv_own, v_own), (wk_peer, k_peer), (wv_peer, v_peer)):
            out[index * rows : (index + 1) * rows, :] = dot_nt(part[...], weight[...]).astype(BF16)


def out_grad_kernel(
    objective, language, dec_len, token_weights, cotangent, down_own, down_peer,
    grad_own, branch_own, branch_peer, act_grad_own, act_grad_peer,
):
    half = grad_own.shape[0]
    length = cotangent.shape[0]
    core = lax.axis_index("tensor") % 2
    weights = token_weights[pl.ds(objective[0] * LANGS + language[0], 1), :]
    position = lax.broadcasted_iota(jnp.int32, (1, length), 1)
    weights = jnp.where(position < dec_len[0], weights, 0.0)

    def rows_of(side):
        row = lax.broadcasted_iota(jnp.int32, (half, length), 0) + side * half
        column = lax.broadcasted_iota(jnp.int32, (half, length), 1)
        factor = jnp.sum(jnp.where(row == column, weights, 0.0), -1, keepdims=True)
        return cotangent[own_rows(side, half), :].astype(F32) * factor

    own = rows_of(core)
    grad_own[...] = own
    branch = own.astype(BF16)
    branch_own[...] = branch
    branch_peer[...] = rows_of(1 - core).astype(BF16)
    act_grad_own[...] = dot_nt(branch, down_own[...])
    act_grad_peer[...] = dot_nt(branch, down_peer[...])


def cross_forward_kernel(
    enc_len, chip_own, chip_other, x, gain, wq_own, wq_peer, wo_own, wo_peer, k_own, v_own, k_peer, v_peer,
    more_k_own, more_v_own, more_k_peer, more_v_peer,
    partial_out, hidden_out, normed_out, q_own, q_peer, context_own, probs_own, probs_peer, pack,
    keys_own, values_own, keys_peer, values_peer,
):
    half, width = chip_own.shape
    tensor = lax.axis_index("tensor")
    resid = x[own_rows(tensor % 2, half), :].astype(F32)
    resid = resid + (chip_own[...].astype(F32) + chip_other[...].astype(F32))
    hidden_out[...] = resid
    normed = (resid * inverse_rms(resid) * row_of(gain)).astype(BF16)
    normed_out[...] = normed
    pack[:, :width] = normed
    part = k_own.shape[0]
    for whole, first, second in (
        (keys_own, k_own, more_k_own),
        (values_own, v_own, more_v_own),
        (keys_peer, k_peer, more_k_peer),
        (values_peer, v_peer, more_v_peer),
    ):
        whole[:part] = first[...]
        whole[part:] = second[...]
    span = 2 * part
    column = lax.broadcasted_iota(jnp.int32, (1, span), 1)
    block = column // half
    flip = jnp.where(block % 2 == 1, 2, 0) + jnp.where(block >= 2, 1, 0)
    position = (tensor ^ flip) * half + column % half
    allowed = position < enc_len[0]

    def finish(head, scores):
        return jnp.where(allowed, scores, NEGATIVE)

    queries = dot_nt(normed, wq_own[...]).astype(BF16)
    q_own[...] = queries
    first = heads_forward(queries, keys_own[...], values_own[...], finish, probs_own)
    context_own[...] = first
    queries = dot_nt(normed, wq_peer[...]).astype(BF16)
    q_peer[...] = queries
    second = heads_forward(queries, keys_peer[...], values_peer[...], finish, probs_peer)
    pack[:, width:] = second
    partial_out[...] = (dot(first, wo_own[...]) + dot(second, wo_peer[...])).astype(BF16)


def ffn_kernel(
    chip_own, chip_other, hidden, gain, up_own, up_peer, act_grad_own, act_grad_peer,
    partial_out, hidden_out, normed_out, act_own, grad_pre_own, pack,
):
    width = hidden.shape[1]
    resid = hidden[...] + (chip_own[...].astype(F32) + chip_other[...].astype(F32))
    hidden_out[...] = resid
    normed = (resid * inverse_rms(resid) * row_of(gain)).astype(BF16)
    normed_out[...] = normed
    pack[:, :width] = normed

    def through(up, act_grad):
        pre = dot(normed, up[...])
        square = pre * pre
        tanh = jnp.tanh(0.7978845608028654 * (pre + 0.044715 * square * pre))
        half_sum = 0.5 * (1.0 + tanh)
        slope = half_sum + 0.5 * pre * (1.0 - tanh * tanh) * (
            0.7978845608028654 * (1.0 + 3.0 * 0.044715 * square)
        )
        return (pre * half_sum).astype(BF16), (act_grad[...] * slope).astype(BF16)

    act, grad_pre = through(up_own, act_grad_own)
    act_own[...] = act
    grad_pre_own[...] = grad_pre
    total = dot_nt(grad_pre, up_own[...])
    act, grad_pre = through(up_peer, act_grad_peer)
    units = act.shape[1]
    pack[:, width : width + units] = act
    pack[:, width + units :] = grad_pre
    total = total + dot_nt(grad_pre, up_peer[...])
    partial_out[...] = total.astype(BF16)


def ffn_out_kernel(act_own, pack, down_own, down_peer, encoded_own, encoded_other, out, encoded_keep, send):
    units = act_own.shape[1]
    half, width = out.shape
    total = dot(act_own[...], down_own[...]) + dot(pack[:, width : width + units], down_peer[...])
    total = total.astype(BF16)
    out[...] = total
    send[:half] = total
    rows = encoded_keep.shape[0]
    encoded_keep[...] = both(encoded_own[:rows], encoded_other[:rows]).astype(BF16)
    send[half:] = both(encoded_own[rows:], encoded_other[rows:]).astype(BF16)


def write_blocks(whole, first_bit, rest_bits, size, targets, extra=None):
    index = lax.axis_index("dp")
    count = 1 << len(rest_bits)
    for first, target in enumerate(targets):
        for entry in range(count):
            relative = first << first_bit
            for place, bit in enumerate(rest_bits):
                if entry >> (len(rest_bits) - 1 - place) & 1:
                    relative |= 1 << bit
            block = index ^ relative
            rows = whole[pl.ds(pl.multiple_of(block * size, size), size), :]
            target[entry, :size, :] = rows
            if extra is not None:
                target[entry, size:, :] = extra


def emit(whole, outs, order, size, extra=None):
    if order is None:
        outs[0][: whole.shape[0], :] = whole[...]
        if extra is not None:
            outs[0][whole.shape[0] :, :] = extra
    else:
        write_blocks(whole, order[0], order[1:], size, outs, extra)


def ffn_weights_kernel(orders, size, normed, pack, act_own, grad_pre_own, branch_own, branch_peer, *refs):
    *outs, whole, left, right = refs
    half, width = normed.shape
    units = act_own.shape[1]
    left[:half] = normed[...]
    left[half:] = pack[:, :width]
    right[:half] = grad_pre_own[...]
    right[half:] = pack[:, width + units :]
    whole[...] = dot_tn(left[...], right[...]).astype(BF16)
    count = 1 if orders[0] is None else 2
    emit(whole, outs[:count], orders[0], size)
    left[:half] = branch_own[...]
    left[half:] = branch_peer[...]
    right[:half] = act_own[...]
    right[half:] = pack[:, width : width + units]
    whole[...] = dot_tn(left[...], right[...]).astype(BF16)
    emit(whole, outs[count:], orders[1], size)


def cross_backward_kernel(
    chip_own, chip_other, hidden, gain, grad_out, wo_own, wo_peer, k_own, v_own, k_peer, v_peer,
    probs_own, probs_peer, wq_own, wq_peer,
    partial_out, grad_hidden, gain_grad, gl_own, gl_peer, gc_own, gc_peer, gq_own, branch, pack,
):
    incoming = chip_own[...].astype(F32) + chip_other[...].astype(F32)
    added, gain_terms = norm_back(hidden[...], row_of(gain), incoming)
    gain_grad[...] = jnp.broadcast_to(gain_terms, gain_grad.shape)
    grad = grad_out[...] + added
    grad_hidden[...] = grad
    rounded = grad.astype(BF16)
    branch[...] = rounded
    width = rounded.shape[1]
    pack[:, :width] = rounded
    context = dot_nt(rounded, wo_own[...]).astype(BF16)
    gc_own[...] = context
    queries = heads_backward(context, k_own[...], v_own[...], probs_own, gl_own)
    gq_own[...] = queries
    total = dot(queries, wq_own[...])
    context = dot_nt(rounded, wo_peer[...]).astype(BF16)
    gc_peer[...] = context
    queries = heads_backward(context, k_peer[...], v_peer[...], probs_peer, gl_peer)
    pack[:, width:] = queries
    total = total + dot(queries, wq_peer[...])
    partial_out[...] = total.astype(BF16)


def source_grad_kernel(gl_peer, probs_peer, gc_peer, q_peer, out):
    span = out.shape[0] // 2
    middle = span // 2
    for start, grads in (
        (0, heads_transposed(gl_peer, q_peer[...], SCALE)),
        (span, heads_transposed(probs_peer, gc_peer[...], 1.0)),
    ):
        out[start : start + middle] = grads[middle:]
        out[start + middle : start + span] = grads[:middle]


def cross_weights_kernel(
    orders, size, gl_own, probs_own, gc_own, q_own, other, e0, e1, e2, e3, normed, pack_forward,
    branch, pack_backward, context_own, gq_own, *refs,
):
    *outs, source, whole, left, right = refs
    count = len(outs) // 2
    span = other.shape[0] // 2
    half, width = normed.shape
    columns = q_own.shape[1]
    source[:, :columns] = low_sum(heads_transposed(gl_own, q_own[...], SCALE), other[:span])
    source[:, columns:] = low_sum(heads_transposed(probs_own, gc_own[...], 1.0), other[span:])
    for index, part in enumerate((e0, e1, e2, e3)):
        left[index * half : (index + 1) * half] = part[...]
    whole[...] = dot_tn(left[...], source[...]).astype(BF16)
    emit(whole, outs[:count], orders[0], size)
    left[:half] = normed[...]
    left[half : 2 * half] = pack_forward[:, :width]
    left[2 * half : 3 * half] = branch[...]
    left[3 * half :] = pack_backward[:, :width]
    right[...] = jnp.zeros_like(right)
    right[:half, :columns] = gq_own[...]
    right[half : 2 * half, :columns] = pack_backward[:, width:]
    right[2 * half : 3 * half, columns:] = context_own[...]
    right[3 * half :, columns:] = pack_forward[:, width:]
    whole[...] = dot_tn(left[...], right[...]).astype(BF16)
    emit(whole, outs[count:], orders[1], size)


def encoded_kernel(source, wk_own, wv_own, keep, send):
    columns = wk_own.shape[0]
    terms = dot(source[:, :columns], wk_own[...]) + dot(source[:, columns:], wv_own[...])
    terms = terms.astype(BF16)
    rows = keep.shape[0]
    keep[...] = terms[:rows]
    send[...] = terms[rows:]


def self_norm_kernel(chip_own, chip_other, hidden, gain, grad_hidden, gain_ffn, grad_out, pack):
    half = hidden.shape[0]
    incoming = chip_own[...].astype(F32) + chip_other[...].astype(F32)
    added, gain_terms = norm_back(hidden[...], row_of(gain), incoming)
    grad = grad_hidden[...] + added
    grad_out[...] = grad
    pack[:half] = grad.astype(BF16)
    row = lax.broadcasted_iota(jnp.int32, (EXTRA, hidden.shape[1]), 0)
    extra = jnp.where(row == 0, gain_terms, 0.0) + jnp.where(row == 1, gain_ffn[:1], 0.0)
    pack[half:] = extra.astype(BF16)


def high_low(vector):
    high = vector.astype(BF16).astype(F32)
    row = lax.broadcasted_iota(jnp.int32, (EXTRA, vector.shape[1]), 0)
    return (jnp.where(row == 0, high, 0.0) + jnp.where(row == 1, vector - high, 0.0)).astype(BF16)


def of_high_low(rows):
    rows = rows.astype(F32)
    return rows[:1] + rows[1:2]


def self_backward_kernel(
    pack_own, pack_peer, w_output, w_query, w_key, w_value, queries, keys, values, probs, x,
    keep, send, branch_out, gq_out, gk_out, gv_out, gl_out, whole,
):
    half = keep.shape[0] - EXTRA
    core = lax.axis_index("tensor") % 2
    branch_out[own_rows(core, half), :] = pack_own[:half]
    branch_out[own_rows(1 - core, half), :] = pack_peer[:half]
    context = dot_nt(branch_out[...], w_output[...]).astype(BF16)
    grad_queries = heads_backward(context, keys[...], values[...], probs, gl_out)
    grad_keys = heads_transposed(gl_out, queries[...], SCALE)
    grad_values = heads_transposed(probs, context, 1.0)
    gq_out[...] = grad_queries
    gk_out[...] = grad_keys
    gv_out[...] = grad_values
    total = dot(grad_queries, w_query[...]) + dot(grad_keys, w_key[...]) + dot(grad_values, w_value[...])
    whole[...] = total.astype(BF16)
    keep[:half] = whole[own_rows(core, half), :]
    send[:half] = whole[own_rows(1 - core, half), :]
    resid = x[...].astype(F32)
    gain_terms = high_low(jnp.sum(total * resid * inverse_rms(resid), 0, keepdims=True))
    keep[half:] = gain_terms
    send[half:] = gain_terms


def input_sum_kernel(own, peer, out):
    half = out.shape[0] - EXTRA
    out[:half] = both(own[:half], peer[:half]).astype(BF16)
    out[half:] = high_low(of_high_low(own[half:]) + of_high_low(peer[half:]))


def self_first_kernel(order, size, normed, gq, gk, *refs):
    *outs, whole, right = refs
    columns = gq.shape[1]
    right[:, :columns] = gq[...]
    right[:, columns:] = gk[...]
    whole[...] = dot_tn(normed[...], right[...]).astype(BF16)
    emit(whole, outs, order, size)


def self_second_kernel(order, size, buckets, normed, branch, gv, context, gl, bucket, pack_own, pack_peer, *refs):
    *outs, whole, right, left = refs
    length, columns = gv.shape
    half = pack_own.shape[0] - EXTRA
    left[:length] = normed[...]
    left[length:] = branch[...]
    right[...] = jnp.zeros_like(right)
    right[:length, :columns] = gv[...]
    right[length:, columns:] = context[...]
    whole[...] = dot_tn(left[...], right[...]).astype(BF16)
    onehot = reversed_onehot(bucket, buckets)
    row = lax.broadcasted_iota(jnp.int32, (length, length), 0)
    column = lax.broadcasted_iota(jnp.int32, (length, length), 1)
    turn = jnp.where(row + column == length - 1, 1.0, 0.0).astype(BF16)
    place = lax.broadcasted_iota(jnp.int32, (8, length), 0)
    sums = jnp.zeros((8, length), F32)
    for head in range(gl.shape[0]):
        skewed = pltpu.roll(dot(turn, gl[head]), 1, 1, stride=1, stride_axis=0)
        sums = sums + jnp.where(place == head, jnp.sum(skewed, 0, keepdims=True), 0.0)
    table = lax.dot_general(
        sums, onehot, (((1,), (1,)), ((), ())), precision=lax.Precision.HIGHEST, preferred_element_type=F32
    )
    gains = both(pack_own[half:], pack_peer[half:])
    wide = whole.shape[1]
    extra = two_rows(gains[:1], wide, 8, 0) + two_rows(gains[1:2], wide, 8, 2)
    table = jnp.concatenate([table, jnp.zeros((8, wide - buckets), F32)], 1)
    emit(whole, outs, order, size, jnp.concatenate([extra, table], 0).astype(BF16))


def two_rows(vector, wide, count, first):
    row = lax.broadcasted_iota(jnp.int32, (count, wide), 0)
    return jnp.where(row == first, vector[:, :wide], 0.0) + jnp.where(row == first + 1, vector[:, wide:], 0.0)


def input_grad_kernel(chip_own, chip_other, x, gain, grad_hidden, hidden_two, out_own, out_other, pack):
    half = hidden_two.shape[0]
    resid = x[own_rows(lax.axis_index("tensor") % 2, half), :].astype(F32)
    added, _ = norm_back(resid, row_of(gain), both(chip_own[:half], chip_other[:half]))
    pack[:half] = (grad_hidden[...] + added).astype(BF16)
    pack[half:] = (hidden_two[...] + both(out_own[...], out_other[:half])).astype(BF16)


def rows_kernel(own, peer, encoded_own, encoded_other, input_grad, layer_out, encoded_grad):
    half = own.shape[0] // 2
    core = lax.axis_index("tensor") % 2
    for place, out in ((0, input_grad), (half, layer_out)):
        out[own_rows(core, half), :] = own[place : place + half]
        out[own_rows(1 - core, half), :] = peer[place : place + half]
    encoded_grad[...] = both(encoded_own[...], encoded_other[half:]).astype(BF16)


def both(left, right):
    return left.astype(F32) + right.astype(F32)


def low_sum(left, right):
    return both(left, right).astype(BF16)


def round_two_kernel(
    up_keep, up_got, down_keep, down_got, ca_send, cb_send, zo_send, up_next, x_send, down_next
):
    wide = ca_send.shape[2]
    for keep, got, new, send, other in (
        (up_keep, up_got, up_next, zo_send, cb_send),
        (down_keep, down_got, down_next, x_send, ca_send),
    ):
        for entry in range(2):
            new[entry] = low_sum(keep[entry], got[entry])
            send[entry] = low_sum(keep[2 + entry], got[2 + entry])
            send[2 + entry, :, :wide] = other[2 * entry]
            send[2 + entry, :, wide:] = other[2 * entry + 1]


def round_three_kernel(
    up_keep, down_keep, zo_got, x_got, ca_keep, cb_keep, sa_send, sb_send, chip_own, chip_other,
    ffn_send, ffn_keep, x_send, zo_send, ca_next, cb_next, gains,
):
    size, wide = ca_keep.shape[1:]
    more = sb_send.shape[1]
    for entry, target in enumerate((ffn_keep, ffn_send)):
        target[:size] = low_sum(up_keep[entry], zo_got[entry])
        target[size:] = low_sum(down_keep[entry], x_got[entry])

    def first_sum(keep, got, entry):
        side = (entry % 2) * wide
        return low_sum(keep[entry], got[2 + entry // 2, :, side : side + wide])

    half = chip_own.shape[0] - EXTRA
    gain = of_high_low(chip_own[half:]) + of_high_low(chip_other[half:])
    gain = two_rows(gain, wide, EXTRA, 4).astype(BF16)
    gains[...] = gain
    for entry in range(2):
        ca_next[entry] = first_sum(ca_keep, x_got, entry)
        cb_next[entry] = first_sum(cb_keep, zo_got, entry)
        x_send[entry] = first_sum(cb_keep, zo_got, 2 + entry)
        zo_send[entry * size : (entry + 1) * size] = first_sum(ca_keep, x_got, 2 + entry)
    for entry in range(4):
        x_send[2 + entry] = sa_send[entry]
        start = 2 * size + entry * more
        zo_send[start : start + size] = sb_send[entry, :size]
        zo_send[start + size : start + more] = low_sum(sb_send[entry, size:], gain)


def round_four_kernel(
    x_got, zo_got, ca_keep, cb_keep, sa_keep, sb_keep, gains,
    cross_send, cross_keep, sa_send, sa_next, sb_send, sb_next,
):
    size = ca_keep.shape[1]
    more = sb_keep.shape[1]
    for entry, target in enumerate((cross_keep, cross_send)):
        target[:size] = low_sum(ca_keep[entry], zo_got[entry * size : (entry + 1) * size])
        target[size:] = low_sum(cb_keep[entry], x_got[entry])
    for first, sa_out, sb_out in ((0, sa_next, sb_next), (2, sa_send, sb_send)):
        for entry in range(2):
            sa_out[entry] = low_sum(sa_keep[first + entry], x_got[2 + first + entry])
            start = 2 * size + (first + entry) * more
            sb_out[entry, :size] = low_sum(sb_keep[first + entry, :size], zo_got[start : start + size])
            extra = low_sum(sb_keep[first + entry, size:], gains[...])
            sb_out[entry, size:] = low_sum(extra, zo_got[start + size : start + more])


def round_five_kernel(sa_keep, sa_got, sb_keep, sb_got, send, keep):
    size = sa_keep.shape[1]
    for entry, target in enumerate((keep, send)):
        target[:size] = low_sum(sa_keep[entry], sa_got[entry])
        target[size:] = low_sum(sb_keep[entry], sb_got[entry])


def ffn_final_kernel(keep, got, up, down):
    size = up.shape[0]
    up[...] = both(keep[:size], got[:size])
    down[...] = both(keep[size:], got[size:])


def pair_final(keep, got, rows, first, second, turn):
    count = first.shape[1]
    total = both(keep[rows], got[rows])
    first[...] = total[:, :count]
    second[...] = total[:, count:].T if turn else total[:, count:]


def cross_final_kernel(keep, got, key, value, query, output):
    size = key.shape[0]
    pair_final(keep, got, slice(0, size), key, value, False)
    pair_final(keep, got, slice(size, 2 * size), query, output, True)


def self_final_kernel(keep, got, query, key, value, output, table, gain_two, gain_three, gain_one):
    size = key.shape[0]
    pair_final(keep, got, slice(0, size), query, key, False)
    pair_final(keep, got, slice(size, 2 * size), value, output, True)
    extra = both(keep[2 * size :], got[2 * size :])
    table[...] = extra[8 : 8 + table.shape[0], : table.shape[1]]
    wide = 2 * extra.shape[1]
    back = wide - lax.axis_index("dp") * size
    for row, out in ((0, gain_two), (2, gain_three), (4, gain_one)):
        whole = jnp.concatenate([extra[row : row + 1], extra[row + 1 : row + 2]], 1)
        out[...] = pltpu.roll(jnp.broadcast_to(whole, (8, wide)), back, 1)[:1, :size]


def run(kernel, name, outs, ins, us=0.0, scratch=(), scalars=0, far=0, sems=0, after=(), limit=VMEM_LIMIT):
    shapes = [jax.ShapeDtypeStruct(shape, dtype) for shape, dtype in outs]
    idle = len(after)
    body = kernel
    if idle:

        def body(*refs):
            kernel(*refs[: len(ins)], *refs[len(ins) + idle :])

    vmem = pl.BlockSpec(memory_space=pltpu.VMEM)
    smem = pl.BlockSpec(memory_space=pltpu.SMEM)
    hbm = pl.BlockSpec(memory_space=pltpu.HBM)
    free = pl.BlockSpec(memory_space=pl.ANY)
    place = [smem] * scalars + [hbm] * far + [vmem] * (len(ins) - scalars - far) + [free] * idle
    ins = [
        pltpu.with_memory_space_constraint(item, pltpu.HBM) if spec is hbm else item for item, spec in zip(ins, place)
    ]
    result = pl.pallas_call(
        body,
        out_shape=shapes,
        in_specs=place,
        out_specs=[vmem] * len(shapes),
        scratch_shapes=[pltpu.VMEM(shape, dtype) for shape, dtype in scratch]
        + ([pltpu.SemaphoreType.DMA((sems,))] if sems else []),
        compiler_params=pltpu.CompilerParams(vmem_limit_bytes=limit),
        cost_estimate=pl.CostEstimate(flops=int(us * 1.15e9), bytes_accessed=0, transcendentals=0),
        name=name,
    )(*ins, *after)
    return result[0] if len(shapes) == 1 else result


def listed(result):
    return list(result) if isinstance(result, (list, tuple)) else [result]


def to_core(value):
    return lax.ppermute(value, "tensor", [(i, i ^ 1) for i in range(lax.axis_size("tensor"))])


def to_chip(value):
    return lax.ppermute(value, "tensor", [(i, i ^ 2) for i in range(lax.axis_size("tensor"))])


def to_peer(value, bit):
    return lax.ppermute(value, "dp", [(i, i ^ (1 << bit)) for i in range(lax.axis_size("dp"))])


def on_device(
    inputs, encoded, dec_len, enc_len, language, objective, distance_bucket, token_weights, cotangent,
    gain_self, self_query, self_key, self_value, self_output, bias_table,
    gain_cross, cross_query, cross_key, cross_value, cross_output, gain_ffn, ffn_up, ffn_down,
):
    seqs, length, width = inputs.shape
    half = length // 2
    columns = self_query.shape[1]
    heads = columns // HEAD_DIM
    units = ffn_up.shape[1]
    span_part = encoded.shape[1]
    span = span_part * lax.axis_size("tensor")
    dp = lax.axis_size("dp")
    size = width // dp
    bits = dp.bit_length() - 1
    halving = bits == 3 and dp == 8 and size % 16 == 0
    along_x, along_z = ((0, 1, 2), (1, 0, 2)) if halving else (None, None)
    latest = []

    def go(kernel, name, outs, ins, last=False, **how):
        after = [item for item in latest if not any(item is one for one in ins)]
        result = run(kernel, name, outs, ins, after=after, **how)
        if not last:
            results = result if isinstance(result, (list, tuple)) else [result]
            latest[:] = [min(results, key=lambda item: item.size * item.dtype.itemsize)]
        return result

    def plus(left, right, name):
        return go(add_kernel, name, [(left.shape, left.dtype)], [left, right])

    def payload(order, wide, extra=0):
        if order is None:
            return [((width + extra, wide), BF16)]
        return [((dp // 2, size + extra, wide), BF16)] * 2

    x = inputs.reshape(length, width)
    cot = cotangent.reshape(length, width)
    gain_one, gain_two, gain_three = gain_self, gain_cross, gain_ffn
    self_query, self_key, self_value = self_query.T, self_key.T, self_value.T
    cross_query, cross_key, cross_value = cross_query.T, cross_key.T, cross_value.T
    table = bias_table.T
    bucket = distance_bucket.reshape(1, length)
    e0 = encoded.reshape(span_part, width)

    e1 = to_chip(e0)
    e2 = to_core(e0)
    e3 = to_core(e1)
    wk_peer = to_core(cross_key)
    wv_peer = to_core(cross_value)
    keep, send, normed_one, query_one, key_one, value_one, context_one, probs_one = go(
        self_forward_kernel, "self_forward",
        [((half, width), BF16)] * 2 + [((length, width), BF16)] + [((length, columns), BF16)] * 4
        + [((heads, length, length), BF16)],
        [dec_len, x, gain_one, self_query, self_key, self_value, self_output, bucket, table],
        scratch=[((length, width), BF16), (x.shape, BF16), (gain_one.shape, F32)] + [(self_query.shape, BF16)] * 3
        + [(self_output.shape, BF16), (bucket.shape, jnp.int32), (table.shape, F32)],
        scalars=1, far=8, sems=8, us=3.5,
    )
    latest.append(e2)
    got = to_core(send)
    source_outs = [((span // 2, columns), BF16)] * 4
    early = go(
        cross_source_kernel, "source_first", source_outs, [e0, e1, cross_key, cross_value, wk_peer, wv_peer], us=LONG
    )
    chip_one = plus(keep, got, "self_sum")
    other_one = to_chip(chip_one)
    wq_source, wo_source, _ = lax.optimization_barrier((cross_query, cross_output, chip_one))
    wq_peer = to_core(wq_source)
    wo_peer = to_core(wo_source)
    late = go(
        cross_source_kernel, "source_second", source_outs, [e2, e3, cross_key, cross_value, wk_peer, wv_peer],
        us=LONG,
    )

    (partial_two, hidden_one, normed_two, q_own, q_peer, context_own, probs_own, probs_peer, pack_forward,
     k_own, v_own, k_peer, v_peer) = go(
        cross_forward_kernel, "cross_forward",
        [((half, width), BF16), ((half, width), F32), ((half, width), BF16)] + [((half, columns), BF16)] * 3
        + [((heads, half, span), BF16)] * 2 + [((half, width + columns), BF16)] + [((span, columns), BF16)] * 4,
        [enc_len, chip_one, other_one, x, gain_two, cross_query, wq_peer, cross_output, wo_peer, *early, *late],
        scalars=1,
    )
    other_two = to_chip(partial_two)
    up_source, down_source, _ = lax.optimization_barrier((ffn_up, ffn_down, partial_two))
    down_peer = to_core(down_source)
    up_peer = to_core(up_source)
    pack_forward_peer = to_core(pack_forward)
    grad_full, branch_three, branch_three_peer, act_grad, act_grad_peer = go(
        out_grad_kernel, "out_grad",
        [((half, width), F32)] + [((half, width), BF16)] * 2 + [((half, units), F32)] * 2,
        [objective, language, dec_len, token_weights, cot, ffn_down, down_peer],
        scalars=3, us=FILL,
    )

    latest.append(pack_forward_peer)
    partial_three, hidden_two, normed_three, act_own, grad_pre_own, pack_ffn = go(
        ffn_kernel, "ffn",
        [((half, width), BF16), ((half, width), F32), ((half, width), BF16)] + [((half, units), BF16)] * 2
        + [((half, width + 2 * units), BF16)],
        [partial_two, other_two, hidden_one, gain_three, ffn_up, up_peer, act_grad, act_grad_peer],
    )
    other_three = to_chip(partial_three)
    pack_ffn_peer = to_core(pack_ffn)

    def ffn_weights(*refs):
        ffn_weights_kernel((along_x, along_z), size, *refs)

    ffn_payloads = go(
        ffn_weights, "ffn_weights", payload(along_x, width) + payload(along_z, width),
        [normed_three, pack_ffn_peer, act_own, grad_pre_own, branch_three, branch_three_peer],
        scratch=[((width, units), BF16), ((length, width), BF16), ((length, units), BF16)], us=FILL,
    )

    (partial_four, grad_two, gain_grad_three, gl_own, gl_peer, gc_own, gc_peer, gq_own, branch_two,
     pack_backward) = go(
        cross_backward_kernel, "cross_backward",
        [((half, width), BF16), ((half, width), F32), ((8, width), F32)] + [((heads, half, span), BF16)] * 2
        + [((half, columns), BF16)] * 3 + [((half, width), BF16), ((half, width + columns), BF16)],
        [partial_three, other_three, hidden_two, gain_three, grad_full, cross_output, wo_peer,
         k_own, v_own, k_peer, v_peer, probs_own, probs_peer, cross_query, wq_peer],
    )
    other_four = to_chip(partial_four)
    pack_backward_peer = to_core(pack_backward)
    source_grad = go(
        source_grad_kernel, "source_grad", [((2 * span, columns), BF16)], [gl_peer, probs_peer, gc_peer, q_peer]
    )
    source_grad_peer = to_core(source_grad)
    wide = 2 * columns

    def cross_weights(*refs):
        cross_weights_kernel((along_x, along_z), size, *refs)

    *cross_payload, source_total = go(
        cross_weights, "cross_weights", payload(along_x, wide) + payload(along_z, wide) + [((span, wide), BF16)],
        [gl_own, probs_own, gc_own, q_own, source_grad_peer, e0, e1, e2, e3, normed_two, pack_forward_peer,
         branch_two, pack_backward_peer, context_own, gq_own],
        scratch=[((width, wide), BF16), ((span, width), BF16), ((4 * half, wide), BF16)],
    )
    ca_payload, cb_payload = cross_payload[: len(cross_payload) // 2], cross_payload[len(cross_payload) // 2 :]

    if halving:
        up_keep, up_send, down_keep, down_send = ffn_payloads
        ca_keep, ca_send = ca_payload
        cb_keep, cb_send = cb_payload
        zo_send, up_keep, x_send, down_keep = go(
            round_two_kernel, "round_two",
            [((4, size, width), BF16), ((2, size, width), BF16)] * 2,
            [up_keep, to_peer(up_send, 0), down_keep, to_peer(down_send, 1), ca_send, cb_send],
        )
        x_got = to_peer(x_send, 0)
        zo_got = to_peer(zo_send, 1)

    grad_one, pack_self = go(
        self_norm_kernel, "self_norm", [((half, width), F32), ((half + EXTRA, width), BF16)],
        [partial_four, other_four, hidden_one, gain_two, grad_two, gain_grad_three],
    )
    pack_self_peer = to_core(pack_self)
    encoded_keep, encoded_send = go(
        encoded_kernel, "encoded", [((span // 2, width), BF16)] * 2, [source_total, cross_key, cross_value], us=FILL
    )
    encoded_got = to_core(encoded_send)
    keep, send, branch_one, gq_one, gk_one, gv_one, gl_one = go(
        self_backward_kernel, "self_backward",
        [((half + EXTRA, width), BF16)] * 2 + [((length, width), BF16)] + [((length, columns), BF16)] * 3
        + [((heads, length, length), BF16)],
        [pack_self, pack_self_peer, self_output, self_query, self_key, self_value, query_one, key_one, value_one,
         probs_one, x],
        scratch=[((length, width), BF16)],
    )
    got = to_core(send)

    def self_first(*refs):
        self_first_kernel(along_x, size, *refs)

    def self_second(*refs):
        self_second_kernel(along_z, size, table.shape[1], *refs)

    sb_payload = listed(go(
        self_second, "self_second", payload(along_z, wide, EXTRA),
        [normed_one, branch_one, gv_one, context_one, gl_one, bucket, pack_self, pack_self_peer],
        scratch=[((width, wide), BF16), ((2 * length, wide), BF16), ((2 * length, width), BF16)], us=FILL,
    ))
    chip_five = go(input_sum_kernel, "input_sum", [(keep.shape, BF16)], [keep, got])
    other_five = to_chip(chip_five)
    sa_payload = listed(go(
        self_first, "self_first", payload(along_x, wide), [normed_one, gq_one, gk_one],
        scratch=[((width, wide), BF16), ((length, wide), BF16)], us=FILL,
    ))

    if halving:
        sa_keep, sa_send = sa_payload
        sb_keep, sb_send = sb_payload
        more = size + EXTRA
        ffn_send, ffn_keep, x_send, zo_send, ca_keep, cb_keep, gains = go(
            round_three_kernel, "round_three",
            [((2 * size, width), BF16)] * 2 + [((6, size, wide), BF16), ((2 * size + 4 * more, wide), BF16)]
            + [((2, size, wide), BF16)] * 2 + [((EXTRA, wide), BF16)],
            [up_keep, down_keep, zo_got, x_got, ca_keep, cb_keep, sa_send, sb_send, chip_five, other_five],
        )
        x_got = to_peer(x_send, 0)
        zo_got = to_peer(zo_send, 1)
        ffn_got = to_peer(ffn_send, 2)

    branch_out, encoded_part, out_send = go(
        ffn_out_kernel, "ffn_out", [((half, width), BF16), ((span_part, width), BF16), ((half + span_part, width), BF16)],
        [act_own, pack_ffn, ffn_down, down_peer, encoded_keep, encoded_got],
    )
    out_other = to_chip(out_send)

    if halving:
        cross_send, cross_keep, sa_send, sa_keep, sb_send, sb_keep = go(
            round_four_kernel, "round_four",
            [((2 * size, wide), BF16)] * 2 + [((2, size, wide), BF16)] * 2 + [((2, more, wide), BF16)] * 2,
            [x_got, zo_got, ca_keep, cb_keep, sa_keep, sb_keep, gains],
        )
        sa_got = to_peer(sa_send, 1)
        sb_got = to_peer(sb_send, 0)
        cross_got = to_peer(cross_send, 2)
        up, down = go(ffn_final_kernel, "ffn_final", [((size, width), F32)] * 2, [ffn_keep, ffn_got], us=LONG, last=True)

    pack_rows = go(
        input_grad_kernel, "input_grad", [((2 * half, width), BF16)],
        [chip_five, other_five, x, gain_one, grad_one, hidden_two, branch_out, out_other],
    )
    pack_rows_peer = to_core(pack_rows)

    if halving:
        self_send, self_keep = go(
            round_five_kernel, "round_five", [((size + more, wide), BF16)] * 2, [sa_keep, sa_got, sb_keep, sb_got]
        )
        self_got = to_peer(self_send, 2)

    input_grad, layer_out, encoded_grad = go(
        rows_kernel, "rows", [((length, width), BF16)] * 2 + [((span_part, width), BF16)],
        [pack_rows, pack_rows_peer, encoded_part, out_other], last=True,
    )

    if halving:
        square = ((size, columns), F32)
        turned = ((columns, size), F32)
        grad_cross_key, grad_cross_value, grad_cross_query, grad_cross_output = go(
            cross_final_kernel, "cross_final", [square] * 3 + [turned], [cross_keep, cross_got], us=LONG, last=True
        )
        (grad_self_query, grad_self_key, grad_self_value, grad_self_output, grad_table, grad_gain_two,
         grad_gain_three, grad_gain_one) = go(
            self_final_kernel, "self_final",
            [square] * 3 + [turned, (table.shape, F32)] + [((1, size), F32)] * 3, [self_keep, self_got], last=True,
        )
        grad_gain_one, grad_gain_two, grad_gain_three = (
            item.reshape(size) for item in (grad_gain_one, grad_gain_two, grad_gain_three)
        )
    else:
        index = lax.axis_index("dp")

        def gain_part(*rows):
            row = lax.psum(jnp.concatenate(rows, 0).astype(F32), "dp")
            return lax.dynamic_slice(row, (index * size,), (size,))

        def scattered(item):
            return lax.psum_scatter(item.astype(F32), "dp", scatter_dimension=0, tiled=True)

        def pair_of(item):
            item = scattered(item)
            return item[:, :columns], item[:, columns:]

        up, down = (scattered(item) for item in ffn_payloads)
        grad_cross_key, grad_cross_value = pair_of(ca_payload[0])
        grad_cross_query, grad_cross_output = pair_of(cb_payload[0])
        grad_self_query, grad_self_key = pair_of(sa_payload[0])
        grad_self_value, grad_self_output = pair_of(sb_payload[0][:width])
        grad_cross_output, grad_self_output = grad_cross_output.T, grad_self_output.T
        extra = sb_payload[0][width:]
        grad_table = lax.psum(extra[8 : 8 + heads, : table.shape[1]].astype(F32), "dp")
        gain_rows = [item[half : half + 2] for item in (chip_five, other_five)]
        grad_gain_one = gain_part(jnp.sum(jnp.concatenate(gain_rows, 0).astype(F32), 0))
        grad_gain_two = gain_part(extra[0], extra[1])
        grad_gain_three = gain_part(extra[2], extra[3])

    return (
        layer_out.reshape(seqs, length, width),
        input_grad.reshape(seqs, length, width),
        encoded_grad.reshape(seqs, span_part, width),
        grad_gain_one,
        grad_self_query,
        grad_self_key,
        grad_self_value,
        grad_self_output,
        grad_table.T,
        grad_gain_two,
        grad_cross_query,
        grad_cross_key,
        grad_cross_value,
        grad_cross_output,
        grad_gain_three,
        up,
        down.T,
    )


def solution(mesh):
    return jax.shard_map(
        on_device,
        mesh=mesh,
        in_specs=(
            P("dp", None, None),
            P("dp", "tensor", None),
            P("dp"),
            P("dp"),
            P("dp"),
            P("dp"),
            P(),
            P(),
            P("dp", None, None),
            P(),
            P(None, "tensor"),
            P(None, "tensor"),
            P(None, "tensor"),
            P("tensor", None),
            P(None, "tensor"),
            P(),
            P(None, "tensor"),
            P(None, "tensor"),
            P(None, "tensor"),
            P("tensor", None),
            P(),
            P(None, "tensor"),
            P("tensor", None),
        ),
        out_specs=(
            P("dp", None, None),
            P("dp", None, None),
            P("dp", "tensor", None),
            P("dp"),
            P("dp", "tensor"),
            P("dp", "tensor"),
            P("dp", "tensor"),
            P("tensor", "dp"),
            P(None, "tensor"),
            P("dp"),
            P("dp", "tensor"),
            P("dp", "tensor"),
            P("dp", "tensor"),
            P("tensor", "dp"),
            P("dp"),
            P("dp", "tensor"),
            P("tensor", "dp"),
        ),
        check_vma=False,
    )
```

time: 170 us -> 108 us (0.64)
  local copies, waits for them, and re-layouts: 24.3 us -> 0.1 us
  waiting for transfers between devices: 69.1 us -> 50.6 us
  starting transfers between devices: 39.1 us -> 26.1 us
  Pallas kernels: 30.6 us -> 27.1 us
  other arithmetic: 2.48 us -> 0 us
    unnamed x85 -> x36, local copies, waits for them, and re-layouts: 20.3 us -> 0.1 us
    ppermute x15 -> x11, waiting for transfers between devices: 51.9 us -> 38.2 us  [to_peer(): lax.ppermute(value, 'dp', [(i, i ^ 1 << bit) for i in range(lax.axis_size...]
    ppermute x15 -> x11, starting transfers between devices: 22.4 us -> 12.2 us  [to_peer(): lax.ppermute(value, 'dp', [(i, i ^ 1 << bit) for i in range(lax.axis_size...]
    ppermute x8 -> x7, waiting for transfers between devices: 15.1 us -> 10.6 us  [to_chip(): lax.ppermute(value, 'tensor', [(i, i ^ 2) for i in range(lax.axis_size('t...]
    pallas_call x33 -> x27, Pallas kernels: 30.6 us -> 27.1 us  [run(): pl.pallas_call(body, out_shape=shapes, in_specs=place, out_specs=[vmem] *...]
    ppermute x8 -> x7, starting transfers between devices: 12.3 us -> 9.81 us  [to_chip(): lax.ppermute(value, 'tensor', [(i, i ^ 2) for i in range(lax.axis_size('t...]
    transpose x3 -> x0, local copies, waits for them, and re-layouts: 2.1 us -> none  [the longest x1 0.78 us: on_device(): own[:size, 3 * columns:]]
    add x3 -> x0, other arithmetic: 1.74 us -> none  [on_device(): left[0].astype(F32) + right[0].astype(F32)]
  transfers between devices with their start and end apart: 42 -> 35, of which waited for: 15 -> 15; matrix products, arithmetic and copies ran while one was open for 7% -> 0% of each run, Pallas kernels for 15% -> 20%
where the time goes in v2:
time: 108 us
  waiting for transfers between devices  50.6 us (47%)
  Pallas kernels  27.1 us (25%)
  starting transfers between devices  26.1 us (24%)
  between operations  3.75 us (3%)
    ppermute x11, waiting for transfers between devices, to_peer(): lax.ppermute(value, 'dp', [(i, i ^ 1 << bit) for i in range(lax.axis_size...  38.2 us
    pallas_call x27, Pallas kernels, run(): pl.pallas_call(body, out_shape=shapes, in_specs=place, out_specs=[vmem] *...  27.1 us
    ppermute x11, starting transfers between devices, to_peer(): lax.ppermute(value, 'dp', [(i, i ^ 1 << bit) for i in range(lax.axis_size...  12.2 us
    ppermute x7, waiting for transfers between devices, to_chip(): lax.ppermute(value, 'tensor', [(i, i ^ 2) for i in range(lax.axis_size('t...  10.6 us
    ppermute x7, starting transfers between devices, to_chip(): lax.ppermute(value, 'tensor', [(i, i ^ 2) for i in range(lax.axis_size('t...  9.81 us
    ppermute x17, starting transfers between devices, to_core(): lax.ppermute(value, 'tensor', [(i, i ^ 1) for i in range(lax.axis_size('t...  4.12 us
  transfers between devices with their start and end apart: 35, of which 15 were waited for; matrix products, arithmetic and copies ran while one was open for 0% of the time, Pallas kernels for 20%

profile of v2, /device:TPU:0, one launch (start us, length us, event | category | flops | bytes accessed | tf_op | source)
XLA Modules:
  0.0 107.7 jit_solution(9235935916654774181)
XLA Ops:
  0.7 0.5 collective-permute-start.4
  1.2 2.6 %collective-permute-start.1 = (bf16[128,768]{1,0:T(8,128)(2,1)}, bf16[128,768]{1,0:T(8,128)(2,1)S(1)}, u32[]{:S(2)}, u32[]{:S(2)}) collective-permute-start(bf16[128,768]{1,0:T(8,128)(2,1)} %bitcast.33), channel_id=1, source_target_pairs={{0,2},{1,3},{2,0},{3,1},{4,6},{5,7},{6,4},{7,5},{8,10},{9,11},{10,... | collective-permute-start | bytes 589832 | tf_op jit(solution)/shard_map/ppermute | solution.py:701
  3.8 0.2 collective-permute-start.2
  3.9 0.3 collective-permute-start.3
  5.0 4.1 %self_forward.1 = (bf16[128,768]{1,0:T(8,128)(2,1)S(1)}, bf16[128,768]{1,0:T(8,128)(2,1)S(1)}, bf16[256,768]{1,0:T(8,128)(2,1)S(1)}, bf16[256,192]{1,0:T(8,128)(...) custom-call(s32[1]{0:T(128)S(6)} %copy.40.dec_len.refs_2_, ...), custom_call_target="tpu_custom_call" | custom-call | flops 4024999936 | tf_op jit(solution)/shard_map/self_forward/pallas_call | solution.py:678
  9.1 0.2 collective-permute-start
  10.0 0.4 collective-permute-start.8
  10.4 0.9 source_first.1
  11.4 1.0 collective-permute-start.5
  12.4 0.2 collective-permute-start.6
  12.6 0.3 collective-permute-start.7
  12.9 0.9 source_second.1
  13.8 4.7 %collective-permute-done.5.chip_other = bf16[128,768]{1,0:T(8,128)(2,1)S(1)} collective-permute-done((bf16[128,768]{1,0:T(8,128)(2,1)S(1)}, bf16[128,768]{1,0:T(8,128)(2,1)S(1)}, u32[]{:S(2)}, u32[]{:S(2)}) %collective-permute-start.5) | collective-permute-done | bytes 196640 | tf_op jit(solution)/shard_map/ppermute | solution.py:701
  18.5 3.2 %cross_forward.1 = (bf16[128,768]{1,0:T(8,128)(2,1)S(1)}, f32[128,768]{1,0:T(8,128)S(1)}, bf16[128,768]{1,0:T(8,128)(2,1)S(1)}, bf16[128,192]{1,0:T(8,128)(2,1)S...) custom-call(s32[1]{0:T(128)S(6)} %copy.41.enc_len, ...), custom_call_target="tpu_custom_call" | custom-call | tf_op jit(solution)/shard_map/cross_forward/pallas_call | solution.py:678
  21.8 0.5 collective-permute-start.10
  23.6 1.3 %collective-permute-start.9 = (bf16[128,768]{1,0:T(8,128)(2,1)S(1)}, bf16[128,768]{1,0:T(8,128)(2,1)S(1)}, u32[]{:S(2)}, u32[]{:S(2)}) collective-permute-start(bf16[128,768]{1,0:T(8,128)(2,1)S(1)} %get-tuple-element.147.refs_0_), channel_id=1, source_target_pairs={{0,2},{1,3},{2,0},{3,1},{4,6},{5,7},{6,4},{7,5},{8,10},{9,11},{10,... | collective-permute-start | bytes 589832 | tf_op jit(solution)/shard_map/ppermute | solution.py:701
  24.9 0.9 out_grad.1
  25.9 4.7 %collective-permute-done.9.refs_1_ = bf16[128,768]{1,0:T(8,128)(2,1)S(1)} collective-permute-done((bf16[128,768]{1,0:T(8,128)(2,1)S(1)}, bf16[128,768]{1,0:T(8,128)(2,1)S(1)}, u32[]{:S(2)}, u32[]{:S(2)}) %collective-permute-start.9) | collective-permute-done | bytes 196640 | tf_op jit(solution)/shard_map/ppermute | solution.py:701
  30.6 1.6 %ffn.1 = (bf16[128,768]{1,0:T(8,128)(2,1)S(1)}, f32[128,768]{1,0:T(8,128)S(1)}, bf16[128,768]{1,0:T(8,128)(2,1)S(1)}, bf16[128,768]{1,0:T(8,128)(2,1)S(1)}, bf16...) custom-call(bf16[128,768]{1,0:T(8,128)(2,1)S(1)} %get-tuple-element.147.refs_0_, ...), custom_call_target="tpu_custom_call" | custom-call | tf_op jit(solution)/shard_map/ffn/pallas_call | solution.py:678
  32.3 1.3 %collective-permute-start.13 = (bf16[128,768]{1,0:T(8,128)(2,1)S(1)}, bf16[128,768]{1,0:T(8,128)(2,1)S(1)}, u32[]{:S(2)}, u32[]{:S(2)}) collective-permute-start(bf16[128,768]{1,0:T(8,128)(2,1)S(1)} %get-tuple-element.156.refs_6_.refs_0_), channel_id=1, source_target_pairs={{0,2},{1,3},{2,0},{3,1},{4,6},{5,7},{6,4},{7,5},{8,10},{9,11},{10,... | collective-permute-start | bytes 589832 | tf_op jit(solution)/shard_map/ppermute | solution.py:701
  33.6 0.7 collective-permute-done.14.refs_1_
  34.3 1.0 ffn_weights.1
  35.3 1.6 %collective-permute-start.16 = (bf16[4,96,768]{2,1,0:T(8,128)(2,1)S(1)}, bf16[4,96,768]{2,1,0:T(8,128)(2,1)S(1)}, u32[]{:S(2)}, u32[]{:S(2)}) collective-permute-start(bf16[4,96,768]{2,1,0:T(8,128)(2,1)S(1)} %get-tuple-element.174), channel_id=1, source_target_pairs={{0,4},{4,0},{8,12},{12,8},{16,20},{20,16},{24,28},{28,24},{1,5},{5... | collective-permute-start | bytes 1769480 | tf_op jit(solution)/shard_map/ppermute | solution.py:705
  36.9 1.6 %collective-permute-start.17 = (bf16[4,96,768]{2,1,0:T(8,128)(2,1)S(1)}, bf16[4,96,768]{2,1,0:T(8,128)(2,1)S(1)}, u32[]{:S(2)}, u32[]{:S(2)}) collective-permute-start(bf16[4,96,768]{2,1,0:T(8,128)(2,1)S(1)} %get-tuple-element.176), channel_id=1, source_target_pairs={{0,8},{4,12},{8,0},{12,4},{16,24},{20,28},{24,16},{28,20},{1,9},{5... | collective-permute-start | bytes 1769480 | tf_op jit(solution)/shard_map/ppermute | solution.py:705
  38.4 1.2 %collective-permute-done.13.refs_1_ = bf16[128,768]{1,0:T(8,128)(2,1)S(1)} collective-permute-done((bf16[128,768]{1,0:T(8,128)(2,1)S(1)}, bf16[128,768]{1,0:T(8,128)(2,1)S(1)}, u32[]{:S(2)}, u32[]{:S(2)}) %collective-permute-start.13) | collective-permute-done | bytes 196640 | tf_op jit(solution)/shard_map/ppermute | solution.py:701
  39.6 2.7 %cross_backward.1 = (bf16[128,768]{1,0:T(8,128)(2,1)S(1)}, f32[128,768]{1,0:T(8,128)S(1)}, f32[8,768]{1,0:T(8,128)S(1)}, bf16[3,128,512]{2,1,0:T(8,128)(2,1)S(1)...) custom-call(bf16[128,768]{1,0:T(8,128)(2,1)S(1)} %get-tuple-element., ...), custom_call_target="tpu_custom_call" | custom-call | tf_op jit(solution)/shard_map/cross_backward/pallas_call | solution.py:678
  42.4 0.4 source_grad.1.refs_15_
  42.8 0.5 collective-permute-start.19
  43.3 1.2 %collective-permute-start.15 = (bf16[128,768]{1,0:T(8,128)(2,1)S(1)}, bf16[128,768]{1,0:T(8,128)(2,1)S(1)}, u32[]{:S(2)}, u32[]{:S(2)}) collective-permute-start(bf16[128,768]{1,0:T(8,128)(2,1)S(1)} %get-tuple-element.171.refs_0_), channel_id=1, source_target_pairs={{0,2},{1,3},{2,0},{3,1},{4,6},{5,7},{6,4},{7,5},{8,10},{9,11},{10,... | collective-permute-start | bytes 589832 | tf_op jit(solution)/shard_map/ppermute | solution.py:701
  44.5 0.6 collective-permute-done.19.refs_12_
  45.1 1.6 %cross_weights.1 = (bf16[4,96,384]{2,1,0:T(8,128)(2,1)S(1)}, bf16[4,96,384]{2,1,0:T(8,128)(2,1)S(1)}, bf16[4,96,384]{2,1,0:T(8,128)(2,1)S(1)}, bf16[4,96,384]{2,1,0:T(8,128)(2,1)S(1)}, bf16[512,384]{1,0:T(8,128)(2,1)S(1)}) custom-call(bf16[3,128,512]{2,1,0:T(8,128)(2,1)S(1)} %get-tuple-element.177.refs_0_, ...), custom_call_target="tpu_custom_call" | custom-call | tf_op jit(solution)/shard_map/cross_weights/pallas_call | solution.py:678
  46.7 4.1 %collective-permute-done.16.refs_1_ = bf16[4,96,768]{2,1,0:T(8,128)(2,1)S(1)} collective-permute-done((bf16[4,96,768]{2,1,0:T(8,128)(2,1)S(1)}, bf16[4,96,768]{2,1,0:T(8,128)(2,1)S(1)}, u32[]{:S(2)}, u32[]{:S(2)}) %collective-permute-start.16) | collective-permute-done | bytes 589856 | tf_op jit(solution)/shard_map/ppermute | solution.py:705
  50.7 1.2 %collective-permute-done.17.refs_3_ = bf16[4,96,768]{2,1,0:T(8,128)(2,1)S(1)} collective-permute-done((bf16[4,96,768]{2,1,0:T(8,128)(2,1)S(1)}, bf16[4,96,768]{2,1,0:T(8,128)(2,1)S(1)}, u32[]{:S(2)}, u32[]{:S(2)}) %collective-permute-start.17) | collective-permute-done | bytes 589856 | tf_op jit(solution)/shard_map/ppermute | solution.py:705
  51.9 0.5 round_two.1
  52.4 0.2 self_norm.1
  52.8 0.6 encoded.1
  53.4 0.5 collective-permute-start.23
  53.9 1.6 %collective-permute-start.24 = (bf16[4,96,768]{2,1,0:T(8,128)(2,1)S(1)}, bf16[4,96,768]{2,1,0:T(8,128)(2,1)S(1)}, u32[]{:S(2)}, u32[]{:S(2)}) collective-permute-start(bf16[4,96,768]{2,1,0:T(8,128)(2,1)S(1)} %get-tuple-element.209), channel_id=1, source_target_pairs={{0,8},{4,12},{8,0},{12,4},{16,24},{20,28},{24,16},{28,20},{1,9},{5... | collective-permute-start | bytes 1769480 | tf_op jit(solution)/shard_map/ppermute | solution.py:705
  55.5 0.5 collective-permute-start.25
  56.1 1.7 %self_backward.1 = (bf16[144,768]{1,0:T(8,128)(2,1)S(1)}, bf16[144,768]{1,0:T(8,128)(2,1)S(1)}, bf16[256,768]{1,0:T(8,128)(2,1)S(1)}, bf16[256,192]{1,0:T(8,128)...) custom-call(bf16[144,768]{1,0:T(8,128)(2,1)S(1)} %get-tuple-element.191.refs, ...), custom_call_target="tpu_custom_call" | custom-call | tf_op jit(solution)/shard_map/self_backward/pallas_call | solution.py:678
  57.9 1.0 self_second.1
  58.9 0.4 collective-permute-done.21.refs_1_
  59.4 1.3 %collective-permute-start.22 = (bf16[144,768]{1,0:T(8,128)(2,1)S(1)}, bf16[144,768]{1,0:T(8,128)(2,1)S(1)}, u32[]{:S(2)}, u32[]{:S(2)}) collective-permute-start(bf16[144,768]{1,0:T(8,128)(2,1)S(1)} %input_sum.1.refs_3_.refs_8_.refs_0_), channel_id=1, source_target_pairs={{0,2},{1,3},{2,0},{3,1},{4,6},{5,7},{6,4},{7,5},{8,10},{9,11},{10,... | collective-permute-start | bytes 663560 | tf_op jit(solution)/shard_map/ppermute | solution.py:701
  60.7 0.5 self_first.1
  61.2 8.1 %collective-permute-done.24.refs_2_ = bf16[4,96,768]{2,1,0:T(8,128)(2,1)S(1)} collective-permute-done((bf16[4,96,768]{2,1,0:T(8,128)(2,1)S(1)}, bf16[4,96,768]{2,1,0:T(8,128)(2,1)S(1)}, u32[]{:S(2)}, u32[]{:S(2)}) %collective-permute-start.24) | collective-permute-done | bytes 589856 | tf_op jit(solution)/shard_map/ppermute | solution.py:705
  69.3 1.3 %collective-permute-done.25.refs_3_ = bf16[4,96,768]{2,1,0:T(8,128)(2,1)S(1)} collective-permute-done((bf16[4,96,768]{2,1,0:T(8,128)(2,1)S(1)}, bf16[4,96,768]{2,1,0:T(8,128)(2,1)S(1)}, u32[]{:S(2)}, u32[]{:S(2)}) %collective-permute-start.25) | collective-permute-done | bytes 589856 | tf_op jit(solution)/shard_map/ppermute | solution.py:705
  70.6 0.3 round_three.1
  70.9 0.5 collective-permute-start.28
  71.4 0.5 collective-permute-start.27
  72.0 0.5 ffn_out.1
  72.5 1.3 %collective-permute-start.26 = (bf16[256,768]{1,0:T(8,128)(2,1)S(1)}, bf16[256,768]{1,0:T(8,128)(2,1)S(1)}, u32[]{:S(2)}, u32[]{:S(2)}) collective-permute-start(bf16[256,768]{1,0:T(8,128)(2,1)S(1)} %get-tuple-element.218), channel_id=1, source_target_pairs={{0,2},{1,3},{2,0},{3,1},{4,6},{5,7},{6,4},{7,5},{8,10},{9,11},{10,... | collective-permute-start | bytes 1179656 | tf_op jit(solution)/shard_map/ppermute | solution.py:701
  73.8 2.6 %collective-permute-start.34 = (bf16[192,768]{1,0:T(8,128)(2,1)S(1)}, bf16[192,768]{1,0:T(8,128)(2,1)S(1)}, u32[]{:S(2)}, u32[]{:S(2)}) collective-permute-start(bf16[192,768]{1,0:T(8,128)(2,1)S(1)} %get-tuple-element.248), channel_id=1, source_target_pairs={{0,16},{4,20},{8,24},{12,28},{16,0},{20,4},{24,8},{28,12},{1,17},{... | collective-permute-start | bytes 884744 | tf_op jit(solution)/shard_map/ppermute | solution.py:705
  76.4 5.9 %collective-permute-done.27.refs_0_ = bf16[6,96,384]{2,1,0:T(8,128)(2,1)S(1)} collective-permute-done((bf16[6,96,384]{2,1,0:T(8,128)(2,1)S(1)}, bf16[6,96,384]{2,1,0:T(8,128)(2,1)S(1)}, u32[]{:S(2)}, u32[]{:S(2)}) %collective-permute-start.27) | collective-permute-done | bytes 442400 | tf_op jit(solution)/shard_map/ppermute | solution.py:705
  82.3 7.1 %collective-permute-done.28.refs_1_ = bf16[640,384]{1,0:T(8,128)(2,1)S(1)} collective-permute-done((bf16[640,384]{1,0:T(8,128)(2,1)S(1)}, bf16[640,384]{1,0:T(8,128)(2,1)S(1)}, u32[]{:S(2)}, u32[]{:S(2)}) %collective-permute-start.28) | collective-permute-done | bytes 491552 | tf_op jit(solution)/shard_map/ppermute | solution.py:705
  89.3 0.2 round_four.1
  89.7 3.2 %collective-permute-start.33 = (bf16[192,384]{1,0:T(8,128)(2,1)S(1)}, bf16[192,384]{1,0:T(8,128)(2,1)S(1)}, u32[]{:S(2)}, u32[]{:S(2)}) collective-permute-start(bf16[192,384]{1,0:T(8,128)(2,1)S(1)} %get-tuple-element.223.refs_8_.refs_2_), channel_id=1, source_target_pairs={{0,16},{4,20},{8,24},{12,28},{16,0},{20,4},{24,8},{28,12},{1,17},{... | collective-permute-start | bytes 442376 | tf_op jit(solution)/shard_map/ppermute | solution.py:705
  92.9 0.3 input_grad.1.refs_4_.refs_0_
  93.3 0.9 ffn_final.1
  94.1 2.3 %collective-permute-done.30.refs_1_ = bf16[2,96,384]{2,1,0:T(8,128)(2,1)S(1)} collective-permute-done((bf16[2,96,384]{2,1,0:T(8,128)(2,1)S(1)}, bf16[2,96,384]{2,1,0:T(8,128)(2,1)S(1)}, u32[]{:S(2)}, u32[]{:S(2)}) %collective-permute-start.30) | collective-permute-done | bytes 147488 | tf_op jit(solution)/shard_map/ppermute | solution.py:705
  96.4 1.8 %collective-permute-done.31.refs_3_ = bf16[2,112,384]{2,1,0:T(8,128)(2,1)S(1)} collective-permute-done((bf16[2,112,384]{2,1,0:T(8,128)(2,1)S(1)}, bf16[2,112,384]{2,1,0:T(8,128)(2,1)S(1)}, u32[]{:S(2)}, u32[]{:S(2)}) %collective-permute-start.31) | collective-permute-done | bytes 172064 | tf_op jit(solution)/shard_map/ppermute | solution.py:705
  98.4 0.8 cross_final.1
  99.3 6.5 %collective-permute-done.32.refs_1_ = bf16[208,384]{1,0:T(8,128)(2,1)S(1)} collective-permute-done((bf16[208,384]{1,0:T(8,128)(2,1)S(1)}, bf16[208,384]{1,0:T(8,128)(2,1)S(1)}, u32[]{:S(2)}, u32[]{:S(2)}) %collective-permute-start.32) | collective-permute-done | bytes 159776 | tf_op jit(solution)/shard_map/ppermute | solution.py:705
  105.8 0.8 self_final.1
  106.7 1.0 rows.1
  (69 shorter events, 0.9 us)
Async XLA Ops:
  0.7 9.7 %collective-permute-start.4 = (bf16[128,768]{1,0:T(8,128)(2,1)}, bf16[128,768]{1,0:T(8,128)(2,1)S(1)}, u32[]{:S(2)}, u32[]{:S(2)}) collective-permute-start(bf16[128,768]{1,0:T(8,128)(2,1)} %bitcast.32), channel_id=1, source_target_pairs={{0,1},{1,0},{2,3},{3,2},{4,5},{5,4},{6,7},{7,6},{8,9},{9,8},{10,11... | collective-permute-start | bytes 589832 | tf_op jit(solution)/shard_map/ppermute | solution.py:697
  1.2 8.8 %collective-permute-start.1 = (bf16[128,768]{1,0:T(8,128)(2,1)}, bf16[128,768]{1,0:T(8,128)(2,1)S(1)}, u32[]{:S(2)}, u32[]{:S(2)}) collective-permute-start(bf16[128,768]{1,0:T(8,128)(2,1)} %bitcast.33), channel_id=1, source_target_pairs={{0,2},{1,3},{2,0},{3,1},{4,6},{5,7},{6,4},{7,5},{8,10},{9,11},{10,... | collective-permute-start | bytes 589832 | tf_op jit(solution)/shard_map/ppermute | solution.py:701
  3.8 6.6 %collective-permute-start.2 = (bf16[192,768]{1,0:T(8,128)(2,1)}, bf16[192,768]{1,0:T(8,128)(2,1)S(1)}, u32[]{:S(2)}, u32[]{:S(2)}) collective-permute-start(bf16[192,768]{1,0:T(8,128)(2,1)} %bitcast.37), channel_id=1, source_target_pairs={{0,1},{1,0},{2,3},{3,2},{4,5},{5,4},{6,7},{7,6},{8,9},{9,8},{10,11... | collective-permute-start | bytes 884744 | tf_op jit(solution)/shard_map/ppermute | solution.py:697
  3.9 6.4 %collective-permute-start.3 = (bf16[192,768]{1,0:T(8,128)(2,1)}, bf16[192,768]{1,0:T(8,128)(2,1)S(1)}, u32[]{:S(2)}, u32[]{:S(2)}) collective-permute-start(bf16[192,768]{1,0:T(8,128)(2,1)} %bitcast.41), channel_id=1, source_target_pairs={{0,1},{1,0},{2,3},{3,2},{4,5},{5,4},{6,7},{7,6},{8,9},{9,8},{10,11... | collective-permute-start | bytes 884744 | tf_op jit(solution)/shard_map/ppermute | solution.py:697
  4.9 5.5 %copy-start.9 = (bf16[1,128,768]{2,1,0:T(8,128)(2,1)S(1)}, bf16[1,128,768]{2,1,0:T(8,128)(2,1)}, u32[]{:S(2)}) copy-start(bf16[1,128,768]{2,1,0:T(8,128)(2,1)} %param.24) | copy-start | bytes 589828
  4.9 5.5 %copy-start.14 = (bf16[768,192]{0,1:T(8,128)(2,1)S(1)}, bf16[768,192]{0,1:T(8,128)(2,1)}, u32[]{:S(2)}) copy-start(bf16[768,192]{0,1:T(8,128)(2,1)} %param.40) | copy-start | bytes 884740
  4.9 5.5 %copy-start.15 = (bf16[768,192]{0,1:T(8,128)(2,1)S(1)}, bf16[768,192]{0,1:T(8,128)(2,1)}, u32[]{:S(2)}) copy-start(bf16[768,192]{0,1:T(8,128)(2,1)} %param.41) | copy-start | bytes 884740
  9.1 2.3 %collective-permute-start = (bf16[128,768]{1,0:T(8,128)(2,1)S(1)}, bf16[128,768]{1,0:T(8,128)(2,1)S(1)}, u32[]{:S(2)}, u32[]{:S(2)}) collective-permute-start(bf16[128,768]{1,0:T(8,128)(2,1)S(1)} %get-tuple-element.135), channel_id=1, source_target_pairs={{0,1},{1,0},{2,3},{3,2},{4,5},{5,4},{6,7},{7,6},{8,9},{9,8},{10,11... | collective-permute-start | bytes 589832 | tf_op jit(solution)/shard_map/ppermute | solution.py:697
  10.0 2.9 %collective-permute-start.8 = (bf16[128,768]{1,0:T(8,128)(2,1)S(1)}, bf16[128,768]{1,0:T(8,128)(2,1)S(1)}, u32[]{:S(2)}, u32[]{:S(2)}) collective-permute-start(bf16[128,768]{1,0:T(8,128)(2,1)S(1)} %collective-permute-done.1.refs_1_.refs_6_), channel_id=1, source_target_pairs={{0,1},{1,0},{2,3},{3,2},{4,5},{5,4},{6,7},{7,6},{8,9},{9,8},{10,11... | collective-permute-start | bytes 589832 | tf_op jit(solution)/shard_map/ppermute | solution.py:697
  10.4 1.9 %copy-start.3 = (bf16[768,192]{0,1:T(8,128)(2,1)S(1)}, bf16[768,192]{0,1:T(8,128)(2,1)}, u32[]{:S(2)}) copy-start(bf16[768,192]{0,1:T(8,128)(2,1)} %param.39) | copy-start | bytes 884740
  10.4 2.2 %copy-start.4 = (bf16[192,768]{1,0:T(8,128)(2,1)S(1)}, bf16[192,768]{1,0:T(8,128)(2,1)}, u32[]{:S(2)}) copy-start(bf16[192,768]{1,0:T(8,128)(2,1)} %refs_5_.3) | copy-start | bytes 884740
  11.4 7.1 %collective-permute-start.5 = (bf16[128,768]{1,0:T(8,128)(2,1)S(1)}, bf16[128,768]{1,0:T(8,128)(2,1)S(1)}, u32[]{:S(2)}, u32[]{:S(2)}) collective-permute-start(bf16[128,768]{1,0:T(8,128)(2,1)S(1)} %self_sum.1.refs_6_.chip_own), channel_id=1, source_target_pairs={{0,2},{1,3},{2,0},{3,1},{4,6},{5,7},{6,4},{7,5},{8,10},{9,11},{10,... | collective-permute-start | bytes 589832 | tf_op jit(solution)/shard_map/ppermute | solution.py:701
  12.4 6.1 %copy-start = (bf16[1,256,768]{2,1,0:T(8,128)(2,1)S(1)}, bf16[1,256,768]{2,1,0:T(8,128)(2,1)}, u32[]{:S(2)}) copy-start(bf16[1,256,768]{2,1,0:T(8,128)(2,1)} %param.23) | copy-start | bytes 1179652
  12.4 6.1 %copy-start.10 = (f32[768]{0:T(1024)S(1)}, f32[768]{0:T(1024)}, u32[]{:S(2)}) copy-start(f32[768]{0:T(1024)} %refs_3_.8) | copy-start | bytes 9220
  12.4 6.1 %collective-permute-start.6 = (bf16[192,768]{1,0:T(8,128)(2,1)S(1)}, bf16[192,768]{1,0:T(8,128)(2,1)S(1)}, u32[]{:S(2)}, u32[]{:S(2)}) collective-permute-start(bf16[192,768]{1,0:T(8,128)(2,1)S(1)} %bitcast.23), channel_id=1, source_target_pairs={{0,1},{1,0},{2,3},{3,2},{4,5},{5,4},{6,7},{7,6},{8,9},{9,8},{10,11... | collective-permute-start | bytes 884744 | tf_op jit(solution)/shard_map/ppermute | solution.py:697
  12.6 5.9 %collective-permute-start.7 = (bf16[192,768]{1,0:T(8,128)(2,1)S(1)}, bf16[192,768]{1,0:T(8,128)(2,1)S(1)}, u32[]{:S(2)}, u32[]{:S(2)}) collective-permute-start(bf16[192,768]{1,0:T(8,128)(2,1)S(1)} %copy-done.4), channel_id=1, source_target_pairs={{0,1},{1,0},{2,3},{3,2},{4,5},{5,4},{6,7},{7,6},{8,9},{9,8},{10,11... | collective-permute-start | bytes 884744 | tf_op jit(solution)/shard_map/ppermute | solution.py:697
  18.5 3.3 %copy-start.2 = (bf16[768,768]{1,0:T(8,128)(2,1)S(1)}, bf16[768,768]{1,0:T(8,128)(2,1)}, u32[]{:S(2)}) copy-start(bf16[768,768]{1,0:T(8,128)(2,1)} %refs_2_.4) | copy-start | bytes 3538948
  18.5 3.3 %copy-start.1 = (bf16[768,768]{1,0:T(8,128)(2,1)S(1)}, bf16[768,768]{1,0:T(8,128)(2,1)}, u32[]{:S(2)}) copy-start(bf16[768,768]{1,0:T(8,128)(2,1)} %refs_4_.1) | copy-start | bytes 3538948
  18.5 6.4 %copy-start.13 = (bf16[1,256,768]{2,1,0:T(8,128)(2,1)S(1)}, bf16[1,256,768]{2,1,0:T(8,128)(2,1)}, u32[]{:S(2)}) copy-start(bf16[1,256,768]{2,1,0:T(8,128)(2,1)} %param.31) | copy-start | bytes 1179652
  18.5 6.4 %copy-start.16 = (f32[16,256]{1,0:T(8,128)S(1)}, f32[16,256]{1,0:T(8,128)}, u32[]{:S(2)}) copy-start(f32[16,256]{1,0:T(8,128)} %refs_3_.5) | copy-start | bytes 49156
  21.8 3.1 %collective-permute-start.11 = (bf16[768,768]{1,0:T(8,128)(2,1)S(1)}, bf16[768,768]{1,0:T(8,128)(2,1)S(1)}, u32[]{:S(2)}, u32[]{:S(2)}) collective-permute-start(bf16[768,768]{1,0:T(8,128)(2,1)S(1)} %copy-done.2), channel_id=1, source_target_pairs={{0,1},{1,0},{2,3},{3,2},{4,5},{5,4},{6,7},{7,6},{8,9},{9,8},{10,11... | collective-permute-start | bytes 3538952 | tf_op jit(solution)/shard_map/ppermute | solution.py:697
  21.8 8.8 %collective-permute-start.10 = (bf16[768,768]{1,0:T(8,128)(2,1)S(1)}, bf16[768,768]{1,0:T(8,128)(2,1)S(1)}, u32[]{:S(2)}, u32[]{:S(2)}) collective-permute-start(bf16[768,768]{1,0:T(8,128)(2,1)S(1)} %copy-done.1), channel_id=1, source_target_pairs={{0,1},{1,0},{2,3},{3,2},{4,5},{5,4},{6,7},{7,6},{8,9},{9,8},{10,11... | collective-permute-start | bytes 3538952 | tf_op jit(solution)/shard_map/ppermute | solution.py:697
  23.6 7.0 %collective-permute-start.9 = (bf16[128,768]{1,0:T(8,128)(2,1)S(1)}, bf16[128,768]{1,0:T(8,128)(2,1)S(1)}, u32[]{:S(2)}, u32[]{:S(2)}) collective-permute-start(bf16[128,768]{1,0:T(8,128)(2,1)S(1)} %get-tuple-element.147.refs_0_), channel_id=1, source_target_pairs={{0,2},{1,3},{2,0},{3,1},{4,6},{5,7},{6,4},{7,5},{8,10},{9,11},{10,... | collective-permute-start | bytes 589832 | tf_op jit(solution)/shard_map/ppermute | solution.py:701
  24.9 5.7 %collective-permute-start.12 = (bf16[128,960]{1,0:T(8,128)(2,1)S(1)}, bf16[128,960]{1,0:T(8,128)(2,1)S(1)}, u32[]{:S(2)}, u32[]{:S(2)}) collective-permute-start(bf16[128,960]{1,0:T(8,128)(2,1)S(1)} %get-tuple-element.155), channel_id=1, source_target_pairs={{0,1},{1,0},{2,3},{3,2},{4,5},{5,4},{6,7},{7,6},{8,9},{9,8},{10,11... | collective-permute-start | bytes 737288 | tf_op jit(solution)/shard_map/ppermute | solution.py:697
  24.9 5.7 %copy-start.11 = (f32[768]{0:T(1024)S(1)}, f32[768]{0:T(1024)}, u32[]{:S(2)}) copy-start(f32[768]{0:T(1024)} %refs_3_.7) | copy-start | bytes 9220
  32.2 2.1 %collective-permute-start.14 = (bf16[128,2304]{1,0:T(8,128)(2,1)S(1)}, bf16[128,2304]{1,0:T(8,128)(2,1)S(1)}, u32[]{:S(2)}, u32[]{:S(2)}) collective-permute-start(bf16[128,2304]{1,0:T(8,128)(2,1)S(1)} %get-tuple-element.166.refs_1_), channel_id=1, source_target_pairs={{0,1},{1,0},{2,3},{3,2},{4,5},{5,4},{6,7},{7,6},{8,9},{9,8},{10,11... | collective-permute-start | bytes 1769480 | tf_op jit(solution)/shard_map/ppermute | solution.py:697
  32.3 7.3 %collective-permute-start.13 = (bf16[128,768]{1,0:T(8,128)(2,1)S(1)}, bf16[128,768]{1,0:T(8,128)(2,1)S(1)}, u32[]{:S(2)}, u32[]{:S(2)}) collective-permute-start(bf16[128,768]{1,0:T(8,128)(2,1)S(1)} %get-tuple-element.156.refs_6_.refs_0_), channel_id=1, source_target_pairs={{0,2},{1,3},{2,0},{3,1},{4,6},{5,7},{6,4},{7,5},{8,10},{9,11},{10,... | collective-permute-start | bytes 589832 | tf_op jit(solution)/shard_map/ppermute | solution.py:701
  35.3 15.4 %collective-permute-start.16 = (bf16[4,96,768]{2,1,0:T(8,128)(2,1)S(1)}, bf16[4,96,768]{2,1,0:T(8,128)(2,1)S(1)}, u32[]{:S(2)}, u32[]{:S(2)}) collective-permute-start(bf16[4,96,768]{2,1,0:T(8,128)(2,1)S(1)} %get-tuple-element.174), channel_id=1, source_target_pairs={{0,4},{4,0},{8,12},{12,8},{16,20},{20,16},{24,28},{28,24},{1,5},{5... | collective-permute-start | bytes 1769480 | tf_op jit(solution)/shard_map/ppermute | solution.py:705
  36.9 15.1 %collective-permute-start.17 = (bf16[4,96,768]{2,1,0:T(8,128)(2,1)S(1)}, bf16[4,96,768]{2,1,0:T(8,128)(2,1)S(1)}, u32[]{:S(2)}, u32[]{:S(2)}) collective-permute-start(bf16[4,96,768]{2,1,0:T(8,128)(2,1)S(1)} %get-tuple-element.176), channel_id=1, source_target_pairs={{0,8},{4,12},{8,0},{12,4},{16,24},{20,28},{24,16},{28,20},{1,9},{5... | collective-permute-start | bytes 1769480 | tf_op jit(solution)/shard_map/ppermute | solution.py:705
  42.8 2.4 %collective-permute-start.18 = (bf16[1024,192]{1,0:T(8,128)(2,1)S(1)}, bf16[1024,192]{1,0:T(8,128)(2,1)S(1)}, u32[]{:S(2)}, u32[]{:S(2)}) collective-permute-start(bf16[1024,192]{1,0:T(8,128)(2,1)S(1)} %source_grad.1.refs_15_), channel_id=1, source_target_pairs={{0,1},{1,0},{2,3},{3,2},{4,5},{5,4},{6,7},{7,6},{8,9},{9,8},{10,11... | collective-permute-start | bytes 1179656 | tf_op jit(solution)/shard_map/ppermute | solution.py:697
  42.8 2.3 %collective-permute-start.19 = (bf16[128,960]{1,0:T(8,128)(2,1)S(1)}, bf16[128,960]{1,0:T(8,128)(2,1)S(1)}, u32[]{:S(2)}, u32[]{:S(2)}) collective-permute-start(bf16[128,960]{1,0:T(8,128)(2,1)S(1)} %get-tuple-element.184), channel_id=1, source_target_pairs={{0,1},{1,0},{2,3},{3,2},{4,5},{5,4},{6,7},{7,6},{8,9},{9,8},{10,11... | collective-permute-start | bytes 737288 | tf_op jit(solution)/shard_map/ppermute | solution.py:697
  43.3 9.1 %collective-permute-start.15 = (bf16[128,768]{1,0:T(8,128)(2,1)S(1)}, bf16[128,768]{1,0:T(8,128)(2,1)S(1)}, u32[]{:S(2)}, u32[]{:S(2)}) collective-permute-start(bf16[128,768]{1,0:T(8,128)(2,1)S(1)} %get-tuple-element.171.refs_0_), channel_id=1, source_target_pairs={{0,2},{1,3},{2,0},{3,1},{4,6},{5,7},{6,4},{7,5},{8,10},{9,11},{10,... | collective-permute-start | bytes 589832 | tf_op jit(solution)/shard_map/ppermute | solution.py:701
  52.7 3.4 %collective-permute-start.20 = (bf16[144,768]{1,0:T(8,128)(2,1)S(1)}, bf16[144,768]{1,0:T(8,128)(2,1)S(1)}, u32[]{:S(2)}, u32[]{:S(2)}) collective-permute-start(bf16[144,768]{1,0:T(8,128)(2,1)S(1)} %get-tuple-element.191.refs_3_.refs_0_.refs_6_), channel_id=1, source_target_pairs={{0,1},{1,0},{2,3},{3,2},{4,5},{5,4},{6,7},{7,6},{8,9},{9,8},{10,11... | collective-permute-start | bytes 663560 | tf_op jit(solution)/shard_map/ppermute | solution.py:697
  52.7 3.3 %copy-start.5 = (bf16[768,192]{0,1:T(8,128)(2,1)S(1)}, bf16[768,192]{0,1:T(8,128)(2,1)}, u32[]{:S(2)}) copy-start(bf16[768,192]{0,1:T(8,128)(2,1)} %param.33) | copy-start | bytes 884740
  52.8 3.3 %copy-start.6 = (bf16[768,192]{0,1:T(8,128)(2,1)S(1)}, bf16[768,192]{0,1:T(8,128)(2,1)}, u32[]{:S(2)}) copy-start(bf16[768,192]{0,1:T(8,128)(2,1)} %param.34) | copy-start | bytes 884740
  52.8 3.3 %copy-start.7 = (bf16[768,192]{0,1:T(8,128)(2,1)S(1)}, bf16[768,192]{0,1:T(8,128)(2,1)}, u32[]{:S(2)}) copy-start(bf16[768,192]{0,1:T(8,128)(2,1)} %param.35) | copy-start | bytes 884740
  52.8 3.3 %copy-start.8 = (bf16[192,768]{1,0:T(8,128)(2,1)S(1)}, bf16[192,768]{1,0:T(8,128)(2,1)}, u32[]{:S(2)}) copy-start(bf16[192,768]{1,0:T(8,128)(2,1)} %refs_2_.3) | copy-start | bytes 884740
  53.4 18.5 %collective-permute-start.23 = (bf16[256,768]{1,0:T(8,128)(2,1)S(1)}, bf16[256,768]{1,0:T(8,128)(2,1)S(1)}, u32[]{:S(2)}, u32[]{:S(2)}) collective-permute-start(bf16[256,768]{1,0:T(8,128)(2,1)S(1)} %get-tuple-element.207), channel_id=1, source_target_pairs={{0,1},{1,0},{2,3},{3,2},{4,5},{5,4},{6,7},{7,6},{8,9},{9,8},{10,11... | collective-permute-start | bytes 1179656 | tf_op jit(solution)/shard_map/ppermute | solution.py:697
  53.9 15.3 %collective-permute-start.24 = (bf16[4,96,768]{2,1,0:T(8,128)(2,1)S(1)}, bf16[4,96,768]{2,1,0:T(8,128)(2,1)S(1)}, u32[]{:S(2)}, u32[]{:S(2)}) collective-permute-start(bf16[4,96,768]{2,1,0:T(8,128)(2,1)S(1)} %get-tuple-element.209), channel_id=1, source_target_pairs={{0,8},{4,12},{8,0},{12,4},{16,24},{20,28},{24,16},{28,20},{1,9},{5... | collective-permute-start | bytes 1769480 | tf_op jit(solution)/shard_map/ppermute | solution.py:705
  55.5 15.0 %collective-permute-start.25 = (bf16[4,96,768]{2,1,0:T(8,128)(2,1)S(1)}, bf16[4,96,768]{2,1,0:T(8,128)(2,1)S(1)}, u32[]{:S(2)}, u32[]{:S(2)}) collective-permute-start(bf16[4,96,768]{2,1,0:T(8,128)(2,1)S(1)} %get-tuple-element.210), channel_id=1, source_target_pairs={{0,4},{4,0},{8,12},{12,8},{16,20},{20,16},{24,28},{28,24},{1,5},{5... | collective-permute-start | bytes 1769480 | tf_op jit(solution)/shard_map/ppermute | solution.py:705
  56.1 1.8 %copy-start.17 = (s32[256]{0:T(256)S(1)}, s32[256]{0:T(256)}, u32[]{:S(2)}) copy-start(s32[256]{0:T(256)} %param.29) | copy-start | bytes 3076
  57.8 1.5 %collective-permute-start.21 = (bf16[144,768]{1,0:T(8,128)(2,1)S(1)}, bf16[144,768]{1,0:T(8,128)(2,1)S(1)}, u32[]{:S(2)}, u32[]{:S(2)}) collective-permute-start(bf16[144,768]{1,0:T(8,128)(2,1)S(1)} %get-tuple-element.198), channel_id=1, source_target_pairs={{0,1},{1,0},{2,3},{3,2},{4,5},{5,4},{6,7},{7,6},{8,9},{9,8},{10,11... | collective-permute-start | bytes 663560 | tf_op jit(solution)/shard_map/ppermute | solution.py:697
  59.4 11.1 %collective-permute-start.22 = (bf16[144,768]{1,0:T(8,128)(2,1)S(1)}, bf16[144,768]{1,0:T(8,128)(2,1)S(1)}, u32[]{:S(2)}, u32[]{:S(2)}) collective-permute-start(bf16[144,768]{1,0:T(8,128)(2,1)S(1)} %input_sum.1.refs_3_.refs_8_.refs_0_), channel_id=1, source_target_pairs={{0,2},{1,3},{2,0},{3,1},{4,6},{5,7},{6,4},{7,5},{8,10},{9,11},{10,... | collective-permute-start | bytes 663560 | tf_op jit(solution)/shard_map/ppermute | solution.py:701
  70.9 18.4 %collective-permute-start.28 = (bf16[640,384]{1,0:T(8,128)(2,1)S(1)}, bf16[640,384]{1,0:T(8,128)(2,1)S(1)}, u32[]{:S(2)}, u32[]{:S(2)}) collective-permute-start(bf16[640,384]{1,0:T(8,128)(2,1)S(1)} %get-tuple-element.220), channel_id=1, source_target_pairs={{0,8},{4,12},{8,0},{12,4},{16,24},{20,28},{24,16},{28,20},{1,9},{5... | collective-permute-start | bytes 1474568 | tf_op jit(solution)/shard_map/ppermute | solution.py:705
  71.4 10.9 %collective-permute-start.27 = (bf16[6,96,384]{2,1,0:T(8,128)(2,1)S(1)}, bf16[6,96,384]{2,1,0:T(8,128)(2,1)S(1)}, u32[]{:S(2)}, u32[]{:S(2)}) collective-permute-start(bf16[6,96,384]{2,1,0:T(8,128)(2,1)S(1)} %get-tuple-element.219), channel_id=1, source_target_pairs={{0,4},{4,0},{8,12},{12,8},{16,20},{20,16},{24,28},{28,24},{1,5},{5... | collective-permute-start | bytes 1327112 | tf_op jit(solution)/shard_map/ppermute | solution.py:705
  72.5 20.3 %copy-start.12 = (f32[768]{0:T(1024)S(1)}, f32[768]{0:T(1024)}, u32[]{:S(2)}) copy-start(f32[768]{0:T(1024)} %refs_3_.9) | copy-start | bytes 9220
  72.5 20.3 %collective-permute-start.26 = (bf16[256,768]{1,0:T(8,128)(2,1)S(1)}, bf16[256,768]{1,0:T(8,128)(2,1)S(1)}, u32[]{:S(2)}, u32[]{:S(2)}) collective-permute-start(bf16[256,768]{1,0:T(8,128)(2,1)S(1)} %get-tuple-element.218), channel_id=1, source_target_pairs={{0,2},{1,3},{2,0},{3,1},{4,6},{5,7},{6,4},{7,5},{8,10},{9,11},{10,... | collective-permute-start | bytes 1179656 | tf_op jit(solution)/shard_map/ppermute | solution.py:701
  73.8 19.5 %collective-permute-start.34 = (bf16[192,768]{1,0:T(8,128)(2,1)S(1)}, bf16[192,768]{1,0:T(8,128)(2,1)S(1)}, u32[]{:S(2)}, u32[]{:S(2)}) collective-permute-start(bf16[192,768]{1,0:T(8,128)(2,1)S(1)} %get-tuple-element.248), channel_id=1, source_target_pairs={{0,16},{4,20},{8,24},{12,28},{16,0},{20,4},{24,8},{28,12},{1,17},{... | collective-permute-start | bytes 884744 | tf_op jit(solution)/shard_map/ppermute | solution.py:705
  89.6 6.8 %collective-permute-start.30 = (bf16[2,96,384]{2,1,0:T(8,128)(2,1)S(1)}, bf16[2,96,384]{2,1,0:T(8,128)(2,1)S(1)}, u32[]{:S(2)}, u32[]{:S(2)}) collective-permute-start(bf16[2,96,384]{2,1,0:T(8,128)(2,1)S(1)} %get-tuple-element.226), channel_id=1, source_target_pairs={{0,8},{4,12},{8,0},{12,4},{16,24},{20,28},{24,16},{28,20},{1,9},{5... | collective-permute-start | bytes 442376 | tf_op jit(solution)/shard_map/ppermute | solution.py:705
  89.7 8.8 %collective-permute-start.33 = (bf16[192,384]{1,0:T(8,128)(2,1)S(1)}, bf16[192,384]{1,0:T(8,128)(2,1)S(1)}, u32[]{:S(2)}, u32[]{:S(2)}) collective-permute-start(bf16[192,384]{1,0:T(8,128)(2,1)S(1)} %get-tuple-element.223.refs_8_.refs_2_), channel_id=1, source_target_pairs={{0,16},{4,20},{8,24},{12,28},{16,0},{20,4},{24,8},{28,12},{1,17},{... | collective-permute-start | bytes 442376 | tf_op jit(solution)/shard_map/ppermute | solution.py:705
  92.8 5.4 %collective-permute-start.31 = (bf16[2,112,384]{2,1,0:T(8,128)(2,1)S(1)}, bf16[2,112,384]{2,1,0:T(8,128)(2,1)S(1)}, u32[]{:S(2)}, u32[]{:S(2)}) collective-permute-start(bf16[2,112,384]{2,1,0:T(8,128)(2,1)S(1)} %get-tuple-element.228), channel_id=1, source_target_pairs={{0,4},{4,0},{8,12},{12,8},{16,20},{20,16},{24,28},{28,24},{1,5},{5... | collective-permute-start | bytes 516104 | tf_op jit(solution)/shard_map/ppermute | solution.py:705
  93.2 13.5 %collective-permute-start.29 = (bf16[256,768]{1,0:T(8,128)(2,1)S(1)}, bf16[256,768]{1,0:T(8,128)(2,1)S(1)}, u32[]{:S(2)}, u32[]{:S(2)}) collective-permute-start(bf16[256,768]{1,0:T(8,128)(2,1)S(1)} %input_grad.1.refs_4_.refs_0_), channel_id=1, source_target_pairs={{0,1},{1,0},{2,3},{3,2},{4,5},{5,4},{6,7},{7,6},{8,9},{9,8},{10,11... | collective-permute-start | bytes 1179656 | tf_op jit(solution)/shard_map/ppermute | solution.py:697
  98.3 7.5 %collective-permute-start.32 = (bf16[208,384]{1,0:T(8,128)(2,1)S(1)}, bf16[208,384]{1,0:T(8,128)(2,1)S(1)}, u32[]{:S(2)}, u32[]{:S(2)}) collective-permute-start(bf16[208,384]{1,0:T(8,128)(2,1)S(1)} %get-tuple-element.229.refs_4_.refs_2_), channel_id=1, source_target_pairs={{0,16},{4,20},{8,24},{12,28},{16,0},{20,4},{24,8},{28,12},{1,17},{... | collective-permute-start | bytes 479240 | tf_op jit(solution)/shard_map/ppermute | solution.py:705

commit v3 on v2

v3 whole, which is shorter than its diff:
```python
import jax
import jax.numpy as jnp
from jax import lax
from jax.experimental import pallas as pl
from jax.experimental.pallas import tpu as pltpu
from jax.sharding import PartitionSpec as P

HEAD_DIM = 64
LANGS = 8
EPSILON = 1e-06
SCALE = 0.125
NEGATIVE = -1e30
F32 = jnp.float32
BF16 = jnp.bfloat16
VMEM_LIMIT = 20 * 1024 * 1024
EXTRA = 16
PIECE = 128
CROSS_X = 384
SELF_X = 512
FILL = 5.0
LONG = 20.0


def dot(left, right):
    return jnp.dot(left, right, preferred_element_type=F32)


def dot_nt(left, right):
    return lax.dot_general(left, right, (((1,), (1,)), ((), ())), preferred_element_type=F32)


def dot_tn(left, right):
    return lax.dot_general(left, right, (((0,), (0,)), ((), ())), preferred_element_type=F32)


def row_of(vector_ref):
    return vector_ref[...].reshape(1, vector_ref.shape[0])


def inverse_rms(resid):
    return lax.rsqrt(jnp.mean(resid * resid, -1, keepdims=True) + EPSILON)


def norm_back(resid, gain, incoming):
    scale = inverse_rms(resid)
    weighted = incoming * gain
    inner = jnp.mean(weighted * resid, -1, keepdims=True)
    grad = scale * weighted - resid * (scale * scale * scale * inner)
    gain_grad = jnp.sum(incoming * resid * scale, 0, keepdims=True)
    return grad, gain_grad


def groups_of(width):
    return [(start, min(2 * HEAD_DIM, width - start)) for start in range(0, width, 2 * HEAD_DIM)]


def head_mask(count, which, value):
    lane = lax.broadcasted_iota(jnp.int32, (1, count), 1)
    return jnp.where(lane // HEAD_DIM == which, value, 0.0).astype(BF16)


def stacked_heads(rows, value):
    width = rows.shape[1]
    if width == HEAD_DIM:
        return rows * jnp.asarray(value, BF16)
    return jnp.concatenate([rows * head_mask(width, inside, value) for inside in range(width // HEAD_DIM)], 0)


def own_blocks(product, count):
    rows = product.shape[1] // count
    return [
        product[inside * HEAD_DIM : (inside + 1) * HEAD_DIM, inside * rows : (inside + 1) * rows]
        for inside in range(count)
    ]


def heads_forward(queries, keys, values_turned, finish, probs_ref):
    rows = queries.shape[0]
    parts = []
    for start, width in groups_of(queries.shape[1]):
        head, count = start // HEAD_DIM, width // HEAD_DIM
        stacked = stacked_heads(queries[:, start : start + width], SCALE)
        logits = finish(head, count, dot_nt(keys[:, start : start + width], stacked))
        expo = jnp.exp(logits - jnp.max(logits, 0, keepdims=True))
        probs = (expo * (1.0 / jnp.sum(expo, 0, keepdims=True))).astype(BF16)
        probs_ref[:, head * rows : (head + count) * rows] = probs
        parts += own_blocks(dot(values_turned[start : start + width], probs), count)
    return jnp.concatenate(parts, 0).astype(BF16)


def heads_backward(grad_context, keys_turned, values, probs_ref, grad_logits_ref):
    rows = grad_context.shape[0]
    parts = []
    for start, width in groups_of(grad_context.shape[1]):
        head, count = start // HEAD_DIM, width // HEAD_DIM
        place = slice(head * rows, (head + count) * rows)
        stacked = stacked_heads(grad_context[:, start : start + width], 1.0)
        grad_probs = dot_nt(values[:, start : start + width], stacked)
        probs = probs_ref[:, place].astype(F32)
        weighted = jnp.sum(grad_probs * probs, 0, keepdims=True)
        grad_logits = (probs * (grad_probs - weighted)).astype(BF16)
        grad_logits_ref[:, place] = grad_logits
        parts += own_blocks(SCALE * dot(keys_turned[start : start + width], grad_logits), count)
    return jnp.concatenate(parts, 0).astype(BF16)


def heads_spread(matrix_ref, rows, factor):
    length = rows.shape[0]
    parts = []
    for start, width in groups_of(rows.shape[1]):
        head, count = start // HEAD_DIM, width // HEAD_DIM
        stacked = stacked_heads(rows[:, start : start + width], 1.0)
        parts.append(factor * dot(matrix_ref[:, head * length : (head + count) * length], stacked))
    return jnp.concatenate(parts, 1).astype(BF16)


def own_rows(core, half):
    return pl.ds(pl.multiple_of(core * half, half), half)


def bucket_onehot(bucket_ref, buckets):
    wanted = lax.broadcasted_iota(jnp.int32, (buckets, bucket_ref.shape[1]), 0)
    return jnp.where(bucket_ref[...] == wanted, 1.0, 0.0)


def add_kernel(left_ref, right_ref, out_ref):
    out_ref[...] = (left_ref[...].astype(F32) + right_ref[...].astype(F32)).astype(out_ref.dtype)


def first_kernel(out):
    out[...] = jnp.zeros_like(out)


def step_kernel(enc_len, objective, language, info, mask):
    info[...] = jnp.full(info.shape, objective[0] * LANGS + language[0], jnp.int32)
    rows = mask.shape[0] // 4
    row = lax.broadcasted_iota(jnp.int32, mask.shape, 0)
    block = row // rows
    flip = jnp.where(block % 2 == 1, 1, 0) + jnp.where(block >= 2, 2, 0)
    position = (lax.axis_index("tensor") ^ flip) * rows + row % rows
    mask[...] = jnp.where(position < enc_len[0], 0.0, NEGATIVE)


def self_sum_kernel(own, first, second, out):
    rows = first.shape[0]
    out[:rows] = both(own[:rows], first[...]).astype(BF16)
    out[rows : 2 * rows] = both(own[rows:], second[...]).astype(BF16)
    out[2 * rows :] = jnp.zeros((out.shape[0] - 2 * rows, out.shape[1]), BF16)


def self_forward_kernel(
    dec_len, bucket, table, x, gain, w_query, w_key, w_value, w_output,
    keep, send, more, normed_out, query_out, context_out, probs_out, dec_out, whole,
):
    dec_out[...] = jnp.full(dec_out.shape, dec_len[0], jnp.int32)
    length = x.shape[0]
    resid = x[...].astype(F32)
    normed = (resid * inverse_rms(resid) * row_of(gain)).astype(BF16)
    normed_out[...] = normed
    queries = dot_nt(normed, w_query[...]).astype(BF16)
    keys = dot_nt(normed, w_key[...]).astype(BF16)
    values = dot_nt(w_value[...], normed).astype(BF16)
    query_out[...] = queries
    by_distance = lax.dot_general(
        table[...],
        bucket_onehot(bucket, table.shape[1]),
        (((1,), (0,)), ((), ())),
        precision=lax.Precision.HIGHEST,
        preferred_element_type=F32,
    )
    row = lax.broadcasted_iota(jnp.int32, (length, length), 0)
    column = lax.broadcasted_iota(jnp.int32, (length, length), 1)
    allowed = (row <= column) & (row < dec_len[0])

    def finish(head, count, scores):
        parts = []
        for inside in range(count):
            spread = jnp.broadcast_to(by_distance[head + inside : head + inside + 1], (length, length))
            bias = pltpu.roll(spread, 0, 1, stride=1, stride_axis=0)
            part = scores[:, inside * length : (inside + 1) * length]
            parts.append(jnp.where(allowed, part + bias, NEGATIVE))
        return jnp.concatenate(parts, 1) if count > 1 else parts[0]

    context = heads_forward(queries, keys, values, finish, probs_out)
    context_out[...] = context.T
    whole[...] = dot_tn(context, w_output[...]).astype(BF16)
    half = keep.shape[0]
    core = lax.axis_index("tensor") % 2
    keep[...] = whole[own_rows(core, half), :]
    rows = send.shape[0]
    send[...] = whole[own_rows(2 - 2 * core, rows), :]
    more[...] = whole[own_rows(3 - 2 * core, rows), :]


def source_first_kernel(first, second, wk_own, wv_own, wk_peer, wv_peer, k_own, v_own, k_peer, v_peer):
    rows = first.shape[0]
    for index, part in enumerate((first, second)):
        place = slice(index * rows, (index + 1) * rows)
        for weight, out in ((wk_own, k_own), (wk_peer, k_peer)):
            out[place, :] = dot_nt(part[...], weight[...]).astype(BF16)
        for weight, out in ((wv_own, v_own), (wv_peer, v_peer)):
            out[:, place] = dot_nt(weight[...], part[...]).astype(BF16)


def source_second_kernel(
    first, second, wk_own, wv_own, wk_peer, wv_peer, early_k_own, early_v_own, early_k_peer, early_v_peer,
    k_own, v_own, k_peer, v_peer,
):
    rows = first.shape[0]
    for early, out in ((early_k_own, k_own), (early_k_peer, k_peer)):
        out[: 2 * rows] = early[...]
    for early, out in ((early_v_own, v_own), (early_v_peer, v_peer)):
        out[:, : 2 * rows] = early[...]
    for index, part in enumerate((first, second)):
        place = slice((2 + index) * rows, (3 + index) * rows)
        for weight, out in ((wk_own, k_own), (wk_peer, k_peer)):
            out[place, :] = dot_nt(part[...], weight[...]).astype(BF16)
        for weight, out in ((wv_own, v_own), (wv_peer, v_peer)):
            out[:, place] = dot_nt(weight[...], part[...]).astype(BF16)


def source_back_kernel(
    normed, w_key, w_value, e0, e1, e2, e3, wk_own, wv_own, wk_peer, wv_peer,
    keys_turned, values, k_own, v_own, k_peer, v_peer,
):
    keys_turned[...] = dot_nt(w_key[...], normed[...]).astype(BF16)
    values[...] = dot_nt(normed[...], w_value[...]).astype(BF16)
    rows = e0.shape[0]
    for index, part in enumerate((e0, e2, e1, e3)):
        place = slice(index * rows, (index + 1) * rows)
        for weight, out in ((wk_own, k_own), (wk_peer, k_peer)):
            out[:, place] = dot_nt(weight[...], part[...]).astype(BF16)
        for weight, out in ((wv_own, v_own), (wv_peer, v_peer)):
            out[place, :] = dot_nt(part[...], weight[...]).astype(BF16)


def out_grad_kernel(info, dec_len, token_weights, cotangent, grad_own, branch_own, branch_peer):
    half = grad_own.shape[0]
    length = cotangent.shape[0]
    core = lax.axis_index("tensor") % 2
    row = lax.broadcasted_iota(jnp.int32, token_weights.shape, 0)
    weights = jnp.sum(jnp.where(row == info[:1, :1], token_weights[...], 0.0), 0, keepdims=True)
    position = lax.broadcasted_iota(jnp.int32, (1, length), 1)
    weights = jnp.where(position < dec_len[:1, :1], weights, 0.0)

    def rows_of(side):
        row = lax.broadcasted_iota(jnp.int32, (half, length), 0) + side * half
        column = lax.broadcasted_iota(jnp.int32, (half, length), 1)
        factor = jnp.sum(jnp.where(row == column, weights, 0.0), -1, keepdims=True)
        return cotangent[own_rows(side, half), :].astype(F32) * factor

    own = rows_of(core)
    grad_own[...] = own
    branch_own[...] = own.astype(BF16)
    branch_peer[...] = rows_of(1 - core).astype(BF16)


def act_grad_kernel(branch, down_own, down_peer, own, peer):
    own[...] = dot_nt(branch[...], down_own[...])
    peer[...] = dot_nt(branch[...], down_peer[...])


def cross_forward_kernel(
    mask, chip_own, chip_other, x, gain, wq_own, wq_peer, wo_own, wo_peer, k_own, v_own, k_peer, v_peer,
    partial_out, hidden_out, normed_out, q_own, q_peer, context_own, probs_own, probs_peer, pack,
):
    half, width = hidden_out.shape
    core = lax.axis_index("tensor") % 2
    resid = x[own_rows(core, half), :].astype(F32)
    resid = resid + both(chip_own[:half], chip_other[:half])
    hidden_out[...] = resid
    normed = (resid * inverse_rms(resid) * row_of(gain)).astype(BF16)
    normed_out[...] = normed
    pack[:, :width] = normed

    def finish(head, count, scores):
        return scores + jnp.concatenate([mask[...]] * count, 1)

    queries = dot_nt(normed, wq_own[...]).astype(BF16)
    q_own[...] = queries
    first = heads_forward(queries, k_own[...], v_own[...], finish, probs_own)
    context_own[...] = first.T
    queries = dot_nt(normed, wq_peer[...]).astype(BF16)
    q_peer[...] = queries
    second = heads_forward(queries, k_peer[...], v_peer[...], finish, probs_peer)
    pack[:, width:] = second.T
    partial_out[...] = (dot_tn(first, wo_own[...]) + dot_tn(second, wo_peer[...])).astype(BF16)


def ffn_kernel(
    chip_own, chip_other, hidden, gain, up_own, up_peer, act_grad_own, act_grad_peer,
    partial_out, hidden_out, normed_out, act_own, grad_pre_own, pack,
):
    width = hidden.shape[1]
    resid = hidden[...] + (chip_own[...].astype(F32) + chip_other[...].astype(F32))
    hidden_out[...] = resid
    normed = (resid * inverse_rms(resid) * row_of(gain)).astype(BF16)
    normed_out[...] = normed
    pack[:, :width] = normed

    def through(up, act_grad):
        pre = dot(normed, up[...])
        square = pre * pre
        tanh = jnp.tanh(0.7978845608028654 * (pre + 0.044715 * square * pre))
        half_sum = 0.5 * (1.0 + tanh)
        slope = half_sum + 0.5 * pre * (1.0 - tanh * tanh) * (
            0.7978845608028654 * (1.0 + 3.0 * 0.044715 * square)
        )
        return (pre * half_sum).astype(BF16), (act_grad[...] * slope).astype(BF16)

    act, grad_pre = through(up_own, act_grad_own)
    act_own[...] = act
    grad_pre_own[...] = grad_pre
    total = dot_nt(grad_pre, up_own[...])
    act, grad_pre = through(up_peer, act_grad_peer)
    units = act.shape[1]
    pack[:, width : width + units] = act
    pack[:, width + units :] = grad_pre
    total = total + dot_nt(grad_pre, up_peer[...])
    partial_out[...] = total.astype(BF16)


def ffn_out_kernel(act_own, pack, down_own, down_peer, out):
    units = act_own.shape[1]
    width = out.shape[1]
    total = dot(act_own[...], down_own[...]) + dot(pack[:, width : width + units], down_peer[...])
    out[...] = total.astype(BF16)


def write_blocks(whole, columns, first_bit, rest_bits, size, targets, extra=None):
    index = lax.axis_index("dp")
    count = 1 << len(rest_bits)
    for first, target in enumerate(targets):
        for entry in range(count):
            relative = first << first_bit
            for place, bit in enumerate(rest_bits):
                if entry >> (len(rest_bits) - 1 - place) & 1:
                    relative |= 1 << bit
            block = index ^ relative
            rows = whole[pl.ds(pl.multiple_of(block * size, size), size), columns]
            target[entry, :size, :] = rows
            if extra is not None:
                target[entry, size:, :] = extra


def emit(whole, outs, order, size, extra=None, columns=slice(None)):
    if order is None:
        outs[0][: whole.shape[0], :] = whole[:, columns]
        if extra is not None:
            outs[0][whole.shape[0] :, :] = extra
    else:
        write_blocks(whole, columns, order[0], order[1:], size, outs, extra)


def ffn_weights_kernel(orders, size, normed, pack, act_own, grad_pre_own, branch_own, branch_peer, *refs):
    *outs, whole, left, right = refs
    half, width = normed.shape
    units = act_own.shape[1]
    left[:half] = normed[...]
    left[half:] = pack[:, :width]
    right[:half] = grad_pre_own[...]
    right[half:] = pack[:, width + units :]
    whole[...] = dot_tn(left[...], right[...]).astype(BF16)
    count = 1 if orders[0] is None else 2
    emit(whole, outs[:count], orders[0], size)
    left[:half] = branch_own[...]
    left[half:] = branch_peer[...]
    right[:half] = act_own[...]
    right[half:] = pack[:, width : width + units]
    whole[...] = dot_tn(left[...], right[...]).astype(BF16)
    emit(whole, outs[count:], orders[1], size)


def cross_backward_kernel(
    chip_own, chip_other, hidden, gain, grad_out, wo_own, wo_peer, k_own, v_own, k_peer, v_peer,
    probs_own, probs_peer, wq_own, wq_peer,
    partial_out, grad_hidden, gain_grad, gl_own, gl_peer, gc_own, gc_peer, gq_own, branch, pack,
):
    incoming = chip_own[...].astype(F32) + chip_other[...].astype(F32)
    added, gain_terms = norm_back(hidden[...], row_of(gain), incoming)
    gain_grad[...] = jnp.broadcast_to(gain_terms, gain_grad.shape)
    grad = grad_out[...] + added
    grad_hidden[...] = grad
    rounded = grad.astype(BF16)
    branch[...] = rounded
    width = rounded.shape[1]
    pack[:, :width] = rounded
    context = dot_nt(rounded, wo_own[...]).astype(BF16)
    gc_own[...] = context
    queries = heads_backward(context, k_own[...], v_own[...], probs_own, gl_own)
    gq_own[...] = queries.T
    total = dot_tn(queries, wq_own[...])
    context = dot_nt(rounded, wo_peer[...]).astype(BF16)
    gc_peer[...] = context
    queries = heads_backward(context, k_peer[...], v_peer[...], probs_peer, gl_peer)
    pack[:, width:] = queries.T
    total = total + dot_tn(queries, wq_peer[...])
    partial_out[...] = total.astype(BF16)


def source_grad_kernel(gl_peer, probs_peer, gc_peer, q_peer, out):
    span = out.shape[0] // 2
    rows = span // 4
    for start, grads in (
        (0, heads_spread(gl_peer, q_peer[...], SCALE)),
        (span, heads_spread(probs_peer, gc_peer[...], 1.0)),
    ):
        for block in range(4):
            there = start + (block ^ 1) * rows
            out[there : there + rows] = grads[block * rows : (block + 1) * rows]


def cross_weights_kernel(
    orders, size, gl_own, probs_own, gc_own, q_own, other, e0, e1, e2, e3, normed, pack_forward,
    branch, pack_backward, context_own, gq_own, *refs,
):
    *outs, source, whole, left, right = refs
    count = len(outs) // 2
    span = other.shape[0] // 2
    half, width = normed.shape
    columns = q_own.shape[1]
    source[:, :columns] = low_sum(heads_spread(gl_own, q_own[...], SCALE), other[:span])
    source[:, columns:] = low_sum(heads_spread(probs_own, gc_own[...], 1.0), other[span:])
    for index, part in enumerate((e0, e2, e1, e3)):
        left[index * half : (index + 1) * half] = part[...]
    whole[:, : 2 * columns] = dot_tn(left[...], source[...]).astype(BF16)
    left[:half] = normed[...]
    left[half : 2 * half] = pack_forward[:, :width]
    left[2 * half : 3 * half] = branch[...]
    left[3 * half :] = pack_backward[:, :width]
    right[...] = jnp.zeros_like(right)
    right[:half, :columns] = gq_own[...]
    right[half : 2 * half, :columns] = pack_backward[:, width:]
    right[2 * half : 3 * half, columns:] = context_own[...]
    right[3 * half :, columns:] = pack_forward[:, width:]
    whole[:, 2 * columns :] = dot_tn(left[...], right[...]).astype(BF16)
    wide = outs[0].shape[-1]
    emit(whole, outs[:count], orders[0], size, columns=slice(0, wide))
    emit(whole, outs[count:], orders[1], size, columns=slice(wide, None))


def encoded_kernel(source, wk_own, wv_own, keep, send):
    columns = wk_own.shape[0]
    terms = dot(source[:, :columns], wk_own[...]) + dot(source[:, columns:], wv_own[...])
    terms = terms.astype(BF16)
    rows = keep.shape[0] // 2
    for block in range(4):
        target = send if block % 2 else keep
        target[block // 2 * rows : (block // 2 + 1) * rows] = terms[block * rows : (block + 1) * rows]


def self_norm_kernel(chip_own, chip_other, hidden, gain, grad_hidden, gain_ffn, grad_out, pack):
    half = hidden.shape[0]
    incoming = chip_own[...].astype(F32) + chip_other[...].astype(F32)
    added, gain_terms = norm_back(hidden[...], row_of(gain), incoming)
    grad = grad_hidden[...] + added
    grad_out[...] = grad
    pack[:half] = grad.astype(BF16)
    row = lax.broadcasted_iota(jnp.int32, (EXTRA, hidden.shape[1]), 0)
    extra = jnp.where(row == 0, gain_terms, 0.0) + jnp.where(row == 1, gain_ffn[:1], 0.0)
    pack[half:] = extra.astype(BF16)


def high_low(vector):
    high = vector.astype(BF16).astype(F32)
    row = lax.broadcasted_iota(jnp.int32, (EXTRA, vector.shape[1]), 0)
    return (jnp.where(row == 0, high, 0.0) + jnp.where(row == 1, vector - high, 0.0)).astype(BF16)


def of_high_low(rows):
    rows = rows.astype(F32)
    return rows[:1] + rows[1:2]


def self_backward_kernel(
    pack_own, pack_peer, w_output, w_query, w_key, w_value, queries, keys, values, probs, x,
    keep, send, branch_out, gq_out, gk_out, gv_out, gl_out, whole,
):
    half = keep.shape[0] - EXTRA
    core = lax.axis_index("tensor") % 2
    branch_out[own_rows(core, half), :] = pack_own[:half]
    branch_out[own_rows(1 - core, half), :] = pack_peer[:half]
    context = dot_nt(branch_out[...], w_output[...]).astype(BF16)
    grad_queries = heads_backward(context, keys[...], values[...], probs, gl_out)
    grad_keys = heads_spread(gl_out, queries[...], SCALE)
    grad_values = heads_spread(probs, context, 1.0)
    gq_out[...] = grad_queries.T
    gk_out[...] = grad_keys
    gv_out[...] = grad_values
    total = dot_tn(grad_queries, w_query[...]) + dot(grad_keys, w_key[...]) + dot(grad_values, w_value[...])
    whole[...] = total.astype(BF16)
    keep[:half] = whole[own_rows(core, half), :]
    send[:half] = whole[own_rows(1 - core, half), :]
    resid = x[...].astype(F32)
    gain_terms = high_low(jnp.sum(total * resid * inverse_rms(resid), 0, keepdims=True))
    keep[half:] = gain_terms
    send[half:] = gain_terms


def input_sum_kernel(own, peer, out):
    half = out.shape[0] - EXTRA
    out[:half] = both(own[:half], peer[:half]).astype(BF16)
    out[half:] = high_low(of_high_low(own[half:]) + of_high_low(peer[half:]))


def self_weights_kernel(
    orders, size, buckets, normed, branch, gq, gk, gv, context, gl, bucket, pack_own, pack_peer, *refs
):
    *outs, whole, right, left = refs
    count = len(outs) // 2
    length, columns = gq.shape
    half = pack_own.shape[0] - EXTRA
    right[:length, :columns] = gq[...]
    right[:length, columns:] = gk[...]
    whole[:, : 2 * columns] = dot_tn(normed[...], right[:length]).astype(BF16)
    left[:length] = normed[...]
    left[length:] = branch[...]
    right[...] = jnp.zeros_like(right)
    right[:length, :columns] = gv[...]
    right[length:, columns:] = context[...]
    whole[:, 2 * columns :] = dot_tn(left[...], right[...]).astype(BF16)
    wide = outs[0].shape[-1]
    emit(whole, outs[:count], orders[0], size, columns=slice(0, wide))
    onehot = bucket_onehot(bucket, buckets)
    row = lax.broadcasted_iota(jnp.int32, (length, length), 0)
    column = lax.broadcasted_iota(jnp.int32, (length, length), 1)
    turn = jnp.where(row + column == length - 1, 1.0, 0.0).astype(BF16)
    place = lax.broadcasted_iota(jnp.int32, (8, length), 0)
    sums = jnp.zeros((8, length), F32)
    heads = gl.shape[1] // length
    for head in range(heads):
        skewed = pltpu.roll(dot(turn, gl[:, head * length : (head + 1) * length]), 1, 1, stride=1, stride_axis=0)
        sums = sums + jnp.where(place == head, jnp.sum(skewed, 0, keepdims=True), 0.0)
    table = lax.dot_general(
        sums, onehot, (((1,), (1,)), ((), ())), precision=lax.Precision.HIGHEST, preferred_element_type=F32
    )
    gains = both(pack_own[half:], pack_peer[half:])
    narrow = outs[-1].shape[-1]
    first, count_rows = extra_rows(gains.shape[1], narrow, heads)
    extra = vector_rows(gains[:1], narrow, count_rows, 0) + vector_rows(gains[1:2], narrow, count_rows, 1)
    table = jnp.concatenate([table, jnp.zeros((8, narrow - buckets), F32)], 1)
    row = lax.broadcasted_iota(jnp.int32, (count_rows, narrow), 0)
    for head in range(heads):
        extra = extra + jnp.where(row == first + head, table[head : head + 1], 0.0)
    extra = extra.astype(BF16)
    emit(whole, outs[count:], orders[1], size, extra, columns=slice(wide, None))


def extra_rows(width, wide, heads):
    first = -(-3 * (width // wide) // 4) * 4
    return first, -(-(first + heads) // 16) * 16


def vector_rows(vector, wide, count, which):
    rows = vector.shape[1] // wide
    row = lax.broadcasted_iota(jnp.int32, (count, wide), 0)
    placed = jnp.zeros((count, wide), F32)
    for index in range(rows):
        piece = vector[:, index * wide : (index + 1) * wide]
        placed = placed + jnp.where(row == which * rows + index, piece, 0.0)
    return placed


def encoded_sum_kernel(own, other, keep, send):
    rows = keep.shape[0]
    keep[...] = low_sum(own[:rows], other[:rows])
    send[...] = low_sum(own[rows:], other[rows:])


def input_grad_kernel(chip_own, chip_other, x, gain, grad_hidden, hidden_two, out_own, out_other, pack):
    half = hidden_two.shape[0]
    resid = x[own_rows(lax.axis_index("tensor") % 2, half), :].astype(F32)
    added, _ = norm_back(resid, row_of(gain), both(chip_own[:half], chip_other[:half]))
    pack[:half] = (grad_hidden[...] + added).astype(BF16)
    pack[half:] = (hidden_two[...] + both(out_own[...], out_other[...])).astype(BF16)


def rows_kernel(own, peer, input_grad, layer_out, token):
    half = own.shape[0] // 2
    core = lax.axis_index("tensor") % 2
    for place, out in ((0, input_grad), (half, layer_out)):
        out[own_rows(core, half), :] = own[place : place + half]
        out[own_rows(1 - core, half), :] = peer[place : place + half]
    token[...] = own[: token.shape[0], : token.shape[1]]


def both(left, right):
    return left.astype(F32) + right.astype(F32)


def low_sum(left, right):
    return both(left, right).astype(BF16)


def ffn_second_kernel(up_keep, up_got, down_keep, down_got, up_send, up_next, down_send, down_next):
    for keep, got, send, new in (
        (up_keep, up_got, up_send, up_next),
        (down_keep, down_got, down_send, down_next),
    ):
        for entry in range(2):
            new[entry] = low_sum(keep[entry], got[entry])
            send[entry] = low_sum(keep[2 + entry], got[2 + entry])


def ffn_third_kernel(up_keep, up_got, down_keep, down_got, send, keep):
    size = up_keep.shape[1]
    for entry, target in enumerate((keep, send)):
        target[:size] = low_sum(up_keep[entry], up_got[entry])
        target[size:] = low_sum(down_keep[entry], down_got[entry])


def round_three_kernel(ca_keep, ca_got, cb_keep, cb_got, sa_send, sb_send, x_send, zo_send, ca_next, cb_next):
    for entry in range(2):
        ca_next[entry] = low_sum(ca_keep[entry], ca_got[entry])
        cb_next[entry] = low_sum(cb_keep[entry], cb_got[entry])
    base = spread_out(x_send, [low_sum(cb_keep[2 + entry], cb_got[2 + entry]) for entry in range(2)])
    spread_out(x_send, [sa_send[entry] for entry in range(4)], base)
    base = spread_out(zo_send, [low_sum(ca_keep[2 + entry], ca_got[2 + entry]) for entry in range(2)])
    spread_out(zo_send, [sb_send[entry] for entry in range(4)], base)


def gain_kernel(chip_own, chip_other, out):
    half = chip_own.shape[0] - EXTRA
    gain = of_high_low(chip_own[half:]) + of_high_low(chip_other[half:])
    out[...] = vector_rows(gain, out.shape[1], out.shape[0], 2).astype(BF16)


def spread_out(target, parts, start=0):
    for part in parts:
        rows = part.shape[0]
        for side in range(part.shape[1] // PIECE):
            target[start : start + rows] = part[:, side * PIECE : (side + 1) * PIECE]
            start += rows
    return start


def gathered(source, rows, wide, start):
    pieces = [source[start + side * rows : start + (side + 1) * rows] for side in range(wide // PIECE)]
    return jnp.concatenate(pieces, 1) if len(pieces) > 1 else pieces[0]


def round_four_kernel(
    x_got, zo_got, ca_keep, cb_keep, sa_keep, sb_keep, gains, gains_got,
    cross_send, cross_keep, sa_send, sa_next, sb_send, sb_next,
):
    size, ca_wide = ca_keep.shape[1:]
    cb_wide = cb_keep.shape[2]
    large, small = sa_keep.shape[2], sb_keep.shape[2]
    more = sb_keep.shape[1]
    zo_base = 2 * size * ca_wide // PIECE
    x_base = 2 * size * cb_wide // PIECE
    for entry, target in enumerate((cross_keep, cross_send)):
        part = low_sum(ca_keep[entry], gathered(zo_got, size, ca_wide, entry * (zo_base // 2)))
        base = spread_out(target, [part])
        part = low_sum(cb_keep[entry], gathered(x_got, size, cb_wide, entry * (x_base // 2)))
        spread_out(target, [part], base)
    gain = low_sum(gains[...], gains_got[...])
    for first, sa_out, sb_out in ((0, sa_next, sb_next), (2, sa_send, sb_send)):
        for entry in range(2):
            start = x_base + (first + entry) * size * (large // PIECE)
            part = slice(entry * size, (entry + 1) * size)
            sa_out[part] = low_sum(sa_keep[first + entry], gathered(x_got, size, large, start))
            start = zo_base + (first + entry) * more * (small // PIECE)
            other = gathered(zo_got, more, small, start)
            sb_out[entry] = low_sum(sb_keep[first + entry], other)
        sa_out[2 * size :, :small] = gain


def round_five_kernel(sa_keep, sa_got, sb_keep, sb_got, send, keep):
    large, small = sa_keep.shape[1], sb_keep.shape[2]
    size = sa_keep.shape[0] - sb_keep.shape[1]
    gain = low_sum(sa_keep[2 * size :, :small], sa_got[2 * size :, :small])
    for entry, target in enumerate((keep, send)):
        part = slice(entry * size, (entry + 1) * size)
        spread_out(target, [low_sum(sa_keep[part], sa_got[part])])
        part = low_sum(sb_keep[entry], sb_got[entry])
        part = jnp.concatenate([part[:size], low_sum(part[size:], gain)], 0)
        spread_out(target, [part], size * (large // PIECE))


def ffn_final_kernel(keep, got, up, down):
    size = up.shape[0]
    up[...] = both(keep[:size], got[:size])
    down[...] = both(keep[size:], got[size:])


def cross_final_kernel(keep, got, key, value, query, output):
    size, count = key.shape
    total = both(gathered(keep, size, 4 * count, 0), gathered(got, size, 4 * count, 0))
    for place, out in enumerate((key, value, query)):
        out[...] = total[:, place * count : (place + 1) * count]
    output[...] = total[:, 3 * count :].T


def self_final_kernel(
    large, keep, got, encoded_own, encoded_other,
    encoded_grad, query, key, value, output, table, gain_two, gain_three, gain_one,
):
    encoded_grad[...] = low_sum(encoded_own[...], encoded_other[...])
    size, count = key.shape
    small = 4 * count - large
    start = size * (large // PIECE)
    first = both(gathered(keep, size, large, 0), gathered(got, size, large, 0))
    table_row, more = extra_rows(4 * count, small, table.shape[0])
    more += size
    second = both(gathered(keep, more, small, start), gathered(got, more, small, start))
    total = jnp.concatenate([first, second[:size]], 1)
    for place, out in enumerate((query, key, value)):
        out[...] = total[:, place * count : (place + 1) * count]
    output[...] = total[:, 3 * count :].T
    extra = second[size:]
    table[...] = extra[table_row : table_row + table.shape[0], : table.shape[1]]
    wide = 4 * count
    back = wide - lax.axis_index("dp") * size
    rows = wide // small
    for which, out in enumerate((gain_two, gain_three, gain_one)):
        pieces = [extra[which * rows + index : which * rows + index + 1] for index in range(rows)]
        whole = jnp.concatenate(pieces, 1)
        out[...] = pltpu.roll(jnp.broadcast_to(whole, (8, wide)), back, 1)[:1, :size]


def run(kernel, name, outs, ins, us=0.0, scratch=(), scalars=0, far=0, sems=0, after=(), limit=VMEM_LIMIT):
    shapes = [jax.ShapeDtypeStruct(shape, dtype) for shape, dtype in outs]
    idle = len(after)
    body = kernel
    if idle:

        def body(*refs):
            kernel(*refs[: len(ins)], *refs[len(ins) + idle :])

    vmem = pl.BlockSpec(memory_space=pltpu.VMEM)
    hbm = pl.BlockSpec(memory_space=pltpu.HBM)
    free = pl.BlockSpec(memory_space=pl.ANY)
    smem = pl.BlockSpec(memory_space=pltpu.SMEM)
    place = [smem] * scalars + [hbm] * far + [vmem] * (len(ins) - scalars - far) + [free] * idle
    ins = [
        pltpu.with_memory_space_constraint(item, pltpu.HBM) if spec is hbm else item for item, spec in zip(ins, place)
    ]
    result = pl.pallas_call(
        body,
        out_shape=shapes,
        in_specs=place,
        out_specs=[vmem] * len(shapes),
        scratch_shapes=[pltpu.VMEM(shape, dtype) for shape, dtype in scratch]
        + ([pltpu.SemaphoreType.DMA((sems,))] if sems else []),
        compiler_params=pltpu.CompilerParams(vmem_limit_bytes=limit),
        cost_estimate=pl.CostEstimate(flops=int(us * 1.15e9), bytes_accessed=0, transcendentals=0),
        name=name,
    )(*ins, *after)
    return result[0] if len(shapes) == 1 else result


def listed(result):
    return list(result) if isinstance(result, (list, tuple)) else [result]


def to_core(value):
    return lax.ppermute(value, "tensor", [(i, i ^ 1) for i in range(lax.axis_size("tensor"))])


def to_chip(value):
    return lax.ppermute(value, "tensor", [(i, i ^ 2) for i in range(lax.axis_size("tensor"))])


def to_peer(value, bit):
    return lax.ppermute(value, "dp", [(i, i ^ (1 << bit)) for i in range(lax.axis_size("dp"))])


def on_device(
    inputs, encoded, dec_len, enc_len, language, objective, distance_bucket, token_weights, cotangent,
    gain_self, self_query, self_key, self_value, self_output, bias_table,
    gain_cross, cross_query, cross_key, cross_value, cross_output, gain_ffn, ffn_up, ffn_down,
):
    seqs, length, width = inputs.shape
    half = length // 2
    columns = self_query.shape[1]
    heads = columns // HEAD_DIM
    units = ffn_up.shape[1]
    span_part = encoded.shape[1]
    span = span_part * lax.axis_size("tensor")
    dp = lax.axis_size("dp")
    size = width // dp
    bits = dp.bit_length() - 1
    halving = bits == 3 and dp == 8 and size % 16 == 0
    along_x, along_z = ((0, 1, 2), (1, 0, 2)) if halving else (None, None)
    latest = []

    def go(kernel, name, outs, ins, last=False, **how):
        after = [item for item in latest if not any(item is one for one in ins)]
        result = run(kernel, name, outs, ins, after=after, **how)
        if not last:
            results = result if isinstance(result, (list, tuple)) else [result]
            latest[:] = [min(results, key=lambda item: item.size * item.dtype.itemsize)]
        return result

    def plus(left, right, name):
        return go(add_kernel, name, [(left.shape, left.dtype)], [left, right])

    def payload(order, wide, extra=0):
        if order is None:
            return [((width + extra, wide), BF16)]
        return [((dp // 2, size + extra, wide), BF16)] * 2

    x = inputs.reshape(length, width)
    cot = cotangent.reshape(length, width)
    gain_one, gain_two, gain_three = gain_self, gain_cross, gain_ffn
    self_query, self_key, self_value = self_query.T, self_key.T, self_value.T
    cross_query, cross_key, cross_value = cross_query.T, cross_key.T, cross_value.T
    table = bias_table.T
    bucket = distance_bucket.reshape(1, length)
    e0 = encoded.reshape(span_part, width)

    first = go(first_kernel, "first", [((8, 128), F32)], [], us=LONG)
    key_source, value_source, _ = lax.optimization_barrier((cross_key, cross_value, first))
    e1 = to_chip(e0)
    e2 = to_core(e0)
    wk_peer = to_core(key_source)
    wv_peer = to_core(value_source)
    keep, send, more, normed_one, query_one, context_one, probs_one, dec_rows = go(
        self_forward_kernel, "self_forward",
        [((half, width), BF16)] + [((half // 2, width), BF16)] * 2 + [((length, width), BF16)]
        + [((length, columns), BF16)] * 2 + [((length, heads * length), BF16), ((8, 128), jnp.int32)],
        [dec_len, bucket, table, x, gain_one, self_query, self_key, self_value, self_output],
        scratch=[((length, width), BF16)], scalars=1, us=3.5,
    )
    first_half, second_half = to_core(send), to_core(more)
    early = go(
        source_first_kernel, "source_first", [((span // 2, columns), BF16), ((columns, span // 2), BF16)] * 2,
        [e0, e2, cross_key, cross_value, wk_peer, wv_peer],
    )
    chip_one = go(self_sum_kernel, "self_sum", [((half + EXTRA, width), BF16)], [keep, first_half, second_half])
    other_one = to_chip(chip_one)
    wq_source, wo_source, _ = lax.optimization_barrier((cross_query, cross_output, chip_one))
    wq_peer = to_core(wq_source)
    wo_peer = to_core(wo_source)
    e3 = to_core(e1)
    late = go(
        source_second_kernel, "source_second", [((span, columns), BF16), ((columns, span), BF16)] * 2,
        [e1, e3, cross_key, cross_value, wk_peer, wv_peer, *early],
    )
    enc_len, objective, language, _ = lax.optimization_barrier((enc_len, objective, language, late[0]))
    info, mask = go(
        step_kernel, "step", [((8, 128), jnp.int32), ((span, half), F32)], [enc_len, objective, language], scalars=3
    )
    up_source, down_source, _ = lax.optimization_barrier((ffn_up, ffn_down, late[0]))
    down_peer = to_core(down_source)
    up_peer = to_core(up_source)

    partial_two, hidden_one, normed_two, q_own, q_peer, context_own, probs_own, probs_peer, pack_forward = go(
        cross_forward_kernel, "cross_forward",
        [((half, width), BF16), ((half, width), F32), ((half, width), BF16)] + [((half, columns), BF16)] * 3
        + [((span, heads * half), BF16)] * 2 + [((half, width + columns), BF16)],
        [mask, chip_one, other_one, x, gain_two, cross_query, wq_peer, cross_output, wo_peer, *late],
    )
    other_two = to_chip(partial_two)
    pack_forward_peer = to_core(pack_forward)
    grad_full, branch_three, branch_three_peer = go(
        out_grad_kernel, "out_grad", [((half, width), F32)] + [((half, width), BF16)] * 2,
        [info, dec_rows, token_weights, cot], us=LONG,
    )
    act_grad, act_grad_peer = go(
        act_grad_kernel, "act_grad", [((half, units), F32)] * 2, [branch_three, ffn_down, down_peer]
    )
    key_one, value_one, k_own, v_own, k_peer, v_peer = go(
        source_back_kernel, "source_back",
        [((columns, length), BF16), ((length, columns), BF16)] + [((columns, span), BF16), ((span, columns), BF16)] * 2,
        [normed_one, self_key, self_value, e0, e1, e2, e3, cross_key, cross_value, wk_peer, wv_peer],
    )

    latest.append(pack_forward_peer)
    partial_three, hidden_two, normed_three, act_own, grad_pre_own, pack_ffn = go(
        ffn_kernel, "ffn",
        [((half, width), BF16), ((half, width), F32), ((half, width), BF16)] + [((half, units), BF16)] * 2
        + [((half, width + 2 * units), BF16)],
        [partial_two, other_two, hidden_one, gain_three, ffn_up, up_peer, act_grad, act_grad_peer],
    )
    other_three = to_chip(partial_three)
    pack_ffn_peer = to_core(pack_ffn)

    def ffn_weights(*refs):
        ffn_weights_kernel((along_x, along_z), size, *refs)

    ffn_payloads = go(
        ffn_weights, "ffn_weights", payload(along_x, width) + payload(along_z, width),
        [normed_three, pack_ffn_peer, act_own, grad_pre_own, branch_three, branch_three_peer],
        scratch=[((width, units), BF16), ((length, width), BF16), ((length, units), BF16)], us=FILL,
    )

    (partial_four, grad_two, gain_grad_three, gl_own, gl_peer, gc_own, gc_peer, gq_own, branch_two,
     pack_backward) = go(
        cross_backward_kernel, "cross_backward",
        [((half, width), BF16), ((half, width), F32), ((8, width), F32)] + [((span, heads * half), BF16)] * 2
        + [((half, columns), BF16)] * 3 + [((half, width), BF16), ((half, width + columns), BF16)],
        [partial_three, other_three, hidden_two, gain_three, grad_full, cross_output, wo_peer,
         k_own, v_own, k_peer, v_peer, probs_own, probs_peer, cross_query, wq_peer],
    )
    other_four = to_chip(partial_four)
    pack_backward_peer = to_core(pack_backward)
    source_grad = go(
        source_grad_kernel, "source_grad", [((2 * span, columns), BF16)], [gl_peer, probs_peer, gc_peer, q_peer]
    )
    source_grad_peer = to_core(source_grad)
    wide = 2 * columns
    ca_wide, cb_wide = (CROSS_X, 2 * wide - CROSS_X) if halving else (wide, wide)

    def cross_weights(*refs):
        cross_weights_kernel((along_x, along_z), size, *refs)

    *cross_payload, source_total = go(
        cross_weights, "cross_weights",
        payload(along_x, ca_wide) + payload(along_z, cb_wide) + [((span, wide), BF16)],
        [gl_own, probs_own, gc_own, q_own, source_grad_peer, e0, e1, e2, e3, normed_two, pack_forward_peer,
         branch_two, pack_backward_peer, context_own, gq_own],
        scratch=[((width, 2 * wide), BF16), ((span, width), BF16), ((4 * half, wide), BF16)],
    )
    ca_payload, cb_payload = cross_payload[: len(cross_payload) // 2], cross_payload[len(cross_payload) // 2 :]
    branch_out = go(ffn_out_kernel, "ffn_out", [((half, width), BF16)], [act_own, pack_ffn, ffn_down, down_peer])

    grad_one, pack_self = go(
        self_norm_kernel, "self_norm", [((half, width), F32), ((half + EXTRA, width), BF16)],
        [partial_four, other_four, hidden_one, gain_two, grad_two, gain_grad_three],
    )
    pack_self_peer = to_core(pack_self)

    if halving:
        up_keep, up_send, down_keep, down_send = ffn_payloads
        half_sent = ((2, size, width), BF16)
        up_send, up_keep, down_send, down_keep = go(
            ffn_second_kernel, "ffn_second", [half_sent] * 4,
            [up_keep, to_peer(up_send, 0), down_keep, to_peer(down_send, 1)], us=1.0,
        )
        up_got = to_peer(up_send, 1)
        down_got = to_peer(down_send, 0)

    keep, send, branch_one, gq_one, gk_one, gv_one, gl_one = go(
        self_backward_kernel, "self_backward",
        [((half + EXTRA, width), BF16)] * 2 + [((length, width), BF16)] + [((length, columns), BF16)] * 3
        + [((length, heads * length), BF16)],
        [pack_self, pack_self_peer, self_output, self_query, self_key, self_value, query_one, key_one, value_one,
         probs_one, x],
        scratch=[((length, width), BF16)],
    )
    got = to_core(send)
    large, small = (SELF_X, 2 * wide - SELF_X) if halving else (wide, wide)
    table_row, extra_count = extra_rows(width, small, heads)

    def self_weights(*refs):
        self_weights_kernel((along_x, along_z), size, table.shape[1], *refs)

    self_payload = listed(go(
        self_weights, "self_weights", payload(along_x, large) + payload(along_z, small, extra_count),
        [normed_one, branch_one, gq_one, gk_one, gv_one, context_one, gl_one, bucket, pack_self, pack_self_peer],
        scratch=[((width, 2 * wide), BF16), ((2 * length, wide), BF16), ((2 * length, width), BF16)],
    ))
    sa_payload, sb_payload = self_payload[: len(self_payload) // 2], self_payload[len(self_payload) // 2 :]

    if halving:
        ca_keep, ca_send = ca_payload
        cb_keep, cb_send = cb_payload
        sa_keep, sa_send = sa_payload
        sb_keep, sb_send = sb_payload
        more = size + extra_count
        x_rows = (2 * size * cb_wide + 4 * size * large) // PIECE
        zo_rows = (2 * size * ca_wide + 4 * more * small) // PIECE
        x_send, zo_send, ca_keep, cb_keep = go(
            round_three_kernel, "round_three",
            [((x_rows, PIECE), BF16), ((zo_rows, PIECE), BF16), ((2, size, ca_wide), BF16), ((2, size, cb_wide), BF16)],
            [ca_keep, to_peer(ca_send, 0), cb_keep, to_peer(cb_send, 1), sa_send, sb_send], us=1.6,
        )
        x_got = to_peer(x_send, 0)
        zo_got = to_peer(zo_send, 1)

    chip_five = go(input_sum_kernel, "input_sum", [(keep.shape, BF16)], [keep, got])
    other_five = to_chip(chip_five)

    if halving:
        ffn_send, ffn_keep = go(
            ffn_third_kernel, "ffn_third", [((2 * size, width), BF16)] * 2, [up_keep, up_got, down_keep, down_got]
        )
        ffn_got = to_peer(ffn_send, 2)
        gains = go(gain_kernel, "gain", [((extra_count, small), BF16)], [chip_five, other_five], us=LONG)
        gains_got = to_peer(gains, 0)
        branch_source, _ = lax.optimization_barrier((branch_out, gains))
    else:
        branch_source = branch_out
    out_other = to_chip(branch_source)
    pack_rows = go(
        input_grad_kernel, "input_grad", [((2 * half, width), BF16)],
        [chip_five, other_five, x, gain_one, grad_one, hidden_two, branch_out, out_other],
    )
    pack_rows_peer = to_core(pack_rows)

    if halving:
        rows = 2 * size + extra_count
        cross_send, cross_keep, sa_send, sa_keep, sb_send, sb_keep = go(
            round_four_kernel, "round_four",
            [((size * 2 * wide // PIECE, PIECE), BF16)] * 2 + [((rows, large), BF16)] * 2 + [((2, more, small), BF16)] * 2,
            [x_got, zo_got, ca_keep, cb_keep, sa_keep, sb_keep, gains, gains_got],
        )
        sa_got = to_peer(sa_send, 1)
        sb_got = to_peer(sb_send, 0)
        up, down = go(ffn_final_kernel, "ffn_final", [((size, width), F32)] * 2, [ffn_keep, ffn_got], us=LONG, last=True)

    encoded_keep, encoded_send = go(
        encoded_kernel, "encoded", [((span // 2, width), BF16)] * 2, [source_total, cross_key, cross_value]
    )
    encoded_got = to_core(encoded_send)
    if halving:
        cross_send, _ = lax.optimization_barrier((cross_send, encoded_send))
        cross_got = to_peer(cross_send, 2)
    encoded_part, encoded_pass = go(
        encoded_sum_kernel, "encoded_sum", [((span_part, width), BF16)] * 2, [encoded_keep, encoded_got]
    )
    encoded_other = to_chip(encoded_pass)

    if halving:
        rows = (size * large + more * small) // PIECE
        self_send, self_keep = go(
            round_five_kernel, "round_five", [((rows, PIECE), BF16)] * 2, [sa_keep, sa_got, sb_keep, sb_got]
        )
        self_got = to_peer(self_send, 2)
        square = ((size, columns), F32)
        turned = ((columns, size), F32)
        grad_cross_key, grad_cross_value, grad_cross_query, grad_cross_output = go(
            cross_final_kernel, "cross_final", [square] * 3 + [turned], [cross_keep, cross_got], us=LONG, last=True
        )

    input_grad, layer_out, _ = go(
        rows_kernel, "rows", [((length, width), BF16)] * 2 + [((16, 128), BF16)], [pack_rows, pack_rows_peer]
    )

    if halving:

        def self_final(*refs):
            self_final_kernel(large, *refs)

        (encoded_grad, grad_self_query, grad_self_key, grad_self_value, grad_self_output, grad_table, grad_gain_two,
         grad_gain_three, grad_gain_one) = go(
            self_final, "self_final",
            [((span_part, width), BF16)] + [square] * 3 + [turned, (table.shape, F32)] + [((1, size), F32)] * 3,
            [self_keep, self_got, encoded_part, encoded_other], last=True,
        )
        grad_gain_one, grad_gain_two, grad_gain_three = (
            item.reshape(size) for item in (grad_gain_one, grad_gain_two, grad_gain_three)
        )
    else:
        index = lax.axis_index("dp")

        def gain_part(*rows):
            row = lax.psum(jnp.concatenate(rows, 0).astype(F32), "dp")
            return lax.dynamic_slice(row, (index * size,), (size,))

        def scattered(item):
            return lax.psum_scatter(item.astype(F32), "dp", scatter_dimension=0, tiled=True)

        def pair_of(item):
            item = scattered(item)
            return item[:, :columns], item[:, columns:]

        up, down = (scattered(item) for item in ffn_payloads)
        grad_cross_key, grad_cross_value = pair_of(ca_payload[0])
        grad_cross_query, grad_cross_output = pair_of(cb_payload[0])
        grad_self_query, grad_self_key = pair_of(sa_payload[0])
        grad_self_value, grad_self_output = pair_of(sb_payload[0][:width])
        grad_cross_output, grad_self_output = grad_cross_output.T, grad_self_output.T
        extra = sb_payload[0][width:]
        grad_table = lax.psum(extra[table_row : table_row + heads, : table.shape[1]].astype(F32), "dp")
        encoded_grad = plus(encoded_part, encoded_other, "encoded_grad")
        gain_rows = [item[half : half + 2] for item in (chip_five, other_five)]
        grad_gain_one = gain_part(jnp.sum(jnp.concatenate(gain_rows, 0).astype(F32), 0))
        grad_gain_two = gain_part(extra[0], extra[1])
        grad_gain_three = gain_part(extra[2], extra[3])

    return (
        layer_out.reshape(seqs, length, width),
        input_grad.reshape(seqs, length, width),
        encoded_grad.reshape(seqs, span_part, width),
        grad_gain_one,
        grad_self_query,
        grad_self_key,
        grad_self_value,
        grad_self_output,
        grad_table.T,
        grad_gain_two,
        grad_cross_query,
        grad_cross_key,
        grad_cross_value,
        grad_cross_output,
        grad_gain_three,
        up,
        down.T,
    )


def solution(mesh):
    return jax.shard_map(
        on_device,
        mesh=mesh,
        in_specs=(
            P("dp", None, None),
            P("dp", "tensor", None),
            P("dp"),
            P("dp"),
            P("dp"),
            P("dp"),
            P(),
            P(),
            P("dp", None, None),
            P(),
            P(None, "tensor"),
            P(None, "tensor"),
            P(None, "tensor"),
            P("tensor", None),
            P(None, "tensor"),
            P(),
            P(None, "tensor"),
            P(None, "tensor"),
            P(None, "tensor"),
            P("tensor", None),
            P(),
            P(None, "tensor"),
            P("tensor", None),
        ),
        out_specs=(
            P("dp", None, None),
            P("dp", None, None),
            P("dp", "tensor", None),
            P("dp"),
            P("dp", "tensor"),
            P("dp", "tensor"),
            P("dp", "tensor"),
            P("tensor", "dp"),
            P(None, "tensor"),
            P("dp"),
            P("dp", "tensor"),
            P("dp", "tensor"),
            P("dp", "tensor"),
            P("tensor", "dp"),
            P("dp"),
            P("dp", "tensor"),
            P("tensor", "dp"),
        ),
        check_vma=False,
    )
```

time: 108 us -> 93.5 us (0.87)
  waiting for transfers between devices: 50.6 us -> 37 us
  Pallas kernels: 27.1 us -> 25.2 us
  starting transfers between devices: 26.1 us -> 27.2 us
    ppermute x11 -> x14, waiting for transfers between devices: 38.2 us -> 22.7 us  [to_peer(): lax.ppermute(value, 'dp', [(i, i ^ 1 << bit) for i in range(lax.axis_size...]
    ppermute x11 -> x14, starting transfers between devices: 12.2 us -> 15.6 us  [to_peer(): lax.ppermute(value, 'dp', [(i, i ^ 1 << bit) for i in range(lax.axis_size...]
    pallas_call x27 -> x33, Pallas kernels: 27.1 us -> 25.2 us  [run(): pl.pallas_call(body, out_shape=shapes, in_specs=place, out_specs=[vmem] *...]
    ppermute x7 -> x8, starting transfers between devices: 9.81 us -> 7.89 us  [to_chip(): lax.ppermute(value, 'tensor', [(i, i ^ 2) for i in range(lax.axis_size('t...]
    ppermute x7 -> x8, waiting for transfers between devices: 10.6 us -> 11.9 us  [to_chip(): lax.ppermute(value, 'tensor', [(i, i ^ 2) for i in range(lax.axis_size('t...]
    ppermute x17 -> x18, waiting for transfers between devices: 1.75 us -> 2.42 us  [to_core(): lax.ppermute(value, 'tensor', [(i, i ^ 1) for i in range(lax.axis_size('t...]
    ppermute x17 -> x18, starting transfers between devices: 4.12 us -> 3.75 us  [to_core(): lax.ppermute(value, 'tensor', [(i, i ^ 1) for i in range(lax.axis_size('t...]
  transfers between devices with their start and end apart: 35 -> 40, of which waited for: 15 -> 16; matrix products, arithmetic and copies ran while one was open for 0% -> 0% of each run, Pallas kernels for 20% -> 24%
where the time goes in v3:
time: 93.5 us; the launch traced here: 93.3 us
  waiting for transfers between devices  37 us (40%)
  starting transfers between devices  27.2 us (29%)
  Pallas kernels  25.2 us (27%)
  between operations  3.8 us (4%)
    pallas_call x33, Pallas kernels, run(): pl.pallas_call(body, out_shape=shapes, in_specs=place, out_specs=[vmem] *...  25.2 us
    ppermute x14, waiting for transfers between devices, to_peer(): lax.ppermute(value, 'dp', [(i, i ^ 1 << bit) for i in range(lax.axis_size...  22.7 us
    ppermute x14, starting transfers between devices, to_peer(): lax.ppermute(value, 'dp', [(i, i ^ 1 << bit) for i in range(lax.axis_size...  15.6 us
    ppermute x8, waiting for transfers between devices, to_chip(): lax.ppermute(value, 'tensor', [(i, i ^ 2) for i in range(lax.axis_size('t...  11.9 us
    ppermute x8, starting transfers between devices, to_chip(): lax.ppermute(value, 'tensor', [(i, i ^ 2) for i in range(lax.axis_size('t...  7.89 us
    ppermute x18, starting transfers between devices, to_core(): lax.ppermute(value, 'tensor', [(i, i ^ 1) for i in range(lax.axis_size('t...  3.75 us
    ppermute x18, waiting for transfers between devices, to_core(): lax.ppermute(value, 'tensor', [(i, i ^ 1) for i in range(lax.axis_size('t...  2.42 us
  transfers between devices with their start and end apart: 40, of which 16 were waited for; matrix products, arithmetic and copies ran while one was open for 0% of the time, Pallas kernels for 24%

profile of v3, /device:TPU:0, one launch (start us, length us, event | category | flops | bytes accessed | tf_op | source)
XLA Modules:
  0.0 93.3 jit_solution(12785968145388186475)
XLA Ops:
  0.8 0.5 collective-permute-start.4
  1.3 2.6 %collective-permute-start = (bf16[128,768]{1,0:T(8,128)(2,1)}, bf16[128,768]{1,0:T(8,128)(2,1)S(1)}, u32[]{:S(2)}, u32[]{:S(2)}) collective-permute-start(bf16[128,768]{1,0:T(8,128)(2,1)} %bitcast.34), channel_id=1, source_target_pairs={{0,2},{1,3},{2,0},{3,1},{4,6},{5,7},{6,4},{7,5},{8,10},{9,11},{10,... | collective-permute-start | bytes 589832 | tf_op jit(solution)/shard_map/ppermute | solution.py:762
  4.0 0.3 collective-permute-start.3
  5.1 1.6 %self_forward.1 = (bf16[128,768]{1,0:T(8,128)(2,1)S(1)}, bf16[64,768]{1,0:T(8,128)(2,1)S(1)}, bf16[64,768]{1,0:T(8,128)(2,1)S(1)}, bf16[256,768]{1,0:T(8,128)(2,...) custom-call(s32[1]{0:T(128)S(6)} %copy.40.refs_0_, ...), custom_call_target="tpu_custom_call" | custom-call | flops 4024999936 | tf_op jit(solution)/shard_map/self_forward/pallas_call | solution.py:739
  7.0 0.3 collective-permute-start.6
  7.3 0.8 source_first.1
  8.3 0.4 collective-permute-start.8
  8.9 0.7 collective-permute-start.7
  11.7 0.9 source_second.1
  12.5 0.5 collective-permute-start.11
  13.2 3.4 %collective-permute-done.7.refs_2_ = bf16[144,768]{1,0:T(8,128)(2,1)S(1)} collective-permute-done((bf16[144,768]{1,0:T(8,128)(2,1)S(1)}, bf16[144,768]{1,0:T(8,128)(2,1)S(1)}, u32[]{:S(2)}, u32[]{:S(2)}) %collective-permute-start.7) | collective-permute-done | bytes 221216 | tf_op jit(solution)/shard_map/ppermute | solution.py:762
  16.6 2.5 %cross_forward.1 = (bf16[128,768]{1,0:T(8,128)(2,1)S(1)}, f32[128,768]{1,0:T(8,128)S(1)}, bf16[128,768]{1,0:T(8,128)(2,1)S(1)}, bf16[128,192]{1,0:T(8,128)(2,1)S...) custom-call(f32[512,128]{1,0:T(8,128)S(1)} %get-tuple-element.158.re, ...), custom_call_target="tpu_custom_call" | custom-call | tf_op jit(solution)/shard_map/cross_forward/pallas_call | solution.py:739
  19.1 0.8 collective-permute-start.10
  20.1 0.9 act_grad.1
  21.0 1.6 %source_back.1 = (bf16[192,256]{1,0:T(8,128)(2,1)S(1)}, bf16[256,192]{1,0:T(8,128)(2,1)S(1)}, bf16[192,512]{1,0:T(8,128)(2,1)S(1)}, bf16[512,192]{1,0:T(8,128)(2...) custom-call(bf16[256,768]{1,0:T(8,128)(2,1)S(1)} %get-tuple-element.173.refs_0_, ...), custom_call_target="tpu_custom_call" | custom-call | tf_op jit(solution)/shard_map/source_back/pallas_call | solution.py:739
  22.6 2.9 %collective-permute-done.10.refs_1_ = bf16[128,768]{1,0:T(8,128)(2,1)S(1)} collective-permute-done((bf16[128,768]{1,0:T(8,128)(2,1)S(1)}, bf16[128,768]{1,0:T(8,128)(2,1)S(1)}, u32[]{:S(2)}, u32[]{:S(2)}) %collective-permute-start.10) | collective-permute-done | bytes 196640 | tf_op jit(solution)/shard_map/ppermute | solution.py:762
  25.5 1.6 %ffn.1 = (bf16[128,768]{1,0:T(8,128)(2,1)S(1)}, f32[128,768]{1,0:T(8,128)S(1)}, bf16[128,768]{1,0:T(8,128)(2,1)S(1)}, bf16[128,768]{1,0:T(8,128)(2,1)S(1)}, bf16...) custom-call(bf16[128,768]{1,0:T(8,128)(2,1)S(1)} %get-tuple-element.165.refs_0_, ...), custom_call_target="tpu_custom_call" | custom-call | tf_op jit(solution)/shard_map/ffn/pallas_call | solution.py:739
  27.2 0.8 collective-permute-start.14
  28.0 1.2 %collective-permute-done.15.refs_1_ = bf16[128,2304]{1,0:T(8,128)(2,1)S(1)} collective-permute-done((bf16[128,2304]{1,0:T(8,128)(2,1)S(1)}, bf16[128,2304]{1,0:T(8,128)(2,1)S(1)}, u32[]{:S(2)}, u32[]{:S(2)}) %collective-permute-start.15) | collective-permute-done | bytes 589856 | tf_op jit(solution)/shard_map/ppermute | solution.py:758
  29.2 1.0 %ffn_weights.1 = (bf16[4,96,768]{2,1,0:T(8,128)(2,1)S(1)}, bf16[4,96,768]{2,1,0:T(8,128)(2,1)S(1)}, bf16[4,96,768]{2,1,0:T(8,128)(2,1)S(1)}, bf16[4,96,768]{2,1,0:T(8,128)(2,1)S(1)}) custom-call(bf16[128,768]{1,0:T(8,128)(2,1)S(1)} %get-tuple-element.185.refs_0_, bf16[128,2304]{1,0:T(8,128)(2,1)S(1)} %collective-permute-done.15.refs_1_, ...), custom_call_target="tpu_custom_call" | custom-call | flops 5750000128 | tf_op jit(solution)/shard_map/ffn_weights/pallas_call | solution.py:739
  30.3 1.6 %collective-permute-start.20 = (bf16[4,96,768]{2,1,0:T(8,128)(2,1)S(1)}, bf16[4,96,768]{2,1,0:T(8,128)(2,1)S(1)}, u32[]{:S(2)}, u32[]{:S(2)}) collective-permute-start(bf16[4,96,768]{2,1,0:T(8,128)(2,1)S(1)} %get-tuple-element.209), channel_id=1, source_target_pairs={{0,4},{4,0},{8,12},{12,8},{16,20},{20,16},{24,28},{28,24},{1,5},{5... | collective-permute-start | bytes 1769480 | tf_op jit(solution)/shard_map/ppermute | solution.py:766
  31.8 1.6 %collective-permute-start.21 = (bf16[4,96,768]{2,1,0:T(8,128)(2,1)S(1)}, bf16[4,96,768]{2,1,0:T(8,128)(2,1)S(1)}, u32[]{:S(2)}, u32[]{:S(2)}) collective-permute-start(bf16[4,96,768]{2,1,0:T(8,128)(2,1)S(1)} %get-tuple-element.211), channel_id=1, source_target_pairs={{0,8},{4,12},{8,0},{12,4},{16,24},{20,28},{24,16},{28,20},{1,9},{5... | collective-permute-start | bytes 1769480 | tf_op jit(solution)/shard_map/ppermute | solution.py:766
  33.4 1.2 %collective-permute-done.14.refs_1_ = bf16[128,768]{1,0:T(8,128)(2,1)S(1)} collective-permute-done((bf16[128,768]{1,0:T(8,128)(2,1)S(1)}, bf16[128,768]{1,0:T(8,128)(2,1)S(1)}, u32[]{:S(2)}, u32[]{:S(2)}) %collective-permute-start.14) | collective-permute-done | bytes 196640 | tf_op jit(solution)/shard_map/ppermute | solution.py:762
  34.6 2.3 %cross_backward.1 = (bf16[128,768]{1,0:T(8,128)(2,1)S(1)}, f32[128,768]{1,0:T(8,128)S(1)}, f32[8,768]{1,0:T(8,128)S(1)}, bf16[512,384]{1,0:T(8,128)(2,1)S(1)}, b...) custom-call(bf16[128,768]{1,0:T(8,128)(2,1)S(1)} %get-tuple-element., ...), custom_call_target="tpu_custom_call" | custom-call | tf_op jit(solution)/shard_map/cross_backward/pallas_call | solution.py:739
  36.9 0.4 source_grad.1.refs_15_
  37.4 0.5 collective-permute-start.18
  37.9 0.7 collective-permute-start.16
  38.6 1.1 %collective-permute-done.18.refs_12_ = bf16[128,960]{1,0:T(8,128)(2,1)S(1)} collective-permute-done((bf16[128,960]{1,0:T(8,128)(2,1)S(1)}, bf16[128,960]{1,0:T(8,128)(2,1)S(1)}, u32[]{:S(2)}, u32[]{:S(2)}) %collective-permute-start.18) | collective-permute-done | bytes 245792 | tf_op jit(solution)/shard_map/ppermute | solution.py:758
  39.6 1.7 %cross_weights.1 = (bf16[4,96,384]{2,1,0:T(8,128)(2,1)S(1)}, bf16[4,96,384]{2,1,0:T(8,128)(2,1)S(1)}, bf16[4,96,384]{2,1,0:T(8,128)(2,1)S(1)}, bf16[4,96,384]{2,1,0:T(8,128)(2,1)S(1)}, bf16[512,384]{1,0:T(8,128)(2,1)S(1)}) custom-call(bf16[512,384]{1,0:T(8,128)(2,1)S(1)} %get-tuple-element.194.refs_0_, ...), custom_call_target="tpu_custom_call" | custom-call | tf_op jit(solution)/shard_map/cross_weights/pallas_call | solution.py:739
  41.4 1.6 %collective-permute-start.23 = (bf16[4,96,384]{2,1,0:T(8,128)(2,1)S(1)}, bf16[4,96,384]{2,1,0:T(8,128)(2,1)S(1)}, u32[]{:S(2)}, u32[]{:S(2)}) collective-permute-start(bf16[4,96,384]{2,1,0:T(8,128)(2,1)S(1)} %get-tuple-element.215), channel_id=1, source_target_pairs={{0,4},{4,0},{8,12},{12,8},{16,20},{20,16},{24,28},{28,24},{1,5},{5... | collective-permute-start | bytes 884744 | tf_op jit(solution)/shard_map/ppermute | solution.py:766
  42.9 1.6 %collective-permute-start.24 = (bf16[4,96,384]{2,1,0:T(8,128)(2,1)S(1)}, bf16[4,96,384]{2,1,0:T(8,128)(2,1)S(1)}, u32[]{:S(2)}, u32[]{:S(2)}) collective-permute-start(bf16[4,96,384]{2,1,0:T(8,128)(2,1)S(1)} %get-tuple-element.217), channel_id=1, source_target_pairs={{0,8},{4,12},{8,0},{12,4},{16,24},{20,28},{24,16},{28,20},{1,9},{5... | collective-permute-start | bytes 884744 | tf_op jit(solution)/shard_map/ppermute | solution.py:766
  44.5 0.5 ffn_out.1.refs_6_
  45.0 0.2 self_norm.1
  45.3 1.2 %collective-permute-done.20.refs_1_ = bf16[4,96,768]{2,1,0:T(8,128)(2,1)S(1)} collective-permute-done((bf16[4,96,768]{2,1,0:T(8,128)(2,1)S(1)}, bf16[4,96,768]{2,1,0:T(8,128)(2,1)S(1)}, u32[]{:S(2)}, u32[]{:S(2)}) %collective-permute-start.20) | collective-permute-done | bytes 589856 | tf_op jit(solution)/shard_map/ppermute | solution.py:766
  46.5 1.5 %collective-permute-done.21.refs_3_ = bf16[4,96,768]{2,1,0:T(8,128)(2,1)S(1)} collective-permute-done((bf16[4,96,768]{2,1,0:T(8,128)(2,1)S(1)}, bf16[4,96,768]{2,1,0:T(8,128)(2,1)S(1)}, u32[]{:S(2)}, u32[]{:S(2)}) %collective-permute-start.21) | collective-permute-done | bytes 589856 | tf_op jit(solution)/shard_map/ppermute | solution.py:766
  48.0 0.3 ffn_second.1
  48.3 1.8 %self_backward.1 = (bf16[144,768]{1,0:T(8,128)(2,1)S(1)}, bf16[144,768]{1,0:T(8,128)(2,1)S(1)}, bf16[256,768]{1,0:T(8,128)(2,1)S(1)}, bf16[256,192]{1,0:T(8,128)...) custom-call(bf16[144,768]{1,0:T(8,128)(2,1)S(1)} %get-tuple-element.205.refs_4_., ...), custom_call_target="tpu_custom_call" | custom-call | tf_op jit(solution)/shard_map/self_backward/pallas_call | solution.py:739
  50.2 1.6 %collective-permute-start.26 = (bf16[2,96,768]{2,1,0:T(8,128)(2,1)S(1)}, bf16[2,96,768]{2,1,0:T(8,128)(2,1)S(1)}, u32[]{:S(2)}, u32[]{:S(2)}) collective-permute-start(bf16[2,96,768]{2,1,0:T(8,128)(2,1)S(1)} %get-tuple-element.212.refs_11_), channel_id=1, source_target_pairs={{0,8},{4,12},{8,0},{12,4},{16,24},{20,28},{24,16},{28,20},{1,9},{5... | collective-permute-start | bytes 884744 | tf_op jit(solution)/shard_map/ppermute | solution.py:766
  51.8 0.5 collective-permute-start.27
  52.4 1.4 %self_weights.1 = (bf16[4,96,512]{2,1,0:T(8,128)(2,1)S(1)}, bf16[4,96,512]{2,1,0:T(8,128)(2,1)S(1)}, bf16[4,112,256]{2,1,0:T(8,128)(2,1)S(1)}, bf16[4,112,256]{2,1,0:T(8,128)(2,1)S(1)}) custom-call(bf16[256,768]{1,0:T(8,128)(2,1)S(1)} %get-tuple-element.173.refs_0_, bf16[256,768]{1,0:T(8,128)(2,1)S(1)} %get-tuple-element.218.refs_1_, ...), custom_call_target="tpu_custom_call" | custom-call | tf_op jit(solution)/shard_map/self_weights/pallas_call | solution.py:739
  53.8 0.2 round_three.1
  54.1 0.8 collective-permute-start.25
  54.9 1.0 %collective-permute-start.31 = (bf16[1472,128]{1,0:T(8,128)(2,1)S(1)}, bf16[1472,128]{1,0:T(8,128)(2,1)S(1)}, u32[]{:S(2)}, u32[]{:S(2)}) collective-permute-start(bf16[1472,128]{1,0:T(8,128)(2,1)S(1)} %get-tuple-element.235), channel_id=1, source_target_pairs={{0,8},{4,12},{8,0},{12,4},{16,24},{20,28},{24,16},{28,20},{1,9},{5... | collective-permute-start | bytes 1130504 | tf_op jit(solution)/shard_map/ppermute | solution.py:766
  55.9 0.9 %collective-permute-start.30 = (bf16[2112,128]{1,0:T(8,128)(2,1)S(1)}, bf16[2112,128]{1,0:T(8,128)(2,1)S(1)}, u32[]{:S(2)}, u32[]{:S(2)}) collective-permute-start(bf16[2112,128]{1,0:T(8,128)(2,1)S(1)} %get-tuple-element.234), channel_id=1, source_target_pairs={{0,4},{4,0},{8,12},{12,8},{16,20},{20,16},{24,28},{28,24},{1,5},{5... | collective-permute-start | bytes 1622024 | tf_op jit(solution)/shard_map/ppermute | solution.py:766
  56.8 4.9 %collective-permute-done.27.refs_3_ = bf16[2,96,768]{2,1,0:T(8,128)(2,1)S(1)} collective-permute-done((bf16[2,96,768]{2,1,0:T(8,128)(2,1)S(1)}, bf16[2,96,768]{2,1,0:T(8,128)(2,1)S(1)}, u32[]{:S(2)}, u32[]{:S(2)}) %collective-permute-start.27) | collective-permute-done | bytes 294944 | tf_op jit(solution)/shard_map/ppermute | solution.py:766
  61.8 2.7 %collective-permute-start.39 = (bf16[192,768]{1,0:T(8,128)(2,1)S(1)}, bf16[192,768]{1,0:T(8,128)(2,1)S(1)}, u32[]{:S(2)}, u32[]{:S(2)}) collective-permute-start(bf16[192,768]{1,0:T(8,128)(2,1)S(1)} %get-tuple-element.232.refs_2_), channel_id=1, source_target_pairs={{0,16},{4,20},{8,24},{12,28},{16,0},{20,4},{24,8},{28,12},{1,17},{... | collective-permute-start | bytes 884744 | tf_op jit(solution)/shard_map/ppermute | solution.py:766
  64.5 0.8 collective-permute-start.28
  65.3 0.5 collective-permute-start.32
  65.8 4.4 %collective-permute-done.28.refs_7_ = bf16[128,768]{1,0:T(8,128)(2,1)S(1)} collective-permute-done((bf16[128,768]{1,0:T(8,128)(2,1)S(1)}, bf16[128,768]{1,0:T(8,128)(2,1)S(1)}, u32[]{:S(2)}, u32[]{:S(2)}) %collective-permute-start.28) | collective-permute-done | bytes 196640 | tf_op jit(solution)/shard_map/ppermute | solution.py:762
  70.3 0.3 input_grad.1.refs_8_.refs_0_
  70.7 2.0 %collective-permute-done.32.refs_7_ = bf16[16,256]{1,0:T(8,128)(2,1)S(1)} collective-permute-done((bf16[16,256]{1,0:T(8,128)(2,1)S(1)}, bf16[16,256]{1,0:T(8,128)(2,1)S(1)}, u32[]{:S(2)}, u32[]{:S(2)}) %collective-permute-start.32) | collective-permute-done | bytes 8224 | tf_op jit(solution)/shard_map/ppermute | solution.py:766
  72.7 0.8 collective-permute-done.31.refs_1_
  73.8 0.6 collective-permute-start.34
  74.4 0.6 encoded.1
  75.1 1.6 %collective-permute-done.39.refs_1_ = bf16[192,768]{1,0:T(8,128)(2,1)S(1)} collective-permute-done((bf16[192,768]{1,0:T(8,128)(2,1)S(1)}, bf16[192,768]{1,0:T(8,128)(2,1)S(1)}, u32[]{:S(2)}, u32[]{:S(2)}) %collective-permute-start.39) | collective-permute-done | bytes 294944 | tf_op jit(solution)/shard_map/ppermute | solution.py:766
  76.7 1.4 %collective-permute-start.38 = (bf16[576,128]{1,0:T(8,128)(2,1)S(1)}, bf16[576,128]{1,0:T(8,128)(2,1)S(1)}, u32[]{:S(2)}, u32[]{:S(2)}) collective-permute-start(bf16[576,128]{1,0:T(8,128)(2,1)S(1)} %get-tuple-element.262), channel_id=1, source_target_pairs={{0,16},{4,20},{8,24},{12,28},{16,0},{20,4},{24,8},{28,12},{1,17},{... | collective-permute-start | bytes 442376 | tf_op jit(solution)/shard_map/ppermute | solution.py:766
  78.0 0.8 ffn_final.1
  79.0 4.7 %collective-permute-done.33.refs_1_ = bf16[208,512]{1,0:T(8,128)(2,1)S(1)} collective-permute-done((bf16[208,512]{1,0:T(8,128)(2,1)S(1)}, bf16[208,512]{1,0:T(8,128)(2,1)S(1)}, u32[]{:S(2)}, u32[]{:S(2)}) %collective-permute-start.33) | collective-permute-done | bytes 213024 | tf_op jit(solution)/shard_map/ppermute | solution.py:766
  83.9 0.8 collective-permute-start.37
  84.7 4.9 %collective-permute-done.38.refs_1_ = bf16[576,128]{1,0:T(8,128)(2,1)S(1)} collective-permute-done((bf16[576,128]{1,0:T(8,128)(2,1)S(1)}, bf16[576,128]{1,0:T(8,128)(2,1)S(1)}, u32[]{:S(2)}, u32[]{:S(2)}) %collective-permute-start.38) | collective-permute-done | bytes 147488 | tf_op jit(solution)/shard_map/ppermute | solution.py:766
  89.6 0.8 cross_final.1
  90.4 0.9 %rows.1 = (bf16[256,768]{1,0:T(8,128)(2,1)}, bf16[256,768]{1,0:T(8,128)(2,1)}, bf16[16,128]{1,0:T(8,128)(2,1)S(1)}) custom-call(bf16[256,768]{1,0:T(8,128)(2,1)S(1)} %input_grad.1.refs_8_.refs_0_, bf16[256,768]{1,0:T(8,128)(2,1)S(1)} %collective-permute-done.29.refs_1_, bf16[608,128]{1,0:T(8,128)(2,1)S(1)} %get-tuple-element.246.refs_2_), custom_call_target="tpu_custom_call" | custom-call | tf_op jit(solution)/shard_map/rows/pallas_call | solution.py:739
  91.4 1.0 %collective-permute-done.36.refs_1_ = bf16[608,128]{1,0:T(8,128)(2,1)S(1)} collective-permute-done((bf16[608,128]{1,0:T(8,128)(2,1)S(1)}, bf16[608,128]{1,0:T(8,128)(2,1)S(1)}, u32[]{:S(2)}, u32[]{:S(2)}) %collective-permute-start.36) | collective-permute-done | bytes 155680 | tf_op jit(solution)/shard_map/ppermute | solution.py:766
  92.4 1.0 %self_final.1 = (bf16[128,768]{1,0:T(8,128)(2,1)}, f32[96,192]{1,0:T(8,128)}, f32[96,192]{1,0:T(8,128)}, f32[96,192]{1,0:T(8,128)}, f32[192,96]{1,0:T(8,128)}, /...) custom-call(bf16[608,128]{1,0:T(8,128)(2,1)S(1)} %get-tuple-element.249.refs_0_, ...), custom_call_target="tpu_custom_call" | custom-call | tf_op jit(solution)/shard_map/self_final/pallas_call | solution.py:739
  (87 shorter events, 2.4 us)
Async XLA Ops:
  0.7 3.2 %copy-start = (bf16[768,192]{0,1:T(8,128)(2,1)S(1)}, bf16[768,192]{0,1:T(8,128)(2,1)}, u32[]{:S(2)}) copy-start(bf16[768,192]{0,1:T(8,128)(2,1)} %param.40) | copy-start | bytes 884740
  0.7 3.4 %copy-start.1 = (bf16[768,192]{0,1:T(8,128)(2,1)S(1)}, bf16[768,192]{0,1:T(8,128)(2,1)}, u32[]{:S(2)}) copy-start(bf16[768,192]{0,1:T(8,128)(2,1)} %param.41) | copy-start | bytes 884740
  0.7 4.4 %copy-start.3 = (bf16[1,256,768]{2,1,0:T(8,128)(2,1)S(1)}, bf16[1,256,768]{2,1,0:T(8,128)(2,1)}, u32[]{:S(2)}) copy-start(bf16[1,256,768]{2,1,0:T(8,128)(2,1)} %param.23) | copy-start | bytes 1179652
  0.7 4.4 %copy-start.5 = (bf16[768,192]{0,1:T(8,128)(2,1)S(1)}, bf16[768,192]{0,1:T(8,128)(2,1)}, u32[]{:S(2)}) copy-start(bf16[768,192]{0,1:T(8,128)(2,1)} %param.34) | copy-start | bytes 884740
  0.7 4.4 %copy-start.6 = (bf16[768,192]{0,1:T(8,128)(2,1)S(1)}, bf16[768,192]{0,1:T(8,128)(2,1)}, u32[]{:S(2)}) copy-start(bf16[768,192]{0,1:T(8,128)(2,1)} %param.35) | copy-start | bytes 884740
  0.7 4.4 %copy-start.10 = (bf16[768,192]{0,1:T(8,128)(2,1)S(1)}, bf16[768,192]{0,1:T(8,128)(2,1)}, u32[]{:S(2)}) copy-start(bf16[768,192]{0,1:T(8,128)(2,1)} %param.33) | copy-start | bytes 884740
  0.7 4.4 %copy-start.11 = (bf16[192,768]{1,0:T(8,128)(2,1)S(1)}, bf16[192,768]{1,0:T(8,128)(2,1)}, u32[]{:S(2)}) copy-start(bf16[192,768]{1,0:T(8,128)(2,1)} %refs_2_.5) | copy-start | bytes 884740
  0.7 4.4 %copy-start.14 = (f32[768]{0:T(1024)S(1)}, f32[768]{0:T(1024)}, u32[]{:S(2)}) copy-start(f32[768]{0:T(1024)} %refs_3_.7) | copy-start | bytes 9220
  0.7 4.4 %copy-start.15 = (s32[256]{0:T(256)S(1)}, s32[256]{0:T(256)}, u32[]{:S(2)}) copy-start(s32[256]{0:T(256)} %param.29) | copy-start | bytes 3076
  0.7 4.4 %copy-start.18 = (f32[32,3]{0,1:T(4,128)S(1)}, f32[32,3]{0,1:T(4,128)}, u32[]{:S(2)}) copy-start(f32[32,3]{0,1:T(4,128)} %param.37) | copy-start | bytes 1156
  0.8 6.2 %collective-permute-start.4 = (bf16[128,768]{1,0:T(8,128)(2,1)}, bf16[128,768]{1,0:T(8,128)(2,1)S(1)}, u32[]{:S(2)}, u32[]{:S(2)}) collective-permute-start(bf16[128,768]{1,0:T(8,128)(2,1)} %bitcast.33), channel_id=1, source_target_pairs={{0,1},{1,0},{2,3},{3,2},{4,5},{5,4},{6,7},{7,6},{8,9},{9,8},{10,11... | collective-permute-start | bytes 589832 | tf_op jit(solution)/shard_map/ppermute | solution.py:758
  1.3 8.3 %collective-permute-start = (bf16[128,768]{1,0:T(8,128)(2,1)}, bf16[128,768]{1,0:T(8,128)(2,1)S(1)}, u32[]{:S(2)}, u32[]{:S(2)}) collective-permute-start(bf16[128,768]{1,0:T(8,128)(2,1)} %bitcast.34), channel_id=1, source_target_pairs={{0,2},{1,3},{2,0},{3,1},{4,6},{5,7},{6,4},{7,5},{8,10},{9,11},{10,... | collective-permute-start | bytes 589832 | tf_op jit(solution)/shard_map/ppermute | solution.py:762
  3.9 3.4 %collective-permute-start.2 = (bf16[192,768]{1,0:T(8,128)(2,1)S(1)}, bf16[192,768]{1,0:T(8,128)(2,1)S(1)}, u32[]{:S(2)}, u32[]{:S(2)}) collective-permute-start(bf16[192,768]{1,0:T(8,128)(2,1)S(1)} %bitcast.19), channel_id=1, source_target_pairs={{0,1},{1,0},{2,3},{3,2},{4,5},{5,4},{6,7},{7,6},{8,9},{9,8},{10,11... | collective-permute-start | bytes 884744 | tf_op jit(solution)/shard_map/ppermute | solution.py:758
  4.0 3.3 %collective-permute-start.3 = (bf16[192,768]{1,0:T(8,128)(2,1)S(1)}, bf16[192,768]{1,0:T(8,128)(2,1)S(1)}, u32[]{:S(2)}, u32[]{:S(2)}) collective-permute-start(bf16[192,768]{1,0:T(8,128)(2,1)S(1)} %bitcast.24), channel_id=1, source_target_pairs={{0,1},{1,0},{2,3},{3,2},{4,5},{5,4},{6,7},{7,6},{8,9},{9,8},{10,11... | collective-permute-start | bytes 884744 | tf_op jit(solution)/shard_map/ppermute | solution.py:758
  5.1 2.2 %copy-start.4 = (bf16[1,128,768]{2,1,0:T(8,128)(2,1)S(1)}, bf16[1,128,768]{2,1,0:T(8,128)(2,1)}, u32[]{:S(2)}) copy-start(bf16[1,128,768]{2,1,0:T(8,128)(2,1)} %param.24) | copy-start | bytes 589828
  6.7 1.6 %copy-start.8 = (bf16[768,192]{0,1:T(8,128)(2,1)S(1)}, bf16[768,192]{0,1:T(8,128)(2,1)}, u32[]{:S(2)}) copy-start(bf16[768,192]{0,1:T(8,128)(2,1)} %param.39) | copy-start | bytes 884740
  6.7 2.0 %copy-start.9 = (bf16[192,768]{1,0:T(8,128)(2,1)S(1)}, bf16[192,768]{1,0:T(8,128)(2,1)}, u32[]{:S(2)}) copy-start(bf16[192,768]{1,0:T(8,128)(2,1)} %refs_5_.1) | copy-start | bytes 884740
  6.7 1.4 %collective-permute-start.5 = (bf16[64,768]{1,0:T(8,128)(2,1)S(1)}, bf16[64,768]{1,0:T(8,128)(2,1)S(1)}, u32[]{:S(2)}, u32[]{:S(2)}) collective-permute-start(bf16[64,768]{1,0:T(8,128)(2,1)S(1)} %get-tuple-element.152), channel_id=1, source_target_pairs={{0,1},{1,0},{2,3},{3,2},{4,5},{5,4},{6,7},{7,6},{8,9},{9,8},{10,11... | collective-permute-start | bytes 294920 | tf_op jit(solution)/shard_map/ppermute | solution.py:758
  7.0 1.3 %collective-permute-start.6 = (bf16[64,768]{1,0:T(8,128)(2,1)S(1)}, bf16[64,768]{1,0:T(8,128)(2,1)S(1)}, u32[]{:S(2)}, u32[]{:S(2)}) collective-permute-start(bf16[64,768]{1,0:T(8,128)(2,1)S(1)} %get-tuple-element.153), channel_id=1, source_target_pairs={{0,1},{1,0},{2,3},{3,2},{4,5},{5,4},{6,7},{7,6},{8,9},{9,8},{10,11... | collective-permute-start | bytes 294920 | tf_op jit(solution)/shard_map/ppermute | solution.py:758
  8.3 4.3 %copy-start.7 = (bf16[768,768]{1,0:T(8,128)(2,1)S(1)}, bf16[768,768]{1,0:T(8,128)(2,1)}, u32[]{:S(2)}) copy-start(bf16[768,768]{1,0:T(8,128)(2,1)} %refs_4_.5) | copy-start | bytes 3538948
  8.3 4.7 %copy-start.2 = (bf16[768,768]{1,0:T(8,128)(2,1)S(1)}, bf16[768,768]{1,0:T(8,128)(2,1)}, u32[]{:S(2)}) copy-start(bf16[768,768]{1,0:T(8,128)(2,1)} %refs_2_.4) | copy-start | bytes 3538948
  8.3 8.3 %collective-permute-start.8 = (bf16[192,768]{1,0:T(8,128)(2,1)S(1)}, bf16[192,768]{1,0:T(8,128)(2,1)S(1)}, u32[]{:S(2)}, u32[]{:S(2)}) collective-permute-start(bf16[192,768]{1,0:T(8,128)(2,1)S(1)} %bitcast.44), channel_id=1, source_target_pairs={{0,1},{1,0},{2,3},{3,2},{4,5},{5,4},{6,7},{7,6},{8,9},{9,8},{10,11... | collective-permute-start | bytes 884744 | tf_op jit(solution)/shard_map/ppermute | solution.py:758
  8.7 7.8 %collective-permute-start.9 = (bf16[192,768]{1,0:T(8,128)(2,1)S(1)}, bf16[192,768]{1,0:T(8,128)(2,1)S(1)}, u32[]{:S(2)}, u32[]{:S(2)}) collective-permute-start(bf16[192,768]{1,0:T(8,128)(2,1)S(1)} %copy-done.9), channel_id=1, source_target_pairs={{0,1},{1,0},{2,3},{3,2},{4,5},{5,4},{6,7},{7,6},{8,9},{9,8},{10,11... | collective-permute-start | bytes 884744 | tf_op jit(solution)/shard_map/ppermute | solution.py:758
  8.9 7.7 %collective-permute-start.7 = (bf16[144,768]{1,0:T(8,128)(2,1)S(1)}, bf16[144,768]{1,0:T(8,128)(2,1)S(1)}, u32[]{:S(2)}, u32[]{:S(2)}) collective-permute-start(bf16[144,768]{1,0:T(8,128)(2,1)S(1)} %self_sum.1.refs_10_.refs_1_), channel_id=1, source_target_pairs={{0,2},{1,3},{2,0},{3,1},{4,6},{5,7},{6,4},{7,5},{8,10},{9,11},{10,... | collective-permute-start | bytes 663560 | tf_op jit(solution)/shard_map/ppermute | solution.py:762
  9.6 2.0 %collective-permute-start.1 = (bf16[128,768]{1,0:T(8,128)(2,1)S(1)}, bf16[128,768]{1,0:T(8,128)(2,1)S(1)}, u32[]{:S(2)}, u32[]{:S(2)}) collective-permute-start(bf16[128,768]{1,0:T(8,128)(2,1)S(1)} %collective-permute-done.refs_0_.refs_4_.refs_6_), channel_id=1, source_target_pairs={{0,1},{1,0},{2,3},{3,2},{4,5},{5,4},{6,7},{7,6},{8,9},{9,8},{10,11... | collective-permute-start | bytes 589832 | tf_op jit(solution)/shard_map/ppermute | solution.py:758
  11.6 4.9 %copy-start.12 = (f32[768]{0:T(1024)S(1)}, f32[768]{0:T(1024)}, u32[]{:S(2)}) copy-start(f32[768]{0:T(1024)} %refs_3_.6) | copy-start | bytes 9220
  12.5 13.0 %collective-permute-start.11 = (bf16[768,768]{1,0:T(8,128)(2,1)S(1)}, bf16[768,768]{1,0:T(8,128)(2,1)S(1)}, u32[]{:S(2)}, u32[]{:S(2)}) collective-permute-start(bf16[768,768]{1,0:T(8,128)(2,1)S(1)} %copy-done.7), channel_id=1, source_target_pairs={{0,1},{1,0},{2,3},{3,2},{4,5},{5,4},{6,7},{7,6},{8,9},{9,8},{10,11... | collective-permute-start | bytes 3538952 | tf_op jit(solution)/shard_map/ppermute | solution.py:758
  13.0 7.1 %collective-permute-start.12 = (bf16[768,768]{1,0:T(8,128)(2,1)S(1)}, bf16[768,768]{1,0:T(8,128)(2,1)S(1)}, u32[]{:S(2)}, u32[]{:S(2)}) collective-permute-start(bf16[768,768]{1,0:T(8,128)(2,1)S(1)} %copy-done.2), channel_id=1, source_target_pairs={{0,1},{1,0},{2,3},{3,2},{4,5},{5,4},{6,7},{7,6},{8,9},{9,8},{10,11... | collective-permute-start | bytes 3538952 | tf_op jit(solution)/shard_map/ppermute | solution.py:758
  16.6 3.3 %copy-start.16 = (bf16[1,256,768]{2,1,0:T(8,128)(2,1)S(1)}, bf16[1,256,768]{2,1,0:T(8,128)(2,1)}, u32[]{:S(2)}) copy-start(bf16[1,256,768]{2,1,0:T(8,128)(2,1)} %param.31) | copy-start | bytes 1179652
  16.6 3.3 %copy-start.17 = (f32[16,256]{1,0:T(8,128)S(1)}, f32[16,256]{1,0:T(8,128)}, u32[]{:S(2)}) copy-start(f32[16,256]{1,0:T(8,128)} %refs_2_.3) | copy-start | bytes 49156
  19.1 6.4 %collective-permute-start.10 = (bf16[128,768]{1,0:T(8,128)(2,1)S(1)}, bf16[128,768]{1,0:T(8,128)(2,1)S(1)}, u32[]{:S(2)}, u32[]{:S(2)}) collective-permute-start(bf16[128,768]{1,0:T(8,128)(2,1)S(1)} %get-tuple-element.165.refs_0_), channel_id=1, source_target_pairs={{0,2},{1,3},{2,0},{3,1},{4,6},{5,7},{6,4},{7,5},{8,10},{9,11},{10,... | collective-permute-start | bytes 589832 | tf_op jit(solution)/shard_map/ppermute | solution.py:762
  19.9 5.6 %collective-permute-start.13 = (bf16[128,960]{1,0:T(8,128)(2,1)S(1)}, bf16[128,960]{1,0:T(8,128)(2,1)S(1)}, u32[]{:S(2)}, u32[]{:S(2)}) collective-permute-start(bf16[128,960]{1,0:T(8,128)(2,1)S(1)} %get-tuple-element.175), channel_id=1, source_target_pairs={{0,1},{1,0},{2,3},{3,2},{4,5},{5,4},{6,7},{7,6},{8,9},{9,8},{10,11... | collective-permute-start | bytes 737288 | tf_op jit(solution)/shard_map/ppermute | solution.py:758
  21.0 4.5 %copy-start.13 = (f32[768]{0:T(1024)S(1)}, f32[768]{0:T(1024)}, u32[]{:S(2)}) copy-start(f32[768]{0:T(1024)} %refs_3_.5) | copy-start | bytes 9220
  27.2 2.1 %collective-permute-start.15 = (bf16[128,2304]{1,0:T(8,128)(2,1)S(1)}, bf16[128,2304]{1,0:T(8,128)(2,1)S(1)}, u32[]{:S(2)}, u32[]{:S(2)}) collective-permute-start(bf16[128,2304]{1,0:T(8,128)(2,1)S(1)} %get-tuple-element.186.refs_1_), channel_id=1, source_target_pairs={{0,1},{1,0},{2,3},{3,2},{4,5},{5,4},{6,7},{7,6},{8,9},{9,8},{10,11... | collective-permute-start | bytes 1769480 | tf_op jit(solution)/shard_map/ppermute | solution.py:758
  27.2 7.3 %collective-permute-start.14 = (bf16[128,768]{1,0:T(8,128)(2,1)S(1)}, bf16[128,768]{1,0:T(8,128)(2,1)S(1)}, u32[]{:S(2)}, u32[]{:S(2)}) collective-permute-start(bf16[128,768]{1,0:T(8,128)(2,1)S(1)} %get-tuple-element.176.refs_6_.refs_0_), channel_id=1, source_target_pairs={{0,2},{1,3},{2,0},{3,1},{4,6},{5,7},{6,4},{7,5},{8,10},{9,11},{10,... | collective-permute-start | bytes 589832 | tf_op jit(solution)/shard_map/ppermute | solution.py:762
  30.3 16.2 %collective-permute-start.20 = (bf16[4,96,768]{2,1,0:T(8,128)(2,1)S(1)}, bf16[4,96,768]{2,1,0:T(8,128)(2,1)S(1)}, u32[]{:S(2)}, u32[]{:S(2)}) collective-permute-start(bf16[4,96,768]{2,1,0:T(8,128)(2,1)S(1)} %get-tuple-element.209), channel_id=1, source_target_pairs={{0,4},{4,0},{8,12},{12,8},{16,20},{20,16},{24,28},{28,24},{1,5},{5... | collective-permute-start | bytes 1769480 | tf_op jit(solution)/shard_map/ppermute | solution.py:766
  31.8 16.2 %collective-permute-start.21 = (bf16[4,96,768]{2,1,0:T(8,128)(2,1)S(1)}, bf16[4,96,768]{2,1,0:T(8,128)(2,1)S(1)}, u32[]{:S(2)}, u32[]{:S(2)}) collective-permute-start(bf16[4,96,768]{2,1,0:T(8,128)(2,1)S(1)} %get-tuple-element.211), channel_id=1, source_target_pairs={{0,8},{4,12},{8,0},{12,4},{16,24},{20,28},{24,16},{28,20},{1,9},{5... | collective-permute-start | bytes 1769480 | tf_op jit(solution)/shard_map/ppermute | solution.py:766
  37.3 2.4 %collective-permute-start.17 = (bf16[1024,192]{1,0:T(8,128)(2,1)S(1)}, bf16[1024,192]{1,0:T(8,128)(2,1)S(1)}, u32[]{:S(2)}, u32[]{:S(2)}) collective-permute-start(bf16[1024,192]{1,0:T(8,128)(2,1)S(1)} %source_grad.1.refs_15_), channel_id=1, source_target_pairs={{0,1},{1,0},{2,3},{3,2},{4,5},{5,4},{6,7},{7,6},{8,9},{9,8},{10,11... | collective-permute-start | bytes 1179656 | tf_op jit(solution)/shard_map/ppermute | solution.py:758
  37.4 2.3 %collective-permute-start.18 = (bf16[128,960]{1,0:T(8,128)(2,1)S(1)}, bf16[128,960]{1,0:T(8,128)(2,1)S(1)}, u32[]{:S(2)}, u32[]{:S(2)}) collective-permute-start(bf16[128,960]{1,0:T(8,128)(2,1)S(1)} %get-tuple-element.201), channel_id=1, source_target_pairs={{0,1},{1,0},{2,3},{3,2},{4,5},{5,4},{6,7},{7,6},{8,9},{9,8},{10,11... | collective-permute-start | bytes 737288 | tf_op jit(solution)/shard_map/ppermute | solution.py:758
  37.9 7.1 %collective-permute-start.16 = (bf16[128,768]{1,0:T(8,128)(2,1)S(1)}, bf16[128,768]{1,0:T(8,128)(2,1)S(1)}, u32[]{:S(2)}, u32[]{:S(2)}) collective-permute-start(bf16[128,768]{1,0:T(8,128)(2,1)S(1)} %get-tuple-element.191.refs_0_), channel_id=1, source_target_pairs={{0,2},{1,3},{2,0},{3,1},{4,6},{5,7},{6,4},{7,5},{8,10},{9,11},{10,... | collective-permute-start | bytes 589832 | tf_op jit(solution)/shard_map/ppermute | solution.py:762
  41.4 12.4 %collective-permute-start.23 = (bf16[4,96,384]{2,1,0:T(8,128)(2,1)S(1)}, bf16[4,96,384]{2,1,0:T(8,128)(2,1)S(1)}, u32[]{:S(2)}, u32[]{:S(2)}) collective-permute-start(bf16[4,96,384]{2,1,0:T(8,128)(2,1)S(1)} %get-tuple-element.215), channel_id=1, source_target_pairs={{0,4},{4,0},{8,12},{12,8},{16,20},{20,16},{24,28},{28,24},{1,5},{5... | collective-permute-start | bytes 884744 | tf_op jit(solution)/shard_map/ppermute | solution.py:766
  42.9 10.8 %collective-permute-start.24 = (bf16[4,96,384]{2,1,0:T(8,128)(2,1)S(1)}, bf16[4,96,384]{2,1,0:T(8,128)(2,1)S(1)}, u32[]{:S(2)}, u32[]{:S(2)}) collective-permute-start(bf16[4,96,384]{2,1,0:T(8,128)(2,1)S(1)} %get-tuple-element.217), channel_id=1, source_target_pairs={{0,8},{4,12},{8,0},{12,4},{16,24},{20,28},{24,16},{28,20},{1,9},{5... | collective-permute-start | bytes 884744 | tf_op jit(solution)/shard_map/ppermute | solution.py:766
  45.2 3.0 %collective-permute-start.19 = (bf16[144,768]{1,0:T(8,128)(2,1)S(1)}, bf16[144,768]{1,0:T(8,128)(2,1)S(1)}, u32[]{:S(2)}, u32[]{:S(2)}) collective-permute-start(bf16[144,768]{1,0:T(8,128)(2,1)S(1)} %get-tuple-element.205.refs_4_.refs_0_.refs_8_), channel_id=1, source_target_pairs={{0,1},{1,0},{2,3},{3,2},{4,5},{5,4},{6,7},{7,6},{8,9},{9,8},{10,11... | collective-permute-start | bytes 663560 | tf_op jit(solution)/shard_map/ppermute | solution.py:758
  50.1 3.9 %collective-permute-start.22 = (bf16[144,768]{1,0:T(8,128)(2,1)S(1)}, bf16[144,768]{1,0:T(8,128)(2,1)S(1)}, u32[]{:S(2)}, u32[]{:S(2)}) collective-permute-start(bf16[144,768]{1,0:T(8,128)(2,1)S(1)} %get-tuple-element.214), channel_id=1, source_target_pairs={{0,1},{1,0},{2,3},{3,2},{4,5},{5,4},{6,7},{7,6},{8,9},{9,8},{10,11... | collective-permute-start | bytes 663560 | tf_op jit(solution)/shard_map/ppermute | solution.py:758
  50.2 11.5 %collective-permute-start.26 = (bf16[2,96,768]{2,1,0:T(8,128)(2,1)S(1)}, bf16[2,96,768]{2,1,0:T(8,128)(2,1)S(1)}, u32[]{:S(2)}, u32[]{:S(2)}) collective-permute-start(bf16[2,96,768]{2,1,0:T(8,128)(2,1)S(1)} %get-tuple-element.212.refs_11_), channel_id=1, source_target_pairs={{0,8},{4,12},{8,0},{12,4},{16,24},{20,28},{24,16},{28,20},{1,9},{5... | collective-permute-start | bytes 884744 | tf_op jit(solution)/shard_map/ppermute | solution.py:766
  51.8 9.9 %collective-permute-start.27 = (bf16[2,96,768]{2,1,0:T(8,128)(2,1)S(1)}, bf16[2,96,768]{2,1,0:T(8,128)(2,1)S(1)}, u32[]{:S(2)}, u32[]{:S(2)}) collective-permute-start(bf16[2,96,768]{2,1,0:T(8,128)(2,1)S(1)} %get-tuple-element.231), channel_id=1, source_target_pairs={{0,4},{4,0},{8,12},{12,8},{16,20},{20,16},{24,28},{28,24},{1,5},{5... | collective-permute-start | bytes 884744 | tf_op jit(solution)/shard_map/ppermute | solution.py:766
  54.1 10.4 %collective-permute-start.25 = (bf16[144,768]{1,0:T(8,128)(2,1)S(1)}, bf16[144,768]{1,0:T(8,128)(2,1)S(1)}, u32[]{:S(2)}, u32[]{:S(2)}) collective-permute-start(bf16[144,768]{1,0:T(8,128)(2,1)S(1)} %input_sum.1.refs_4_.refs_0_), channel_id=1, source_target_pairs={{0,2},{1,3},{2,0},{3,1},{4,6},{5,7},{6,4},{7,5},{8,10},{9,11},{10,... | collective-permute-start | bytes 663560 | tf_op jit(solution)/shard_map/ppermute | solution.py:762
  54.9 18.6 %collective-permute-start.31 = (bf16[1472,128]{1,0:T(8,128)(2,1)S(1)}, bf16[1472,128]{1,0:T(8,128)(2,1)S(1)}, u32[]{:S(2)}, u32[]{:S(2)}) collective-permute-start(bf16[1472,128]{1,0:T(8,128)(2,1)S(1)} %get-tuple-element.235), channel_id=1, source_target_pairs={{0,8},{4,12},{8,0},{12,4},{16,24},{20,28},{24,16},{28,20},{1,9},{5... | collective-permute-start | bytes 1130504 | tf_op jit(solution)/shard_map/ppermute | solution.py:766
  55.9 17.6 %collective-permute-start.30 = (bf16[2112,128]{1,0:T(8,128)(2,1)S(1)}, bf16[2112,128]{1,0:T(8,128)(2,1)S(1)}, u32[]{:S(2)}, u32[]{:S(2)}) collective-permute-start(bf16[2112,128]{1,0:T(8,128)(2,1)S(1)} %get-tuple-element.234), channel_id=1, source_target_pairs={{0,4},{4,0},{8,12},{12,8},{16,20},{20,16},{24,28},{28,24},{1,5},{5... | collective-permute-start | bytes 1622024 | tf_op jit(solution)/shard_map/ppermute | solution.py:766
  61.8 14.8 %collective-permute-start.39 = (bf16[192,768]{1,0:T(8,128)(2,1)S(1)}, bf16[192,768]{1,0:T(8,128)(2,1)S(1)}, u32[]{:S(2)}, u32[]{:S(2)}) collective-permute-start(bf16[192,768]{1,0:T(8,128)(2,1)S(1)} %get-tuple-element.232.refs_2_), channel_id=1, source_target_pairs={{0,16},{4,20},{8,24},{12,28},{16,0},{20,4},{24,8},{28,12},{1,17},{... | collective-permute-start | bytes 884744 | tf_op jit(solution)/shard_map/ppermute | solution.py:766
  64.5 5.7 %collective-permute-start.28 = (bf16[128,768]{1,0:T(8,128)(2,1)S(1)}, bf16[128,768]{1,0:T(8,128)(2,1)S(1)}, u32[]{:S(2)}, u32[]{:S(2)}) collective-permute-start(bf16[128,768]{1,0:T(8,128)(2,1)S(1)} %ffn_out.1.refs_6_), channel_id=1, source_target_pairs={{0,2},{1,3},{2,0},{3,1},{4,6},{5,7},{6,4},{7,5},{8,10},{9,11},{10,... | collective-permute-start | bytes 589832 | tf_op jit(solution)/shard_map/ppermute | solution.py:762
  65.3 7.4 %collective-permute-start.32 = (bf16[16,256]{1,0:T(8,128)(2,1)S(1)}, bf16[16,256]{1,0:T(8,128)(2,1)S(1)}, u32[]{:S(2)}, u32[]{:S(2)}) collective-permute-start(bf16[16,256]{1,0:T(8,128)(2,1)S(1)} %gain.1.refs_8_.refs_6_), channel_id=1, source_target_pairs={{0,4},{4,0},{8,12},{12,8},{16,20},{20,16},{24,28},{28,24},{1,5},{5... | collective-permute-start | bytes 24584 | tf_op jit(solution)/shard_map/ppermute | solution.py:766
  70.6 19.8 %collective-permute-start.29 = (bf16[256,768]{1,0:T(8,128)(2,1)S(1)}, bf16[256,768]{1,0:T(8,128)(2,1)S(1)}, u32[]{:S(2)}, u32[]{:S(2)}) collective-permute-start(bf16[256,768]{1,0:T(8,128)(2,1)S(1)} %input_grad.1.refs_8_.refs_0_), channel_id=1, source_target_pairs={{0,1},{1,0},{2,3},{3,2},{4,5},{5,4},{6,7},{7,6},{8,9},{9,8},{10,11... | collective-permute-start | bytes 1179656 | tf_op jit(solution)/shard_map/ppermute | solution.py:758
  73.8 5.2 %collective-permute-start.34 = (bf16[2,112,256]{2,1,0:T(8,128)(2,1)S(1)}, bf16[2,112,256]{2,1,0:T(8,128)(2,1)S(1)}, u32[]{:S(2)}, u32[]{:S(2)}) collective-permute-start(bf16[2,112,256]{2,1,0:T(8,128)(2,1)S(1)} %get-tuple-element.241.refs_3_.refs_2_), channel_id=1, source_target_pairs={{0,4},{4,0},{8,12},{12,8},{16,20},{20,16},{24,28},{28,24},{1,5},{5... | collective-permute-start | bytes 344072 | tf_op jit(solution)/shard_map/ppermute | solution.py:766
  74.4 9.4 %collective-permute-start.33 = (bf16[208,512]{1,0:T(8,128)(2,1)S(1)}, bf16[208,512]{1,0:T(8,128)(2,1)S(1)}, u32[]{:S(2)}, u32[]{:S(2)}) collective-permute-start(bf16[208,512]{1,0:T(8,128)(2,1)S(1)} %get-tuple-element.239), channel_id=1, source_target_pairs={{0,8},{4,12},{8,0},{12,4},{16,24},{20,28},{24,16},{28,20},{1,9},{5... | collective-permute-start | bytes 638984 | tf_op jit(solution)/shard_map/ppermute | solution.py:766
  75.0 3.9 %collective-permute-start.35 = (bf16[256,768]{1,0:T(8,128)(2,1)S(1)}, bf16[256,768]{1,0:T(8,128)(2,1)S(1)}, u32[]{:S(2)}, u32[]{:S(2)}) collective-permute-start(bf16[256,768]{1,0:T(8,128)(2,1)S(1)} %get-tuple-element.244), channel_id=1, source_target_pairs={{0,1},{1,0},{2,3},{3,2},{4,5},{5,4},{6,7},{7,6},{8,9},{9,8},{10,11... | collective-permute-start | bytes 1179656 | tf_op jit(solution)/shard_map/ppermute | solution.py:758
  76.7 12.9 %collective-permute-start.38 = (bf16[576,128]{1,0:T(8,128)(2,1)S(1)}, bf16[576,128]{1,0:T(8,128)(2,1)S(1)}, u32[]{:S(2)}, u32[]{:S(2)}) collective-permute-start(bf16[576,128]{1,0:T(8,128)(2,1)S(1)} %get-tuple-element.262), channel_id=1, source_target_pairs={{0,16},{4,20},{8,24},{12,28},{16,0},{20,4},{24,8},{28,12},{1,17},{... | collective-permute-start | bytes 442376 | tf_op jit(solution)/shard_map/ppermute | solution.py:766
  83.8 8.5 %collective-permute-start.36 = (bf16[608,128]{1,0:T(8,128)(2,1)S(1)}, bf16[608,128]{1,0:T(8,128)(2,1)S(1)}, u32[]{:S(2)}, u32[]{:S(2)}) collective-permute-start(bf16[608,128]{1,0:T(8,128)(2,1)S(1)} %get-tuple-element.246.refs_2_), channel_id=1, source_target_pairs={{0,16},{4,20},{8,24},{12,28},{16,0},{20,4},{24,8},{28,12},{1,17},{... | collective-permute-start | bytes 466952 | tf_op jit(solution)/shard_map/ppermute | solution.py:766
  83.9 8.5 %collective-permute-start.37 = (bf16[128,768]{1,0:T(8,128)(2,1)S(1)}, bf16[128,768]{1,0:T(8,128)(2,1)S(1)}, u32[]{:S(2)}, u32[]{:S(2)}) collective-permute-start(bf16[128,768]{1,0:T(8,128)(2,1)S(1)} %get-tuple-element.250), channel_id=1, source_target_pairs={{0,2},{1,3},{2,0},{3,1},{4,6},{5,7},{6,4},{7,5},{8,10},{9,11},{10,... | collective-permute-start | bytes 589832 | tf_op jit(solution)/shard_map/ppermute | solution.py:762

commit v4 on v3

--- a/solution.py
+++ b/solution.py
@@ -327,7 +327,7 @@
     out[...] = total.astype(BF16)
 
 
-def write_blocks(whole, columns, first_bit, rest_bits, size, targets, extra=None):
+def write_blocks(whole, columns, first_bit, rest_bits, size, targets):
     index = lax.axis_index("dp")
     count = 1 << len(rest_bits)
     for first, target in enumerate(targets):
@@ -337,19 +337,14 @@
                 if entry >> (len(rest_bits) - 1 - place) & 1:
                     relative |= 1 << bit
             block = index ^ relative
-            rows = whole[pl.ds(pl.multiple_of(block * size, size), size), columns]
-            target[entry, :size, :] = rows
-            if extra is not None:
-                target[entry, size:, :] = extra
-
-
-def emit(whole, outs, order, size, extra=None, columns=slice(None)):
+            target[entry] = whole[pl.ds(pl.multiple_of(block * size, size), size), columns]
+
+
+def emit(whole, outs, order, size, columns=slice(None)):
     if order is None:
-        outs[0][: whole.shape[0], :] = whole[:, columns]
-        if extra is not None:
-            outs[0][whole.shape[0] :, :] = extra
+        outs[0][...] = whole[:, columns]
     else:
-        write_blocks(whole, columns, order[0], order[1:], size, outs, extra)
+        write_blocks(whole, columns, order[0], order[1:], size, outs)
 
 
 def ffn_weights_kernel(orders, size, normed, pack, act_own, grad_pre_own, branch_own, branch_peer, *refs):
@@ -506,7 +501,7 @@
 def self_weights_kernel(
     orders, size, buckets, normed, branch, gq, gk, gv, context, gl, bucket, pack_own, pack_peer, *refs
 ):
-    *outs, whole, right, left = refs
+    *outs, extra_out, whole, right, left = refs
     count = len(outs) // 2
     length, columns = gq.shape
     half = pack_own.shape[0] - EXTRA
@@ -542,8 +537,8 @@
     row = lax.broadcasted_iota(jnp.int32, (count_rows, narrow), 0)
     for head in range(heads):
         extra = extra + jnp.where(row == first + head, table[head : head + 1], 0.0)
-    extra = extra.astype(BF16)
-    emit(whole, outs[count:], orders[1], size, extra, columns=slice(wide, None))
+    extra_out[...] = extra.astype(BF16)
+    emit(whole, outs[count:], orders[1], size, columns=slice(wide, None))
 
 
 def extra_rows(width, wide, heads):
@@ -609,14 +604,17 @@
         target[size:] = low_sum(down_keep[entry], down_got[entry])
 
 
-def round_three_kernel(ca_keep, ca_got, cb_keep, cb_got, sa_send, sb_send, x_send, zo_send, ca_next, cb_next):
+def round_three_kernel(
+    ca_keep, ca_got, cb_keep, cb_got, sa_send, sb_send, extra, x_send, zo_send, ca_next, cb_next
+):
     for entry in range(2):
         ca_next[entry] = low_sum(ca_keep[entry], ca_got[entry])
         cb_next[entry] = low_sum(cb_keep[entry], cb_got[entry])
     base = spread_out(x_send, [low_sum(cb_keep[2 + entry], cb_got[2 + entry]) for entry in range(2)])
     spread_out(x_send, [sa_send[entry] for entry in range(4)], base)
     base = spread_out(zo_send, [low_sum(ca_keep[2 + entry], ca_got[2 + entry]) for entry in range(2)])
-    spread_out(zo_send, [sb_send[entry] for entry in range(4)], base)
+    base = spread_out(zo_send, [sb_send[entry] for entry in range(4)], base)
+    spread_out(zo_send, [extra[...]], base)
 
 
 def gain_kernel(chip_own, chip_other, out):
@@ -640,13 +638,12 @@
 
 
 def round_four_kernel(
-    x_got, zo_got, ca_keep, cb_keep, sa_keep, sb_keep, gains, gains_got,
+    x_got, zo_got, ca_keep, cb_keep, sa_keep, sb_keep, extra, gains, gains_got,
     cross_send, cross_keep, sa_send, sa_next, sb_send, sb_next,
 ):
     size, ca_wide = ca_keep.shape[1:]
     cb_wide = cb_keep.shape[2]
     large, small = sa_keep.shape[2], sb_keep.shape[2]
-    more = sb_keep.shape[1]
     zo_base = 2 * size * ca_wide // PIECE
     x_base = 2 * size * cb_wide // PIECE
     for entry, target in enumerate((cross_keep, cross_send)):
@@ -655,27 +652,29 @@
         part = low_sum(cb_keep[entry], gathered(x_got, size, cb_wide, entry * (x_base // 2)))
         spread_out(target, [part], base)
     gain = low_sum(gains[...], gains_got[...])
+    step = size * (small // PIECE)
+    extra = low_sum(extra[...], gathered(zo_got, extra.shape[0], small, zo_base + 4 * step))
     for first, sa_out, sb_out in ((0, sa_next, sb_next), (2, sa_send, sb_send)):
         for entry in range(2):
+            part = slice(entry * size, (entry + 1) * size)
             start = x_base + (first + entry) * size * (large // PIECE)
-            part = slice(entry * size, (entry + 1) * size)
             sa_out[part] = low_sum(sa_keep[first + entry], gathered(x_got, size, large, start))
-            start = zo_base + (first + entry) * more * (small // PIECE)
-            other = gathered(zo_got, more, small, start)
-            sb_out[entry] = low_sum(sb_keep[first + entry], other)
+            start = zo_base + (first + entry) * step
+            sb_out[part] = low_sum(sb_keep[first + entry], gathered(zo_got, size, small, start))
         sa_out[2 * size :, :small] = gain
-
-
-def round_five_kernel(sa_keep, sa_got, sb_keep, sb_got, send, keep):
-    large, small = sa_keep.shape[1], sb_keep.shape[2]
-    size = sa_keep.shape[0] - sb_keep.shape[1]
-    gain = low_sum(sa_keep[2 * size :, :small], sa_got[2 * size :, :small])
+        sb_out[2 * size :] = extra
+
+
+def round_five_kernel(size, sa_keep, sa_got, sb_keep, sb_got, send, keep):
+    large, small = sa_keep.shape[1], sb_keep.shape[1]
+    extra = low_sum(
+        low_sum(sa_keep[2 * size :, :small], sa_got[2 * size :, :small]), low_sum(sb_keep[2 * size :], sb_got[2 * size :])
+    )
     for entry, target in enumerate((keep, send)):
         part = slice(entry * size, (entry + 1) * size)
-        spread_out(target, [low_sum(sa_keep[part], sa_got[part])])
-        part = low_sum(sb_keep[entry], sb_got[entry])
-        part = jnp.concatenate([part[:size], low_sum(part[size:], gain)], 0)
-        spread_out(target, [part], size * (large // PIECE))
+        base = spread_out(target, [low_sum(sa_keep[part], sa_got[part])])
+        part = jnp.concatenate([low_sum(sb_keep[part], sb_got[part]), extra], 0)
+        spread_out(target, [part], base)
 
 
 def ffn_final_kernel(keep, got, up, down):
@@ -796,10 +795,10 @@
     def plus(left, right, name):
         return go(add_kernel, name, [(left.shape, left.dtype)], [left, right])
 
-    def payload(order, wide, extra=0):
+    def payload(order, wide):
         if order is None:
-            return [((width + extra, wide), BF16)]
-        return [((dp // 2, size + extra, wide), BF16)] * 2
+            return [((width, wide), BF16)]
+        return [((dp // 2, size, wide), BF16)] * 2
 
     x = inputs.reshape(length, width)
     cot = cotangent.reshape(length, width)
@@ -830,9 +829,8 @@
     )
     chip_one = go(self_sum_kernel, "self_sum", [((half + EXTRA, width), BF16)], [keep, first_half, second_half])
     other_one = to_chip(chip_one)
-    wq_source, wo_source, _ = lax.optimization_barrier((cross_query, cross_output, chip_one))
-    wq_peer = to_core(wq_source)
-    wo_peer = to_core(wo_source)
+    wq_peer = to_core(cross_query)
+    wo_peer = to_core(cross_output)
     e3 = to_core(e1)
     late = go(
         source_second_kernel, "source_second", [((span, columns), BF16), ((columns, span), BF16)] * 2,
@@ -947,8 +945,9 @@
     def self_weights(*refs):
         self_weights_kernel((along_x, along_z), size, table.shape[1], *refs)
 
-    self_payload = listed(go(
-        self_weights, "self_weights", payload(along_x, large) + payload(along_z, small, extra_count),
+    *self_payload, extra = listed(go(
+        self_weights, "self_weights",
+        payload(along_x, large) + payload(along_z, small) + [((extra_count, small), BF16)],
         [normed_one, branch_one, gq_one, gk_one, gv_one, context_one, gl_one, bucket, pack_self, pack_self_peer],
         scratch=[((width, 2 * wide), BF16), ((2 * length, wide), BF16), ((2 * length, width), BF16)],
     ))
@@ -961,11 +960,11 @@
         sb_keep, sb_send = sb_payload
         more = size + extra_count
         x_rows = (2 * size * cb_wide + 4 * size * large) // PIECE
-        zo_rows = (2 * size * ca_wide + 4 * more * small) // PIECE
+        zo_rows = (2 * size * ca_wide + (4 * size + extra_count) * small) // PIECE
         x_send, zo_send, ca_keep, cb_keep = go(
             round_three_kernel, "round_three",
             [((x_rows, PIECE), BF16), ((zo_rows, PIECE), BF16), ((2, size, ca_wide), BF16), ((2, size, cb_wide), BF16)],
-            [ca_keep, to_peer(ca_send, 0), cb_keep, to_peer(cb_send, 1), sa_send, sb_send], us=1.6,
+            [ca_keep, to_peer(ca_send, 0), cb_keep, to_peer(cb_send, 1), sa_send, sb_send, extra], us=1.6,
         )
         x_got = to_peer(x_send, 0)
         zo_got = to_peer(zo_send, 1)
@@ -984,28 +983,28 @@
     else:
         branch_source = branch_out
     out_other = to_chip(branch_source)
-    pack_rows = go(
-        input_grad_kernel, "input_grad", [((2 * half, width), BF16)],
-        [chip_five, other_five, x, gain_one, grad_one, hidden_two, branch_out, out_other],
-    )
-    pack_rows_peer = to_core(pack_rows)
 
     if halving:
         rows = 2 * size + extra_count
         cross_send, cross_keep, sa_send, sa_keep, sb_send, sb_keep = go(
             round_four_kernel, "round_four",
-            [((size * 2 * wide // PIECE, PIECE), BF16)] * 2 + [((rows, large), BF16)] * 2 + [((2, more, small), BF16)] * 2,
-            [x_got, zo_got, ca_keep, cb_keep, sa_keep, sb_keep, gains, gains_got],
+            [((size * 2 * wide // PIECE, PIECE), BF16)] * 2 + [((rows, large), BF16)] * 2 + [((rows, small), BF16)] * 2,
+            [x_got, zo_got, ca_keep, cb_keep, sa_keep, sb_keep, extra, gains, gains_got],
         )
         sa_got = to_peer(sa_send, 1)
         sb_got = to_peer(sb_send, 0)
-        up, down = go(ffn_final_kernel, "ffn_final", [((size, width), F32)] * 2, [ffn_keep, ffn_got], us=LONG, last=True)
 
     encoded_keep, encoded_send = go(
         encoded_kernel, "encoded", [((span // 2, width), BF16)] * 2, [source_total, cross_key, cross_value]
     )
     encoded_got = to_core(encoded_send)
+    pack_rows = go(
+        input_grad_kernel, "input_grad", [((2 * half, width), BF16)],
+        [chip_five, other_five, x, gain_one, grad_one, hidden_two, branch_out, out_other],
+    )
+    pack_rows_peer = to_core(pack_rows)
     if halving:
+        up, down = go(ffn_final_kernel, "ffn_final", [((size, width), F32)] * 2, [ffn_keep, ffn_got], us=LONG, last=True)
         cross_send, _ = lax.optimization_barrier((cross_send, encoded_send))
         cross_got = to_peer(cross_send, 2)
     encoded_part, encoded_pass = go(
@@ -1015,8 +1014,12 @@
 
     if halving:
         rows = (size * large + more * small) // PIECE
+
+        def round_five(*refs):
+            round_five_kernel(size, *refs)
+
         self_send, self_keep = go(
-            round_five_kernel, "round_five", [((rows, PIECE), BF16)] * 2, [sa_keep, sa_got, sb_keep, sb_got]
+            round_five, "round_five", [((rows, PIECE), BF16)] * 2, [sa_keep, sa_got, sb_keep, sb_got]
         )
         self_got = to_peer(self_send, 2)
         square = ((size, columns), F32)
@@ -1061,9 +1064,8 @@
         grad_cross_key, grad_cross_value = pair_of(ca_payload[0])
         grad_cross_query, grad_cross_output = pair_of(cb_payload[0])
         grad_self_query, grad_self_key = pair_of(sa_payload[0])
-        grad_self_value, grad_self_output = pair_of(sb_payload[0][:width])
+        grad_self_value, grad_self_output = pair_of(sb_payload[0])
         grad_cross_output, grad_self_output = grad_cross_output.T, grad_self_output.T
-        extra = sb_payload[0][width:]
         grad_table = lax.psum(extra[table_row : table_row + heads, : table.shape[1]].astype(F32), "dp")
         encoded_grad = plus(encoded_part, encoded_other, "encoded_grad")
         gain_rows = [item[half : half + 2] for item in (chip_five, other_five)]

time: 93.5 us -> 92.4 us (0.988)
  waiting for transfers between devices: 37 us -> 35 us
  starting transfers between devices: 27.2 us -> 28.2 us
    ppermute x8, waiting for transfers between devices: 11.9 us -> 7.09 us  [to_chip(): lax.ppermute(value, 'tensor', [(i, i ^ 2) for i in range(lax.axis_size('t...]
    ppermute x14, waiting for transfers between devices: 22.7 us -> 25.3 us  [to_peer(): lax.ppermute(value, 'dp', [(i, i ^ 1 << bit) for i in range(lax.axis_size...]
    ppermute x14, starting transfers between devices: 15.6 us -> 17.4 us  [to_peer(): lax.ppermute(value, 'dp', [(i, i ^ 1 << bit) for i in range(lax.axis_size...]
  transfers between devices with their start and end apart: 40 -> 40, of which waited for: 16 -> 13; matrix products, arithmetic and copies ran while one was open for 0% -> 0% of each run, Pallas kernels for 24% -> 24%
where the time goes in v4:
time: 92.4 us; the launch traced here: 92.2 us
  waiting for transfers between devices  35 us (38%)
  starting transfers between devices  28.2 us (31%)
  Pallas kernels  25.1 us (27%)
  between operations  3.81 us (4%)
    ppermute x14, waiting for transfers between devices, to_peer(): lax.ppermute(value, 'dp', [(i, i ^ 1 << bit) for i in range(lax.axis_size...  25.3 us
    pallas_call x33, Pallas kernels, run(): pl.pallas_call(body, out_shape=shapes, in_specs=place, out_specs=[vmem] *...  25.1 us
    ppermute x14, starting transfers between devices, to_peer(): lax.ppermute(value, 'dp', [(i, i ^ 1 << bit) for i in range(lax.axis_size...  17.4 us
    ppermute x8, waiting for transfers between devices, to_chip(): lax.ppermute(value, 'tensor', [(i, i ^ 2) for i in range(lax.axis_size('t...  7.09 us
    ppermute x8, starting transfers between devices, to_chip(): lax.ppermute(value, 'tensor', [(i, i ^ 2) for i in range(lax.axis_size('t...  6.96 us
    ppermute x18, starting transfers between devices, to_core(): lax.ppermute(value, 'tensor', [(i, i ^ 1) for i in range(lax.axis_size('t...  3.85 us
    ppermute x18, waiting for transfers between devices, to_core(): lax.ppermute(value, 'tensor', [(i, i ^ 1) for i in range(lax.axis_size('t...  2.57 us
  transfers between devices with their start and end apart: 40, of which 13 were waited for; matrix products, arithmetic and copies ran while one was open for 0% of the time, Pallas kernels for 24%

profile of v4, /device:TPU:0, one launch (start us, length us, event | category | flops | bytes accessed | tf_op | source)
XLA Modules:
  0.0 92.2 jit_solution(5188897146166031354)
XLA Ops:
  0.8 0.5 collective-permute-start.4
  1.3 2.6 %collective-permute-start = (bf16[128,768]{1,0:T(8,128)(2,1)}, bf16[128,768]{1,0:T(8,128)(2,1)S(1)}, u32[]{:S(2)}, u32[]{:S(2)}) collective-permute-start(bf16[128,768]{1,0:T(8,128)(2,1)} %bitcast.34), channel_id=1, source_target_pairs={{0,2},{1,3},{2,0},{3,1},{4,6},{5,7},{6,4},{7,5},{8,10},{9,11},{10,... | collective-permute-start | bytes 589832 | tf_op jit(solution)/shard_map/ppermute | solution.py:761
  4.0 0.3 collective-permute-start.3
  5.2 1.6 %self_forward.1 = (bf16[128,768]{1,0:T(8,128)(2,1)S(1)}, bf16[64,768]{1,0:T(8,128)(2,1)S(1)}, bf16[64,768]{1,0:T(8,128)(2,1)S(1)}, bf16[256,768]{1,0:T(8,128)(2,...) custom-call(s32[1]{0:T(128)S(6)} %copy.40.refs_0_, ...), custom_call_target="tpu_custom_call" | custom-call | flops 4024999936 | tf_op jit(solution)/shard_map/self_forward/pallas_call | solution.py:738
  6.7 0.2 collective-permute-start.5
  7.0 0.3 collective-permute-start.6
  7.5 0.3 collective-permute-start.9
  7.8 0.8 source_first.1
  8.8 0.8 collective-permute-start.7
  11.5 0.9 source_second.1
  12.4 0.6 collective-permute-start.11
  13.2 3.2 %collective-permute-done.7.refs_2_ = bf16[144,768]{1,0:T(8,128)(2,1)S(1)} collective-permute-done((bf16[144,768]{1,0:T(8,128)(2,1)S(1)}, bf16[144,768]{1,0:T(8,128)(2,1)S(1)}, u32[]{:S(2)}, u32[]{:S(2)}) %collective-permute-start.7) | collective-permute-done | bytes 221216 | tf_op jit(solution)/shard_map/ppermute | solution.py:761
  16.3 2.5 %cross_forward.1 = (bf16[128,768]{1,0:T(8,128)(2,1)S(1)}, f32[128,768]{1,0:T(8,128)S(1)}, bf16[128,768]{1,0:T(8,128)(2,1)S(1)}, bf16[128,192]{1,0:T(8,128)(2,1)S...) custom-call(f32[512,128]{1,0:T(8,128)S(1)} %get-tuple-element.157.re, ...), custom_call_target="tpu_custom_call" | custom-call | tf_op jit(solution)/shard_map/cross_forward/pallas_call | solution.py:738
  18.8 0.7 collective-permute-start.10
  19.7 0.9 act_grad.1
  20.6 1.6 %source_back.1 = (bf16[192,256]{1,0:T(8,128)(2,1)S(1)}, bf16[256,192]{1,0:T(8,128)(2,1)S(1)}, bf16[192,512]{1,0:T(8,128)(2,1)S(1)}, bf16[512,192]{1,0:T(8,128)(2...) custom-call(bf16[256,768]{1,0:T(8,128)(2,1)S(1)} %get-tuple-element.170.refs_0_, ...), custom_call_target="tpu_custom_call" | custom-call | tf_op jit(solution)/shard_map/source_back/pallas_call | solution.py:738
  22.3 2.7 %collective-permute-done.10.refs_1_ = bf16[128,768]{1,0:T(8,128)(2,1)S(1)} collective-permute-done((bf16[128,768]{1,0:T(8,128)(2,1)S(1)}, bf16[128,768]{1,0:T(8,128)(2,1)S(1)}, u32[]{:S(2)}, u32[]{:S(2)}) %collective-permute-start.10) | collective-permute-done | bytes 196640 | tf_op jit(solution)/shard_map/ppermute | solution.py:761
  25.0 1.6 %ffn.1 = (bf16[128,768]{1,0:T(8,128)(2,1)S(1)}, f32[128,768]{1,0:T(8,128)S(1)}, bf16[128,768]{1,0:T(8,128)(2,1)S(1)}, bf16[128,768]{1,0:T(8,128)(2,1)S(1)}, bf16...) custom-call(bf16[128,768]{1,0:T(8,128)(2,1)S(1)} %get-tuple-element.162.refs_0_, ...), custom_call_target="tpu_custom_call" | custom-call | tf_op jit(solution)/shard_map/ffn/pallas_call | solution.py:738
  26.7 0.6 collective-permute-start.14
  27.4 1.3 %collective-permute-done.15.refs_1_ = bf16[128,2304]{1,0:T(8,128)(2,1)S(1)} collective-permute-done((bf16[128,2304]{1,0:T(8,128)(2,1)S(1)}, bf16[128,2304]{1,0:T(8,128)(2,1)S(1)}, u32[]{:S(2)}, u32[]{:S(2)}) %collective-permute-start.15) | collective-permute-done | bytes 589856 | tf_op jit(solution)/shard_map/ppermute | solution.py:757
  28.7 1.0 %ffn_weights.1 = (bf16[4,96,768]{2,1,0:T(8,128)(2,1)S(1)}, bf16[4,96,768]{2,1,0:T(8,128)(2,1)S(1)}, bf16[4,96,768]{2,1,0:T(8,128)(2,1)S(1)}, bf16[4,96,768]{2,1,0:T(8,128)(2,1)S(1)}) custom-call(bf16[128,768]{1,0:T(8,128)(2,1)S(1)} %get-tuple-element.182.refs_0_, bf16[128,2304]{1,0:T(8,128)(2,1)S(1)} %collective-permute-done.15.refs_1_, ...), custom_call_target="tpu_custom_call" | custom-call | flops 5750000128 | tf_op jit(solution)/shard_map/ffn_weights/pallas_call | solution.py:738
  29.7 1.6 %collective-permute-start.20 = (bf16[4,96,768]{2,1,0:T(8,128)(2,1)S(1)}, bf16[4,96,768]{2,1,0:T(8,128)(2,1)S(1)}, u32[]{:S(2)}, u32[]{:S(2)}) collective-permute-start(bf16[4,96,768]{2,1,0:T(8,128)(2,1)S(1)} %get-tuple-element.206), channel_id=1, source_target_pairs={{0,4},{4,0},{8,12},{12,8},{16,20},{20,16},{24,28},{28,24},{1,5},{5... | collective-permute-start | bytes 1769480 | tf_op jit(solution)/shard_map/ppermute | solution.py:765
  31.3 1.6 %collective-permute-start.21 = (bf16[4,96,768]{2,1,0:T(8,128)(2,1)S(1)}, bf16[4,96,768]{2,1,0:T(8,128)(2,1)S(1)}, u32[]{:S(2)}, u32[]{:S(2)}) collective-permute-start(bf16[4,96,768]{2,1,0:T(8,128)(2,1)S(1)} %get-tuple-element.208), channel_id=1, source_target_pairs={{0,8},{4,12},{8,0},{12,4},{16,24},{20,28},{24,16},{28,20},{1,9},{5... | collective-permute-start | bytes 1769480 | tf_op jit(solution)/shard_map/ppermute | solution.py:765
  32.9 1.1 %collective-permute-done.14.refs_1_ = bf16[128,768]{1,0:T(8,128)(2,1)S(1)} collective-permute-done((bf16[128,768]{1,0:T(8,128)(2,1)S(1)}, bf16[128,768]{1,0:T(8,128)(2,1)S(1)}, u32[]{:S(2)}, u32[]{:S(2)}) %collective-permute-start.14) | collective-permute-done | bytes 196640 | tf_op jit(solution)/shard_map/ppermute | solution.py:761
  34.0 2.3 %cross_backward.1 = (bf16[128,768]{1,0:T(8,128)(2,1)S(1)}, f32[128,768]{1,0:T(8,128)S(1)}, f32[8,768]{1,0:T(8,128)S(1)}, bf16[512,384]{1,0:T(8,128)(2,1)S(1)}, b...) custom-call(bf16[128,768]{1,0:T(8,128)(2,1)S(1)} %get-tuple-element., ...), custom_call_target="tpu_custom_call" | custom-call | tf_op jit(solution)/shard_map/cross_backward/pallas_call | solution.py:738
  36.4 0.4 source_grad.1.refs_15_
  36.8 0.5 collective-permute-start.18
  37.3 0.6 collective-permute-start.16
  37.9 1.2 %collective-permute-done.18.refs_12_ = bf16[128,960]{1,0:T(8,128)(2,1)S(1)} collective-permute-done((bf16[128,960]{1,0:T(8,128)(2,1)S(1)}, bf16[128,960]{1,0:T(8,128)(2,1)S(1)}, u32[]{:S(2)}, u32[]{:S(2)}) %collective-permute-start.18) | collective-permute-done | bytes 245792 | tf_op jit(solution)/shard_map/ppermute | solution.py:757
  39.1 1.7 %cross_weights.1 = (bf16[4,96,384]{2,1,0:T(8,128)(2,1)S(1)}, bf16[4,96,384]{2,1,0:T(8,128)(2,1)S(1)}, bf16[4,96,384]{2,1,0:T(8,128)(2,1)S(1)}, bf16[4,96,384]{2,1,0:T(8,128)(2,1)S(1)}, bf16[512,384]{1,0:T(8,128)(2,1)S(1)}) custom-call(bf16[512,384]{1,0:T(8,128)(2,1)S(1)} %get-tuple-element.191.refs_0_, ...), custom_call_target="tpu_custom_call" | custom-call | tf_op jit(solution)/shard_map/cross_weights/pallas_call | solution.py:738
  40.8 1.6 %collective-permute-start.23 = (bf16[4,96,384]{2,1,0:T(8,128)(2,1)S(1)}, bf16[4,96,384]{2,1,0:T(8,128)(2,1)S(1)}, u32[]{:S(2)}, u32[]{:S(2)}) collective-permute-start(bf16[4,96,384]{2,1,0:T(8,128)(2,1)S(1)} %get-tuple-element.212), channel_id=1, source_target_pairs={{0,4},{4,0},{8,12},{12,8},{16,20},{20,16},{24,28},{28,24},{1,5},{5... | collective-permute-start | bytes 884744 | tf_op jit(solution)/shard_map/ppermute | solution.py:765
  42.4 1.6 %collective-permute-start.24 = (bf16[4,96,384]{2,1,0:T(8,128)(2,1)S(1)}, bf16[4,96,384]{2,1,0:T(8,128)(2,1)S(1)}, u32[]{:S(2)}, u32[]{:S(2)}) collective-permute-start(bf16[4,96,384]{2,1,0:T(8,128)(2,1)S(1)} %get-tuple-element.214), channel_id=1, source_target_pairs={{0,8},{4,12},{8,0},{12,4},{16,24},{20,28},{24,16},{28,20},{1,9},{5... | collective-permute-start | bytes 884744 | tf_op jit(solution)/shard_map/ppermute | solution.py:765
  44.0 0.5 ffn_out.1.refs_6_
  44.5 0.2 self_norm.1
  44.8 1.1 %collective-permute-done.20.refs_1_ = bf16[4,96,768]{2,1,0:T(8,128)(2,1)S(1)} collective-permute-done((bf16[4,96,768]{2,1,0:T(8,128)(2,1)S(1)}, bf16[4,96,768]{2,1,0:T(8,128)(2,1)S(1)}, u32[]{:S(2)}, u32[]{:S(2)}) %collective-permute-start.20) | collective-permute-done | bytes 589856 | tf_op jit(solution)/shard_map/ppermute | solution.py:765
  46.0 1.6 %collective-permute-done.21.refs_3_ = bf16[4,96,768]{2,1,0:T(8,128)(2,1)S(1)} collective-permute-done((bf16[4,96,768]{2,1,0:T(8,128)(2,1)S(1)}, bf16[4,96,768]{2,1,0:T(8,128)(2,1)S(1)}, u32[]{:S(2)}, u32[]{:S(2)}) %collective-permute-start.21) | collective-permute-done | bytes 589856 | tf_op jit(solution)/shard_map/ppermute | solution.py:765
  47.5 0.3 ffn_second.1
  47.8 1.8 %self_backward.1 = (bf16[144,768]{1,0:T(8,128)(2,1)S(1)}, bf16[144,768]{1,0:T(8,128)(2,1)S(1)}, bf16[256,768]{1,0:T(8,128)(2,1)S(1)}, bf16[256,192]{1,0:T(8,128)...) custom-call(bf16[144,768]{1,0:T(8,128)(2,1)S(1)} %get-tuple-element.202.refs_4_., ...), custom_call_target="tpu_custom_call" | custom-call | tf_op jit(solution)/shard_map/self_backward/pallas_call | solution.py:738
  49.7 1.6 %collective-permute-start.26 = (bf16[2,96,768]{2,1,0:T(8,128)(2,1)S(1)}, bf16[2,96,768]{2,1,0:T(8,128)(2,1)S(1)}, u32[]{:S(2)}, u32[]{:S(2)}) collective-permute-start(bf16[2,96,768]{2,1,0:T(8,128)(2,1)S(1)} %get-tuple-element.209.refs_11_), channel_id=1, source_target_pairs={{0,8},{4,12},{8,0},{12,4},{16,24},{20,28},{24,16},{28,20},{1,9},{5... | collective-permute-start | bytes 884744 | tf_op jit(solution)/shard_map/ppermute | solution.py:765
  51.4 0.5 collective-permute-start.27
  51.9 1.4 %self_weights.1 = (bf16[4,96,512]{2,1,0:T(8,128)(2,1)S(1)}, bf16[4,96,512]{2,1,0:T(8,128)(2,1)S(1)}, bf16[4,96,256]{2,1,0:T(8,128)(2,1)S(1)}, bf16[4,96,256]{2,1,0:T(8,128)(2,1)S(1)}, bf16[16,256]{1,0:T(8,128)(2,1)S(1)}) custom-call(bf16[256,768]{1,0:T(8,128)(2,1)S(1)} %get-tuple-element.170.refs_0_, bf16[256,768]{1,0:T(8,128)(2,1)S(1)} %get-tuple-element.215.refs_1_, ...), custom_call_target="tpu_custom_call" | custom-call | tf_op jit(solution)/shard_map/self_weights/pallas_call | solution.py:738
  53.3 0.2 round_three.1
  53.6 0.6 collective-permute-start.25
  54.2 1.0 %collective-permute-start.30 = (bf16[1376,128]{1,0:T(8,128)(2,1)S(1)}, bf16[1376,128]{1,0:T(8,128)(2,1)S(1)}, u32[]{:S(2)}, u32[]{:S(2)}) collective-permute-start(bf16[1376,128]{1,0:T(8,128)(2,1)S(1)} %get-tuple-element.233), channel_id=1, source_target_pairs={{0,8},{4,12},{8,0},{12,4},{16,24},{20,28},{24,16},{28,20},{1,9},{5... | collective-permute-start | bytes 1056776 | tf_op jit(solution)/shard_map/ppermute | solution.py:765
  55.2 0.9 %collective-permute-start.29 = (bf16[2112,128]{1,0:T(8,128)(2,1)S(1)}, bf16[2112,128]{1,0:T(8,128)(2,1)S(1)}, u32[]{:S(2)}, u32[]{:S(2)}) collective-permute-start(bf16[2112,128]{1,0:T(8,128)(2,1)S(1)} %get-tuple-element.232), channel_id=1, source_target_pairs={{0,4},{4,0},{8,12},{12,8},{16,20},{20,16},{24,28},{28,24},{1,5},{5... | collective-permute-start | bytes 1622024 | tf_op jit(solution)/shard_map/ppermute | solution.py:765
  56.2 5.0 %collective-permute-done.27.refs_3_ = bf16[2,96,768]{2,1,0:T(8,128)(2,1)S(1)} collective-permute-done((bf16[2,96,768]{2,1,0:T(8,128)(2,1)S(1)}, bf16[2,96,768]{2,1,0:T(8,128)(2,1)S(1)}, u32[]{:S(2)}, u32[]{:S(2)}) %collective-permute-start.27) | collective-permute-done | bytes 294944 | tf_op jit(solution)/shard_map/ppermute | solution.py:765
  61.4 2.6 %collective-permute-start.39 = (bf16[192,768]{1,0:T(8,128)(2,1)S(1)}, bf16[192,768]{1,0:T(8,128)(2,1)S(1)}, u32[]{:S(2)}, u32[]{:S(2)}) collective-permute-start(bf16[192,768]{1,0:T(8,128)(2,1)S(1)} %get-tuple-element.229.refs_2_), channel_id=1, source_target_pairs={{0,16},{4,20},{8,24},{12,28},{16,0},{20,4},{24,8},{28,12},{1,17},{... | collective-permute-start | bytes 884744 | tf_op jit(solution)/shard_map/ppermute | solution.py:765
  64.0 0.6 collective-permute-start.28
  64.6 0.5 collective-permute-start.31
  65.1 6.8 %collective-permute-done.30.zo_got = bf16[1376,128]{1,0:T(8,128)(2,1)S(1)} collective-permute-done((bf16[1376,128]{1,0:T(8,128)(2,1)S(1)}, bf16[1376,128]{1,0:T(8,128)(2,1)S(1)}, u32[]{:S(2)}, u32[]{:S(2)}) %collective-permute-start.30) | collective-permute-done | bytes 352288 | tf_op jit(solution)/shard_map/ppermute | solution.py:765
  71.9 0.2 collective-permute-done.31.gains_got
  72.4 0.6 collective-permute-start.34
  73.0 0.4 collective-permute-start.33
  73.4 0.6 encoded.1
  74.2 2.7 %collective-permute-start.38 = (bf16[576,128]{1,0:T(8,128)(2,1)S(1)}, bf16[576,128]{1,0:T(8,128)(2,1)S(1)}, u32[]{:S(2)}, u32[]{:S(2)}) collective-permute-start(bf16[576,128]{1,0:T(8,128)(2,1)S(1)} %get-tuple-element.260), channel_id=1, source_target_pairs={{0,16},{4,20},{8,24},{12,28},{16,0},{20,4},{24,8},{28,12},{1,17},{... | collective-permute-start | bytes 442376 | tf_op jit(solution)/shard_map/ppermute | solution.py:765
  76.8 0.3 input_grad.1.refs_2_.refs_0_
  77.4 0.8 ffn_final.1
  78.3 5.2 %collective-permute-done.33.refs_1_ = bf16[208,512]{1,0:T(8,128)(2,1)S(1)} collective-permute-done((bf16[208,512]{1,0:T(8,128)(2,1)S(1)}, bf16[208,512]{1,0:T(8,128)(2,1)S(1)}, u32[]{:S(2)}, u32[]{:S(2)}) %collective-permute-start.33) | collective-permute-done | bytes 213024 | tf_op jit(solution)/shard_map/ppermute | solution.py:765
  83.7 0.4 collective-permute-start.37
  84.1 2.1 %collective-permute-done.38.refs_1_ = bf16[576,128]{1,0:T(8,128)(2,1)S(1)} collective-permute-done((bf16[576,128]{1,0:T(8,128)(2,1)S(1)}, bf16[576,128]{1,0:T(8,128)(2,1)S(1)}, u32[]{:S(2)}, u32[]{:S(2)}) %collective-permute-start.38) | collective-permute-done | bytes 147488 | tf_op jit(solution)/shard_map/ppermute | solution.py:765
  86.2 0.8 cross_final.1
  87.0 0.9 %rows.1 = (bf16[256,768]{1,0:T(8,128)(2,1)}, bf16[256,768]{1,0:T(8,128)(2,1)}, bf16[16,128]{1,0:T(8,128)(2,1)S(1)}) custom-call(bf16[256,768]{1,0:T(8,128)(2,1)S(1)} %input_grad.1.refs_2_.refs_0_, bf16[256,768]{1,0:T(8,128)(2,1)S(1)} %collective-permute-done.32.refs_1_, bf16[608,128]{1,0:T(8,128)(2,1)S(1)} %get-tuple-element.244.refs_2_), custom_call_target="tpu_custom_call" | custom-call | tf_op jit(solution)/shard_map/rows/pallas_call | solution.py:738
  88.0 3.2 %collective-permute-done.36.refs_1_ = bf16[608,128]{1,0:T(8,128)(2,1)S(1)} collective-permute-done((bf16[608,128]{1,0:T(8,128)(2,1)S(1)}, bf16[608,128]{1,0:T(8,128)(2,1)S(1)}, u32[]{:S(2)}, u32[]{:S(2)}) %collective-permute-start.36) | collective-permute-done | bytes 155680 | tf_op jit(solution)/shard_map/ppermute | solution.py:765
  91.2 1.0 %self_final.1 = (bf16[128,768]{1,0:T(8,128)(2,1)}, f32[96,192]{1,0:T(8,128)}, f32[96,192]{1,0:T(8,128)}, f32[96,192]{1,0:T(8,128)}, f32[192,96]{1,0:T(8,128)}, /...) custom-call(bf16[608,128]{1,0:T(8,128)(2,1)S(1)} %get-tuple-element.247.refs_0_, ...), custom_call_target="tpu_custom_call" | custom-call | tf_op jit(solution)/shard_map/self_final/pallas_call | solution.py:738
  (87 shorter events, 2.2 us)
Async XLA Ops:
  0.7 3.2 %copy-start = (bf16[768,192]{0,1:T(8,128)(2,1)S(1)}, bf16[768,192]{0,1:T(8,128)(2,1)}, u32[]{:S(2)}) copy-start(bf16[768,192]{0,1:T(8,128)(2,1)} %param.40) | copy-start | bytes 884740
  0.7 3.4 %copy-start.1 = (bf16[768,192]{0,1:T(8,128)(2,1)S(1)}, bf16[768,192]{0,1:T(8,128)(2,1)}, u32[]{:S(2)}) copy-start(bf16[768,192]{0,1:T(8,128)(2,1)} %param.41) | copy-start | bytes 884740
  0.7 4.4 %copy-start.3 = (bf16[1,256,768]{2,1,0:T(8,128)(2,1)S(1)}, bf16[1,256,768]{2,1,0:T(8,128)(2,1)}, u32[]{:S(2)}) copy-start(bf16[1,256,768]{2,1,0:T(8,128)(2,1)} %param.23) | copy-start | bytes 1179652
  0.7 4.4 %copy-start.5 = (bf16[768,192]{0,1:T(8,128)(2,1)S(1)}, bf16[768,192]{0,1:T(8,128)(2,1)}, u32[]{:S(2)}) copy-start(bf16[768,192]{0,1:T(8,128)(2,1)} %param.34) | copy-start | bytes 884740
  0.7 4.4 %copy-start.6 = (bf16[768,192]{0,1:T(8,128)(2,1)S(1)}, bf16[768,192]{0,1:T(8,128)(2,1)}, u32[]{:S(2)}) copy-start(bf16[768,192]{0,1:T(8,128)(2,1)} %param.35) | copy-start | bytes 884740
  0.7 4.4 %copy-start.10 = (bf16[768,192]{0,1:T(8,128)(2,1)S(1)}, bf16[768,192]{0,1:T(8,128)(2,1)}, u32[]{:S(2)}) copy-start(bf16[768,192]{0,1:T(8,128)(2,1)} %param.33) | copy-start | bytes 884740
  0.7 4.4 %copy-start.11 = (bf16[192,768]{1,0:T(8,128)(2,1)S(1)}, bf16[192,768]{1,0:T(8,128)(2,1)}, u32[]{:S(2)}) copy-start(bf16[192,768]{1,0:T(8,128)(2,1)} %refs_2_.5) | copy-start | bytes 884740
  0.7 4.4 %copy-start.14 = (f32[768]{0:T(1024)S(1)}, f32[768]{0:T(1024)}, u32[]{:S(2)}) copy-start(f32[768]{0:T(1024)} %refs_3_.7) | copy-start | bytes 9220
  0.7 4.4 %copy-start.15 = (s32[256]{0:T(256)S(1)}, s32[256]{0:T(256)}, u32[]{:S(2)}) copy-start(s32[256]{0:T(256)} %param.29) | copy-start | bytes 3076
  0.7 4.4 %copy-start.18 = (f32[32,3]{0,1:T(4,128)S(1)}, f32[32,3]{0,1:T(4,128)}, u32[]{:S(2)}) copy-start(f32[32,3]{0,1:T(4,128)} %param.37) | copy-start | bytes 1156
  0.8 6.2 %collective-permute-start.4 = (bf16[128,768]{1,0:T(8,128)(2,1)}, bf16[128,768]{1,0:T(8,128)(2,1)S(1)}, u32[]{:S(2)}, u32[]{:S(2)}) collective-permute-start(bf16[128,768]{1,0:T(8,128)(2,1)} %bitcast.33), channel_id=1, source_target_pairs={{0,1},{1,0},{2,3},{3,2},{4,5},{5,4},{6,7},{7,6},{8,9},{9,8},{10,11... | collective-permute-start | bytes 589832 | tf_op jit(solution)/shard_map/ppermute | solution.py:757
  1.3 8.3 %collective-permute-start = (bf16[128,768]{1,0:T(8,128)(2,1)}, bf16[128,768]{1,0:T(8,128)(2,1)S(1)}, u32[]{:S(2)}, u32[]{:S(2)}) collective-permute-start(bf16[128,768]{1,0:T(8,128)(2,1)} %bitcast.34), channel_id=1, source_target_pairs={{0,2},{1,3},{2,0},{3,1},{4,6},{5,7},{6,4},{7,5},{8,10},{9,11},{10,... | collective-permute-start | bytes 589832 | tf_op jit(solution)/shard_map/ppermute | solution.py:761
  3.9 3.4 %collective-permute-start.2 = (bf16[192,768]{1,0:T(8,128)(2,1)S(1)}, bf16[192,768]{1,0:T(8,128)(2,1)S(1)}, u32[]{:S(2)}, u32[]{:S(2)}) collective-permute-start(bf16[192,768]{1,0:T(8,128)(2,1)S(1)} %bitcast.19), channel_id=1, source_target_pairs={{0,1},{1,0},{2,3},{3,2},{4,5},{5,4},{6,7},{7,6},{8,9},{9,8},{10,11... | collective-permute-start | bytes 884744 | tf_op jit(solution)/shard_map/ppermute | solution.py:757
  4.0 3.4 %collective-permute-start.3 = (bf16[192,768]{1,0:T(8,128)(2,1)S(1)}, bf16[192,768]{1,0:T(8,128)(2,1)S(1)}, u32[]{:S(2)}, u32[]{:S(2)}) collective-permute-start(bf16[192,768]{1,0:T(8,128)(2,1)S(1)} %bitcast.24), channel_id=1, source_target_pairs={{0,1},{1,0},{2,3},{3,2},{4,5},{5,4},{6,7},{7,6},{8,9},{9,8},{10,11... | collective-permute-start | bytes 884744 | tf_op jit(solution)/shard_map/ppermute | solution.py:757
  5.1 2.2 %copy-start.8 = (bf16[768,192]{0,1:T(8,128)(2,1)S(1)}, bf16[768,192]{0,1:T(8,128)(2,1)}, u32[]{:S(2)}) copy-start(bf16[768,192]{0,1:T(8,128)(2,1)} %param.39) | copy-start | bytes 884740
  5.1 2.3 %copy-start.9 = (bf16[192,768]{1,0:T(8,128)(2,1)S(1)}, bf16[192,768]{1,0:T(8,128)(2,1)}, u32[]{:S(2)}) copy-start(bf16[192,768]{1,0:T(8,128)(2,1)} %refs_5_.1) | copy-start | bytes 884740
  5.1 2.7 %copy-start.4 = (bf16[1,128,768]{2,1,0:T(8,128)(2,1)S(1)}, bf16[1,128,768]{2,1,0:T(8,128)(2,1)}, u32[]{:S(2)}) copy-start(bf16[1,128,768]{2,1,0:T(8,128)(2,1)} %param.24) | copy-start | bytes 589828
  6.7 1.9 %collective-permute-start.5 = (bf16[64,768]{1,0:T(8,128)(2,1)S(1)}, bf16[64,768]{1,0:T(8,128)(2,1)S(1)}, u32[]{:S(2)}, u32[]{:S(2)}) collective-permute-start(bf16[64,768]{1,0:T(8,128)(2,1)S(1)} %get-tuple-element.151), channel_id=1, source_target_pairs={{0,1},{1,0},{2,3},{3,2},{4,5},{5,4},{6,7},{7,6},{8,9},{9,8},{10,11... | collective-permute-start | bytes 294920 | tf_op jit(solution)/shard_map/ppermute | solution.py:757
  7.0 1.7 %collective-permute-start.6 = (bf16[64,768]{1,0:T(8,128)(2,1)S(1)}, bf16[64,768]{1,0:T(8,128)(2,1)S(1)}, u32[]{:S(2)}, u32[]{:S(2)}) collective-permute-start(bf16[64,768]{1,0:T(8,128)(2,1)S(1)} %get-tuple-element.152), channel_id=1, source_target_pairs={{0,1},{1,0},{2,3},{3,2},{4,5},{5,4},{6,7},{7,6},{8,9},{9,8},{10,11... | collective-permute-start | bytes 294920 | tf_op jit(solution)/shard_map/ppermute | solution.py:757
  7.3 5.8 %collective-permute-start.8 = (bf16[192,768]{1,0:T(8,128)(2,1)S(1)}, bf16[192,768]{1,0:T(8,128)(2,1)S(1)}, u32[]{:S(2)}, u32[]{:S(2)}) collective-permute-start(bf16[192,768]{1,0:T(8,128)(2,1)S(1)} %bitcast.44), channel_id=1, source_target_pairs={{0,1},{1,0},{2,3},{3,2},{4,5},{5,4},{6,7},{7,6},{8,9},{9,8},{10,11... | collective-permute-start | bytes 884744 | tf_op jit(solution)/shard_map/ppermute | solution.py:757
  7.5 5.7 %collective-permute-start.9 = (bf16[192,768]{1,0:T(8,128)(2,1)S(1)}, bf16[192,768]{1,0:T(8,128)(2,1)S(1)}, u32[]{:S(2)}, u32[]{:S(2)}) collective-permute-start(bf16[192,768]{1,0:T(8,128)(2,1)S(1)} %copy-done.9), channel_id=1, source_target_pairs={{0,1},{1,0},{2,3},{3,2},{4,5},{5,4},{6,7},{7,6},{8,9},{9,8},{10,11... | collective-permute-start | bytes 884744 | tf_op jit(solution)/shard_map/ppermute | solution.py:757
  8.7 3.7 %copy-start.7 = (bf16[768,768]{1,0:T(8,128)(2,1)S(1)}, bf16[768,768]{1,0:T(8,128)(2,1)}, u32[]{:S(2)}) copy-start(bf16[768,768]{1,0:T(8,128)(2,1)} %refs_4_.5) | copy-start | bytes 3538948
  8.7 4.2 %copy-start.2 = (bf16[768,768]{1,0:T(8,128)(2,1)S(1)}, bf16[768,768]{1,0:T(8,128)(2,1)}, u32[]{:S(2)}) copy-start(bf16[768,768]{1,0:T(8,128)(2,1)} %refs_2_.4) | copy-start | bytes 3538948
  8.8 7.6 %collective-permute-start.7 = (bf16[144,768]{1,0:T(8,128)(2,1)S(1)}, bf16[144,768]{1,0:T(8,128)(2,1)S(1)}, u32[]{:S(2)}, u32[]{:S(2)}) collective-permute-start(bf16[144,768]{1,0:T(8,128)(2,1)S(1)} %self_sum.1.refs_10_.refs_1_), channel_id=1, source_target_pairs={{0,2},{1,3},{2,0},{3,1},{4,6},{5,7},{6,4},{7,5},{8,10},{9,11},{10,... | collective-permute-start | bytes 663560 | tf_op jit(solution)/shard_map/ppermute | solution.py:761
  9.6 2.0 %collective-permute-start.1 = (bf16[128,768]{1,0:T(8,128)(2,1)S(1)}, bf16[128,768]{1,0:T(8,128)(2,1)S(1)}, u32[]{:S(2)}, u32[]{:S(2)}) collective-permute-start(bf16[128,768]{1,0:T(8,128)(2,1)S(1)} %collective-permute-done.refs_0_.refs_4_.refs_6_), channel_id=1, source_target_pairs={{0,1},{1,0},{2,3},{3,2},{4,5},{5,4},{6,7},{7,6},{8,9},{9,8},{10,11... | collective-permute-start | bytes 589832 | tf_op jit(solution)/shard_map/ppermute | solution.py:757
  11.5 4.8 %copy-start.12 = (f32[768]{0:T(1024)S(1)}, f32[768]{0:T(1024)}, u32[]{:S(2)}) copy-start(f32[768]{0:T(1024)} %refs_3_.6) | copy-start | bytes 9220
  12.4 12.6 %collective-permute-start.11 = (bf16[768,768]{1,0:T(8,128)(2,1)S(1)}, bf16[768,768]{1,0:T(8,128)(2,1)S(1)}, u32[]{:S(2)}, u32[]{:S(2)}) collective-permute-start(bf16[768,768]{1,0:T(8,128)(2,1)S(1)} %copy-done.7), channel_id=1, source_target_pairs={{0,1},{1,0},{2,3},{3,2},{4,5},{5,4},{6,7},{7,6},{8,9},{9,8},{10,11... | collective-permute-start | bytes 3538952 | tf_op jit(solution)/shard_map/ppermute | solution.py:757
  13.0 6.7 %collective-permute-start.12 = (bf16[768,768]{1,0:T(8,128)(2,1)S(1)}, bf16[768,768]{1,0:T(8,128)(2,1)S(1)}, u32[]{:S(2)}, u32[]{:S(2)}) collective-permute-start(bf16[768,768]{1,0:T(8,128)(2,1)S(1)} %copy-done.2), channel_id=1, source_target_pairs={{0,1},{1,0},{2,3},{3,2},{4,5},{5,4},{6,7},{7,6},{8,9},{9,8},{10,11... | collective-permute-start | bytes 3538952 | tf_op jit(solution)/shard_map/ppermute | solution.py:757
  16.3 3.2 %copy-start.16 = (bf16[1,256,768]{2,1,0:T(8,128)(2,1)S(1)}, bf16[1,256,768]{2,1,0:T(8,128)(2,1)}, u32[]{:S(2)}) copy-start(bf16[1,256,768]{2,1,0:T(8,128)(2,1)} %param.31) | copy-start | bytes 1179652
  16.3 3.2 %copy-start.17 = (f32[16,256]{1,0:T(8,128)S(1)}, f32[16,256]{1,0:T(8,128)}, u32[]{:S(2)}) copy-start(f32[16,256]{1,0:T(8,128)} %refs_2_.3) | copy-start | bytes 49156
  18.8 6.2 %collective-permute-start.10 = (bf16[128,768]{1,0:T(8,128)(2,1)S(1)}, bf16[128,768]{1,0:T(8,128)(2,1)S(1)}, u32[]{:S(2)}, u32[]{:S(2)}) collective-permute-start(bf16[128,768]{1,0:T(8,128)(2,1)S(1)} %get-tuple-element.162.refs_0_), channel_id=1, source_target_pairs={{0,2},{1,3},{2,0},{3,1},{4,6},{5,7},{6,4},{7,5},{8,10},{9,11},{10,... | collective-permute-start | bytes 589832 | tf_op jit(solution)/shard_map/ppermute | solution.py:761
  19.5 5.5 %collective-permute-start.13 = (bf16[128,960]{1,0:T(8,128)(2,1)S(1)}, bf16[128,960]{1,0:T(8,128)(2,1)S(1)}, u32[]{:S(2)}, u32[]{:S(2)}) collective-permute-start(bf16[128,960]{1,0:T(8,128)(2,1)S(1)} %get-tuple-element.172), channel_id=1, source_target_pairs={{0,1},{1,0},{2,3},{3,2},{4,5},{5,4},{6,7},{7,6},{8,9},{9,8},{10,11... | collective-permute-start | bytes 737288 | tf_op jit(solution)/shard_map/ppermute | solution.py:757
  20.6 4.4 %copy-start.13 = (f32[768]{0:T(1024)S(1)}, f32[768]{0:T(1024)}, u32[]{:S(2)}) copy-start(f32[768]{0:T(1024)} %refs_3_.5) | copy-start | bytes 9220
  26.6 2.1 %collective-permute-start.15 = (bf16[128,2304]{1,0:T(8,128)(2,1)S(1)}, bf16[128,2304]{1,0:T(8,128)(2,1)S(1)}, u32[]{:S(2)}, u32[]{:S(2)}) collective-permute-start(bf16[128,2304]{1,0:T(8,128)(2,1)S(1)} %get-tuple-element.183.refs_1_), channel_id=1, source_target_pairs={{0,1},{1,0},{2,3},{3,2},{4,5},{5,4},{6,7},{7,6},{8,9},{9,8},{10,11... | collective-permute-start | bytes 1769480 | tf_op jit(solution)/shard_map/ppermute | solution.py:757
  26.7 7.3 %collective-permute-start.14 = (bf16[128,768]{1,0:T(8,128)(2,1)S(1)}, bf16[128,768]{1,0:T(8,128)(2,1)S(1)}, u32[]{:S(2)}, u32[]{:S(2)}) collective-permute-start(bf16[128,768]{1,0:T(8,128)(2,1)S(1)} %get-tuple-element.173.refs_6_.refs_0_), channel_id=1, source_target_pairs={{0,2},{1,3},{2,0},{3,1},{4,6},{5,7},{6,4},{7,5},{8,10},{9,11},{10,... | collective-permute-start | bytes 589832 | tf_op jit(solution)/shard_map/ppermute | solution.py:761
  29.7 16.2 %collective-permute-start.20 = (bf16[4,96,768]{2,1,0:T(8,128)(2,1)S(1)}, bf16[4,96,768]{2,1,0:T(8,128)(2,1)S(1)}, u32[]{:S(2)}, u32[]{:S(2)}) collective-permute-start(bf16[4,96,768]{2,1,0:T(8,128)(2,1)S(1)} %get-tuple-element.206), channel_id=1, source_target_pairs={{0,4},{4,0},{8,12},{12,8},{16,20},{20,16},{24,28},{28,24},{1,5},{5... | collective-permute-start | bytes 1769480 | tf_op jit(solution)/shard_map/ppermute | solution.py:765
  31.3 16.2 %collective-permute-start.21 = (bf16[4,96,768]{2,1,0:T(8,128)(2,1)S(1)}, bf16[4,96,768]{2,1,0:T(8,128)(2,1)S(1)}, u32[]{:S(2)}, u32[]{:S(2)}) collective-permute-start(bf16[4,96,768]{2,1,0:T(8,128)(2,1)S(1)} %get-tuple-element.208), channel_id=1, source_target_pairs={{0,8},{4,12},{8,0},{12,4},{16,24},{20,28},{24,16},{28,20},{1,9},{5... | collective-permute-start | bytes 1769480 | tf_op jit(solution)/shard_map/ppermute | solution.py:765
  36.8 2.4 %collective-permute-start.17 = (bf16[1024,192]{1,0:T(8,128)(2,1)S(1)}, bf16[1024,192]{1,0:T(8,128)(2,1)S(1)}, u32[]{:S(2)}, u32[]{:S(2)}) collective-permute-start(bf16[1024,192]{1,0:T(8,128)(2,1)S(1)} %source_grad.1.refs_15_), channel_id=1, source_target_pairs={{0,1},{1,0},{2,3},{3,2},{4,5},{5,4},{6,7},{7,6},{8,9},{9,8},{10,11... | collective-permute-start | bytes 1179656 | tf_op jit(solution)/shard_map/ppermute | solution.py:757
  36.8 2.3 %collective-permute-start.18 = (bf16[128,960]{1,0:T(8,128)(2,1)S(1)}, bf16[128,960]{1,0:T(8,128)(2,1)S(1)}, u32[]{:S(2)}, u32[]{:S(2)}) collective-permute-start(bf16[128,960]{1,0:T(8,128)(2,1)S(1)} %get-tuple-element.198), channel_id=1, source_target_pairs={{0,1},{1,0},{2,3},{3,2},{4,5},{5,4},{6,7},{7,6},{8,9},{9,8},{10,11... | collective-permute-start | bytes 737288 | tf_op jit(solution)/shard_map/ppermute | solution.py:757
  37.3 7.2 %collective-permute-start.16 = (bf16[128,768]{1,0:T(8,128)(2,1)S(1)}, bf16[128,768]{1,0:T(8,128)(2,1)S(1)}, u32[]{:S(2)}, u32[]{:S(2)}) collective-permute-start(bf16[128,768]{1,0:T(8,128)(2,1)S(1)} %get-tuple-element.188.refs_0_), channel_id=1, source_target_pairs={{0,2},{1,3},{2,0},{3,1},{4,6},{5,7},{6,4},{7,5},{8,10},{9,11},{10,... | collective-permute-start | bytes 589832 | tf_op jit(solution)/shard_map/ppermute | solution.py:761
  40.8 12.4 %collective-permute-start.23 = (bf16[4,96,384]{2,1,0:T(8,128)(2,1)S(1)}, bf16[4,96,384]{2,1,0:T(8,128)(2,1)S(1)}, u32[]{:S(2)}, u32[]{:S(2)}) collective-permute-start(bf16[4,96,384]{2,1,0:T(8,128)(2,1)S(1)} %get-tuple-element.212), channel_id=1, source_target_pairs={{0,4},{4,0},{8,12},{12,8},{16,20},{20,16},{24,28},{28,24},{1,5},{5... | collective-permute-start | bytes 884744 | tf_op jit(solution)/shard_map/ppermute | solution.py:765
  42.4 10.8 %collective-permute-start.24 = (bf16[4,96,384]{2,1,0:T(8,128)(2,1)S(1)}, bf16[4,96,384]{2,1,0:T(8,128)(2,1)S(1)}, u32[]{:S(2)}, u32[]{:S(2)}) collective-permute-start(bf16[4,96,384]{2,1,0:T(8,128)(2,1)S(1)} %get-tuple-element.214), channel_id=1, source_target_pairs={{0,8},{4,12},{8,0},{12,4},{16,24},{20,28},{24,16},{28,20},{1,9},{5... | collective-permute-start | bytes 884744 | tf_op jit(solution)/shard_map/ppermute | solution.py:765
  44.7 3.1 %collective-permute-start.19 = (bf16[144,768]{1,0:T(8,128)(2,1)S(1)}, bf16[144,768]{1,0:T(8,128)(2,1)S(1)}, u32[]{:S(2)}, u32[]{:S(2)}) collective-permute-start(bf16[144,768]{1,0:T(8,128)(2,1)S(1)} %get-tuple-element.202.refs_4_.refs_0_.refs_8_), channel_id=1, source_target_pairs={{0,1},{1,0},{2,3},{3,2},{4,5},{5,4},{6,7},{7,6},{8,9},{9,8},{10,11... | collective-permute-start | bytes 663560 | tf_op jit(solution)/shard_map/ppermute | solution.py:757
  49.6 3.9 %collective-permute-start.22 = (bf16[144,768]{1,0:T(8,128)(2,1)S(1)}, bf16[144,768]{1,0:T(8,128)(2,1)S(1)}, u32[]{:S(2)}, u32[]{:S(2)}) collective-permute-start(bf16[144,768]{1,0:T(8,128)(2,1)S(1)} %get-tuple-element.211), channel_id=1, source_target_pairs={{0,1},{1,0},{2,3},{3,2},{4,5},{5,4},{6,7},{7,6},{8,9},{9,8},{10,11... | collective-permute-start | bytes 663560 | tf_op jit(solution)/shard_map/ppermute | solution.py:757
  49.7 11.5 %collective-permute-start.26 = (bf16[2,96,768]{2,1,0:T(8,128)(2,1)S(1)}, bf16[2,96,768]{2,1,0:T(8,128)(2,1)S(1)}, u32[]{:S(2)}, u32[]{:S(2)}) collective-permute-start(bf16[2,96,768]{2,1,0:T(8,128)(2,1)S(1)} %get-tuple-element.209.refs_11_), channel_id=1, source_target_pairs={{0,8},{4,12},{8,0},{12,4},{16,24},{20,28},{24,16},{28,20},{1,9},{5... | collective-permute-start | bytes 884744 | tf_op jit(solution)/shard_map/ppermute | solution.py:765
  51.4 9.9 %collective-permute-start.27 = (bf16[2,96,768]{2,1,0:T(8,128)(2,1)S(1)}, bf16[2,96,768]{2,1,0:T(8,128)(2,1)S(1)}, u32[]{:S(2)}, u32[]{:S(2)}) collective-permute-start(bf16[2,96,768]{2,1,0:T(8,128)(2,1)S(1)} %get-tuple-element.228), channel_id=1, source_target_pairs={{0,4},{4,0},{8,12},{12,8},{16,20},{20,16},{24,28},{28,24},{1,5},{5... | collective-permute-start | bytes 884744 | tf_op jit(solution)/shard_map/ppermute | solution.py:765
  53.6 10.4 %collective-permute-start.25 = (bf16[144,768]{1,0:T(8,128)(2,1)S(1)}, bf16[144,768]{1,0:T(8,128)(2,1)S(1)}, u32[]{:S(2)}, u32[]{:S(2)}) collective-permute-start(bf16[144,768]{1,0:T(8,128)(2,1)S(1)} %input_sum.1.refs_4_.refs_0_), channel_id=1, source_target_pairs={{0,2},{1,3},{2,0},{3,1},{4,6},{5,7},{6,4},{7,5},{8,10},{9,11},{10,... | collective-permute-start | bytes 663560 | tf_op jit(solution)/shard_map/ppermute | solution.py:761
  54.2 17.8 %collective-permute-start.30 = (bf16[1376,128]{1,0:T(8,128)(2,1)S(1)}, bf16[1376,128]{1,0:T(8,128)(2,1)S(1)}, u32[]{:S(2)}, u32[]{:S(2)}) collective-permute-start(bf16[1376,128]{1,0:T(8,128)(2,1)S(1)} %get-tuple-element.233), channel_id=1, source_target_pairs={{0,8},{4,12},{8,0},{12,4},{16,24},{20,28},{24,16},{28,20},{1,9},{5... | collective-permute-start | bytes 1056776 | tf_op jit(solution)/shard_map/ppermute | solution.py:765
  55.2 17.0 %collective-permute-start.29 = (bf16[2112,128]{1,0:T(8,128)(2,1)S(1)}, bf16[2112,128]{1,0:T(8,128)(2,1)S(1)}, u32[]{:S(2)}, u32[]{:S(2)}) collective-permute-start(bf16[2112,128]{1,0:T(8,128)(2,1)S(1)} %get-tuple-element.232), channel_id=1, source_target_pairs={{0,4},{4,0},{8,12},{12,8},{16,20},{20,16},{24,28},{28,24},{1,5},{5... | collective-permute-start | bytes 1622024 | tf_op jit(solution)/shard_map/ppermute | solution.py:765
  61.4 15.8 %collective-permute-start.39 = (bf16[192,768]{1,0:T(8,128)(2,1)S(1)}, bf16[192,768]{1,0:T(8,128)(2,1)S(1)}, u32[]{:S(2)}, u32[]{:S(2)}) collective-permute-start(bf16[192,768]{1,0:T(8,128)(2,1)S(1)} %get-tuple-element.229.refs_2_), channel_id=1, source_target_pairs={{0,16},{4,20},{8,24},{12,28},{16,0},{20,4},{24,8},{28,12},{1,17},{... | collective-permute-start | bytes 884744 | tf_op jit(solution)/shard_map/ppermute | solution.py:765
  64.0 10.1 %collective-permute-start.28 = (bf16[128,768]{1,0:T(8,128)(2,1)S(1)}, bf16[128,768]{1,0:T(8,128)(2,1)S(1)}, u32[]{:S(2)}, u32[]{:S(2)}) collective-permute-start(bf16[128,768]{1,0:T(8,128)(2,1)S(1)} %ffn_out.1.refs_6_), channel_id=1, source_target_pairs={{0,2},{1,3},{2,0},{3,1},{4,6},{5,7},{6,4},{7,5},{8,10},{9,11},{10,... | collective-permute-start | bytes 589832 | tf_op jit(solution)/shard_map/ppermute | solution.py:761
  64.6 7.6 %collective-permute-start.31 = (bf16[16,256]{1,0:T(8,128)(2,1)S(1)}, bf16[16,256]{1,0:T(8,128)(2,1)S(1)}, u32[]{:S(2)}, u32[]{:S(2)}) collective-permute-start(bf16[16,256]{1,0:T(8,128)(2,1)S(1)} %gain.1.gains), channel_id=1, source_target_pairs={{0,4},{4,0},{8,12},{12,8},{16,20},{20,16},{24,28},{28,24},{1,5},{5... | collective-permute-start | bytes 24584 | tf_op jit(solution)/shard_map/ppermute | solution.py:765
  72.4 5.9 %collective-permute-start.34 = (bf16[208,256]{1,0:T(8,128)(2,1)S(1)}, bf16[208,256]{1,0:T(8,128)(2,1)S(1)}, u32[]{:S(2)}, u32[]{:S(2)}) collective-permute-start(bf16[208,256]{1,0:T(8,128)(2,1)S(1)} %get-tuple-element.237.refs_3_), channel_id=1, source_target_pairs={{0,4},{4,0},{8,12},{12,8},{16,20},{20,16},{24,28},{28,24},{1,5},{5... | collective-permute-start | bytes 319496 | tf_op jit(solution)/shard_map/ppermute | solution.py:765
  73.0 10.5 %collective-permute-start.33 = (bf16[208,512]{1,0:T(8,128)(2,1)S(1)}, bf16[208,512]{1,0:T(8,128)(2,1)S(1)}, u32[]{:S(2)}, u32[]{:S(2)}) collective-permute-start(bf16[208,512]{1,0:T(8,128)(2,1)S(1)} %get-tuple-element.240), channel_id=1, source_target_pairs={{0,8},{4,12},{8,0},{12,4},{16,24},{20,28},{24,16},{28,20},{1,9},{5... | collective-permute-start | bytes 638984 | tf_op jit(solution)/shard_map/ppermute | solution.py:765
  74.1 4.1 %collective-permute-start.35 = (bf16[256,768]{1,0:T(8,128)(2,1)S(1)}, bf16[256,768]{1,0:T(8,128)(2,1)S(1)}, u32[]{:S(2)}, u32[]{:S(2)}) collective-permute-start(bf16[256,768]{1,0:T(8,128)(2,1)S(1)} %get-tuple-element.242), channel_id=1, source_target_pairs={{0,1},{1,0},{2,3},{3,2},{4,5},{5,4},{6,7},{7,6},{8,9},{9,8},{10,11... | collective-permute-start | bytes 1179656 | tf_op jit(solution)/shard_map/ppermute | solution.py:757
  74.2 12.0 %collective-permute-start.38 = (bf16[576,128]{1,0:T(8,128)(2,1)S(1)}, bf16[576,128]{1,0:T(8,128)(2,1)S(1)}, u32[]{:S(2)}, u32[]{:S(2)}) collective-permute-start(bf16[576,128]{1,0:T(8,128)(2,1)S(1)} %get-tuple-element.260), channel_id=1, source_target_pairs={{0,16},{4,20},{8,24},{12,28},{16,0},{20,4},{24,8},{28,12},{1,17},{... | collective-permute-start | bytes 442376 | tf_op jit(solution)/shard_map/ppermute | solution.py:765
  77.1 9.9 %collective-permute-start.32 = (bf16[256,768]{1,0:T(8,128)(2,1)S(1)}, bf16[256,768]{1,0:T(8,128)(2,1)S(1)}, u32[]{:S(2)}, u32[]{:S(2)}) collective-permute-start(bf16[256,768]{1,0:T(8,128)(2,1)S(1)} %input_grad.1.refs_2_.refs_0_), channel_id=1, source_target_pairs={{0,1},{1,0},{2,3},{3,2},{4,5},{5,4},{6,7},{7,6},{8,9},{9,8},{10,11... | collective-permute-start | bytes 1179656 | tf_op jit(solution)/shard_map/ppermute | solution.py:757
  83.6 7.6 %collective-permute-start.36 = (bf16[608,128]{1,0:T(8,128)(2,1)S(1)}, bf16[608,128]{1,0:T(8,128)(2,1)S(1)}, u32[]{:S(2)}, u32[]{:S(2)}) collective-permute-start(bf16[608,128]{1,0:T(8,128)(2,1)S(1)} %get-tuple-element.244.refs_2_), channel_id=1, source_target_pairs={{0,16},{4,20},{8,24},{12,28},{16,0},{20,4},{24,8},{28,12},{1,17},{... | collective-permute-start | bytes 466952 | tf_op jit(solution)/shard_map/ppermute | solution.py:765
  83.7 7.5 %collective-permute-start.37 = (bf16[128,768]{1,0:T(8,128)(2,1)S(1)}, bf16[128,768]{1,0:T(8,128)(2,1)S(1)}, u32[]{:S(2)}, u32[]{:S(2)}) collective-permute-start(bf16[128,768]{1,0:T(8,128)(2,1)S(1)} %get-tuple-element.248), channel_id=1, source_target_pairs={{0,2},{1,3},{2,0},{3,1},{4,6},{5,7},{6,4},{7,5},{8,10},{9,11},{10,... | collective-permute-start | bytes 589832 | tf_op jit(solution)/shard_map/ppermute | solution.py:761

commit v5 on v4

--- a/solution.py
+++ b/solution.py
@@ -192,31 +192,30 @@
     more[...] = whole[own_rows(3 - 2 * core, rows), :]
 
 
-def source_first_kernel(first, second, wk_own, wv_own, wk_peer, wv_peer, k_own, v_own, k_peer, v_peer):
-    rows = first.shape[0]
-    for index, part in enumerate((first, second)):
-        place = slice(index * rows, (index + 1) * rows)
+def source_rows(parts, start, wk_own, wv_own, wk_peer, wv_peer, k_own, v_own, k_peer, v_peer):
+    rows = parts[0].shape[0]
+    for index, part in enumerate(parts):
+        place = slice(start + index * rows, start + (index + 1) * rows)
         for weight, out in ((wk_own, k_own), (wk_peer, k_peer)):
             out[place, :] = dot_nt(part[...], weight[...]).astype(BF16)
         for weight, out in ((wv_own, v_own), (wv_peer, v_peer)):
             out[:, place] = dot_nt(weight[...], part[...]).astype(BF16)
 
 
+def source_first_kernel(first, *refs):
+    source_rows([first], 0, *refs)
+
+
 def source_second_kernel(
-    first, second, wk_own, wv_own, wk_peer, wv_peer, early_k_own, early_v_own, early_k_peer, early_v_peer,
+    first, second, third, wk_own, wv_own, wk_peer, wv_peer, early_k_own, early_v_own, early_k_peer, early_v_peer,
     k_own, v_own, k_peer, v_peer,
 ):
     rows = first.shape[0]
     for early, out in ((early_k_own, k_own), (early_k_peer, k_peer)):
-        out[: 2 * rows] = early[...]
+        out[:rows] = early[...]
     for early, out in ((early_v_own, v_own), (early_v_peer, v_peer)):
-        out[:, : 2 * rows] = early[...]
-    for index, part in enumerate((first, second)):
-        place = slice((2 + index) * rows, (3 + index) * rows)
-        for weight, out in ((wk_own, k_own), (wk_peer, k_peer)):
-            out[place, :] = dot_nt(part[...], weight[...]).astype(BF16)
-        for weight, out in ((wv_own, v_own), (wv_peer, v_peer)):
-            out[:, place] = dot_nt(weight[...], part[...]).astype(BF16)
+        out[:, :rows] = early[...]
+    source_rows([first, second, third], rows, wk_own, wv_own, wk_peer, wv_peer, k_own, v_own, k_peer, v_peer)
 
 
 def source_back_kernel(
@@ -287,37 +286,36 @@
     partial_out[...] = (dot_tn(first, wo_own[...]) + dot_tn(second, wo_peer[...])).astype(BF16)
 
 
-def ffn_kernel(
-    chip_own, chip_other, hidden, gain, up_own, up_peer, act_grad_own, act_grad_peer,
-    partial_out, hidden_out, normed_out, act_own, grad_pre_own, pack,
-):
+def through_units(normed, up, act_grad):
+    pre = dot(normed, up[...])
+    square = pre * pre
+    tanh = jnp.tanh(0.7978845608028654 * (pre + 0.044715 * square * pre))
+    half_sum = 0.5 * (1.0 + tanh)
+    slope = half_sum + 0.5 * pre * (1.0 - tanh * tanh) * (
+        0.7978845608028654 * (1.0 + 3.0 * 0.044715 * square)
+    )
+    return (pre * half_sum).astype(BF16), (act_grad[...] * slope).astype(BF16)
+
+
+def ffn_peer_kernel(chip_own, chip_other, hidden, gain, up_peer, act_grad_peer, hidden_out, normed_out, part_out, pack):
     width = hidden.shape[1]
-    resid = hidden[...] + (chip_own[...].astype(F32) + chip_other[...].astype(F32))
+    resid = hidden[...] + both(chip_own[...], chip_other[...])
     hidden_out[...] = resid
     normed = (resid * inverse_rms(resid) * row_of(gain)).astype(BF16)
     normed_out[...] = normed
     pack[:, :width] = normed
-
-    def through(up, act_grad):
-        pre = dot(normed, up[...])
-        square = pre * pre
-        tanh = jnp.tanh(0.7978845608028654 * (pre + 0.044715 * square * pre))
-        half_sum = 0.5 * (1.0 + tanh)
-        slope = half_sum + 0.5 * pre * (1.0 - tanh * tanh) * (
-            0.7978845608028654 * (1.0 + 3.0 * 0.044715 * square)
-        )
-        return (pre * half_sum).astype(BF16), (act_grad[...] * slope).astype(BF16)
-
-    act, grad_pre = through(up_own, act_grad_own)
-    act_own[...] = act
-    grad_pre_own[...] = grad_pre
-    total = dot_nt(grad_pre, up_own[...])
-    act, grad_pre = through(up_peer, act_grad_peer)
+    act, grad_pre = through_units(normed, up_peer, act_grad_peer)
     units = act.shape[1]
     pack[:, width : width + units] = act
     pack[:, width + units :] = grad_pre
-    total = total + dot_nt(grad_pre, up_peer[...])
-    partial_out[...] = total.astype(BF16)
+    part_out[...] = dot_nt(grad_pre, up_peer[...])
+
+
+def ffn_own_kernel(normed, up_own, act_grad_own, part, partial_out, act_own, grad_pre_own):
+    act, grad_pre = through_units(normed[...], up_own, act_grad_own)
+    act_own[...] = act
+    grad_pre_own[...] = grad_pre
+    partial_out[...] = (part[...] + dot_nt(grad_pre, up_own[...])).astype(BF16)
 
 
 def ffn_out_kernel(act_own, pack, down_own, down_peer, out):
@@ -824,8 +822,8 @@
     )
     first_half, second_half = to_core(send), to_core(more)
     early = go(
-        source_first_kernel, "source_first", [((span // 2, columns), BF16), ((columns, span // 2), BF16)] * 2,
-        [e0, e2, cross_key, cross_value, wk_peer, wv_peer],
+        source_first_kernel, "source_first", [((span_part, columns), BF16), ((columns, span_part), BF16)] * 2,
+        [e0, cross_key, cross_value, wk_peer, wv_peer],
     )
     chip_one = go(self_sum_kernel, "self_sum", [((half + EXTRA, width), BF16)], [keep, first_half, second_half])
     other_one = to_chip(chip_one)
@@ -834,7 +832,7 @@
     e3 = to_core(e1)
     late = go(
         source_second_kernel, "source_second", [((span, columns), BF16), ((columns, span), BF16)] * 2,
-        [e1, e3, cross_key, cross_value, wk_peer, wv_peer, *early],
+        [e2, e1, e3, cross_key, cross_value, wk_peer, wv_peer, *early],
     )
     enc_len, objective, language, _ = lax.optimization_barrier((enc_len, objective, language, late[0]))
     info, mask = go(
@@ -866,14 +864,17 @@
     )
 
     latest.append(pack_forward_peer)
-    partial_three, hidden_two, normed_three, act_own, grad_pre_own, pack_ffn = go(
-        ffn_kernel, "ffn",
-        [((half, width), BF16), ((half, width), F32), ((half, width), BF16)] + [((half, units), BF16)] * 2
-        + [((half, width + 2 * units), BF16)],
-        [partial_two, other_two, hidden_one, gain_three, ffn_up, up_peer, act_grad, act_grad_peer],
+    hidden_two, normed_three, part_three, pack_ffn = go(
+        ffn_peer_kernel, "ffn_peer",
+        [((half, width), F32), ((half, width), BF16), ((half, width), F32), ((half, width + 2 * units), BF16)],
+        [partial_two, other_two, hidden_one, gain_three, up_peer, act_grad_peer],
+    )
+    pack_ffn_peer = to_core(pack_ffn)
+    partial_three, act_own, grad_pre_own = go(
+        ffn_own_kernel, "ffn_own", [((half, width), BF16)] + [((half, units), BF16)] * 2,
+        [normed_three, ffn_up, act_grad, part_three],
     )
     other_three = to_chip(partial_three)
-    pack_ffn_peer = to_core(pack_ffn)
 
     def ffn_weights(*refs):
         ffn_weights_kernel((along_x, along_z), size, *refs)

time: 92.4 us -> 91.5 us (level)
  waiting for transfers between devices: 35 us -> 30.4 us
  starting transfers between devices: 28.2 us -> 31.6 us
    ppermute x14, waiting for transfers between devices: 25.3 us -> 21.9 us  [to_peer(): lax.ppermute(value, 'dp', [(i, i ^ 1 << bit) for i in range(lax.axis_size...]
    ppermute x8, starting transfers between devices: 6.96 us -> 9.62 us  [to_chip(): lax.ppermute(value, 'tensor', [(i, i ^ 2) for i in range(lax.axis_size('t...]
    ppermute x18, waiting for transfers between devices: 2.57 us -> 1.3 us  [to_core(): lax.ppermute(value, 'tensor', [(i, i ^ 1) for i in range(lax.axis_size('t...]
    pallas_call x33 -> x34, Pallas kernels: 25.1 us -> 25.3 us  [run(): pl.pallas_call(body, out_shape=shapes, in_specs=place, out_specs=[vmem] *...]
  transfers between devices with their start and end apart: 40 -> 40, of which waited for: 13 -> 11; matrix products, arithmetic and copies ran while one was open for 0% -> 0% of each run, Pallas kernels for 24% -> 26%
where the time goes in v5:
time: 91.5 us; the launch traced here: 91.3 us
  starting transfers between devices  31.6 us (35%)
  waiting for transfers between devices  30.4 us (33%)
  Pallas kernels  25.3 us (28%)
  between operations  3.83 us (4%)
    pallas_call x34, Pallas kernels, run(): pl.pallas_call(body, out_shape=shapes, in_specs=place, out_specs=[vmem] *...  25.3 us
    ppermute x14, waiting for transfers between devices, to_peer(): lax.ppermute(value, 'dp', [(i, i ^ 1 << bit) for i in range(lax.axis_size...  21.9 us
    ppermute x14, starting transfers between devices, to_peer(): lax.ppermute(value, 'dp', [(i, i ^ 1 << bit) for i in range(lax.axis_size...  18.2 us
    ppermute x8, starting transfers between devices, to_chip(): lax.ppermute(value, 'tensor', [(i, i ^ 2) for i in range(lax.axis_size('t...  9.62 us
    ppermute x8, waiting for transfers between devices, to_chip(): lax.ppermute(value, 'tensor', [(i, i ^ 2) for i in range(lax.axis_size('t...  7.19 us
    ppermute x18, starting transfers between devices, to_core(): lax.ppermute(value, 'tensor', [(i, i ^ 1) for i in range(lax.axis_size('t...  3.87 us
  transfers between devices with their start and end apart: 40, of which 11 were waited for; matrix products, arithmetic and copies ran while one was open for 0% of the time, Pallas kernels for 26%

profile of v5, /device:TPU:0, one launch (start us, length us, event | category | flops | bytes accessed | tf_op | source)
XLA Modules:
  0.0 91.3 jit_solution(11151172000748177697)
XLA Ops:
  0.8 3.0 %collective-permute-start.1 = (bf16[128,768]{1,0:T(8,128)(2,1)}, bf16[128,768]{1,0:T(8,128)(2,1)S(1)}, u32[]{:S(2)}, u32[]{:S(2)}) collective-permute-start(bf16[128,768]{1,0:T(8,128)(2,1)} %bitcast.33), channel_id=1, source_target_pairs={{0,2},{1,3},{2,0},{3,1},{4,6},{5,7},{6,4},{7,5},{8,10},{9,11},{10,... | collective-permute-start | bytes 589832 | tf_op jit(solution)/shard_map/ppermute | solution.py:759
  3.8 0.5 collective-permute-start.4
  5.1 1.6 %self_forward.1 = (bf16[128,768]{1,0:T(8,128)(2,1)S(1)}, bf16[64,768]{1,0:T(8,128)(2,1)S(1)}, bf16[64,768]{1,0:T(8,128)(2,1)S(1)}, bf16[256,768]{1,0:T(8,128)(2,...) custom-call(s32[1]{0:T(128)S(6)} %copy.40.refs_0_, ...), custom_call_target="tpu_custom_call" | custom-call | flops 4024999936 | tf_op jit(solution)/shard_map/self_forward/pallas_call | solution.py:736
  6.8 0.4 collective-permute-start.6
  7.3 0.4 collective-permute-start.9
  7.7 0.5 source_first.1
  8.3 0.9 collective-permute-start.7
  9.2 0.5 collective-permute-start.2
  11.7 1.2 %source_second.1 = (bf16[512,192]{1,0:T(8,128)(2,1)S(1)}, bf16[192,512]{1,0:T(8,128)(2,1)S(1)}, bf16[512,192]{1,0:T(8,128)(2,1)S(1)}, bf16[192,512]{1,0:T(8,128)(2,1)S(1)}) custom-call(bf16[128,768]{1,0:T(8,128)(2,1)S(1)} %collective-permute-done.refs_0_.refs_5_.refs_7_, bf16[128,768]{1,0:T(8,128)(2,1)S(1)} %collective-permute-done.1.refs_1_.refs_4_.refs_6_, ...), custom_call_target="tpu_custom_call" | custom-call | tf_op jit(solution)/shard_map/source_second/pallas_call | solution.py:736
  13.0 0.5 collective-permute-start.12
  13.5 2.4 %collective-permute-done.7.refs_2_ = bf16[144,768]{1,0:T(8,128)(2,1)S(1)} collective-permute-done((bf16[144,768]{1,0:T(8,128)(2,1)S(1)}, bf16[144,768]{1,0:T(8,128)(2,1)S(1)}, u32[]{:S(2)}, u32[]{:S(2)}) %collective-permute-start.7) | collective-permute-done | bytes 221216 | tf_op jit(solution)/shard_map/ppermute | solution.py:759
  16.0 2.5 %cross_forward.1 = (bf16[128,768]{1,0:T(8,128)(2,1)S(1)}, f32[128,768]{1,0:T(8,128)S(1)}, bf16[128,768]{1,0:T(8,128)(2,1)S(1)}, bf16[128,192]{1,0:T(8,128)(2,1)S...) custom-call(f32[512,128]{1,0:T(8,128)S(1)} %get-tuple-element.158.re, ...), custom_call_target="tpu_custom_call" | custom-call | tf_op jit(solution)/shard_map/cross_forward/pallas_call | solution.py:736
  18.4 0.9 collective-permute-start.10
  19.5 0.9 act_grad.1
  20.5 1.6 %source_back.1 = (bf16[192,256]{1,0:T(8,128)(2,1)S(1)}, bf16[256,192]{1,0:T(8,128)(2,1)S(1)}, bf16[192,512]{1,0:T(8,128)(2,1)S(1)}, bf16[512,192]{1,0:T(8,128)(2...) custom-call(bf16[256,768]{1,0:T(8,128)(2,1)S(1)} %get-tuple-element.170.refs_0_, ...), custom_call_target="tpu_custom_call" | custom-call | tf_op jit(solution)/shard_map/source_back/pallas_call | solution.py:736
  22.1 2.7 %collective-permute-done.10.refs_1_ = bf16[128,768]{1,0:T(8,128)(2,1)S(1)} collective-permute-done((bf16[128,768]{1,0:T(8,128)(2,1)S(1)}, bf16[128,768]{1,0:T(8,128)(2,1)S(1)}, u32[]{:S(2)}, u32[]{:S(2)}) %collective-permute-start.10) | collective-permute-done | bytes 196640 | tf_op jit(solution)/shard_map/ppermute | solution.py:759
  24.7 1.0 %ffn_peer.1 = (f32[128,768]{1,0:T(8,128)S(1)}, bf16[128,768]{1,0:T(8,128)(2,1)S(1)}, f32[128,768]{1,0:T(8,128)S(1)}, bf16[128,2304]{1,0:T(8,128)(2,1)S(1)}) custom-call(bf16[128,768]{1,0:T(8,128)(2,1)S(1)} %get-tuple-element.163.refs_0_, bf16[128,768]{1,0:T(8,128)(2,1)S(1)} %collective-permute-done.10.refs_1_, f32[128,768]{1,0:T(8,128)S(1)} %get-tuple-element.164.refs_2_, ...), custom_call_target="tpu_custom_call" | custom-call | tf_op jit(solution)/shard_map/ffn_peer/pallas_call | solution.py:736
  25.8 0.9 ffn_own.1
  26.6 0.9 collective-permute-start.14
  27.5 0.3 collective-permute-done.15.refs_1_
  27.8 1.0 %ffn_weights.1 = (bf16[4,96,768]{2,1,0:T(8,128)(2,1)S(1)}, bf16[4,96,768]{2,1,0:T(8,128)(2,1)S(1)}, bf16[4,96,768]{2,1,0:T(8,128)(2,1)S(1)}, bf16[4,96,768]{2,1,0:T(8,128)(2,1)S(1)}) custom-call(bf16[128,768]{1,0:T(8,128)(2,1)S(1)} %get-tuple-element.174.normed.refs_0_, bf16[128,2304]{1,0:T(8,128)(2,1)S(1)} %collective-permute-done.15.refs_1_, ...), custom_call_target="tpu_custom_call" | custom-call | flops 5750000128 | tf_op jit(solution)/shard_map/ffn_weights/pallas_call | solution.py:736
  28.8 1.6 %collective-permute-start.20 = (bf16[4,96,768]{2,1,0:T(8,128)(2,1)S(1)}, bf16[4,96,768]{2,1,0:T(8,128)(2,1)S(1)}, u32[]{:S(2)}, u32[]{:S(2)}) collective-permute-start(bf16[4,96,768]{2,1,0:T(8,128)(2,1)S(1)} %get-tuple-element.208), channel_id=1, source_target_pairs={{0,4},{4,0},{8,12},{12,8},{16,20},{20,16},{24,28},{28,24},{1,5},{5... | collective-permute-start | bytes 1769480 | tf_op jit(solution)/shard_map/ppermute | solution.py:763
  30.4 1.6 %collective-permute-start.21 = (bf16[4,96,768]{2,1,0:T(8,128)(2,1)S(1)}, bf16[4,96,768]{2,1,0:T(8,128)(2,1)S(1)}, u32[]{:S(2)}, u32[]{:S(2)}) collective-permute-start(bf16[4,96,768]{2,1,0:T(8,128)(2,1)S(1)} %get-tuple-element.210), channel_id=1, source_target_pairs={{0,8},{4,12},{8,0},{12,4},{16,24},{20,28},{24,16},{28,20},{1,9},{5... | collective-permute-start | bytes 1769480 | tf_op jit(solution)/shard_map/ppermute | solution.py:763
  31.9 2.1 %collective-permute-done.14.refs_1_ = bf16[128,768]{1,0:T(8,128)(2,1)S(1)} collective-permute-done((bf16[128,768]{1,0:T(8,128)(2,1)S(1)}, bf16[128,768]{1,0:T(8,128)(2,1)S(1)}, u32[]{:S(2)}, u32[]{:S(2)}) %collective-permute-start.14) | collective-permute-done | bytes 196640 | tf_op jit(solution)/shard_map/ppermute | solution.py:759
  34.0 2.3 %cross_backward.1 = (bf16[128,768]{1,0:T(8,128)(2,1)S(1)}, f32[128,768]{1,0:T(8,128)S(1)}, f32[8,768]{1,0:T(8,128)S(1)}, bf16[512,384]{1,0:T(8,128)(2,1)S(1)}, b...) custom-call(bf16[128,768]{1,0:T(8,128)(2,1)S(1)} %get-tuple-element., ...), custom_call_target="tpu_custom_call" | custom-call | tf_op jit(solution)/shard_map/cross_backward/pallas_call | solution.py:736
  36.4 0.4 source_grad.1.refs_15_
  36.8 0.5 collective-permute-start.18
  37.3 0.8 collective-permute-start.16
  38.1 1.0 %collective-permute-done.18.refs_12_ = bf16[128,960]{1,0:T(8,128)(2,1)S(1)} collective-permute-done((bf16[128,960]{1,0:T(8,128)(2,1)S(1)}, bf16[128,960]{1,0:T(8,128)(2,1)S(1)}, u32[]{:S(2)}, u32[]{:S(2)}) %collective-permute-start.18) | collective-permute-done | bytes 245792 | tf_op jit(solution)/shard_map/ppermute | solution.py:755
  39.1 1.7 %cross_weights.1 = (bf16[4,96,384]{2,1,0:T(8,128)(2,1)S(1)}, bf16[4,96,384]{2,1,0:T(8,128)(2,1)S(1)}, bf16[4,96,384]{2,1,0:T(8,128)(2,1)S(1)}, bf16[4,96,384]{2,1,0:T(8,128)(2,1)S(1)}, bf16[512,384]{1,0:T(8,128)(2,1)S(1)}) custom-call(bf16[512,384]{1,0:T(8,128)(2,1)S(1)} %get-tuple-element.193.refs_0_, ...), custom_call_target="tpu_custom_call" | custom-call | tf_op jit(solution)/shard_map/cross_weights/pallas_call | solution.py:736
  40.8 1.6 %collective-permute-start.23 = (bf16[4,96,384]{2,1,0:T(8,128)(2,1)S(1)}, bf16[4,96,384]{2,1,0:T(8,128)(2,1)S(1)}, u32[]{:S(2)}, u32[]{:S(2)}) collective-permute-start(bf16[4,96,384]{2,1,0:T(8,128)(2,1)S(1)} %get-tuple-element.214), channel_id=1, source_target_pairs={{0,4},{4,0},{8,12},{12,8},{16,20},{20,16},{24,28},{28,24},{1,5},{5... | collective-permute-start | bytes 884744 | tf_op jit(solution)/shard_map/ppermute | solution.py:763
  42.4 1.6 %collective-permute-start.24 = (bf16[4,96,384]{2,1,0:T(8,128)(2,1)S(1)}, bf16[4,96,384]{2,1,0:T(8,128)(2,1)S(1)}, u32[]{:S(2)}, u32[]{:S(2)}) collective-permute-start(bf16[4,96,384]{2,1,0:T(8,128)(2,1)S(1)} %get-tuple-element.216), channel_id=1, source_target_pairs={{0,8},{4,12},{8,0},{12,4},{16,24},{20,28},{24,16},{28,20},{1,9},{5... | collective-permute-start | bytes 884744 | tf_op jit(solution)/shard_map/ppermute | solution.py:763
  44.0 0.5 ffn_out.1.refs_6_
  44.5 0.2 self_norm.1
  44.8 1.2 %collective-permute-done.21.refs_3_ = bf16[4,96,768]{2,1,0:T(8,128)(2,1)S(1)} collective-permute-done((bf16[4,96,768]{2,1,0:T(8,128)(2,1)S(1)}, bf16[4,96,768]{2,1,0:T(8,128)(2,1)S(1)}, u32[]{:S(2)}, u32[]{:S(2)}) %collective-permute-start.21) | collective-permute-done | bytes 589856 | tf_op jit(solution)/shard_map/ppermute | solution.py:763
  46.0 0.3 ffn_second.1
  46.2 1.8 %self_backward.1 = (bf16[144,768]{1,0:T(8,128)(2,1)S(1)}, bf16[144,768]{1,0:T(8,128)(2,1)S(1)}, bf16[256,768]{1,0:T(8,128)(2,1)S(1)}, bf16[256,192]{1,0:T(8,128)...) custom-call(bf16[144,768]{1,0:T(8,128)(2,1)S(1)} %get-tuple-element.204.refs_4_., ...), custom_call_target="tpu_custom_call" | custom-call | tf_op jit(solution)/shard_map/self_backward/pallas_call | solution.py:736
  48.3 1.5 %collective-permute-start.26 = (bf16[2,96,768]{2,1,0:T(8,128)(2,1)S(1)}, bf16[2,96,768]{2,1,0:T(8,128)(2,1)S(1)}, u32[]{:S(2)}, u32[]{:S(2)}) collective-permute-start(bf16[2,96,768]{2,1,0:T(8,128)(2,1)S(1)} %get-tuple-element.211.refs_11_), channel_id=1, source_target_pairs={{0,8},{4,12},{8,0},{12,4},{16,24},{20,28},{24,16},{28,20},{1,9},{5... | collective-permute-start | bytes 884744 | tf_op jit(solution)/shard_map/ppermute | solution.py:763
  49.8 1.3 %collective-permute-start.27 = (bf16[2,96,768]{2,1,0:T(8,128)(2,1)S(1)}, bf16[2,96,768]{2,1,0:T(8,128)(2,1)S(1)}, u32[]{:S(2)}, u32[]{:S(2)}) collective-permute-start(bf16[2,96,768]{2,1,0:T(8,128)(2,1)S(1)} %get-tuple-element.230), channel_id=1, source_target_pairs={{0,4},{4,0},{8,12},{12,8},{16,20},{20,16},{24,28},{28,24},{1,5},{5... | collective-permute-start | bytes 884744 | tf_op jit(solution)/shard_map/ppermute | solution.py:763
  51.1 1.4 %self_weights.1 = (bf16[4,96,512]{2,1,0:T(8,128)(2,1)S(1)}, bf16[4,96,512]{2,1,0:T(8,128)(2,1)S(1)}, bf16[4,96,256]{2,1,0:T(8,128)(2,1)S(1)}, bf16[4,96,256]{2,1,0:T(8,128)(2,1)S(1)}, bf16[16,256]{1,0:T(8,128)(2,1)S(1)}) custom-call(bf16[256,768]{1,0:T(8,128)(2,1)S(1)} %get-tuple-element.170.refs_0_, bf16[256,768]{1,0:T(8,128)(2,1)S(1)} %get-tuple-element.217.refs_1_, ...), custom_call_target="tpu_custom_call" | custom-call | tf_op jit(solution)/shard_map/self_weights/pallas_call | solution.py:736
  52.5 0.2 round_three.1
  52.8 0.9 collective-permute-start.25
  53.6 1.3 %collective-permute-start.30 = (bf16[1376,128]{1,0:T(8,128)(2,1)S(1)}, bf16[1376,128]{1,0:T(8,128)(2,1)S(1)}, u32[]{:S(2)}, u32[]{:S(2)}) collective-permute-start(bf16[1376,128]{1,0:T(8,128)(2,1)S(1)} %get-tuple-element.235), channel_id=1, source_target_pairs={{0,8},{4,12},{8,0},{12,4},{16,24},{20,28},{24,16},{28,20},{1,9},{5... | collective-permute-start | bytes 1056776 | tf_op jit(solution)/shard_map/ppermute | solution.py:763
  54.9 0.4 collective-permute-start.29
  55.4 4.3 %collective-permute-done.27.refs_3_ = bf16[2,96,768]{2,1,0:T(8,128)(2,1)S(1)} collective-permute-done((bf16[2,96,768]{2,1,0:T(8,128)(2,1)S(1)}, bf16[2,96,768]{2,1,0:T(8,128)(2,1)S(1)}, u32[]{:S(2)}, u32[]{:S(2)}) %collective-permute-start.27) | collective-permute-done | bytes 294944 | tf_op jit(solution)/shard_map/ppermute | solution.py:763
  59.8 2.7 %collective-permute-start.39 = (bf16[192,768]{1,0:T(8,128)(2,1)S(1)}, bf16[192,768]{1,0:T(8,128)(2,1)S(1)}, u32[]{:S(2)}, u32[]{:S(2)}) collective-permute-start(bf16[192,768]{1,0:T(8,128)(2,1)S(1)} %get-tuple-element.231.refs_2_), channel_id=1, source_target_pairs={{0,16},{4,20},{8,24},{12,28},{16,0},{20,4},{24,8},{28,12},{1,17},{... | collective-permute-start | bytes 884744 | tf_op jit(solution)/shard_map/ppermute | solution.py:763
  62.4 1.4 %collective-permute-start.28 = (bf16[128,768]{1,0:T(8,128)(2,1)S(1)}, bf16[128,768]{1,0:T(8,128)(2,1)S(1)}, u32[]{:S(2)}, u32[]{:S(2)}) collective-permute-start(bf16[128,768]{1,0:T(8,128)(2,1)S(1)} %ffn_out.1.refs_6_), channel_id=1, source_target_pairs={{0,2},{1,3},{2,0},{3,1},{4,6},{5,7},{6,4},{7,5},{8,10},{9,11},{10,... | collective-permute-start | bytes 589832 | tf_op jit(solution)/shard_map/ppermute | solution.py:759
  63.8 0.8 collective-permute-start.31
  64.6 6.8 %collective-permute-done.30.zo_got = bf16[1376,128]{1,0:T(8,128)(2,1)S(1)} collective-permute-done((bf16[1376,128]{1,0:T(8,128)(2,1)S(1)}, bf16[1376,128]{1,0:T(8,128)(2,1)S(1)}, u32[]{:S(2)}, u32[]{:S(2)}) %collective-permute-start.30) | collective-permute-done | bytes 352288 | tf_op jit(solution)/shard_map/ppermute | solution.py:763
  71.7 0.4 collective-permute-start.34
  72.1 0.5 collective-permute-start.33
  72.6 0.6 encoded.1
  73.3 2.6 %collective-permute-start.38 = (bf16[576,128]{1,0:T(8,128)(2,1)S(1)}, bf16[576,128]{1,0:T(8,128)(2,1)S(1)}, u32[]{:S(2)}, u32[]{:S(2)}) collective-permute-start(bf16[576,128]{1,0:T(8,128)(2,1)S(1)} %get-tuple-element.262), channel_id=1, source_target_pairs={{0,16},{4,20},{8,24},{12,28},{16,0},{20,4},{24,8},{28,12},{1,17},{... | collective-permute-start | bytes 442376 | tf_op jit(solution)/shard_map/ppermute | solution.py:763
  75.9 0.3 input_grad.1.refs_2_.refs_0_
  76.3 0.2 collective-permute-start.32
  76.5 0.8 ffn_final.1
  77.4 4.6 %collective-permute-done.33.refs_1_ = bf16[208,512]{1,0:T(8,128)(2,1)S(1)} collective-permute-done((bf16[208,512]{1,0:T(8,128)(2,1)S(1)}, bf16[208,512]{1,0:T(8,128)(2,1)S(1)}, u32[]{:S(2)}, u32[]{:S(2)}) %collective-permute-start.33) | collective-permute-done | bytes 213024 | tf_op jit(solution)/shard_map/ppermute | solution.py:763
  82.2 0.4 collective-permute-start.36
  82.6 1.0 %collective-permute-start.37 = (bf16[128,768]{1,0:T(8,128)(2,1)S(1)}, bf16[128,768]{1,0:T(8,128)(2,1)S(1)}, u32[]{:S(2)}, u32[]{:S(2)}) collective-permute-start(bf16[128,768]{1,0:T(8,128)(2,1)S(1)} %get-tuple-element.250), channel_id=1, source_target_pairs={{0,2},{1,3},{2,0},{3,1},{4,6},{5,7},{6,4},{7,5},{8,10},{9,11},{10,... | collective-permute-start | bytes 589832 | tf_op jit(solution)/shard_map/ppermute | solution.py:759
  83.5 1.9 %collective-permute-done.38.refs_1_ = bf16[576,128]{1,0:T(8,128)(2,1)S(1)} collective-permute-done((bf16[576,128]{1,0:T(8,128)(2,1)S(1)}, bf16[576,128]{1,0:T(8,128)(2,1)S(1)}, u32[]{:S(2)}, u32[]{:S(2)}) %collective-permute-start.38) | collective-permute-done | bytes 147488 | tf_op jit(solution)/shard_map/ppermute | solution.py:763
  85.5 0.8 cross_final.1
  86.3 0.9 %rows.1 = (bf16[256,768]{1,0:T(8,128)(2,1)}, bf16[256,768]{1,0:T(8,128)(2,1)}, bf16[16,128]{1,0:T(8,128)(2,1)S(1)}) custom-call(bf16[256,768]{1,0:T(8,128)(2,1)S(1)} %input_grad.1.refs_2_.refs_0_, bf16[256,768]{1,0:T(8,128)(2,1)S(1)} %collective-permute-done.32.refs_1_, bf16[608,128]{1,0:T(8,128)(2,1)S(1)} %get-tuple-element.246.refs_2_), custom_call_target="tpu_custom_call" | custom-call | tf_op jit(solution)/shard_map/rows/pallas_call | solution.py:736
  87.2 3.1 %collective-permute-done.36.refs_1_ = bf16[608,128]{1,0:T(8,128)(2,1)S(1)} collective-permute-done((bf16[608,128]{1,0:T(8,128)(2,1)S(1)}, bf16[608,128]{1,0:T(8,128)(2,1)S(1)}, u32[]{:S(2)}, u32[]{:S(2)}) %collective-permute-start.36) | collective-permute-done | bytes 155680 | tf_op jit(solution)/shard_map/ppermute | solution.py:763
  90.3 1.0 %self_final.1 = (bf16[128,768]{1,0:T(8,128)(2,1)}, f32[96,192]{1,0:T(8,128)}, f32[96,192]{1,0:T(8,128)}, f32[96,192]{1,0:T(8,128)}, f32[192,96]{1,0:T(8,128)}, /...) custom-call(bf16[608,128]{1,0:T(8,128)(2,1)S(1)} %get-tuple-element.249.refs_0_, ...), custom_call_target="tpu_custom_call" | custom-call | tf_op jit(solution)/shard_map/self_final/pallas_call | solution.py:736
  (88 shorter events, 1.9 us)
Async XLA Ops:
  0.7 3.1 %copy-start = (bf16[768,192]{0,1:T(8,128)(2,1)S(1)}, bf16[768,192]{0,1:T(8,128)(2,1)}, u32[]{:S(2)}) copy-start(bf16[768,192]{0,1:T(8,128)(2,1)} %param.40) | copy-start | bytes 884740
  0.7 3.1 %copy-start.1 = (bf16[768,192]{0,1:T(8,128)(2,1)S(1)}, bf16[768,192]{0,1:T(8,128)(2,1)}, u32[]{:S(2)}) copy-start(bf16[768,192]{0,1:T(8,128)(2,1)} %param.41) | copy-start | bytes 884740
  0.7 4.3 %copy-start.3 = (bf16[1,256,768]{2,1,0:T(8,128)(2,1)S(1)}, bf16[1,256,768]{2,1,0:T(8,128)(2,1)}, u32[]{:S(2)}) copy-start(bf16[1,256,768]{2,1,0:T(8,128)(2,1)} %param.23) | copy-start | bytes 1179652
  0.7 4.3 %copy-start.5 = (bf16[768,192]{0,1:T(8,128)(2,1)S(1)}, bf16[768,192]{0,1:T(8,128)(2,1)}, u32[]{:S(2)}) copy-start(bf16[768,192]{0,1:T(8,128)(2,1)} %param.34) | copy-start | bytes 884740
  0.7 4.3 %copy-start.6 = (bf16[768,192]{0,1:T(8,128)(2,1)S(1)}, bf16[768,192]{0,1:T(8,128)(2,1)}, u32[]{:S(2)}) copy-start(bf16[768,192]{0,1:T(8,128)(2,1)} %param.35) | copy-start | bytes 884740
  0.7 4.3 %copy-start.10 = (bf16[768,192]{0,1:T(8,128)(2,1)S(1)}, bf16[768,192]{0,1:T(8,128)(2,1)}, u32[]{:S(2)}) copy-start(bf16[768,192]{0,1:T(8,128)(2,1)} %param.33) | copy-start | bytes 884740
  0.7 4.3 %copy-start.11 = (bf16[192,768]{1,0:T(8,128)(2,1)S(1)}, bf16[192,768]{1,0:T(8,128)(2,1)}, u32[]{:S(2)}) copy-start(bf16[192,768]{1,0:T(8,128)(2,1)} %refs_2_.5) | copy-start | bytes 884740
  0.7 4.3 %copy-start.14 = (f32[768]{0:T(1024)S(1)}, f32[768]{0:T(1024)}, u32[]{:S(2)}) copy-start(f32[768]{0:T(1024)} %refs_3_.7) | copy-start | bytes 9220
  0.7 4.3 %copy-start.15 = (s32[256]{0:T(256)S(1)}, s32[256]{0:T(256)}, u32[]{:S(2)}) copy-start(s32[256]{0:T(256)} %param.29) | copy-start | bytes 3076
  0.7 4.3 %copy-start.18 = (f32[32,3]{0,1:T(4,128)S(1)}, f32[32,3]{0,1:T(4,128)}, u32[]{:S(2)}) copy-start(f32[32,3]{0,1:T(4,128)} %param.37) | copy-start | bytes 1156
  0.8 8.5 %collective-permute-start.1 = (bf16[128,768]{1,0:T(8,128)(2,1)}, bf16[128,768]{1,0:T(8,128)(2,1)S(1)}, u32[]{:S(2)}, u32[]{:S(2)}) collective-permute-start(bf16[128,768]{1,0:T(8,128)(2,1)} %bitcast.33), channel_id=1, source_target_pairs={{0,2},{1,3},{2,0},{3,1},{4,6},{5,7},{6,4},{7,5},{8,10},{9,11},{10,... | collective-permute-start | bytes 589832 | tf_op jit(solution)/shard_map/ppermute | solution.py:759
  3.8 3.4 %collective-permute-start.3 = (bf16[192,768]{1,0:T(8,128)(2,1)S(1)}, bf16[192,768]{1,0:T(8,128)(2,1)S(1)}, u32[]{:S(2)}, u32[]{:S(2)}) collective-permute-start(bf16[192,768]{1,0:T(8,128)(2,1)S(1)} %bitcast.19), channel_id=1, source_target_pairs={{0,1},{1,0},{2,3},{3,2},{4,5},{5,4},{6,7},{7,6},{8,9},{9,8},{10,11... | collective-permute-start | bytes 884744 | tf_op jit(solution)/shard_map/ppermute | solution.py:755
  3.8 3.5 %collective-permute-start.4 = (bf16[192,768]{1,0:T(8,128)(2,1)S(1)}, bf16[192,768]{1,0:T(8,128)(2,1)S(1)}, u32[]{:S(2)}, u32[]{:S(2)}) collective-permute-start(bf16[192,768]{1,0:T(8,128)(2,1)S(1)} %bitcast.24), channel_id=1, source_target_pairs={{0,1},{1,0},{2,3},{3,2},{4,5},{5,4},{6,7},{7,6},{8,9},{9,8},{10,11... | collective-permute-start | bytes 884744 | tf_op jit(solution)/shard_map/ppermute | solution.py:755
  5.0 2.2 %copy-start.8 = (bf16[768,192]{0,1:T(8,128)(2,1)S(1)}, bf16[768,192]{0,1:T(8,128)(2,1)}, u32[]{:S(2)}) copy-start(bf16[768,192]{0,1:T(8,128)(2,1)} %param.39) | copy-start | bytes 884740
  5.1 2.2 %copy-start.9 = (bf16[192,768]{1,0:T(8,128)(2,1)S(1)}, bf16[192,768]{1,0:T(8,128)(2,1)}, u32[]{:S(2)}) copy-start(bf16[192,768]{1,0:T(8,128)(2,1)} %refs_5_.1) | copy-start | bytes 884740
  5.1 2.7 %copy-start.4 = (bf16[1,128,768]{2,1,0:T(8,128)(2,1)S(1)}, bf16[1,128,768]{2,1,0:T(8,128)(2,1)}, u32[]{:S(2)}) copy-start(bf16[1,128,768]{2,1,0:T(8,128)(2,1)} %param.24) | copy-start | bytes 589828
  6.6 1.6 %collective-permute-start.5 = (bf16[64,768]{1,0:T(8,128)(2,1)S(1)}, bf16[64,768]{1,0:T(8,128)(2,1)S(1)}, u32[]{:S(2)}, u32[]{:S(2)}) collective-permute-start(bf16[64,768]{1,0:T(8,128)(2,1)S(1)} %get-tuple-element.152), channel_id=1, source_target_pairs={{0,1},{1,0},{2,3},{3,2},{4,5},{5,4},{6,7},{7,6},{8,9},{9,8},{10,11... | collective-permute-start | bytes 294920 | tf_op jit(solution)/shard_map/ppermute | solution.py:755
  6.8 1.5 %collective-permute-start.6 = (bf16[64,768]{1,0:T(8,128)(2,1)S(1)}, bf16[64,768]{1,0:T(8,128)(2,1)S(1)}, u32[]{:S(2)}, u32[]{:S(2)}) collective-permute-start(bf16[64,768]{1,0:T(8,128)(2,1)S(1)} %get-tuple-element.153), channel_id=1, source_target_pairs={{0,1},{1,0},{2,3},{3,2},{4,5},{5,4},{6,7},{7,6},{8,9},{9,8},{10,11... | collective-permute-start | bytes 294920 | tf_op jit(solution)/shard_map/ppermute | solution.py:755
  7.2 6.3 %collective-permute-start.8 = (bf16[192,768]{1,0:T(8,128)(2,1)S(1)}, bf16[192,768]{1,0:T(8,128)(2,1)S(1)}, u32[]{:S(2)}, u32[]{:S(2)}) collective-permute-start(bf16[192,768]{1,0:T(8,128)(2,1)S(1)} %bitcast.44), channel_id=1, source_target_pairs={{0,1},{1,0},{2,3},{3,2},{4,5},{5,4},{6,7},{7,6},{8,9},{9,8},{10,11... | collective-permute-start | bytes 884744 | tf_op jit(solution)/shard_map/ppermute | solution.py:755
  7.3 6.2 %collective-permute-start.9 = (bf16[192,768]{1,0:T(8,128)(2,1)S(1)}, bf16[192,768]{1,0:T(8,128)(2,1)S(1)}, u32[]{:S(2)}, u32[]{:S(2)}) collective-permute-start(bf16[192,768]{1,0:T(8,128)(2,1)S(1)} %copy-done.9), channel_id=1, source_target_pairs={{0,1},{1,0},{2,3},{3,2},{4,5},{5,4},{6,7},{7,6},{8,9},{9,8},{10,11... | collective-permute-start | bytes 884744 | tf_op jit(solution)/shard_map/ppermute | solution.py:755
  8.3 4.6 %copy-start.7 = (bf16[768,768]{1,0:T(8,128)(2,1)S(1)}, bf16[768,768]{1,0:T(8,128)(2,1)}, u32[]{:S(2)}) copy-start(bf16[768,768]{1,0:T(8,128)(2,1)} %up_own.1) | copy-start | bytes 3538948
  8.3 4.6 %copy-start.2 = (bf16[768,768]{1,0:T(8,128)(2,1)S(1)}, bf16[768,768]{1,0:T(8,128)(2,1)}, u32[]{:S(2)}) copy-start(bf16[768,768]{1,0:T(8,128)(2,1)} %refs_2_.4) | copy-start | bytes 3538948
  8.3 7.6 %collective-permute-start.7 = (bf16[144,768]{1,0:T(8,128)(2,1)S(1)}, bf16[144,768]{1,0:T(8,128)(2,1)S(1)}, u32[]{:S(2)}, u32[]{:S(2)}) collective-permute-start(bf16[144,768]{1,0:T(8,128)(2,1)S(1)} %self_sum.1.refs_11_.refs_1_), channel_id=1, source_target_pairs={{0,2},{1,3},{2,0},{3,1},{4,6},{5,7},{6,4},{7,5},{8,10},{9,11},{10,... | collective-permute-start | bytes 663560 | tf_op jit(solution)/shard_map/ppermute | solution.py:759
  9.2 2.5 %collective-permute-start = (bf16[128,768]{1,0:T(8,128)(2,1)S(1)}, bf16[128,768]{1,0:T(8,128)(2,1)S(1)}, u32[]{:S(2)}, u32[]{:S(2)}) collective-permute-start(bf16[128,768]{1,0:T(8,128)(2,1)S(1)} %bitcast.35), channel_id=1, source_target_pairs={{0,1},{1,0},{2,3},{3,2},{4,5},{5,4},{6,7},{7,6},{8,9},{9,8},{10,11... | collective-permute-start | bytes 589832 | tf_op jit(solution)/shard_map/ppermute | solution.py:755
  9.2 2.5 %collective-permute-start.2 = (bf16[128,768]{1,0:T(8,128)(2,1)S(1)}, bf16[128,768]{1,0:T(8,128)(2,1)S(1)}, u32[]{:S(2)}, u32[]{:S(2)}) collective-permute-start(bf16[128,768]{1,0:T(8,128)(2,1)S(1)} %collective-permute-done.1.refs_1_.refs_4_.refs_6_), channel_id=1, source_target_pairs={{0,1},{1,0},{2,3},{3,2},{4,5},{5,4},{6,7},{7,6},{8,9},{9,8},{10,11... | collective-permute-start | bytes 589832 | tf_op jit(solution)/shard_map/ppermute | solution.py:755
  11.7 4.3 %copy-start.12 = (f32[768]{0:T(1024)S(1)}, f32[768]{0:T(1024)}, u32[]{:S(2)}) copy-start(f32[768]{0:T(1024)} %refs_3_.6) | copy-start | bytes 9220
  12.9 11.8 %collective-permute-start.11 = (bf16[768,768]{1,0:T(8,128)(2,1)S(1)}, bf16[768,768]{1,0:T(8,128)(2,1)S(1)}, u32[]{:S(2)}, u32[]{:S(2)}) collective-permute-start(bf16[768,768]{1,0:T(8,128)(2,1)S(1)} %copy-done.7), channel_id=1, source_target_pairs={{0,1},{1,0},{2,3},{3,2},{4,5},{5,4},{6,7},{7,6},{8,9},{9,8},{10,11... | collective-permute-start | bytes 3538952 | tf_op jit(solution)/shard_map/ppermute | solution.py:755
  13.0 6.6 %collective-permute-start.12 = (bf16[768,768]{1,0:T(8,128)(2,1)S(1)}, bf16[768,768]{1,0:T(8,128)(2,1)S(1)}, u32[]{:S(2)}, u32[]{:S(2)}) collective-permute-start(bf16[768,768]{1,0:T(8,128)(2,1)S(1)} %copy-done.2), channel_id=1, source_target_pairs={{0,1},{1,0},{2,3},{3,2},{4,5},{5,4},{6,7},{7,6},{8,9},{9,8},{10,11... | collective-permute-start | bytes 3538952 | tf_op jit(solution)/shard_map/ppermute | solution.py:755
  16.0 3.3 %copy-start.16 = (bf16[1,256,768]{2,1,0:T(8,128)(2,1)S(1)}, bf16[1,256,768]{2,1,0:T(8,128)(2,1)}, u32[]{:S(2)}) copy-start(bf16[1,256,768]{2,1,0:T(8,128)(2,1)} %param.31) | copy-start | bytes 1179652
  16.0 3.3 %copy-start.17 = (f32[16,256]{1,0:T(8,128)S(1)}, f32[16,256]{1,0:T(8,128)}, u32[]{:S(2)}) copy-start(f32[16,256]{1,0:T(8,128)} %refs_2_.3) | copy-start | bytes 49156
  18.4 6.3 %collective-permute-start.10 = (bf16[128,768]{1,0:T(8,128)(2,1)S(1)}, bf16[128,768]{1,0:T(8,128)(2,1)S(1)}, u32[]{:S(2)}, u32[]{:S(2)}) collective-permute-start(bf16[128,768]{1,0:T(8,128)(2,1)S(1)} %get-tuple-element.163.refs_0_), channel_id=1, source_target_pairs={{0,2},{1,3},{2,0},{3,1},{4,6},{5,7},{6,4},{7,5},{8,10},{9,11},{10,... | collective-permute-start | bytes 589832 | tf_op jit(solution)/shard_map/ppermute | solution.py:759
  19.3 5.4 %collective-permute-start.13 = (bf16[128,960]{1,0:T(8,128)(2,1)S(1)}, bf16[128,960]{1,0:T(8,128)(2,1)S(1)}, u32[]{:S(2)}, u32[]{:S(2)}) collective-permute-start(bf16[128,960]{1,0:T(8,128)(2,1)S(1)} %get-tuple-element.173), channel_id=1, source_target_pairs={{0,1},{1,0},{2,3},{3,2},{4,5},{5,4},{6,7},{7,6},{8,9},{9,8},{10,11... | collective-permute-start | bytes 737288 | tf_op jit(solution)/shard_map/ppermute | solution.py:755
  20.4 4.3 %copy-start.13 = (f32[768]{0:T(1024)S(1)}, f32[768]{0:T(1024)}, u32[]{:S(2)}) copy-start(f32[768]{0:T(1024)} %refs_3_.5) | copy-start | bytes 9220
  25.7 2.1 %collective-permute-start.15 = (bf16[128,2304]{1,0:T(8,128)(2,1)S(1)}, bf16[128,2304]{1,0:T(8,128)(2,1)S(1)}, u32[]{:S(2)}, u32[]{:S(2)}) collective-permute-start(bf16[128,2304]{1,0:T(8,128)(2,1)S(1)} %get-tuple-element.185.refs_1_), channel_id=1, source_target_pairs={{0,1},{1,0},{2,3},{3,2},{4,5},{5,4},{6,7},{7,6},{8,9},{9,8},{10,11... | collective-permute-start | bytes 1769480 | tf_op jit(solution)/shard_map/ppermute | solution.py:755
  26.6 7.4 %collective-permute-start.14 = (bf16[128,768]{1,0:T(8,128)(2,1)S(1)}, bf16[128,768]{1,0:T(8,128)(2,1)S(1)}, u32[]{:S(2)}, u32[]{:S(2)}) collective-permute-start(bf16[128,768]{1,0:T(8,128)(2,1)S(1)} %get-tuple-element.176.refs_6_.refs_0_), channel_id=1, source_target_pairs={{0,2},{1,3},{2,0},{3,1},{4,6},{5,7},{6,4},{7,5},{8,10},{9,11},{10,... | collective-permute-start | bytes 589832 | tf_op jit(solution)/shard_map/ppermute | solution.py:759
  28.8 16.0 %collective-permute-start.20 = (bf16[4,96,768]{2,1,0:T(8,128)(2,1)S(1)}, bf16[4,96,768]{2,1,0:T(8,128)(2,1)S(1)}, u32[]{:S(2)}, u32[]{:S(2)}) collective-permute-start(bf16[4,96,768]{2,1,0:T(8,128)(2,1)S(1)} %get-tuple-element.208), channel_id=1, source_target_pairs={{0,4},{4,0},{8,12},{12,8},{16,20},{20,16},{24,28},{28,24},{1,5},{5... | collective-permute-start | bytes 1769480 | tf_op jit(solution)/shard_map/ppermute | solution.py:763
  30.4 15.6 %collective-permute-start.21 = (bf16[4,96,768]{2,1,0:T(8,128)(2,1)S(1)}, bf16[4,96,768]{2,1,0:T(8,128)(2,1)S(1)}, u32[]{:S(2)}, u32[]{:S(2)}) collective-permute-start(bf16[4,96,768]{2,1,0:T(8,128)(2,1)S(1)} %get-tuple-element.210), channel_id=1, source_target_pairs={{0,8},{4,12},{8,0},{12,4},{16,24},{20,28},{24,16},{28,20},{1,9},{5... | collective-permute-start | bytes 1769480 | tf_op jit(solution)/shard_map/ppermute | solution.py:763
  36.7 2.4 %collective-permute-start.17 = (bf16[1024,192]{1,0:T(8,128)(2,1)S(1)}, bf16[1024,192]{1,0:T(8,128)(2,1)S(1)}, u32[]{:S(2)}, u32[]{:S(2)}) collective-permute-start(bf16[1024,192]{1,0:T(8,128)(2,1)S(1)} %source_grad.1.refs_15_), channel_id=1, source_target_pairs={{0,1},{1,0},{2,3},{3,2},{4,5},{5,4},{6,7},{7,6},{8,9},{9,8},{10,11... | collective-permute-start | bytes 1179656 | tf_op jit(solution)/shard_map/ppermute | solution.py:755
  36.8 2.3 %collective-permute-start.18 = (bf16[128,960]{1,0:T(8,128)(2,1)S(1)}, bf16[128,960]{1,0:T(8,128)(2,1)S(1)}, u32[]{:S(2)}, u32[]{:S(2)}) collective-permute-start(bf16[128,960]{1,0:T(8,128)(2,1)S(1)} %get-tuple-element.200), channel_id=1, source_target_pairs={{0,1},{1,0},{2,3},{3,2},{4,5},{5,4},{6,7},{7,6},{8,9},{9,8},{10,11... | collective-permute-start | bytes 737288 | tf_op jit(solution)/shard_map/ppermute | solution.py:755
  37.3 7.2 %collective-permute-start.16 = (bf16[128,768]{1,0:T(8,128)(2,1)S(1)}, bf16[128,768]{1,0:T(8,128)(2,1)S(1)}, u32[]{:S(2)}, u32[]{:S(2)}) collective-permute-start(bf16[128,768]{1,0:T(8,128)(2,1)S(1)} %get-tuple-element.190.refs_0_), channel_id=1, source_target_pairs={{0,2},{1,3},{2,0},{3,1},{4,6},{5,7},{6,4},{7,5},{8,10},{9,11},{10,... | collective-permute-start | bytes 589832 | tf_op jit(solution)/shard_map/ppermute | solution.py:759
  40.8 11.6 %collective-permute-start.23 = (bf16[4,96,384]{2,1,0:T(8,128)(2,1)S(1)}, bf16[4,96,384]{2,1,0:T(8,128)(2,1)S(1)}, u32[]{:S(2)}, u32[]{:S(2)}) collective-permute-start(bf16[4,96,384]{2,1,0:T(8,128)(2,1)S(1)} %get-tuple-element.214), channel_id=1, source_target_pairs={{0,4},{4,0},{8,12},{12,8},{16,20},{20,16},{24,28},{28,24},{1,5},{5... | collective-permute-start | bytes 884744 | tf_op jit(solution)/shard_map/ppermute | solution.py:763
  42.4 10.1 %collective-permute-start.24 = (bf16[4,96,384]{2,1,0:T(8,128)(2,1)S(1)}, bf16[4,96,384]{2,1,0:T(8,128)(2,1)S(1)}, u32[]{:S(2)}, u32[]{:S(2)}) collective-permute-start(bf16[4,96,384]{2,1,0:T(8,128)(2,1)S(1)} %get-tuple-element.216), channel_id=1, source_target_pairs={{0,8},{4,12},{8,0},{12,4},{16,24},{20,28},{24,16},{28,20},{1,9},{5... | collective-permute-start | bytes 884744 | tf_op jit(solution)/shard_map/ppermute | solution.py:763
  44.7 1.5 %collective-permute-start.19 = (bf16[144,768]{1,0:T(8,128)(2,1)S(1)}, bf16[144,768]{1,0:T(8,128)(2,1)S(1)}, u32[]{:S(2)}, u32[]{:S(2)}) collective-permute-start(bf16[144,768]{1,0:T(8,128)(2,1)S(1)} %get-tuple-element.204.refs_4_.refs_0_.refs_8_), channel_id=1, source_target_pairs={{0,1},{1,0},{2,3},{3,2},{4,5},{5,4},{6,7},{7,6},{8,9},{9,8},{10,11... | collective-permute-start | bytes 663560 | tf_op jit(solution)/shard_map/ppermute | solution.py:755
  48.1 4.6 %collective-permute-start.22 = (bf16[144,768]{1,0:T(8,128)(2,1)S(1)}, bf16[144,768]{1,0:T(8,128)(2,1)S(1)}, u32[]{:S(2)}, u32[]{:S(2)}) collective-permute-start(bf16[144,768]{1,0:T(8,128)(2,1)S(1)} %get-tuple-element.213), channel_id=1, source_target_pairs={{0,1},{1,0},{2,3},{3,2},{4,5},{5,4},{6,7},{7,6},{8,9},{9,8},{10,11... | collective-permute-start | bytes 663560 | tf_op jit(solution)/shard_map/ppermute | solution.py:755
  48.3 11.4 %collective-permute-start.26 = (bf16[2,96,768]{2,1,0:T(8,128)(2,1)S(1)}, bf16[2,96,768]{2,1,0:T(8,128)(2,1)S(1)}, u32[]{:S(2)}, u32[]{:S(2)}) collective-permute-start(bf16[2,96,768]{2,1,0:T(8,128)(2,1)S(1)} %get-tuple-element.211.refs_11_), channel_id=1, source_target_pairs={{0,8},{4,12},{8,0},{12,4},{16,24},{20,28},{24,16},{28,20},{1,9},{5... | collective-permute-start | bytes 884744 | tf_op jit(solution)/shard_map/ppermute | solution.py:763
  49.8 9.9 %collective-permute-start.27 = (bf16[2,96,768]{2,1,0:T(8,128)(2,1)S(1)}, bf16[2,96,768]{2,1,0:T(8,128)(2,1)S(1)}, u32[]{:S(2)}, u32[]{:S(2)}) collective-permute-start(bf16[2,96,768]{2,1,0:T(8,128)(2,1)S(1)} %get-tuple-element.230), channel_id=1, source_target_pairs={{0,4},{4,0},{8,12},{12,8},{16,20},{20,16},{24,28},{28,24},{1,5},{5... | collective-permute-start | bytes 884744 | tf_op jit(solution)/shard_map/ppermute | solution.py:763
  52.8 9.6 %collective-permute-start.25 = (bf16[144,768]{1,0:T(8,128)(2,1)S(1)}, bf16[144,768]{1,0:T(8,128)(2,1)S(1)}, u32[]{:S(2)}, u32[]{:S(2)}) collective-permute-start(bf16[144,768]{1,0:T(8,128)(2,1)S(1)} %input_sum.1.refs_4_.refs_0_), channel_id=1, source_target_pairs={{0,2},{1,3},{2,0},{3,1},{4,6},{5,7},{6,4},{7,5},{8,10},{9,11},{10,... | collective-permute-start | bytes 663560 | tf_op jit(solution)/shard_map/ppermute | solution.py:759
  53.6 17.8 %collective-permute-start.30 = (bf16[1376,128]{1,0:T(8,128)(2,1)S(1)}, bf16[1376,128]{1,0:T(8,128)(2,1)S(1)}, u32[]{:S(2)}, u32[]{:S(2)}) collective-permute-start(bf16[1376,128]{1,0:T(8,128)(2,1)S(1)} %get-tuple-element.235), channel_id=1, source_target_pairs={{0,8},{4,12},{8,0},{12,4},{16,24},{20,28},{24,16},{28,20},{1,9},{5... | collective-permute-start | bytes 1056776 | tf_op jit(solution)/shard_map/ppermute | solution.py:763
  54.9 16.5 %collective-permute-start.29 = (bf16[2112,128]{1,0:T(8,128)(2,1)S(1)}, bf16[2112,128]{1,0:T(8,128)(2,1)S(1)}, u32[]{:S(2)}, u32[]{:S(2)}) collective-permute-start(bf16[2112,128]{1,0:T(8,128)(2,1)S(1)} %get-tuple-element.234), channel_id=1, source_target_pairs={{0,4},{4,0},{8,12},{12,8},{16,20},{20,16},{24,28},{28,24},{1,5},{5... | collective-permute-start | bytes 1622024 | tf_op jit(solution)/shard_map/ppermute | solution.py:763
  59.8 16.5 %collective-permute-start.39 = (bf16[192,768]{1,0:T(8,128)(2,1)S(1)}, bf16[192,768]{1,0:T(8,128)(2,1)S(1)}, u32[]{:S(2)}, u32[]{:S(2)}) collective-permute-start(bf16[192,768]{1,0:T(8,128)(2,1)S(1)} %get-tuple-element.231.refs_2_), channel_id=1, source_target_pairs={{0,16},{4,20},{8,24},{12,28},{16,0},{20,4},{24,8},{28,12},{1,17},{... | collective-permute-start | bytes 884744 | tf_op jit(solution)/shard_map/ppermute | solution.py:763
  62.4 10.8 %collective-permute-start.28 = (bf16[128,768]{1,0:T(8,128)(2,1)S(1)}, bf16[128,768]{1,0:T(8,128)(2,1)S(1)}, u32[]{:S(2)}, u32[]{:S(2)}) collective-permute-start(bf16[128,768]{1,0:T(8,128)(2,1)S(1)} %ffn_out.1.refs_6_), channel_id=1, source_target_pairs={{0,2},{1,3},{2,0},{3,1},{4,6},{5,7},{6,4},{7,5},{8,10},{9,11},{10,... | collective-permute-start | bytes 589832 | tf_op jit(solution)/shard_map/ppermute | solution.py:759
  63.8 7.6 %collective-permute-start.31 = (bf16[16,256]{1,0:T(8,128)(2,1)S(1)}, bf16[16,256]{1,0:T(8,128)(2,1)S(1)}, u32[]{:S(2)}, u32[]{:S(2)}) collective-permute-start(bf16[16,256]{1,0:T(8,128)(2,1)S(1)} %gain.1.gains), channel_id=1, source_target_pairs={{0,4},{4,0},{8,12},{12,8},{16,20},{20,16},{24,28},{28,24},{1,5},{5... | collective-permute-start | bytes 24584 | tf_op jit(solution)/shard_map/ppermute | solution.py:763
  71.7 5.8 %collective-permute-start.34 = (bf16[208,256]{1,0:T(8,128)(2,1)S(1)}, bf16[208,256]{1,0:T(8,128)(2,1)S(1)}, u32[]{:S(2)}, u32[]{:S(2)}) collective-permute-start(bf16[208,256]{1,0:T(8,128)(2,1)S(1)} %get-tuple-element.239.refs_3_), channel_id=1, source_target_pairs={{0,4},{4,0},{8,12},{12,8},{16,20},{20,16},{24,28},{28,24},{1,5},{5... | collective-permute-start | bytes 319496 | tf_op jit(solution)/shard_map/ppermute | solution.py:763
  72.1 10.0 %collective-permute-start.33 = (bf16[208,512]{1,0:T(8,128)(2,1)S(1)}, bf16[208,512]{1,0:T(8,128)(2,1)S(1)}, u32[]{:S(2)}, u32[]{:S(2)}) collective-permute-start(bf16[208,512]{1,0:T(8,128)(2,1)S(1)} %get-tuple-element.242), channel_id=1, source_target_pairs={{0,8},{4,12},{8,0},{12,4},{16,24},{20,28},{24,16},{28,20},{1,9},{5... | collective-permute-start | bytes 638984 | tf_op jit(solution)/shard_map/ppermute | solution.py:763
  73.2 4.1 %collective-permute-start.35 = (bf16[256,768]{1,0:T(8,128)(2,1)S(1)}, bf16[256,768]{1,0:T(8,128)(2,1)S(1)}, u32[]{:S(2)}, u32[]{:S(2)}) collective-permute-start(bf16[256,768]{1,0:T(8,128)(2,1)S(1)} %get-tuple-element.244), channel_id=1, source_target_pairs={{0,1},{1,0},{2,3},{3,2},{4,5},{5,4},{6,7},{7,6},{8,9},{9,8},{10,11... | collective-permute-start | bytes 1179656 | tf_op jit(solution)/shard_map/ppermute | solution.py:755
  73.3 12.2 %collective-permute-start.38 = (bf16[576,128]{1,0:T(8,128)(2,1)S(1)}, bf16[576,128]{1,0:T(8,128)(2,1)S(1)}, u32[]{:S(2)}, u32[]{:S(2)}) collective-permute-start(bf16[576,128]{1,0:T(8,128)(2,1)S(1)} %get-tuple-element.262), channel_id=1, source_target_pairs={{0,16},{4,20},{8,24},{12,28},{16,0},{20,4},{24,8},{28,12},{1,17},{... | collective-permute-start | bytes 442376 | tf_op jit(solution)/shard_map/ppermute | solution.py:763
  76.3 10.0 %collective-permute-start.32 = (bf16[256,768]{1,0:T(8,128)(2,1)S(1)}, bf16[256,768]{1,0:T(8,128)(2,1)S(1)}, u32[]{:S(2)}, u32[]{:S(2)}) collective-permute-start(bf16[256,768]{1,0:T(8,128)(2,1)S(1)} %input_grad.1.refs_2_.refs_0_), channel_id=1, source_target_pairs={{0,1},{1,0},{2,3},{3,2},{4,5},{5,4},{6,7},{7,6},{8,9},{9,8},{10,11... | collective-permute-start | bytes 1179656 | tf_op jit(solution)/shard_map/ppermute | solution.py:755
  82.2 8.1 %collective-permute-start.36 = (bf16[608,128]{1,0:T(8,128)(2,1)S(1)}, bf16[608,128]{1,0:T(8,128)(2,1)S(1)}, u32[]{:S(2)}, u32[]{:S(2)}) collective-permute-start(bf16[608,128]{1,0:T(8,128)(2,1)S(1)} %get-tuple-element.246.refs_2_), channel_id=1, source_target_pairs={{0,16},{4,20},{8,24},{12,28},{16,0},{20,4},{24,8},{28,12},{1,17},{... | collective-permute-start | bytes 466952 | tf_op jit(solution)/shard_map/ppermute | solution.py:763
  82.6 7.8 %collective-permute-start.37 = (bf16[128,768]{1,0:T(8,128)(2,1)S(1)}, bf16[128,768]{1,0:T(8,128)(2,1)S(1)}, u32[]{:S(2)}, u32[]{:S(2)}) collective-permute-start(bf16[128,768]{1,0:T(8,128)(2,1)S(1)} %get-tuple-element.250), channel_id=1, source_target_pairs={{0,2},{1,3},{2,0},{3,1},{4,6},{5,7},{6,4},{7,5},{8,10},{9,11},{10,... | collective-permute-start | bytes 589832 | tf_op jit(solution)/shard_map/ppermute | solution.py:759

commit v6 on v5

--- a/solution.py
+++ b/solution.py
@@ -995,19 +995,23 @@
         sa_got = to_peer(sa_send, 1)
         sb_got = to_peer(sb_send, 0)
 
-    encoded_keep, encoded_send = go(
-        encoded_kernel, "encoded", [((span // 2, width), BF16)] * 2, [source_total, cross_key, cross_value]
-    )
-    encoded_got = to_core(encoded_send)
     pack_rows = go(
         input_grad_kernel, "input_grad", [((2 * half, width), BF16)],
         [chip_five, other_five, x, gain_one, grad_one, hidden_two, branch_out, out_other],
     )
     pack_rows_peer = to_core(pack_rows)
     if halving:
+        cross_send, _ = lax.optimization_barrier((cross_send, pack_rows))
+        cross_got = to_peer(cross_send, 2)
+
+    encoded_keep, encoded_send = go(
+        encoded_kernel, "encoded", [((span // 2, width), BF16)] * 2, [source_total, cross_key, cross_value]
+    )
+    encoded_got = to_core(encoded_send)
+
+    if halving:
         up, down = go(ffn_final_kernel, "ffn_final", [((size, width), F32)] * 2, [ffn_keep, ffn_got], us=LONG, last=True)
-        cross_send, _ = lax.optimization_barrier((cross_send, encoded_send))
-        cross_got = to_peer(cross_send, 2)
+
     encoded_part, encoded_pass = go(
         encoded_sum_kernel, "encoded_sum", [((span_part, width), BF16)] * 2, [encoded_keep, encoded_got]
     )

time: 91.5 us -> 91.3 us (level)
    ppermute x14, waiting for transfers between devices: 21.9 us -> 21 us  [to_peer(): lax.ppermute(value, 'dp', [(i, i ^ 1 << bit) for i in range(lax.axis_size...]
where the time goes in v6:
time: 91.3 us; the launch traced here: 91.1 us
  starting transfers between devices  31.6 us (35%)
  waiting for transfers between devices  30.2 us (33%)
  Pallas kernels  25.4 us (28%)
  between operations  3.82 us (4%)
    pallas_call x34, Pallas kernels, run(): pl.pallas_call(body, out_shape=shapes, in_specs=place, out_specs=[vmem] *...  25.4 us
    ppermute x14, waiting for transfers between devices, to_peer(): lax.ppermute(value, 'dp', [(i, i ^ 1 << bit) for i in range(lax.axis_size...  21 us
    ppermute x14, starting transfers between devices, to_peer(): lax.ppermute(value, 'dp', [(i, i ^ 1 << bit) for i in range(lax.axis_size...  17.9 us
    ppermute x8, starting transfers between devices, to_chip(): lax.ppermute(value, 'tensor', [(i, i ^ 2) for i in range(lax.axis_size('t...  9.82 us
    ppermute x8, waiting for transfers between devices, to_chip(): lax.ppermute(value, 'tensor', [(i, i ^ 2) for i in range(lax.axis_size('t...  7.18 us
    ppermute x18, starting transfers between devices, to_core(): lax.ppermute(value, 'tensor', [(i, i ^ 1) for i in range(lax.axis_size('t...  3.88 us
    ppermute x18, waiting for transfers between devices, to_core(): lax.ppermute(value, 'tensor', [(i, i ^ 1) for i in range(lax.axis_size('t...  2.02 us
  transfers between devices with their start and end apart: 40, of which 11 were waited for; matrix products, arithmetic and copies ran while one was open for 0% of the time, Pallas kernels for 26%

profile of v6, /device:TPU:0, one launch (start us, length us, event | category | flops | bytes accessed | tf_op | source)
XLA Modules:
  0.0 91.1 jit_solution(7433027565563945564)
XLA Ops:
  0.8 3.0 %collective-permute-start.1 = (bf16[128,768]{1,0:T(8,128)(2,1)}, bf16[128,768]{1,0:T(8,128)(2,1)S(1)}, u32[]{:S(2)}, u32[]{:S(2)}) collective-permute-start(bf16[128,768]{1,0:T(8,128)(2,1)} %bitcast.33), channel_id=1, source_target_pairs={{0,2},{1,3},{2,0},{3,1},{4,6},{5,7},{6,4},{7,5},{8,10},{9,11},{10,... | collective-permute-start | bytes 589832 | tf_op jit(solution)/shard_map/ppermute | solution.py:759
  3.8 0.5 collective-permute-start.4
  5.1 1.6 %self_forward.1 = (bf16[128,768]{1,0:T(8,128)(2,1)S(1)}, bf16[64,768]{1,0:T(8,128)(2,1)S(1)}, bf16[64,768]{1,0:T(8,128)(2,1)S(1)}, bf16[256,768]{1,0:T(8,128)(2,...) custom-call(s32[1]{0:T(128)S(6)} %copy.40.refs_0_, ...), custom_call_target="tpu_custom_call" | custom-call | flops 4024999936 | tf_op jit(solution)/shard_map/self_forward/pallas_call | solution.py:736
  6.8 0.4 collective-permute-start.6
  7.3 0.4 collective-permute-start.9
  7.7 0.5 source_first.1
  8.3 0.9 collective-permute-start.7
  9.2 0.5 collective-permute-start.2
  11.7 1.2 %source_second.1 = (bf16[512,192]{1,0:T(8,128)(2,1)S(1)}, bf16[192,512]{1,0:T(8,128)(2,1)S(1)}, bf16[512,192]{1,0:T(8,128)(2,1)S(1)}, bf16[192,512]{1,0:T(8,128)(2,1)S(1)}) custom-call(bf16[128,768]{1,0:T(8,128)(2,1)S(1)} %collective-permute-done.refs_0_.refs_5_.refs_7_, bf16[128,768]{1,0:T(8,128)(2,1)S(1)} %collective-permute-done.1.refs_1_.refs_4_.refs_6_, ...), custom_call_target="tpu_custom_call" | custom-call | tf_op jit(solution)/shard_map/source_second/pallas_call | solution.py:736
  13.0 0.5 collective-permute-start.12
  13.5 2.4 %collective-permute-done.7.refs_2_ = bf16[144,768]{1,0:T(8,128)(2,1)S(1)} collective-permute-done((bf16[144,768]{1,0:T(8,128)(2,1)S(1)}, bf16[144,768]{1,0:T(8,128)(2,1)S(1)}, u32[]{:S(2)}, u32[]{:S(2)}) %collective-permute-start.7) | collective-permute-done | bytes 221216 | tf_op jit(solution)/shard_map/ppermute | solution.py:759
  16.0 2.5 %cross_forward.1 = (bf16[128,768]{1,0:T(8,128)(2,1)S(1)}, f32[128,768]{1,0:T(8,128)S(1)}, bf16[128,768]{1,0:T(8,128)(2,1)S(1)}, bf16[128,192]{1,0:T(8,128)(2,1)S...) custom-call(f32[512,128]{1,0:T(8,128)S(1)} %get-tuple-element.158.re, ...), custom_call_target="tpu_custom_call" | custom-call | tf_op jit(solution)/shard_map/cross_forward/pallas_call | solution.py:736
  18.4 0.9 collective-permute-start.10
  19.5 0.9 act_grad.1
  20.5 1.6 %source_back.1 = (bf16[192,256]{1,0:T(8,128)(2,1)S(1)}, bf16[256,192]{1,0:T(8,128)(2,1)S(1)}, bf16[192,512]{1,0:T(8,128)(2,1)S(1)}, bf16[512,192]{1,0:T(8,128)(2...) custom-call(bf16[256,768]{1,0:T(8,128)(2,1)S(1)} %get-tuple-element.170.refs_0_, ...), custom_call_target="tpu_custom_call" | custom-call | tf_op jit(solution)/shard_map/source_back/pallas_call | solution.py:736
  22.1 2.7 %collective-permute-done.10.refs_1_ = bf16[128,768]{1,0:T(8,128)(2,1)S(1)} collective-permute-done((bf16[128,768]{1,0:T(8,128)(2,1)S(1)}, bf16[128,768]{1,0:T(8,128)(2,1)S(1)}, u32[]{:S(2)}, u32[]{:S(2)}) %collective-permute-start.10) | collective-permute-done | bytes 196640 | tf_op jit(solution)/shard_map/ppermute | solution.py:759
  24.7 1.0 %ffn_peer.1 = (f32[128,768]{1,0:T(8,128)S(1)}, bf16[128,768]{1,0:T(8,128)(2,1)S(1)}, f32[128,768]{1,0:T(8,128)S(1)}, bf16[128,2304]{1,0:T(8,128)(2,1)S(1)}) custom-call(bf16[128,768]{1,0:T(8,128)(2,1)S(1)} %get-tuple-element.163.refs_0_, bf16[128,768]{1,0:T(8,128)(2,1)S(1)} %collective-permute-done.10.refs_1_, f32[128,768]{1,0:T(8,128)S(1)} %get-tuple-element.164.refs_2_, ...), custom_call_target="tpu_custom_call" | custom-call | tf_op jit(solution)/shard_map/ffn_peer/pallas_call | solution.py:736
  25.8 0.9 ffn_own.1
  26.6 0.9 collective-permute-start.14
  27.5 0.3 collective-permute-done.15.refs_1_
  27.8 1.0 %ffn_weights.1 = (bf16[4,96,768]{2,1,0:T(8,128)(2,1)S(1)}, bf16[4,96,768]{2,1,0:T(8,128)(2,1)S(1)}, bf16[4,96,768]{2,1,0:T(8,128)(2,1)S(1)}, bf16[4,96,768]{2,1,0:T(8,128)(2,1)S(1)}) custom-call(bf16[128,768]{1,0:T(8,128)(2,1)S(1)} %get-tuple-element.174.normed.refs_0_, bf16[128,2304]{1,0:T(8,128)(2,1)S(1)} %collective-permute-done.15.refs_1_, ...), custom_call_target="tpu_custom_call" | custom-call | flops 5750000128 | tf_op jit(solution)/shard_map/ffn_weights/pallas_call | solution.py:736
  28.8 1.6 %collective-permute-start.20 = (bf16[4,96,768]{2,1,0:T(8,128)(2,1)S(1)}, bf16[4,96,768]{2,1,0:T(8,128)(2,1)S(1)}, u32[]{:S(2)}, u32[]{:S(2)}) collective-permute-start(bf16[4,96,768]{2,1,0:T(8,128)(2,1)S(1)} %get-tuple-element.208), channel_id=1, source_target_pairs={{0,4},{4,0},{8,12},{12,8},{16,20},{20,16},{24,28},{28,24},{1,5},{5... | collective-permute-start | bytes 1769480 | tf_op jit(solution)/shard_map/ppermute | solution.py:763
  30.4 1.6 %collective-permute-start.21 = (bf16[4,96,768]{2,1,0:T(8,128)(2,1)S(1)}, bf16[4,96,768]{2,1,0:T(8,128)(2,1)S(1)}, u32[]{:S(2)}, u32[]{:S(2)}) collective-permute-start(bf16[4,96,768]{2,1,0:T(8,128)(2,1)S(1)} %get-tuple-element.210), channel_id=1, source_target_pairs={{0,8},{4,12},{8,0},{12,4},{16,24},{20,28},{24,16},{28,20},{1,9},{5... | collective-permute-start | bytes 1769480 | tf_op jit(solution)/shard_map/ppermute | solution.py:763
  31.9 2.1 %collective-permute-done.14.refs_1_ = bf16[128,768]{1,0:T(8,128)(2,1)S(1)} collective-permute-done((bf16[128,768]{1,0:T(8,128)(2,1)S(1)}, bf16[128,768]{1,0:T(8,128)(2,1)S(1)}, u32[]{:S(2)}, u32[]{:S(2)}) %collective-permute-start.14) | collective-permute-done | bytes 196640 | tf_op jit(solution)/shard_map/ppermute | solution.py:759
  34.0 2.3 %cross_backward.1 = (bf16[128,768]{1,0:T(8,128)(2,1)S(1)}, f32[128,768]{1,0:T(8,128)S(1)}, f32[8,768]{1,0:T(8,128)S(1)}, bf16[512,384]{1,0:T(8,128)(2,1)S(1)}, b...) custom-call(bf16[128,768]{1,0:T(8,128)(2,1)S(1)} %get-tuple-element., ...), custom_call_target="tpu_custom_call" | custom-call | tf_op jit(solution)/shard_map/cross_backward/pallas_call | solution.py:736
  36.4 0.4 source_grad.1.refs_15_
  36.8 0.5 collective-permute-start.18
  37.3 0.8 collective-permute-start.16
  38.1 1.0 %collective-permute-done.18.refs_12_ = bf16[128,960]{1,0:T(8,128)(2,1)S(1)} collective-permute-done((bf16[128,960]{1,0:T(8,128)(2,1)S(1)}, bf16[128,960]{1,0:T(8,128)(2,1)S(1)}, u32[]{:S(2)}, u32[]{:S(2)}) %collective-permute-start.18) | collective-permute-done | bytes 245792 | tf_op jit(solution)/shard_map/ppermute | solution.py:755
  39.1 1.8 %cross_weights.1 = (bf16[4,96,384]{2,1,0:T(8,128)(2,1)S(1)}, bf16[4,96,384]{2,1,0:T(8,128)(2,1)S(1)}, bf16[4,96,384]{2,1,0:T(8,128)(2,1)S(1)}, bf16[4,96,384]{2,1,0:T(8,128)(2,1)S(1)}, bf16[512,384]{1,0:T(8,128)(2,1)S(1)}) custom-call(bf16[512,384]{1,0:T(8,128)(2,1)S(1)} %get-tuple-element.193.refs_0_, ...), custom_call_target="tpu_custom_call" | custom-call | tf_op jit(solution)/shard_map/cross_weights/pallas_call | solution.py:736
  40.8 1.6 %collective-permute-start.23 = (bf16[4,96,384]{2,1,0:T(8,128)(2,1)S(1)}, bf16[4,96,384]{2,1,0:T(8,128)(2,1)S(1)}, u32[]{:S(2)}, u32[]{:S(2)}) collective-permute-start(bf16[4,96,384]{2,1,0:T(8,128)(2,1)S(1)} %get-tuple-element.214), channel_id=1, source_target_pairs={{0,4},{4,0},{8,12},{12,8},{16,20},{20,16},{24,28},{28,24},{1,5},{5... | collective-permute-start | bytes 884744 | tf_op jit(solution)/shard_map/ppermute | solution.py:763
  42.4 1.6 %collective-permute-start.24 = (bf16[4,96,384]{2,1,0:T(8,128)(2,1)S(1)}, bf16[4,96,384]{2,1,0:T(8,128)(2,1)S(1)}, u32[]{:S(2)}, u32[]{:S(2)}) collective-permute-start(bf16[4,96,384]{2,1,0:T(8,128)(2,1)S(1)} %get-tuple-element.216), channel_id=1, source_target_pairs={{0,8},{4,12},{8,0},{12,4},{16,24},{20,28},{24,16},{28,20},{1,9},{5... | collective-permute-start | bytes 884744 | tf_op jit(solution)/shard_map/ppermute | solution.py:763
  44.0 0.5 ffn_out.1.refs_6_
  44.5 0.2 self_norm.1
  44.8 1.2 %collective-permute-done.21.refs_3_ = bf16[4,96,768]{2,1,0:T(8,128)(2,1)S(1)} collective-permute-done((bf16[4,96,768]{2,1,0:T(8,128)(2,1)S(1)}, bf16[4,96,768]{2,1,0:T(8,128)(2,1)S(1)}, u32[]{:S(2)}, u32[]{:S(2)}) %collective-permute-start.21) | collective-permute-done | bytes 589856 | tf_op jit(solution)/shard_map/ppermute | solution.py:763
  46.0 0.3 ffn_second.1
  46.3 1.8 %self_backward.1 = (bf16[144,768]{1,0:T(8,128)(2,1)S(1)}, bf16[144,768]{1,0:T(8,128)(2,1)S(1)}, bf16[256,768]{1,0:T(8,128)(2,1)S(1)}, bf16[256,192]{1,0:T(8,128)...) custom-call(bf16[144,768]{1,0:T(8,128)(2,1)S(1)} %get-tuple-element.204.refs_4_., ...), custom_call_target="tpu_custom_call" | custom-call | tf_op jit(solution)/shard_map/self_backward/pallas_call | solution.py:736
  48.3 1.5 %collective-permute-start.26 = (bf16[2,96,768]{2,1,0:T(8,128)(2,1)S(1)}, bf16[2,96,768]{2,1,0:T(8,128)(2,1)S(1)}, u32[]{:S(2)}, u32[]{:S(2)}) collective-permute-start(bf16[2,96,768]{2,1,0:T(8,128)(2,1)S(1)} %get-tuple-element.211.refs_11_), channel_id=1, source_target_pairs={{0,8},{4,12},{8,0},{12,4},{16,24},{20,28},{24,16},{28,20},{1,9},{5... | collective-permute-start | bytes 884744 | tf_op jit(solution)/shard_map/ppermute | solution.py:763
  49.8 1.3 %collective-permute-start.27 = (bf16[2,96,768]{2,1,0:T(8,128)(2,1)S(1)}, bf16[2,96,768]{2,1,0:T(8,128)(2,1)S(1)}, u32[]{:S(2)}, u32[]{:S(2)}) collective-permute-start(bf16[2,96,768]{2,1,0:T(8,128)(2,1)S(1)} %get-tuple-element.230), channel_id=1, source_target_pairs={{0,4},{4,0},{8,12},{12,8},{16,20},{20,16},{24,28},{28,24},{1,5},{5... | collective-permute-start | bytes 884744 | tf_op jit(solution)/shard_map/ppermute | solution.py:763
  51.1 1.4 %self_weights.1 = (bf16[4,96,512]{2,1,0:T(8,128)(2,1)S(1)}, bf16[4,96,512]{2,1,0:T(8,128)(2,1)S(1)}, bf16[4,96,256]{2,1,0:T(8,128)(2,1)S(1)}, bf16[4,96,256]{2,1,0:T(8,128)(2,1)S(1)}, bf16[16,256]{1,0:T(8,128)(2,1)S(1)}) custom-call(bf16[256,768]{1,0:T(8,128)(2,1)S(1)} %get-tuple-element.170.refs_0_, bf16[256,768]{1,0:T(8,128)(2,1)S(1)} %get-tuple-element.217.refs_1_, ...), custom_call_target="tpu_custom_call" | custom-call | tf_op jit(solution)/shard_map/self_weights/pallas_call | solution.py:736
  52.5 0.2 round_three.1
  52.8 0.9 collective-permute-start.25
  53.7 1.3 %collective-permute-start.30 = (bf16[1376,128]{1,0:T(8,128)(2,1)S(1)}, bf16[1376,128]{1,0:T(8,128)(2,1)S(1)}, u32[]{:S(2)}, u32[]{:S(2)}) collective-permute-start(bf16[1376,128]{1,0:T(8,128)(2,1)S(1)} %get-tuple-element.234), channel_id=1, source_target_pairs={{0,8},{4,12},{8,0},{12,4},{16,24},{20,28},{24,16},{28,20},{1,9},{5... | collective-permute-start | bytes 1056776 | tf_op jit(solution)/shard_map/ppermute | solution.py:763
  55.0 0.4 collective-permute-start.29
  55.4 4.3 %collective-permute-done.27.refs_3_ = bf16[2,96,768]{2,1,0:T(8,128)(2,1)S(1)} collective-permute-done((bf16[2,96,768]{2,1,0:T(8,128)(2,1)S(1)}, bf16[2,96,768]{2,1,0:T(8,128)(2,1)S(1)}, u32[]{:S(2)}, u32[]{:S(2)}) %collective-permute-start.27) | collective-permute-done | bytes 294944 | tf_op jit(solution)/shard_map/ppermute | solution.py:763
  59.8 2.7 %collective-permute-start.39 = (bf16[192,768]{1,0:T(8,128)(2,1)S(1)}, bf16[192,768]{1,0:T(8,128)(2,1)S(1)}, u32[]{:S(2)}, u32[]{:S(2)}) collective-permute-start(bf16[192,768]{1,0:T(8,128)(2,1)S(1)} %get-tuple-element.231.refs_2_), channel_id=1, source_target_pairs={{0,16},{4,20},{8,24},{12,28},{16,0},{20,4},{24,8},{28,12},{1,17},{... | collective-permute-start | bytes 884744 | tf_op jit(solution)/shard_map/ppermute | solution.py:763
  62.4 1.4 %collective-permute-start.28 = (bf16[128,768]{1,0:T(8,128)(2,1)S(1)}, bf16[128,768]{1,0:T(8,128)(2,1)S(1)}, u32[]{:S(2)}, u32[]{:S(2)}) collective-permute-start(bf16[128,768]{1,0:T(8,128)(2,1)S(1)} %ffn_out.1.refs_6_), channel_id=1, source_target_pairs={{0,2},{1,3},{2,0},{3,1},{4,6},{5,7},{6,4},{7,5},{8,10},{9,11},{10,... | collective-permute-start | bytes 589832 | tf_op jit(solution)/shard_map/ppermute | solution.py:759
  63.8 0.8 collective-permute-start.31
  64.6 6.8 %collective-permute-done.30.zo_got = bf16[1376,128]{1,0:T(8,128)(2,1)S(1)} collective-permute-done((bf16[1376,128]{1,0:T(8,128)(2,1)S(1)}, bf16[1376,128]{1,0:T(8,128)(2,1)S(1)}, u32[]{:S(2)}, u32[]{:S(2)}) %collective-permute-start.30) | collective-permute-done | bytes 352288 | tf_op jit(solution)/shard_map/ppermute | solution.py:763
  71.5 0.2 round_four.1
  71.7 0.4 collective-permute-start.34
  72.1 0.5 collective-permute-start.33
  72.6 0.3 input_grad.1.refs_3_.refs_0_
  73.0 2.6 %collective-permute-start.38 = (bf16[576,128]{1,0:T(8,128)(2,1)S(1)}, bf16[576,128]{1,0:T(8,128)(2,1)S(1)}, u32[]{:S(2)}, u32[]{:S(2)}) collective-permute-start(bf16[576,128]{1,0:T(8,128)(2,1)S(1)} %get-tuple-element.262), channel_id=1, source_target_pairs={{0,16},{4,20},{8,24},{12,28},{16,0},{20,4},{24,8},{28,12},{1,17},{... | collective-permute-start | bytes 442376 | tf_op jit(solution)/shard_map/ppermute | solution.py:763
  75.6 0.6 encoded.1
  76.3 0.2 collective-permute-start.35
  76.5 0.8 ffn_final.1
  77.3 0.7 collective-permute-done.35.other
  78.2 4.1 %collective-permute-done.33.refs_1_ = bf16[208,512]{1,0:T(8,128)(2,1)S(1)} collective-permute-done((bf16[208,512]{1,0:T(8,128)(2,1)S(1)}, bf16[208,512]{1,0:T(8,128)(2,1)S(1)}, u32[]{:S(2)}, u32[]{:S(2)}) %collective-permute-start.33) | collective-permute-done | bytes 213024 | tf_op jit(solution)/shard_map/ppermute | solution.py:763
  82.6 1.2 %collective-permute-start.37 = (bf16[128,768]{1,0:T(8,128)(2,1)S(1)}, bf16[128,768]{1,0:T(8,128)(2,1)S(1)}, u32[]{:S(2)}, u32[]{:S(2)}) collective-permute-start(bf16[128,768]{1,0:T(8,128)(2,1)S(1)} %get-tuple-element.250), channel_id=1, source_target_pairs={{0,2},{1,3},{2,0},{3,1},{4,6},{5,7},{6,4},{7,5},{8,10},{9,11},{10,... | collective-permute-start | bytes 589832 | tf_op jit(solution)/shard_map/ppermute | solution.py:759
  83.8 0.8 cross_final.1
  84.6 0.9 %rows.1 = (bf16[256,768]{1,0:T(8,128)(2,1)}, bf16[256,768]{1,0:T(8,128)(2,1)}, bf16[16,128]{1,0:T(8,128)(2,1)S(1)}) custom-call(bf16[256,768]{1,0:T(8,128)(2,1)S(1)} %input_grad.1.refs_3_.refs_0_, bf16[256,768]{1,0:T(8,128)(2,1)S(1)} %collective-permute-done.32.refs_1_, bf16[608,128]{1,0:T(8,128)(2,1)S(1)} %get-tuple-element.246.refs_2_), custom_call_target="tpu_custom_call" | custom-call | tf_op jit(solution)/shard_map/rows/pallas_call | solution.py:736
  85.6 4.5 %collective-permute-done.36.refs_1_ = bf16[608,128]{1,0:T(8,128)(2,1)S(1)} collective-permute-done((bf16[608,128]{1,0:T(8,128)(2,1)S(1)}, bf16[608,128]{1,0:T(8,128)(2,1)S(1)}, u32[]{:S(2)}, u32[]{:S(2)}) %collective-permute-start.36) | collective-permute-done | bytes 155680 | tf_op jit(solution)/shard_map/ppermute | solution.py:763
  90.1 1.0 %self_final.1 = (bf16[128,768]{1,0:T(8,128)(2,1)}, f32[96,192]{1,0:T(8,128)}, f32[96,192]{1,0:T(8,128)}, f32[96,192]{1,0:T(8,128)}, f32[192,96]{1,0:T(8,128)}, /...) custom-call(bf16[608,128]{1,0:T(8,128)(2,1)S(1)} %get-tuple-element.249.refs_0_, ...), custom_call_target="tpu_custom_call" | custom-call | tf_op jit(solution)/shard_map/self_final/pallas_call | solution.py:736
  (88 shorter events, 1.9 us)
Async XLA Ops:
  0.7 3.1 %copy-start = (bf16[768,192]{0,1:T(8,128)(2,1)S(1)}, bf16[768,192]{0,1:T(8,128)(2,1)}, u32[]{:S(2)}) copy-start(bf16[768,192]{0,1:T(8,128)(2,1)} %param.40) | copy-start | bytes 884740
  0.7 3.1 %copy-start.1 = (bf16[768,192]{0,1:T(8,128)(2,1)S(1)}, bf16[768,192]{0,1:T(8,128)(2,1)}, u32[]{:S(2)}) copy-start(bf16[768,192]{0,1:T(8,128)(2,1)} %param.41) | copy-start | bytes 884740
  0.7 4.3 %copy-start.3 = (bf16[1,256,768]{2,1,0:T(8,128)(2,1)S(1)}, bf16[1,256,768]{2,1,0:T(8,128)(2,1)}, u32[]{:S(2)}) copy-start(bf16[1,256,768]{2,1,0:T(8,128)(2,1)} %param.23) | copy-start | bytes 1179652
  0.7 4.3 %copy-start.5 = (bf16[768,192]{0,1:T(8,128)(2,1)S(1)}, bf16[768,192]{0,1:T(8,128)(2,1)}, u32[]{:S(2)}) copy-start(bf16[768,192]{0,1:T(8,128)(2,1)} %param.34) | copy-start | bytes 884740
  0.7 4.3 %copy-start.6 = (bf16[768,192]{0,1:T(8,128)(2,1)S(1)}, bf16[768,192]{0,1:T(8,128)(2,1)}, u32[]{:S(2)}) copy-start(bf16[768,192]{0,1:T(8,128)(2,1)} %param.35) | copy-start | bytes 884740
  0.7 4.3 %copy-start.10 = (bf16[768,192]{0,1:T(8,128)(2,1)S(1)}, bf16[768,192]{0,1:T(8,128)(2,1)}, u32[]{:S(2)}) copy-start(bf16[768,192]{0,1:T(8,128)(2,1)} %param.33) | copy-start | bytes 884740
  0.7 4.3 %copy-start.11 = (bf16[192,768]{1,0:T(8,128)(2,1)S(1)}, bf16[192,768]{1,0:T(8,128)(2,1)}, u32[]{:S(2)}) copy-start(bf16[192,768]{1,0:T(8,128)(2,1)} %refs_2_.5) | copy-start | bytes 884740
  0.7 4.3 %copy-start.14 = (f32[768]{0:T(1024)S(1)}, f32[768]{0:T(1024)}, u32[]{:S(2)}) copy-start(f32[768]{0:T(1024)} %refs_3_.7) | copy-start | bytes 9220
  0.7 4.3 %copy-start.15 = (s32[256]{0:T(256)S(1)}, s32[256]{0:T(256)}, u32[]{:S(2)}) copy-start(s32[256]{0:T(256)} %param.29) | copy-start | bytes 3076
  0.7 4.3 %copy-start.18 = (f32[32,3]{0,1:T(4,128)S(1)}, f32[32,3]{0,1:T(4,128)}, u32[]{:S(2)}) copy-start(f32[32,3]{0,1:T(4,128)} %param.37) | copy-start | bytes 1156
  0.8 8.5 %collective-permute-start.1 = (bf16[128,768]{1,0:T(8,128)(2,1)}, bf16[128,768]{1,0:T(8,128)(2,1)S(1)}, u32[]{:S(2)}, u32[]{:S(2)}) collective-permute-start(bf16[128,768]{1,0:T(8,128)(2,1)} %bitcast.33), channel_id=1, source_target_pairs={{0,2},{1,3},{2,0},{3,1},{4,6},{5,7},{6,4},{7,5},{8,10},{9,11},{10,... | collective-permute-start | bytes 589832 | tf_op jit(solution)/shard_map/ppermute | solution.py:759
  3.8 3.4 %collective-permute-start.3 = (bf16[192,768]{1,0:T(8,128)(2,1)S(1)}, bf16[192,768]{1,0:T(8,128)(2,1)S(1)}, u32[]{:S(2)}, u32[]{:S(2)}) collective-permute-start(bf16[192,768]{1,0:T(8,128)(2,1)S(1)} %bitcast.19), channel_id=1, source_target_pairs={{0,1},{1,0},{2,3},{3,2},{4,5},{5,4},{6,7},{7,6},{8,9},{9,8},{10,11... | collective-permute-start | bytes 884744 | tf_op jit(solution)/shard_map/ppermute | solution.py:755
  3.8 3.5 %collective-permute-start.4 = (bf16[192,768]{1,0:T(8,128)(2,1)S(1)}, bf16[192,768]{1,0:T(8,128)(2,1)S(1)}, u32[]{:S(2)}, u32[]{:S(2)}) collective-permute-start(bf16[192,768]{1,0:T(8,128)(2,1)S(1)} %bitcast.24), channel_id=1, source_target_pairs={{0,1},{1,0},{2,3},{3,2},{4,5},{5,4},{6,7},{7,6},{8,9},{9,8},{10,11... | collective-permute-start | bytes 884744 | tf_op jit(solution)/shard_map/ppermute | solution.py:755
  5.0 2.2 %copy-start.8 = (bf16[768,192]{0,1:T(8,128)(2,1)S(1)}, bf16[768,192]{0,1:T(8,128)(2,1)}, u32[]{:S(2)}) copy-start(bf16[768,192]{0,1:T(8,128)(2,1)} %param.39) | copy-start | bytes 884740
  5.1 2.2 %copy-start.9 = (bf16[192,768]{1,0:T(8,128)(2,1)S(1)}, bf16[192,768]{1,0:T(8,128)(2,1)}, u32[]{:S(2)}) copy-start(bf16[192,768]{1,0:T(8,128)(2,1)} %refs_5_.1) | copy-start | bytes 884740
  5.1 2.7 %copy-start.4 = (bf16[1,128,768]{2,1,0:T(8,128)(2,1)S(1)}, bf16[1,128,768]{2,1,0:T(8,128)(2,1)}, u32[]{:S(2)}) copy-start(bf16[1,128,768]{2,1,0:T(8,128)(2,1)} %param.24) | copy-start | bytes 589828
  6.6 1.6 %collective-permute-start.5 = (bf16[64,768]{1,0:T(8,128)(2,1)S(1)}, bf16[64,768]{1,0:T(8,128)(2,1)S(1)}, u32[]{:S(2)}, u32[]{:S(2)}) collective-permute-start(bf16[64,768]{1,0:T(8,128)(2,1)S(1)} %get-tuple-element.152), channel_id=1, source_target_pairs={{0,1},{1,0},{2,3},{3,2},{4,5},{5,4},{6,7},{7,6},{8,9},{9,8},{10,11... | collective-permute-start | bytes 294920 | tf_op jit(solution)/shard_map/ppermute | solution.py:755
  6.8 1.5 %collective-permute-start.6 = (bf16[64,768]{1,0:T(8,128)(2,1)S(1)}, bf16[64,768]{1,0:T(8,128)(2,1)S(1)}, u32[]{:S(2)}, u32[]{:S(2)}) collective-permute-start(bf16[64,768]{1,0:T(8,128)(2,1)S(1)} %get-tuple-element.153), channel_id=1, source_target_pairs={{0,1},{1,0},{2,3},{3,2},{4,5},{5,4},{6,7},{7,6},{8,9},{9,8},{10,11... | collective-permute-start | bytes 294920 | tf_op jit(solution)/shard_map/ppermute | solution.py:755
  7.2 6.3 %collective-permute-start.8 = (bf16[192,768]{1,0:T(8,128)(2,1)S(1)}, bf16[192,768]{1,0:T(8,128)(2,1)S(1)}, u32[]{:S(2)}, u32[]{:S(2)}) collective-permute-start(bf16[192,768]{1,0:T(8,128)(2,1)S(1)} %bitcast.44), channel_id=1, source_target_pairs={{0,1},{1,0},{2,3},{3,2},{4,5},{5,4},{6,7},{7,6},{8,9},{9,8},{10,11... | collective-permute-start | bytes 884744 | tf_op jit(solution)/shard_map/ppermute | solution.py:755
  7.3 6.2 %collective-permute-start.9 = (bf16[192,768]{1,0:T(8,128)(2,1)S(1)}, bf16[192,768]{1,0:T(8,128)(2,1)S(1)}, u32[]{:S(2)}, u32[]{:S(2)}) collective-permute-start(bf16[192,768]{1,0:T(8,128)(2,1)S(1)} %copy-done.9), channel_id=1, source_target_pairs={{0,1},{1,0},{2,3},{3,2},{4,5},{5,4},{6,7},{7,6},{8,9},{9,8},{10,11... | collective-permute-start | bytes 884744 | tf_op jit(solution)/shard_map/ppermute | solution.py:755
  8.3 4.6 %copy-start.7 = (bf16[768,768]{1,0:T(8,128)(2,1)S(1)}, bf16[768,768]{1,0:T(8,128)(2,1)}, u32[]{:S(2)}) copy-start(bf16[768,768]{1,0:T(8,128)(2,1)} %up_own.1) | copy-start | bytes 3538948
  8.3 4.6 %copy-start.2 = (bf16[768,768]{1,0:T(8,128)(2,1)S(1)}, bf16[768,768]{1,0:T(8,128)(2,1)}, u32[]{:S(2)}) copy-start(bf16[768,768]{1,0:T(8,128)(2,1)} %refs_2_.4) | copy-start | bytes 3538948
  8.3 7.6 %collective-permute-start.7 = (bf16[144,768]{1,0:T(8,128)(2,1)S(1)}, bf16[144,768]{1,0:T(8,128)(2,1)S(1)}, u32[]{:S(2)}, u32[]{:S(2)}) collective-permute-start(bf16[144,768]{1,0:T(8,128)(2,1)S(1)} %self_sum.1.refs_11_.refs_1_), channel_id=1, source_target_pairs={{0,2},{1,3},{2,0},{3,1},{4,6},{5,7},{6,4},{7,5},{8,10},{9,11},{10,... | collective-permute-start | bytes 663560 | tf_op jit(solution)/shard_map/ppermute | solution.py:759
  9.2 2.5 %collective-permute-start = (bf16[128,768]{1,0:T(8,128)(2,1)S(1)}, bf16[128,768]{1,0:T(8,128)(2,1)S(1)}, u32[]{:S(2)}, u32[]{:S(2)}) collective-permute-start(bf16[128,768]{1,0:T(8,128)(2,1)S(1)} %bitcast.35), channel_id=1, source_target_pairs={{0,1},{1,0},{2,3},{3,2},{4,5},{5,4},{6,7},{7,6},{8,9},{9,8},{10,11... | collective-permute-start | bytes 589832 | tf_op jit(solution)/shard_map/ppermute | solution.py:755
  9.2 2.5 %collective-permute-start.2 = (bf16[128,768]{1,0:T(8,128)(2,1)S(1)}, bf16[128,768]{1,0:T(8,128)(2,1)S(1)}, u32[]{:S(2)}, u32[]{:S(2)}) collective-permute-start(bf16[128,768]{1,0:T(8,128)(2,1)S(1)} %collective-permute-done.1.refs_1_.refs_4_.refs_6_), channel_id=1, source_target_pairs={{0,1},{1,0},{2,3},{3,2},{4,5},{5,4},{6,7},{7,6},{8,9},{9,8},{10,11... | collective-permute-start | bytes 589832 | tf_op jit(solution)/shard_map/ppermute | solution.py:755
  11.7 4.3 %copy-start.12 = (f32[768]{0:T(1024)S(1)}, f32[768]{0:T(1024)}, u32[]{:S(2)}) copy-start(f32[768]{0:T(1024)} %refs_3_.6) | copy-start | bytes 9220
  12.9 11.8 %collective-permute-start.11 = (bf16[768,768]{1,0:T(8,128)(2,1)S(1)}, bf16[768,768]{1,0:T(8,128)(2,1)S(1)}, u32[]{:S(2)}, u32[]{:S(2)}) collective-permute-start(bf16[768,768]{1,0:T(8,128)(2,1)S(1)} %copy-done.7), channel_id=1, source_target_pairs={{0,1},{1,0},{2,3},{3,2},{4,5},{5,4},{6,7},{7,6},{8,9},{9,8},{10,11... | collective-permute-start | bytes 3538952 | tf_op jit(solution)/shard_map/ppermute | solution.py:755
  13.0 6.6 %collective-permute-start.12 = (bf16[768,768]{1,0:T(8,128)(2,1)S(1)}, bf16[768,768]{1,0:T(8,128)(2,1)S(1)}, u32[]{:S(2)}, u32[]{:S(2)}) collective-permute-start(bf16[768,768]{1,0:T(8,128)(2,1)S(1)} %copy-done.2), channel_id=1, source_target_pairs={{0,1},{1,0},{2,3},{3,2},{4,5},{5,4},{6,7},{7,6},{8,9},{9,8},{10,11... | collective-permute-start | bytes 3538952 | tf_op jit(solution)/shard_map/ppermute | solution.py:755
  16.0 3.3 %copy-start.16 = (bf16[1,256,768]{2,1,0:T(8,128)(2,1)S(1)}, bf16[1,256,768]{2,1,0:T(8,128)(2,1)}, u32[]{:S(2)}) copy-start(bf16[1,256,768]{2,1,0:T(8,128)(2,1)} %param.31) | copy-start | bytes 1179652
  16.0 3.3 %copy-start.17 = (f32[16,256]{1,0:T(8,128)S(1)}, f32[16,256]{1,0:T(8,128)}, u32[]{:S(2)}) copy-start(f32[16,256]{1,0:T(8,128)} %refs_2_.3) | copy-start | bytes 49156
  18.4 6.3 %collective-permute-start.10 = (bf16[128,768]{1,0:T(8,128)(2,1)S(1)}, bf16[128,768]{1,0:T(8,128)(2,1)S(1)}, u32[]{:S(2)}, u32[]{:S(2)}) collective-permute-start(bf16[128,768]{1,0:T(8,128)(2,1)S(1)} %get-tuple-element.163.refs_0_), channel_id=1, source_target_pairs={{0,2},{1,3},{2,0},{3,1},{4,6},{5,7},{6,4},{7,5},{8,10},{9,11},{10,... | collective-permute-start | bytes 589832 | tf_op jit(solution)/shard_map/ppermute | solution.py:759
  19.3 5.4 %collective-permute-start.13 = (bf16[128,960]{1,0:T(8,128)(2,1)S(1)}, bf16[128,960]{1,0:T(8,128)(2,1)S(1)}, u32[]{:S(2)}, u32[]{:S(2)}) collective-permute-start(bf16[128,960]{1,0:T(8,128)(2,1)S(1)} %get-tuple-element.173), channel_id=1, source_target_pairs={{0,1},{1,0},{2,3},{3,2},{4,5},{5,4},{6,7},{7,6},{8,9},{9,8},{10,11... | collective-permute-start | bytes 737288 | tf_op jit(solution)/shard_map/ppermute | solution.py:755
  20.4 4.3 %copy-start.13 = (f32[768]{0:T(1024)S(1)}, f32[768]{0:T(1024)}, u32[]{:S(2)}) copy-start(f32[768]{0:T(1024)} %refs_3_.5) | copy-start | bytes 9220
  25.7 2.1 %collective-permute-start.15 = (bf16[128,2304]{1,0:T(8,128)(2,1)S(1)}, bf16[128,2304]{1,0:T(8,128)(2,1)S(1)}, u32[]{:S(2)}, u32[]{:S(2)}) collective-permute-start(bf16[128,2304]{1,0:T(8,128)(2,1)S(1)} %get-tuple-element.185.refs_1_), channel_id=1, source_target_pairs={{0,1},{1,0},{2,3},{3,2},{4,5},{5,4},{6,7},{7,6},{8,9},{9,8},{10,11... | collective-permute-start | bytes 1769480 | tf_op jit(solution)/shard_map/ppermute | solution.py:755
  26.6 7.4 %collective-permute-start.14 = (bf16[128,768]{1,0:T(8,128)(2,1)S(1)}, bf16[128,768]{1,0:T(8,128)(2,1)S(1)}, u32[]{:S(2)}, u32[]{:S(2)}) collective-permute-start(bf16[128,768]{1,0:T(8,128)(2,1)S(1)} %get-tuple-element.176.refs_6_.refs_0_), channel_id=1, source_target_pairs={{0,2},{1,3},{2,0},{3,1},{4,6},{5,7},{6,4},{7,5},{8,10},{9,11},{10,... | collective-permute-start | bytes 589832 | tf_op jit(solution)/shard_map/ppermute | solution.py:759
  28.8 16.0 %collective-permute-start.20 = (bf16[4,96,768]{2,1,0:T(8,128)(2,1)S(1)}, bf16[4,96,768]{2,1,0:T(8,128)(2,1)S(1)}, u32[]{:S(2)}, u32[]{:S(2)}) collective-permute-start(bf16[4,96,768]{2,1,0:T(8,128)(2,1)S(1)} %get-tuple-element.208), channel_id=1, source_target_pairs={{0,4},{4,0},{8,12},{12,8},{16,20},{20,16},{24,28},{28,24},{1,5},{5... | collective-permute-start | bytes 1769480 | tf_op jit(solution)/shard_map/ppermute | solution.py:763
  30.4 15.6 %collective-permute-start.21 = (bf16[4,96,768]{2,1,0:T(8,128)(2,1)S(1)}, bf16[4,96,768]{2,1,0:T(8,128)(2,1)S(1)}, u32[]{:S(2)}, u32[]{:S(2)}) collective-permute-start(bf16[4,96,768]{2,1,0:T(8,128)(2,1)S(1)} %get-tuple-element.210), channel_id=1, source_target_pairs={{0,8},{4,12},{8,0},{12,4},{16,24},{20,28},{24,16},{28,20},{1,9},{5... | collective-permute-start | bytes 1769480 | tf_op jit(solution)/shard_map/ppermute | solution.py:763
  36.7 2.4 %collective-permute-start.17 = (bf16[1024,192]{1,0:T(8,128)(2,1)S(1)}, bf16[1024,192]{1,0:T(8,128)(2,1)S(1)}, u32[]{:S(2)}, u32[]{:S(2)}) collective-permute-start(bf16[1024,192]{1,0:T(8,128)(2,1)S(1)} %source_grad.1.refs_15_), channel_id=1, source_target_pairs={{0,1},{1,0},{2,3},{3,2},{4,5},{5,4},{6,7},{7,6},{8,9},{9,8},{10,11... | collective-permute-start | bytes 1179656 | tf_op jit(solution)/shard_map/ppermute | solution.py:755
  36.8 2.3 %collective-permute-start.18 = (bf16[128,960]{1,0:T(8,128)(2,1)S(1)}, bf16[128,960]{1,0:T(8,128)(2,1)S(1)}, u32[]{:S(2)}, u32[]{:S(2)}) collective-permute-start(bf16[128,960]{1,0:T(8,128)(2,1)S(1)} %get-tuple-element.200), channel_id=1, source_target_pairs={{0,1},{1,0},{2,3},{3,2},{4,5},{5,4},{6,7},{7,6},{8,9},{9,8},{10,11... | collective-permute-start | bytes 737288 | tf_op jit(solution)/shard_map/ppermute | solution.py:755
  37.3 7.2 %collective-permute-start.16 = (bf16[128,768]{1,0:T(8,128)(2,1)S(1)}, bf16[128,768]{1,0:T(8,128)(2,1)S(1)}, u32[]{:S(2)}, u32[]{:S(2)}) collective-permute-start(bf16[128,768]{1,0:T(8,128)(2,1)S(1)} %get-tuple-element.190.refs_0_), channel_id=1, source_target_pairs={{0,2},{1,3},{2,0},{3,1},{4,6},{5,7},{6,4},{7,5},{8,10},{9,11},{10,... | collective-permute-start | bytes 589832 | tf_op jit(solution)/shard_map/ppermute | solution.py:759
  40.8 11.6 %collective-permute-start.23 = (bf16[4,96,384]{2,1,0:T(8,128)(2,1)S(1)}, bf16[4,96,384]{2,1,0:T(8,128)(2,1)S(1)}, u32[]{:S(2)}, u32[]{:S(2)}) collective-permute-start(bf16[4,96,384]{2,1,0:T(8,128)(2,1)S(1)} %get-tuple-element.214), channel_id=1, source_target_pairs={{0,4},{4,0},{8,12},{12,8},{16,20},{20,16},{24,28},{28,24},{1,5},{5... | collective-permute-start | bytes 884744 | tf_op jit(solution)/shard_map/ppermute | solution.py:763
  42.4 10.1 %collective-permute-start.24 = (bf16[4,96,384]{2,1,0:T(8,128)(2,1)S(1)}, bf16[4,96,384]{2,1,0:T(8,128)(2,1)S(1)}, u32[]{:S(2)}, u32[]{:S(2)}) collective-permute-start(bf16[4,96,384]{2,1,0:T(8,128)(2,1)S(1)} %get-tuple-element.216), channel_id=1, source_target_pairs={{0,8},{4,12},{8,0},{12,4},{16,24},{20,28},{24,16},{28,20},{1,9},{5... | collective-permute-start | bytes 884744 | tf_op jit(solution)/shard_map/ppermute | solution.py:763
  44.7 1.5 %collective-permute-start.19 = (bf16[144,768]{1,0:T(8,128)(2,1)S(1)}, bf16[144,768]{1,0:T(8,128)(2,1)S(1)}, u32[]{:S(2)}, u32[]{:S(2)}) collective-permute-start(bf16[144,768]{1,0:T(8,128)(2,1)S(1)} %get-tuple-element.204.refs_4_.refs_0_.refs_8_), channel_id=1, source_target_pairs={{0,1},{1,0},{2,3},{3,2},{4,5},{5,4},{6,7},{7,6},{8,9},{9,8},{10,11... | collective-permute-start | bytes 663560 | tf_op jit(solution)/shard_map/ppermute | solution.py:755
  48.1 4.7 %collective-permute-start.22 = (bf16[144,768]{1,0:T(8,128)(2,1)S(1)}, bf16[144,768]{1,0:T(8,128)(2,1)S(1)}, u32[]{:S(2)}, u32[]{:S(2)}) collective-permute-start(bf16[144,768]{1,0:T(8,128)(2,1)S(1)} %get-tuple-element.213), channel_id=1, source_target_pairs={{0,1},{1,0},{2,3},{3,2},{4,5},{5,4},{6,7},{7,6},{8,9},{9,8},{10,11... | collective-permute-start | bytes 663560 | tf_op jit(solution)/shard_map/ppermute | solution.py:755
  48.3 11.4 %collective-permute-start.26 = (bf16[2,96,768]{2,1,0:T(8,128)(2,1)S(1)}, bf16[2,96,768]{2,1,0:T(8,128)(2,1)S(1)}, u32[]{:S(2)}, u32[]{:S(2)}) collective-permute-start(bf16[2,96,768]{2,1,0:T(8,128)(2,1)S(1)} %get-tuple-element.211.refs_11_), channel_id=1, source_target_pairs={{0,8},{4,12},{8,0},{12,4},{16,24},{20,28},{24,16},{28,20},{1,9},{5... | collective-permute-start | bytes 884744 | tf_op jit(solution)/shard_map/ppermute | solution.py:763
  49.8 9.9 %collective-permute-start.27 = (bf16[2,96,768]{2,1,0:T(8,128)(2,1)S(1)}, bf16[2,96,768]{2,1,0:T(8,128)(2,1)S(1)}, u32[]{:S(2)}, u32[]{:S(2)}) collective-permute-start(bf16[2,96,768]{2,1,0:T(8,128)(2,1)S(1)} %get-tuple-element.230), channel_id=1, source_target_pairs={{0,4},{4,0},{8,12},{12,8},{16,20},{20,16},{24,28},{28,24},{1,5},{5... | collective-permute-start | bytes 884744 | tf_op jit(solution)/shard_map/ppermute | solution.py:763
  52.8 9.6 %collective-permute-start.25 = (bf16[144,768]{1,0:T(8,128)(2,1)S(1)}, bf16[144,768]{1,0:T(8,128)(2,1)S(1)}, u32[]{:S(2)}, u32[]{:S(2)}) collective-permute-start(bf16[144,768]{1,0:T(8,128)(2,1)S(1)} %input_sum.1.refs_4_.refs_0_), channel_id=1, source_target_pairs={{0,2},{1,3},{2,0},{3,1},{4,6},{5,7},{6,4},{7,5},{8,10},{9,11},{10,... | collective-permute-start | bytes 663560 | tf_op jit(solution)/shard_map/ppermute | solution.py:759
  53.7 17.8 %collective-permute-start.30 = (bf16[1376,128]{1,0:T(8,128)(2,1)S(1)}, bf16[1376,128]{1,0:T(8,128)(2,1)S(1)}, u32[]{:S(2)}, u32[]{:S(2)}) collective-permute-start(bf16[1376,128]{1,0:T(8,128)(2,1)S(1)} %get-tuple-element.234), channel_id=1, source_target_pairs={{0,8},{4,12},{8,0},{12,4},{16,24},{20,28},{24,16},{28,20},{1,9},{5... | collective-permute-start | bytes 1056776 | tf_op jit(solution)/shard_map/ppermute | solution.py:763
  55.0 16.5 %collective-permute-start.29 = (bf16[2112,128]{1,0:T(8,128)(2,1)S(1)}, bf16[2112,128]{1,0:T(8,128)(2,1)S(1)}, u32[]{:S(2)}, u32[]{:S(2)}) collective-permute-start(bf16[2112,128]{1,0:T(8,128)(2,1)S(1)} %get-tuple-element.233), channel_id=1, source_target_pairs={{0,4},{4,0},{8,12},{12,8},{16,20},{20,16},{24,28},{28,24},{1,5},{5... | collective-permute-start | bytes 1622024 | tf_op jit(solution)/shard_map/ppermute | solution.py:763
  59.8 16.5 %collective-permute-start.39 = (bf16[192,768]{1,0:T(8,128)(2,1)S(1)}, bf16[192,768]{1,0:T(8,128)(2,1)S(1)}, u32[]{:S(2)}, u32[]{:S(2)}) collective-permute-start(bf16[192,768]{1,0:T(8,128)(2,1)S(1)} %get-tuple-element.231.refs_2_), channel_id=1, source_target_pairs={{0,16},{4,20},{8,24},{12,28},{16,0},{20,4},{24,8},{28,12},{1,17},{... | collective-permute-start | bytes 884744 | tf_op jit(solution)/shard_map/ppermute | solution.py:763
  62.4 10.1 %collective-permute-start.28 = (bf16[128,768]{1,0:T(8,128)(2,1)S(1)}, bf16[128,768]{1,0:T(8,128)(2,1)S(1)}, u32[]{:S(2)}, u32[]{:S(2)}) collective-permute-start(bf16[128,768]{1,0:T(8,128)(2,1)S(1)} %ffn_out.1.refs_6_), channel_id=1, source_target_pairs={{0,2},{1,3},{2,0},{3,1},{4,6},{5,7},{6,4},{7,5},{8,10},{9,11},{10,... | collective-permute-start | bytes 589832 | tf_op jit(solution)/shard_map/ppermute | solution.py:759
  63.8 7.7 %collective-permute-start.31 = (bf16[16,256]{1,0:T(8,128)(2,1)S(1)}, bf16[16,256]{1,0:T(8,128)(2,1)S(1)}, u32[]{:S(2)}, u32[]{:S(2)}) collective-permute-start(bf16[16,256]{1,0:T(8,128)(2,1)S(1)} %gain.1.gains), channel_id=1, source_target_pairs={{0,4},{4,0},{8,12},{12,8},{16,20},{20,16},{24,28},{28,24},{1,5},{5... | collective-permute-start | bytes 24584 | tf_op jit(solution)/shard_map/ppermute | solution.py:763
  71.7 6.5 %collective-permute-start.34 = (bf16[208,256]{1,0:T(8,128)(2,1)S(1)}, bf16[208,256]{1,0:T(8,128)(2,1)S(1)}, u32[]{:S(2)}, u32[]{:S(2)}) collective-permute-start(bf16[208,256]{1,0:T(8,128)(2,1)S(1)} %get-tuple-element.238.refs_8_), channel_id=1, source_target_pairs={{0,4},{4,0},{8,12},{12,8},{16,20},{20,16},{24,28},{28,24},{1,5},{5... | collective-permute-start | bytes 319496 | tf_op jit(solution)/shard_map/ppermute | solution.py:763
  72.1 10.2 %collective-permute-start.33 = (bf16[208,512]{1,0:T(8,128)(2,1)S(1)}, bf16[208,512]{1,0:T(8,128)(2,1)S(1)}, u32[]{:S(2)}, u32[]{:S(2)}) collective-permute-start(bf16[208,512]{1,0:T(8,128)(2,1)S(1)} %get-tuple-element.240), channel_id=1, source_target_pairs={{0,8},{4,12},{8,0},{12,4},{16,24},{20,28},{24,16},{28,20},{1,9},{5... | collective-permute-start | bytes 638984 | tf_op jit(solution)/shard_map/ppermute | solution.py:763
  72.9 11.7 %collective-permute-start.32 = (bf16[256,768]{1,0:T(8,128)(2,1)S(1)}, bf16[256,768]{1,0:T(8,128)(2,1)S(1)}, u32[]{:S(2)}, u32[]{:S(2)}) collective-permute-start(bf16[256,768]{1,0:T(8,128)(2,1)S(1)} %input_grad.1.refs_3_.refs_0_), channel_id=1, source_target_pairs={{0,1},{1,0},{2,3},{3,2},{4,5},{5,4},{6,7},{7,6},{8,9},{9,8},{10,11... | collective-permute-start | bytes 1179656 | tf_op jit(solution)/shard_map/ppermute | solution.py:755
  73.0 10.8 %collective-permute-start.38 = (bf16[576,128]{1,0:T(8,128)(2,1)S(1)}, bf16[576,128]{1,0:T(8,128)(2,1)S(1)}, u32[]{:S(2)}, u32[]{:S(2)}) collective-permute-start(bf16[576,128]{1,0:T(8,128)(2,1)S(1)} %get-tuple-element.262), channel_id=1, source_target_pairs={{0,16},{4,20},{8,24},{12,28},{16,0},{20,4},{24,8},{28,12},{1,17},{... | collective-permute-start | bytes 442376 | tf_op jit(solution)/shard_map/ppermute | solution.py:763
  76.3 1.8 %collective-permute-start.35 = (bf16[256,768]{1,0:T(8,128)(2,1)S(1)}, bf16[256,768]{1,0:T(8,128)(2,1)S(1)}, u32[]{:S(2)}, u32[]{:S(2)}) collective-permute-start(bf16[256,768]{1,0:T(8,128)(2,1)S(1)} %get-tuple-element.244), channel_id=1, source_target_pairs={{0,1},{1,0},{2,3},{3,2},{4,5},{5,4},{6,7},{7,6},{8,9},{9,8},{10,11... | collective-permute-start | bytes 1179656 | tf_op jit(solution)/shard_map/ppermute | solution.py:755
  82.4 7.7 %collective-permute-start.36 = (bf16[608,128]{1,0:T(8,128)(2,1)S(1)}, bf16[608,128]{1,0:T(8,128)(2,1)S(1)}, u32[]{:S(2)}, u32[]{:S(2)}) collective-permute-start(bf16[608,128]{1,0:T(8,128)(2,1)S(1)} %get-tuple-element.246.refs_2_), channel_id=1, source_target_pairs={{0,16},{4,20},{8,24},{12,28},{16,0},{20,4},{24,8},{28,12},{1,17},{... | collective-permute-start | bytes 466952 | tf_op jit(solution)/shard_map/ppermute | solution.py:763
  82.6 7.5 %collective-permute-start.37 = (bf16[128,768]{1,0:T(8,128)(2,1)S(1)}, bf16[128,768]{1,0:T(8,128)(2,1)S(1)}, u32[]{:S(2)}, u32[]{:S(2)}) collective-permute-start(bf16[128,768]{1,0:T(8,128)(2,1)S(1)} %get-tuple-element.250), channel_id=1, source_target_pairs={{0,2},{1,3},{2,0},{3,1},{4,6},{5,7},{6,4},{7,5},{8,10},{9,11},{10,... | collective-permute-start | bytes 589832 | tf_op jit(solution)/shard_map/ppermute | solution.py:759

commit v7 on v6

--- a/solution.py
+++ b/solution.py
@@ -618,7 +618,7 @@
 def gain_kernel(chip_own, chip_other, out):
     half = chip_own.shape[0] - EXTRA
     gain = of_high_low(chip_own[half:]) + of_high_low(chip_other[half:])
-    out[...] = vector_rows(gain, out.shape[1], out.shape[0], 2).astype(BF16)
+    out[...] = vector_rows(gain, out.shape[1], out.shape[0], 0).astype(BF16)
 
 
 def spread_out(target, parts, start=0):
@@ -656,23 +656,29 @@
         for entry in range(2):
             part = slice(entry * size, (entry + 1) * size)
             start = x_base + (first + entry) * size * (large // PIECE)
-            sa_out[part] = low_sum(sa_keep[first + entry], gathered(x_got, size, large, start))
+            part_sum = low_sum(sa_keep[first + entry], gathered(x_got, size, large, start))
+            base = spread_out(sa_out, [part_sum], entry * size * (large // PIECE))
             start = zo_base + (first + entry) * step
             sb_out[part] = low_sum(sb_keep[first + entry], gathered(zo_got, size, small, start))
-        sa_out[2 * size :, :small] = gain
+        sa_out[base:] = gain
         sb_out[2 * size :] = extra
 
 
 def round_five_kernel(size, sa_keep, sa_got, sb_keep, sb_got, send, keep):
-    large, small = sa_keep.shape[1], sb_keep.shape[1]
-    extra = low_sum(
-        low_sum(sa_keep[2 * size :, :small], sa_got[2 * size :, :small]), low_sum(sb_keep[2 * size :], sb_got[2 * size :])
-    )
+    small = sb_keep.shape[1]
+    extra_count = sb_keep.shape[0] - 2 * size
+    step = (sa_keep.shape[0] - EXTRA) // 2
+    large = step // size * PIECE
+    gain = both(sa_keep[2 * step :], sa_got[2 * step :])
+    gain = jnp.concatenate([gain[index : index + 1] for index in range((large + small) // PIECE)], 1)
+    extra = vector_rows(gain, small, extra_count, 2) + both(sb_keep[2 * size :], sb_got[2 * size :])
+    extra = extra.astype(BF16)
     for entry, target in enumerate((keep, send)):
         part = slice(entry * size, (entry + 1) * size)
-        base = spread_out(target, [low_sum(sa_keep[part], sa_got[part])])
+        whole = slice(entry * step, (entry + 1) * step)
+        target[:step] = low_sum(sa_keep[whole], sa_got[whole])
         part = jnp.concatenate([low_sum(sb_keep[part], sb_got[part]), extra], 0)
-        spread_out(target, [part], base)
+        spread_out(target, [part], step)
 
 
 def ffn_final_kernel(keep, got, up, down):
@@ -978,7 +984,7 @@
             ffn_third_kernel, "ffn_third", [((2 * size, width), BF16)] * 2, [up_keep, up_got, down_keep, down_got]
         )
         ffn_got = to_peer(ffn_send, 2)
-        gains = go(gain_kernel, "gain", [((extra_count, small), BF16)], [chip_five, other_five], us=LONG)
+        gains = go(gain_kernel, "gain", [((EXTRA, PIECE), BF16)], [chip_five, other_five], us=LONG)
         gains_got = to_peer(gains, 0)
         branch_source, _ = lax.optimization_barrier((branch_out, gains))
     else:
@@ -989,7 +995,8 @@
         rows = 2 * size + extra_count
         cross_send, cross_keep, sa_send, sa_keep, sb_send, sb_keep = go(
             round_four_kernel, "round_four",
-            [((size * 2 * wide // PIECE, PIECE), BF16)] * 2 + [((rows, large), BF16)] * 2 + [((rows, small), BF16)] * 2,
+            [((size * 2 * wide // PIECE, PIECE), BF16)] * 2 + [((2 * size * large // PIECE + EXTRA, PIECE), BF16)] * 2
+            + [((rows, small), BF16)] * 2,
             [x_got, zo_got, ca_keep, cb_keep, sa_keep, sb_keep, extra, gains, gains_got],
         )
         sa_got = to_peer(sa_send, 1)

time: 91.3 us -> 91.1 us (level)
  transfers between devices with their start and end apart: 40 -> 40, of which waited for: 11 -> 12; matrix products, arithmetic and copies ran while one was open for 0% -> 0% of each run, Pallas kernels for 26% -> 26%
where the time goes in v7:
time: 91.1 us; the launch traced here: 90.9 us
  starting transfers between devices  31.7 us (35%)
  waiting for transfers between devices  30 us (33%)
  Pallas kernels  25.4 us (28%)
  between operations  3.82 us (4%)
    pallas_call x34, Pallas kernels, run(): pl.pallas_call(body, out_shape=shapes, in_specs=place, out_specs=[vmem] *...  25.4 us
    ppermute x14, waiting for transfers between devices, to_peer(): lax.ppermute(value, 'dp', [(i, i ^ 1 << bit) for i in range(lax.axis_size...  20.8 us
    ppermute x14, starting transfers between devices, to_peer(): lax.ppermute(value, 'dp', [(i, i ^ 1 << bit) for i in range(lax.axis_size...  18 us
    ppermute x8, starting transfers between devices, to_chip(): lax.ppermute(value, 'tensor', [(i, i ^ 2) for i in range(lax.axis_size('t...  9.82 us
    ppermute x8, waiting for transfers between devices, to_chip(): lax.ppermute(value, 'tensor', [(i, i ^ 2) for i in range(lax.axis_size('t...  7.18 us
    ppermute x18, starting transfers between devices, to_core(): lax.ppermute(value, 'tensor', [(i, i ^ 1) for i in range(lax.axis_size('t...  3.88 us
    ppermute x18, waiting for transfers between devices, to_core(): lax.ppermute(value, 'tensor', [(i, i ^ 1) for i in range(lax.axis_size('t...  2.02 us
  transfers between devices with their start and end apart: 40, of which 12 were waited for; matrix products, arithmetic and copies ran while one was open for 0% of the time, Pallas kernels for 26%

profile of v7, /device:TPU:0, one launch (start us, length us, event | category | flops | bytes accessed | tf_op | source)
XLA Modules:
  0.0 90.9 jit_solution(1506800070025113104)
XLA Ops:
  0.8 3.0 %collective-permute-start.1 = (bf16[128,768]{1,0:T(8,128)(2,1)}, bf16[128,768]{1,0:T(8,128)(2,1)S(1)}, u32[]{:S(2)}, u32[]{:S(2)}) collective-permute-start(bf16[128,768]{1,0:T(8,128)(2,1)} %bitcast.33), channel_id=1, source_target_pairs={{0,2},{1,3},{2,0},{3,1},{4,6},{5,7},{6,4},{7,5},{8,10},{9,11},{10,... | collective-permute-start | bytes 589832 | tf_op jit(solution)/shard_map/ppermute | solution.py:765
  3.8 0.5 collective-permute-start.4
  5.1 1.6 %self_forward.1 = (bf16[128,768]{1,0:T(8,128)(2,1)S(1)}, bf16[64,768]{1,0:T(8,128)(2,1)S(1)}, bf16[64,768]{1,0:T(8,128)(2,1)S(1)}, bf16[256,768]{1,0:T(8,128)(2,...) custom-call(s32[1]{0:T(128)S(6)} %copy.40.refs_0_, ...), custom_call_target="tpu_custom_call" | custom-call | flops 4024999936 | tf_op jit(solution)/shard_map/self_forward/pallas_call | solution.py:742
  6.8 0.4 collective-permute-start.6
  7.3 0.4 collective-permute-start.9
  7.7 0.5 source_first.1
  8.3 0.9 collective-permute-start.7
  9.2 0.5 collective-permute-start.2
  11.7 1.2 %source_second.1 = (bf16[512,192]{1,0:T(8,128)(2,1)S(1)}, bf16[192,512]{1,0:T(8,128)(2,1)S(1)}, bf16[512,192]{1,0:T(8,128)(2,1)S(1)}, bf16[192,512]{1,0:T(8,128)(2,1)S(1)}) custom-call(bf16[128,768]{1,0:T(8,128)(2,1)S(1)} %collective-permute-done.refs_0_.refs_5_.refs_7_, bf16[128,768]{1,0:T(8,128)(2,1)S(1)} %collective-permute-done.1.refs_1_.refs_4_.refs_6_, ...), custom_call_target="tpu_custom_call" | custom-call | tf_op jit(solution)/shard_map/source_second/pallas_call | solution.py:742
  13.0 0.5 collective-permute-start.12
  13.5 2.4 %collective-permute-done.7.refs_2_ = bf16[144,768]{1,0:T(8,128)(2,1)S(1)} collective-permute-done((bf16[144,768]{1,0:T(8,128)(2,1)S(1)}, bf16[144,768]{1,0:T(8,128)(2,1)S(1)}, u32[]{:S(2)}, u32[]{:S(2)}) %collective-permute-start.7) | collective-permute-done | bytes 221216 | tf_op jit(solution)/shard_map/ppermute | solution.py:765
  16.0 2.5 %cross_forward.1 = (bf16[128,768]{1,0:T(8,128)(2,1)S(1)}, f32[128,768]{1,0:T(8,128)S(1)}, bf16[128,768]{1,0:T(8,128)(2,1)S(1)}, bf16[128,192]{1,0:T(8,128)(2,1)S...) custom-call(f32[512,128]{1,0:T(8,128)S(1)} %get-tuple-element.158.re, ...), custom_call_target="tpu_custom_call" | custom-call | tf_op jit(solution)/shard_map/cross_forward/pallas_call | solution.py:742
  18.4 0.9 collective-permute-start.10
  19.5 0.9 act_grad.1
  20.5 1.6 %source_back.1 = (bf16[192,256]{1,0:T(8,128)(2,1)S(1)}, bf16[256,192]{1,0:T(8,128)(2,1)S(1)}, bf16[192,512]{1,0:T(8,128)(2,1)S(1)}, bf16[512,192]{1,0:T(8,128)(2...) custom-call(bf16[256,768]{1,0:T(8,128)(2,1)S(1)} %get-tuple-element.170.refs_0_, ...), custom_call_target="tpu_custom_call" | custom-call | tf_op jit(solution)/shard_map/source_back/pallas_call | solution.py:742
  22.1 2.7 %collective-permute-done.10.refs_1_ = bf16[128,768]{1,0:T(8,128)(2,1)S(1)} collective-permute-done((bf16[128,768]{1,0:T(8,128)(2,1)S(1)}, bf16[128,768]{1,0:T(8,128)(2,1)S(1)}, u32[]{:S(2)}, u32[]{:S(2)}) %collective-permute-start.10) | collective-permute-done | bytes 196640 | tf_op jit(solution)/shard_map/ppermute | solution.py:765
  24.7 1.0 %ffn_peer.1 = (f32[128,768]{1,0:T(8,128)S(1)}, bf16[128,768]{1,0:T(8,128)(2,1)S(1)}, f32[128,768]{1,0:T(8,128)S(1)}, bf16[128,2304]{1,0:T(8,128)(2,1)S(1)}) custom-call(bf16[128,768]{1,0:T(8,128)(2,1)S(1)} %get-tuple-element.163.refs_0_, bf16[128,768]{1,0:T(8,128)(2,1)S(1)} %collective-permute-done.10.refs_1_, f32[128,768]{1,0:T(8,128)S(1)} %get-tuple-element.164.refs_2_, ...), custom_call_target="tpu_custom_call" | custom-call | tf_op jit(solution)/shard_map/ffn_peer/pallas_call | solution.py:742
  25.8 0.9 ffn_own.1
  26.6 0.9 collective-permute-start.14
  27.5 0.3 collective-permute-done.15.refs_1_
  27.8 1.0 %ffn_weights.1 = (bf16[4,96,768]{2,1,0:T(8,128)(2,1)S(1)}, bf16[4,96,768]{2,1,0:T(8,128)(2,1)S(1)}, bf16[4,96,768]{2,1,0:T(8,128)(2,1)S(1)}, bf16[4,96,768]{2,1,0:T(8,128)(2,1)S(1)}) custom-call(bf16[128,768]{1,0:T(8,128)(2,1)S(1)} %get-tuple-element.174.normed.refs_0_, bf16[128,2304]{1,0:T(8,128)(2,1)S(1)} %collective-permute-done.15.refs_1_, ...), custom_call_target="tpu_custom_call" | custom-call | flops 5750000128 | tf_op jit(solution)/shard_map/ffn_weights/pallas_call | solution.py:742
  28.8 1.6 %collective-permute-start.20 = (bf16[4,96,768]{2,1,0:T(8,128)(2,1)S(1)}, bf16[4,96,768]{2,1,0:T(8,128)(2,1)S(1)}, u32[]{:S(2)}, u32[]{:S(2)}) collective-permute-start(bf16[4,96,768]{2,1,0:T(8,128)(2,1)S(1)} %get-tuple-element.208), channel_id=1, source_target_pairs={{0,4},{4,0},{8,12},{12,8},{16,20},{20,16},{24,28},{28,24},{1,5},{5... | collective-permute-start | bytes 1769480 | tf_op jit(solution)/shard_map/ppermute | solution.py:769
  30.4 1.6 %collective-permute-start.21 = (bf16[4,96,768]{2,1,0:T(8,128)(2,1)S(1)}, bf16[4,96,768]{2,1,0:T(8,128)(2,1)S(1)}, u32[]{:S(2)}, u32[]{:S(2)}) collective-permute-start(bf16[4,96,768]{2,1,0:T(8,128)(2,1)S(1)} %get-tuple-element.210), channel_id=1, source_target_pairs={{0,8},{4,12},{8,0},{12,4},{16,24},{20,28},{24,16},{28,20},{1,9},{5... | collective-permute-start | bytes 1769480 | tf_op jit(solution)/shard_map/ppermute | solution.py:769
  31.9 2.1 %collective-permute-done.14.refs_1_ = bf16[128,768]{1,0:T(8,128)(2,1)S(1)} collective-permute-done((bf16[128,768]{1,0:T(8,128)(2,1)S(1)}, bf16[128,768]{1,0:T(8,128)(2,1)S(1)}, u32[]{:S(2)}, u32[]{:S(2)}) %collective-permute-start.14) | collective-permute-done | bytes 196640 | tf_op jit(solution)/shard_map/ppermute | solution.py:765
  34.0 2.3 %cross_backward.1 = (bf16[128,768]{1,0:T(8,128)(2,1)S(1)}, f32[128,768]{1,0:T(8,128)S(1)}, f32[8,768]{1,0:T(8,128)S(1)}, bf16[512,384]{1,0:T(8,128)(2,1)S(1)}, b...) custom-call(bf16[128,768]{1,0:T(8,128)(2,1)S(1)} %get-tuple-element., ...), custom_call_target="tpu_custom_call" | custom-call | tf_op jit(solution)/shard_map/cross_backward/pallas_call | solution.py:742
  36.4 0.4 source_grad.1.refs_15_
  36.8 0.5 collective-permute-start.18
  37.3 0.8 collective-permute-start.16
  38.1 1.0 %collective-permute-done.18.refs_12_ = bf16[128,960]{1,0:T(8,128)(2,1)S(1)} collective-permute-done((bf16[128,960]{1,0:T(8,128)(2,1)S(1)}, bf16[128,960]{1,0:T(8,128)(2,1)S(1)}, u32[]{:S(2)}, u32[]{:S(2)}) %collective-permute-start.18) | collective-permute-done | bytes 245792 | tf_op jit(solution)/shard_map/ppermute | solution.py:761
  39.1 1.8 %cross_weights.1 = (bf16[4,96,384]{2,1,0:T(8,128)(2,1)S(1)}, bf16[4,96,384]{2,1,0:T(8,128)(2,1)S(1)}, bf16[4,96,384]{2,1,0:T(8,128)(2,1)S(1)}, bf16[4,96,384]{2,1,0:T(8,128)(2,1)S(1)}, bf16[512,384]{1,0:T(8,128)(2,1)S(1)}) custom-call(bf16[512,384]{1,0:T(8,128)(2,1)S(1)} %get-tuple-element.193.refs_0_, ...), custom_call_target="tpu_custom_call" | custom-call | tf_op jit(solution)/shard_map/cross_weights/pallas_call | solution.py:742
  40.8 1.6 %collective-permute-start.23 = (bf16[4,96,384]{2,1,0:T(8,128)(2,1)S(1)}, bf16[4,96,384]{2,1,0:T(8,128)(2,1)S(1)}, u32[]{:S(2)}, u32[]{:S(2)}) collective-permute-start(bf16[4,96,384]{2,1,0:T(8,128)(2,1)S(1)} %get-tuple-element.214), channel_id=1, source_target_pairs={{0,4},{4,0},{8,12},{12,8},{16,20},{20,16},{24,28},{28,24},{1,5},{5... | collective-permute-start | bytes 884744 | tf_op jit(solution)/shard_map/ppermute | solution.py:769
  42.4 1.6 %collective-permute-start.24 = (bf16[4,96,384]{2,1,0:T(8,128)(2,1)S(1)}, bf16[4,96,384]{2,1,0:T(8,128)(2,1)S(1)}, u32[]{:S(2)}, u32[]{:S(2)}) collective-permute-start(bf16[4,96,384]{2,1,0:T(8,128)(2,1)S(1)} %get-tuple-element.216), channel_id=1, source_target_pairs={{0,8},{4,12},{8,0},{12,4},{16,24},{20,28},{24,16},{28,20},{1,9},{5... | collective-permute-start | bytes 884744 | tf_op jit(solution)/shard_map/ppermute | solution.py:769
  44.0 0.5 ffn_out.1.refs_6_
  44.5 0.2 self_norm.1
  44.8 1.2 %collective-permute-done.21.refs_3_ = bf16[4,96,768]{2,1,0:T(8,128)(2,1)S(1)} collective-permute-done((bf16[4,96,768]{2,1,0:T(8,128)(2,1)S(1)}, bf16[4,96,768]{2,1,0:T(8,128)(2,1)S(1)}, u32[]{:S(2)}, u32[]{:S(2)}) %collective-permute-start.21) | collective-permute-done | bytes 589856 | tf_op jit(solution)/shard_map/ppermute | solution.py:769
  46.0 0.3 ffn_second.1
  46.3 1.8 %self_backward.1 = (bf16[144,768]{1,0:T(8,128)(2,1)S(1)}, bf16[144,768]{1,0:T(8,128)(2,1)S(1)}, bf16[256,768]{1,0:T(8,128)(2,1)S(1)}, bf16[256,192]{1,0:T(8,128)...) custom-call(bf16[144,768]{1,0:T(8,128)(2,1)S(1)} %get-tuple-element.204.refs_4_., ...), custom_call_target="tpu_custom_call" | custom-call | tf_op jit(solution)/shard_map/self_backward/pallas_call | solution.py:742
  48.3 1.5 %collective-permute-start.26 = (bf16[2,96,768]{2,1,0:T(8,128)(2,1)S(1)}, bf16[2,96,768]{2,1,0:T(8,128)(2,1)S(1)}, u32[]{:S(2)}, u32[]{:S(2)}) collective-permute-start(bf16[2,96,768]{2,1,0:T(8,128)(2,1)S(1)} %get-tuple-element.211.refs_11_), channel_id=1, source_target_pairs={{0,8},{4,12},{8,0},{12,4},{16,24},{20,28},{24,16},{28,20},{1,9},{5... | collective-permute-start | bytes 884744 | tf_op jit(solution)/shard_map/ppermute | solution.py:769
  49.8 1.3 %collective-permute-start.27 = (bf16[2,96,768]{2,1,0:T(8,128)(2,1)S(1)}, bf16[2,96,768]{2,1,0:T(8,128)(2,1)S(1)}, u32[]{:S(2)}, u32[]{:S(2)}) collective-permute-start(bf16[2,96,768]{2,1,0:T(8,128)(2,1)S(1)} %get-tuple-element.230), channel_id=1, source_target_pairs={{0,4},{4,0},{8,12},{12,8},{16,20},{20,16},{24,28},{28,24},{1,5},{5... | collective-permute-start | bytes 884744 | tf_op jit(solution)/shard_map/ppermute | solution.py:769
  51.1 1.4 %self_weights.1 = (bf16[4,96,512]{2,1,0:T(8,128)(2,1)S(1)}, bf16[4,96,512]{2,1,0:T(8,128)(2,1)S(1)}, bf16[4,96,256]{2,1,0:T(8,128)(2,1)S(1)}, bf16[4,96,256]{2,1,0:T(8,128)(2,1)S(1)}, bf16[16,256]{1,0:T(8,128)(2,1)S(1)}) custom-call(bf16[256,768]{1,0:T(8,128)(2,1)S(1)} %get-tuple-element.170.refs_0_, bf16[256,768]{1,0:T(8,128)(2,1)S(1)} %get-tuple-element.217.refs_1_, ...), custom_call_target="tpu_custom_call" | custom-call | tf_op jit(solution)/shard_map/self_weights/pallas_call | solution.py:742
  52.5 0.2 round_three.1
  52.8 0.9 collective-permute-start.25
  53.7 1.3 %collective-permute-start.30 = (bf16[1376,128]{1,0:T(8,128)(2,1)S(1)}, bf16[1376,128]{1,0:T(8,128)(2,1)S(1)}, u32[]{:S(2)}, u32[]{:S(2)}) collective-permute-start(bf16[1376,128]{1,0:T(8,128)(2,1)S(1)} %get-tuple-element.234), channel_id=1, source_target_pairs={{0,8},{4,12},{8,0},{12,4},{16,24},{20,28},{24,16},{28,20},{1,9},{5... | collective-permute-start | bytes 1056776 | tf_op jit(solution)/shard_map/ppermute | solution.py:769
  55.0 0.4 collective-permute-start.29
  55.4 4.3 %collective-permute-done.27.refs_3_ = bf16[2,96,768]{2,1,0:T(8,128)(2,1)S(1)} collective-permute-done((bf16[2,96,768]{2,1,0:T(8,128)(2,1)S(1)}, bf16[2,96,768]{2,1,0:T(8,128)(2,1)S(1)}, u32[]{:S(2)}, u32[]{:S(2)}) %collective-permute-start.27) | collective-permute-done | bytes 294944 | tf_op jit(solution)/shard_map/ppermute | solution.py:769
  59.8 2.7 %collective-permute-start.39 = (bf16[192,768]{1,0:T(8,128)(2,1)S(1)}, bf16[192,768]{1,0:T(8,128)(2,1)S(1)}, u32[]{:S(2)}, u32[]{:S(2)}) collective-permute-start(bf16[192,768]{1,0:T(8,128)(2,1)S(1)} %get-tuple-element.231.refs_2_), channel_id=1, source_target_pairs={{0,16},{4,20},{8,24},{12,28},{16,0},{20,4},{24,8},{28,12},{1,17},{... | collective-permute-start | bytes 884744 | tf_op jit(solution)/shard_map/ppermute | solution.py:769
  62.4 1.4 %collective-permute-start.28 = (bf16[128,768]{1,0:T(8,128)(2,1)S(1)}, bf16[128,768]{1,0:T(8,128)(2,1)S(1)}, u32[]{:S(2)}, u32[]{:S(2)}) collective-permute-start(bf16[128,768]{1,0:T(8,128)(2,1)S(1)} %ffn_out.1.refs_6_), channel_id=1, source_target_pairs={{0,2},{1,3},{2,0},{3,1},{4,6},{5,7},{6,4},{7,5},{8,10},{9,11},{10,... | collective-permute-start | bytes 589832 | tf_op jit(solution)/shard_map/ppermute | solution.py:765
  63.8 0.8 collective-permute-start.31
  64.6 6.8 %collective-permute-done.30.zo_got = bf16[1376,128]{1,0:T(8,128)(2,1)S(1)} collective-permute-done((bf16[1376,128]{1,0:T(8,128)(2,1)S(1)}, bf16[1376,128]{1,0:T(8,128)(2,1)S(1)}, u32[]{:S(2)}, u32[]{:S(2)}) %collective-permute-start.30) | collective-permute-done | bytes 352288 | tf_op jit(solution)/shard_map/ppermute | solution.py:769
  71.7 0.3 collective-permute-start.34
  72.0 0.5 collective-permute-start.33
  72.5 0.3 input_grad.1.refs_3_.refs_0_
  72.9 2.6 %collective-permute-start.38 = (bf16[576,128]{1,0:T(8,128)(2,1)S(1)}, bf16[576,128]{1,0:T(8,128)(2,1)S(1)}, u32[]{:S(2)}, u32[]{:S(2)}) collective-permute-start(bf16[576,128]{1,0:T(8,128)(2,1)S(1)} %get-tuple-element.262), channel_id=1, source_target_pairs={{0,16},{4,20},{8,24},{12,28},{16,0},{20,4},{24,8},{28,12},{1,17},{... | collective-permute-start | bytes 442376 | tf_op jit(solution)/shard_map/ppermute | solution.py:769
  75.5 0.6 encoded.1
  76.4 0.8 ffn_final.1
  77.3 0.7 collective-permute-done.35.other
  78.1 3.8 %collective-permute-done.33.refs_1_ = bf16[784,128]{1,0:T(8,128)(2,1)S(1)} collective-permute-done((bf16[784,128]{1,0:T(8,128)(2,1)S(1)}, bf16[784,128]{1,0:T(8,128)(2,1)S(1)}, u32[]{:S(2)}, u32[]{:S(2)}) %collective-permute-start.33) | collective-permute-done | bytes 200736 | tf_op jit(solution)/shard_map/ppermute | solution.py:769
  81.9 0.3 collective-permute-start.36
  82.2 1.2 %collective-permute-start.37 = (bf16[128,768]{1,0:T(8,128)(2,1)S(1)}, bf16[128,768]{1,0:T(8,128)(2,1)S(1)}, u32[]{:S(2)}, u32[]{:S(2)}) collective-permute-start(bf16[128,768]{1,0:T(8,128)(2,1)S(1)} %get-tuple-element.250), channel_id=1, source_target_pairs={{0,2},{1,3},{2,0},{3,1},{4,6},{5,7},{6,4},{7,5},{8,10},{9,11},{10,... | collective-permute-start | bytes 589832 | tf_op jit(solution)/shard_map/ppermute | solution.py:765
  83.4 1.7 %collective-permute-done.38.refs_1_ = bf16[576,128]{1,0:T(8,128)(2,1)S(1)} collective-permute-done((bf16[576,128]{1,0:T(8,128)(2,1)S(1)}, bf16[576,128]{1,0:T(8,128)(2,1)S(1)}, u32[]{:S(2)}, u32[]{:S(2)}) %collective-permute-start.38) | collective-permute-done | bytes 147488 | tf_op jit(solution)/shard_map/ppermute | solution.py:769
  85.1 0.8 cross_final.1
  85.9 0.9 %rows.1 = (bf16[256,768]{1,0:T(8,128)(2,1)}, bf16[256,768]{1,0:T(8,128)(2,1)}, bf16[16,128]{1,0:T(8,128)(2,1)S(1)}) custom-call(bf16[256,768]{1,0:T(8,128)(2,1)S(1)} %input_grad.1.refs_3_.refs_0_, bf16[256,768]{1,0:T(8,128)(2,1)S(1)} %collective-permute-done.32.refs_1_, bf16[608,128]{1,0:T(8,128)(2,1)S(1)} %get-tuple-element.246.refs_2_), custom_call_target="tpu_custom_call" | custom-call | tf_op jit(solution)/shard_map/rows/pallas_call | solution.py:742
  86.9 3.1 %collective-permute-done.36.refs_1_ = bf16[608,128]{1,0:T(8,128)(2,1)S(1)} collective-permute-done((bf16[608,128]{1,0:T(8,128)(2,1)S(1)}, bf16[608,128]{1,0:T(8,128)(2,1)S(1)}, u32[]{:S(2)}, u32[]{:S(2)}) %collective-permute-start.36) | collective-permute-done | bytes 155680 | tf_op jit(solution)/shard_map/ppermute | solution.py:769
  89.9 1.0 %self_final.1 = (bf16[128,768]{1,0:T(8,128)(2,1)}, f32[96,192]{1,0:T(8,128)}, f32[96,192]{1,0:T(8,128)}, f32[96,192]{1,0:T(8,128)}, f32[192,96]{1,0:T(8,128)}, /...) custom-call(bf16[608,128]{1,0:T(8,128)(2,1)S(1)} %get-tuple-element.249.refs_0_, ...), custom_call_target="tpu_custom_call" | custom-call | tf_op jit(solution)/shard_map/self_final/pallas_call | solution.py:742
  (88 shorter events, 2.1 us)
Async XLA Ops:
  0.7 3.1 %copy-start = (bf16[768,192]{0,1:T(8,128)(2,1)S(1)}, bf16[768,192]{0,1:T(8,128)(2,1)}, u32[]{:S(2)}) copy-start(bf16[768,192]{0,1:T(8,128)(2,1)} %param.40) | copy-start | bytes 884740
  0.7 3.1 %copy-start.1 = (bf16[768,192]{0,1:T(8,128)(2,1)S(1)}, bf16[768,192]{0,1:T(8,128)(2,1)}, u32[]{:S(2)}) copy-start(bf16[768,192]{0,1:T(8,128)(2,1)} %param.41) | copy-start | bytes 884740
  0.7 4.3 %copy-start.3 = (bf16[1,256,768]{2,1,0:T(8,128)(2,1)S(1)}, bf16[1,256,768]{2,1,0:T(8,128)(2,1)}, u32[]{:S(2)}) copy-start(bf16[1,256,768]{2,1,0:T(8,128)(2,1)} %param.23) | copy-start | bytes 1179652
  0.7 4.3 %copy-start.5 = (bf16[768,192]{0,1:T(8,128)(2,1)S(1)}, bf16[768,192]{0,1:T(8,128)(2,1)}, u32[]{:S(2)}) copy-start(bf16[768,192]{0,1:T(8,128)(2,1)} %param.34) | copy-start | bytes 884740
  0.7 4.3 %copy-start.6 = (bf16[768,192]{0,1:T(8,128)(2,1)S(1)}, bf16[768,192]{0,1:T(8,128)(2,1)}, u32[]{:S(2)}) copy-start(bf16[768,192]{0,1:T(8,128)(2,1)} %param.35) | copy-start | bytes 884740
  0.7 4.3 %copy-start.10 = (bf16[768,192]{0,1:T(8,128)(2,1)S(1)}, bf16[768,192]{0,1:T(8,128)(2,1)}, u32[]{:S(2)}) copy-start(bf16[768,192]{0,1:T(8,128)(2,1)} %param.33) | copy-start | bytes 884740
  0.7 4.3 %copy-start.11 = (bf16[192,768]{1,0:T(8,128)(2,1)S(1)}, bf16[192,768]{1,0:T(8,128)(2,1)}, u32[]{:S(2)}) copy-start(bf16[192,768]{1,0:T(8,128)(2,1)} %refs_2_.5) | copy-start | bytes 884740
  0.7 4.3 %copy-start.14 = (f32[768]{0:T(1024)S(1)}, f32[768]{0:T(1024)}, u32[]{:S(2)}) copy-start(f32[768]{0:T(1024)} %refs_3_.7) | copy-start | bytes 9220
  0.7 4.3 %copy-start.15 = (s32[256]{0:T(256)S(1)}, s32[256]{0:T(256)}, u32[]{:S(2)}) copy-start(s32[256]{0:T(256)} %param.29) | copy-start | bytes 3076
  0.7 4.3 %copy-start.18 = (f32[32,3]{0,1:T(4,128)S(1)}, f32[32,3]{0,1:T(4,128)}, u32[]{:S(2)}) copy-start(f32[32,3]{0,1:T(4,128)} %param.37) | copy-start | bytes 1156
  0.8 8.5 %collective-permute-start.1 = (bf16[128,768]{1,0:T(8,128)(2,1)}, bf16[128,768]{1,0:T(8,128)(2,1)S(1)}, u32[]{:S(2)}, u32[]{:S(2)}) collective-permute-start(bf16[128,768]{1,0:T(8,128)(2,1)} %bitcast.33), channel_id=1, source_target_pairs={{0,2},{1,3},{2,0},{3,1},{4,6},{5,7},{6,4},{7,5},{8,10},{9,11},{10,... | collective-permute-start | bytes 589832 | tf_op jit(solution)/shard_map/ppermute | solution.py:765
  3.8 3.4 %collective-permute-start.3 = (bf16[192,768]{1,0:T(8,128)(2,1)S(1)}, bf16[192,768]{1,0:T(8,128)(2,1)S(1)}, u32[]{:S(2)}, u32[]{:S(2)}) collective-permute-start(bf16[192,768]{1,0:T(8,128)(2,1)S(1)} %bitcast.19), channel_id=1, source_target_pairs={{0,1},{1,0},{2,3},{3,2},{4,5},{5,4},{6,7},{7,6},{8,9},{9,8},{10,11... | collective-permute-start | bytes 884744 | tf_op jit(solution)/shard_map/ppermute | solution.py:761
  3.8 3.5 %collective-permute-start.4 = (bf16[192,768]{1,0:T(8,128)(2,1)S(1)}, bf16[192,768]{1,0:T(8,128)(2,1)S(1)}, u32[]{:S(2)}, u32[]{:S(2)}) collective-permute-start(bf16[192,768]{1,0:T(8,128)(2,1)S(1)} %bitcast.24), channel_id=1, source_target_pairs={{0,1},{1,0},{2,3},{3,2},{4,5},{5,4},{6,7},{7,6},{8,9},{9,8},{10,11... | collective-permute-start | bytes 884744 | tf_op jit(solution)/shard_map/ppermute | solution.py:761
  5.0 2.2 %copy-start.8 = (bf16[768,192]{0,1:T(8,128)(2,1)S(1)}, bf16[768,192]{0,1:T(8,128)(2,1)}, u32[]{:S(2)}) copy-start(bf16[768,192]{0,1:T(8,128)(2,1)} %param.39) | copy-start | bytes 884740
  5.1 2.2 %copy-start.9 = (bf16[192,768]{1,0:T(8,128)(2,1)S(1)}, bf16[192,768]{1,0:T(8,128)(2,1)}, u32[]{:S(2)}) copy-start(bf16[192,768]{1,0:T(8,128)(2,1)} %refs_5_.1) | copy-start | bytes 884740
  5.1 2.7 %copy-start.4 = (bf16[1,128,768]{2,1,0:T(8,128)(2,1)S(1)}, bf16[1,128,768]{2,1,0:T(8,128)(2,1)}, u32[]{:S(2)}) copy-start(bf16[1,128,768]{2,1,0:T(8,128)(2,1)} %param.24) | copy-start | bytes 589828
  6.6 1.6 %collective-permute-start.5 = (bf16[64,768]{1,0:T(8,128)(2,1)S(1)}, bf16[64,768]{1,0:T(8,128)(2,1)S(1)}, u32[]{:S(2)}, u32[]{:S(2)}) collective-permute-start(bf16[64,768]{1,0:T(8,128)(2,1)S(1)} %get-tuple-element.152), channel_id=1, source_target_pairs={{0,1},{1,0},{2,3},{3,2},{4,5},{5,4},{6,7},{7,6},{8,9},{9,8},{10,11... | collective-permute-start | bytes 294920 | tf_op jit(solution)/shard_map/ppermute | solution.py:761
  6.8 1.5 %collective-permute-start.6 = (bf16[64,768]{1,0:T(8,128)(2,1)S(1)}, bf16[64,768]{1,0:T(8,128)(2,1)S(1)}, u32[]{:S(2)}, u32[]{:S(2)}) collective-permute-start(bf16[64,768]{1,0:T(8,128)(2,1)S(1)} %get-tuple-element.153), channel_id=1, source_target_pairs={{0,1},{1,0},{2,3},{3,2},{4,5},{5,4},{6,7},{7,6},{8,9},{9,8},{10,11... | collective-permute-start | bytes 294920 | tf_op jit(solution)/shard_map/ppermute | solution.py:761
  7.2 6.3 %collective-permute-start.8 = (bf16[192,768]{1,0:T(8,128)(2,1)S(1)}, bf16[192,768]{1,0:T(8,128)(2,1)S(1)}, u32[]{:S(2)}, u32[]{:S(2)}) collective-permute-start(bf16[192,768]{1,0:T(8,128)(2,1)S(1)} %bitcast.44), channel_id=1, source_target_pairs={{0,1},{1,0},{2,3},{3,2},{4,5},{5,4},{6,7},{7,6},{8,9},{9,8},{10,11... | collective-permute-start | bytes 884744 | tf_op jit(solution)/shard_map/ppermute | solution.py:761
  7.3 6.2 %collective-permute-start.9 = (bf16[192,768]{1,0:T(8,128)(2,1)S(1)}, bf16[192,768]{1,0:T(8,128)(2,1)S(1)}, u32[]{:S(2)}, u32[]{:S(2)}) collective-permute-start(bf16[192,768]{1,0:T(8,128)(2,1)S(1)} %copy-done.9), channel_id=1, source_target_pairs={{0,1},{1,0},{2,3},{3,2},{4,5},{5,4},{6,7},{7,6},{8,9},{9,8},{10,11... | collective-permute-start | bytes 884744 | tf_op jit(solution)/shard_map/ppermute | solution.py:761
  8.3 4.6 %copy-start.7 = (bf16[768,768]{1,0:T(8,128)(2,1)S(1)}, bf16[768,768]{1,0:T(8,128)(2,1)}, u32[]{:S(2)}) copy-start(bf16[768,768]{1,0:T(8,128)(2,1)} %up_own.1) | copy-start | bytes 3538948
  8.3 4.6 %copy-start.2 = (bf16[768,768]{1,0:T(8,128)(2,1)S(1)}, bf16[768,768]{1,0:T(8,128)(2,1)}, u32[]{:S(2)}) copy-start(bf16[768,768]{1,0:T(8,128)(2,1)} %refs_2_.4) | copy-start | bytes 3538948
  8.3 7.6 %collective-permute-start.7 = (bf16[144,768]{1,0:T(8,128)(2,1)S(1)}, bf16[144,768]{1,0:T(8,128)(2,1)S(1)}, u32[]{:S(2)}, u32[]{:S(2)}) collective-permute-start(bf16[144,768]{1,0:T(8,128)(2,1)S(1)} %self_sum.1.refs_11_.refs_1_), channel_id=1, source_target_pairs={{0,2},{1,3},{2,0},{3,1},{4,6},{5,7},{6,4},{7,5},{8,10},{9,11},{10,... | collective-permute-start | bytes 663560 | tf_op jit(solution)/shard_map/ppermute | solution.py:765
  9.2 2.5 %collective-permute-start = (bf16[128,768]{1,0:T(8,128)(2,1)S(1)}, bf16[128,768]{1,0:T(8,128)(2,1)S(1)}, u32[]{:S(2)}, u32[]{:S(2)}) collective-permute-start(bf16[128,768]{1,0:T(8,128)(2,1)S(1)} %bitcast.35), channel_id=1, source_target_pairs={{0,1},{1,0},{2,3},{3,2},{4,5},{5,4},{6,7},{7,6},{8,9},{9,8},{10,11... | collective-permute-start | bytes 589832 | tf_op jit(solution)/shard_map/ppermute | solution.py:761
  9.2 2.5 %collective-permute-start.2 = (bf16[128,768]{1,0:T(8,128)(2,1)S(1)}, bf16[128,768]{1,0:T(8,128)(2,1)S(1)}, u32[]{:S(2)}, u32[]{:S(2)}) collective-permute-start(bf16[128,768]{1,0:T(8,128)(2,1)S(1)} %collective-permute-done.1.refs_1_.refs_4_.refs_6_), channel_id=1, source_target_pairs={{0,1},{1,0},{2,3},{3,2},{4,5},{5,4},{6,7},{7,6},{8,9},{9,8},{10,11... | collective-permute-start | bytes 589832 | tf_op jit(solution)/shard_map/ppermute | solution.py:761
  11.7 4.3 %copy-start.12 = (f32[768]{0:T(1024)S(1)}, f32[768]{0:T(1024)}, u32[]{:S(2)}) copy-start(f32[768]{0:T(1024)} %refs_3_.6) | copy-start | bytes 9220
  12.9 11.8 %collective-permute-start.11 = (bf16[768,768]{1,0:T(8,128)(2,1)S(1)}, bf16[768,768]{1,0:T(8,128)(2,1)S(1)}, u32[]{:S(2)}, u32[]{:S(2)}) collective-permute-start(bf16[768,768]{1,0:T(8,128)(2,1)S(1)} %copy-done.7), channel_id=1, source_target_pairs={{0,1},{1,0},{2,3},{3,2},{4,5},{5,4},{6,7},{7,6},{8,9},{9,8},{10,11... | collective-permute-start | bytes 3538952 | tf_op jit(solution)/shard_map/ppermute | solution.py:761
  13.0 6.6 %collective-permute-start.12 = (bf16[768,768]{1,0:T(8,128)(2,1)S(1)}, bf16[768,768]{1,0:T(8,128)(2,1)S(1)}, u32[]{:S(2)}, u32[]{:S(2)}) collective-permute-start(bf16[768,768]{1,0:T(8,128)(2,1)S(1)} %copy-done.2), channel_id=1, source_target_pairs={{0,1},{1,0},{2,3},{3,2},{4,5},{5,4},{6,7},{7,6},{8,9},{9,8},{10,11... | collective-permute-start | bytes 3538952 | tf_op jit(solution)/shard_map/ppermute | solution.py:761
  16.0 3.3 %copy-start.16 = (bf16[1,256,768]{2,1,0:T(8,128)(2,1)S(1)}, bf16[1,256,768]{2,1,0:T(8,128)(2,1)}, u32[]{:S(2)}) copy-start(bf16[1,256,768]{2,1,0:T(8,128)(2,1)} %param.31) | copy-start | bytes 1179652
  16.0 3.3 %copy-start.17 = (f32[16,256]{1,0:T(8,128)S(1)}, f32[16,256]{1,0:T(8,128)}, u32[]{:S(2)}) copy-start(f32[16,256]{1,0:T(8,128)} %refs_2_.3) | copy-start | bytes 49156
  18.4 6.3 %collective-permute-start.10 = (bf16[128,768]{1,0:T(8,128)(2,1)S(1)}, bf16[128,768]{1,0:T(8,128)(2,1)S(1)}, u32[]{:S(2)}, u32[]{:S(2)}) collective-permute-start(bf16[128,768]{1,0:T(8,128)(2,1)S(1)} %get-tuple-element.163.refs_0_), channel_id=1, source_target_pairs={{0,2},{1,3},{2,0},{3,1},{4,6},{5,7},{6,4},{7,5},{8,10},{9,11},{10,... | collective-permute-start | bytes 589832 | tf_op jit(solution)/shard_map/ppermute | solution.py:765
  19.3 5.4 %collective-permute-start.13 = (bf16[128,960]{1,0:T(8,128)(2,1)S(1)}, bf16[128,960]{1,0:T(8,128)(2,1)S(1)}, u32[]{:S(2)}, u32[]{:S(2)}) collective-permute-start(bf16[128,960]{1,0:T(8,128)(2,1)S(1)} %get-tuple-element.173), channel_id=1, source_target_pairs={{0,1},{1,0},{2,3},{3,2},{4,5},{5,4},{6,7},{7,6},{8,9},{9,8},{10,11... | collective-permute-start | bytes 737288 | tf_op jit(solution)/shard_map/ppermute | solution.py:761
  20.4 4.3 %copy-start.13 = (f32[768]{0:T(1024)S(1)}, f32[768]{0:T(1024)}, u32[]{:S(2)}) copy-start(f32[768]{0:T(1024)} %refs_3_.5) | copy-start | bytes 9220
  25.7 2.1 %collective-permute-start.15 = (bf16[128,2304]{1,0:T(8,128)(2,1)S(1)}, bf16[128,2304]{1,0:T(8,128)(2,1)S(1)}, u32[]{:S(2)}, u32[]{:S(2)}) collective-permute-start(bf16[128,2304]{1,0:T(8,128)(2,1)S(1)} %get-tuple-element.185.refs_1_), channel_id=1, source_target_pairs={{0,1},{1,0},{2,3},{3,2},{4,5},{5,4},{6,7},{7,6},{8,9},{9,8},{10,11... | collective-permute-start | bytes 1769480 | tf_op jit(solution)/shard_map/ppermute | solution.py:761
  26.6 7.4 %collective-permute-start.14 = (bf16[128,768]{1,0:T(8,128)(2,1)S(1)}, bf16[128,768]{1,0:T(8,128)(2,1)S(1)}, u32[]{:S(2)}, u32[]{:S(2)}) collective-permute-start(bf16[128,768]{1,0:T(8,128)(2,1)S(1)} %get-tuple-element.176.refs_6_.refs_0_), channel_id=1, source_target_pairs={{0,2},{1,3},{2,0},{3,1},{4,6},{5,7},{6,4},{7,5},{8,10},{9,11},{10,... | collective-permute-start | bytes 589832 | tf_op jit(solution)/shard_map/ppermute | solution.py:765
  28.8 16.0 %collective-permute-start.20 = (bf16[4,96,768]{2,1,0:T(8,128)(2,1)S(1)}, bf16[4,96,768]{2,1,0:T(8,128)(2,1)S(1)}, u32[]{:S(2)}, u32[]{:S(2)}) collective-permute-start(bf16[4,96,768]{2,1,0:T(8,128)(2,1)S(1)} %get-tuple-element.208), channel_id=1, source_target_pairs={{0,4},{4,0},{8,12},{12,8},{16,20},{20,16},{24,28},{28,24},{1,5},{5... | collective-permute-start | bytes 1769480 | tf_op jit(solution)/shard_map/ppermute | solution.py:769
  30.4 15.6 %collective-permute-start.21 = (bf16[4,96,768]{2,1,0:T(8,128)(2,1)S(1)}, bf16[4,96,768]{2,1,0:T(8,128)(2,1)S(1)}, u32[]{:S(2)}, u32[]{:S(2)}) collective-permute-start(bf16[4,96,768]{2,1,0:T(8,128)(2,1)S(1)} %get-tuple-element.210), channel_id=1, source_target_pairs={{0,8},{4,12},{8,0},{12,4},{16,24},{20,28},{24,16},{28,20},{1,9},{5... | collective-permute-start | bytes 1769480 | tf_op jit(solution)/shard_map/ppermute | solution.py:769
  36.7 2.4 %collective-permute-start.17 = (bf16[1024,192]{1,0:T(8,128)(2,1)S(1)}, bf16[1024,192]{1,0:T(8,128)(2,1)S(1)}, u32[]{:S(2)}, u32[]{:S(2)}) collective-permute-start(bf16[1024,192]{1,0:T(8,128)(2,1)S(1)} %source_grad.1.refs_15_), channel_id=1, source_target_pairs={{0,1},{1,0},{2,3},{3,2},{4,5},{5,4},{6,7},{7,6},{8,9},{9,8},{10,11... | collective-permute-start | bytes 1179656 | tf_op jit(solution)/shard_map/ppermute | solution.py:761
  36.8 2.3 %collective-permute-start.18 = (bf16[128,960]{1,0:T(8,128)(2,1)S(1)}, bf16[128,960]{1,0:T(8,128)(2,1)S(1)}, u32[]{:S(2)}, u32[]{:S(2)}) collective-permute-start(bf16[128,960]{1,0:T(8,128)(2,1)S(1)} %get-tuple-element.200), channel_id=1, source_target_pairs={{0,1},{1,0},{2,3},{3,2},{4,5},{5,4},{6,7},{7,6},{8,9},{9,8},{10,11... | collective-permute-start | bytes 737288 | tf_op jit(solution)/shard_map/ppermute | solution.py:761
  37.3 7.2 %collective-permute-start.16 = (bf16[128,768]{1,0:T(8,128)(2,1)S(1)}, bf16[128,768]{1,0:T(8,128)(2,1)S(1)}, u32[]{:S(2)}, u32[]{:S(2)}) collective-permute-start(bf16[128,768]{1,0:T(8,128)(2,1)S(1)} %get-tuple-element.190.refs_0_), channel_id=1, source_target_pairs={{0,2},{1,3},{2,0},{3,1},{4,6},{5,7},{6,4},{7,5},{8,10},{9,11},{10,... | collective-permute-start | bytes 589832 | tf_op jit(solution)/shard_map/ppermute | solution.py:765
  40.8 11.6 %collective-permute-start.23 = (bf16[4,96,384]{2,1,0:T(8,128)(2,1)S(1)}, bf16[4,96,384]{2,1,0:T(8,128)(2,1)S(1)}, u32[]{:S(2)}, u32[]{:S(2)}) collective-permute-start(bf16[4,96,384]{2,1,0:T(8,128)(2,1)S(1)} %get-tuple-element.214), channel_id=1, source_target_pairs={{0,4},{4,0},{8,12},{12,8},{16,20},{20,16},{24,28},{28,24},{1,5},{5... | collective-permute-start | bytes 884744 | tf_op jit(solution)/shard_map/ppermute | solution.py:769
  42.4 10.1 %collective-permute-start.24 = (bf16[4,96,384]{2,1,0:T(8,128)(2,1)S(1)}, bf16[4,96,384]{2,1,0:T(8,128)(2,1)S(1)}, u32[]{:S(2)}, u32[]{:S(2)}) collective-permute-start(bf16[4,96,384]{2,1,0:T(8,128)(2,1)S(1)} %get-tuple-element.216), channel_id=1, source_target_pairs={{0,8},{4,12},{8,0},{12,4},{16,24},{20,28},{24,16},{28,20},{1,9},{5... | collective-permute-start | bytes 884744 | tf_op jit(solution)/shard_map/ppermute | solution.py:769
  44.7 1.5 %collective-permute-start.19 = (bf16[144,768]{1,0:T(8,128)(2,1)S(1)}, bf16[144,768]{1,0:T(8,128)(2,1)S(1)}, u32[]{:S(2)}, u32[]{:S(2)}) collective-permute-start(bf16[144,768]{1,0:T(8,128)(2,1)S(1)} %get-tuple-element.204.refs_4_.refs_0_.refs_8_), channel_id=1, source_target_pairs={{0,1},{1,0},{2,3},{3,2},{4,5},{5,4},{6,7},{7,6},{8,9},{9,8},{10,11... | collective-permute-start | bytes 663560 | tf_op jit(solution)/shard_map/ppermute | solution.py:761
  48.1 4.7 %collective-permute-start.22 = (bf16[144,768]{1,0:T(8,128)(2,1)S(1)}, bf16[144,768]{1,0:T(8,128)(2,1)S(1)}, u32[]{:S(2)}, u32[]{:S(2)}) collective-permute-start(bf16[144,768]{1,0:T(8,128)(2,1)S(1)} %get-tuple-element.213), channel_id=1, source_target_pairs={{0,1},{1,0},{2,3},{3,2},{4,5},{5,4},{6,7},{7,6},{8,9},{9,8},{10,11... | collective-permute-start | bytes 663560 | tf_op jit(solution)/shard_map/ppermute | solution.py:761
  48.3 11.4 %collective-permute-start.26 = (bf16[2,96,768]{2,1,0:T(8,128)(2,1)S(1)}, bf16[2,96,768]{2,1,0:T(8,128)(2,1)S(1)}, u32[]{:S(2)}, u32[]{:S(2)}) collective-permute-start(bf16[2,96,768]{2,1,0:T(8,128)(2,1)S(1)} %get-tuple-element.211.refs_11_), channel_id=1, source_target_pairs={{0,8},{4,12},{8,0},{12,4},{16,24},{20,28},{24,16},{28,20},{1,9},{5... | collective-permute-start | bytes 884744 | tf_op jit(solution)/shard_map/ppermute | solution.py:769
  49.8 9.9 %collective-permute-start.27 = (bf16[2,96,768]{2,1,0:T(8,128)(2,1)S(1)}, bf16[2,96,768]{2,1,0:T(8,128)(2,1)S(1)}, u32[]{:S(2)}, u32[]{:S(2)}) collective-permute-start(bf16[2,96,768]{2,1,0:T(8,128)(2,1)S(1)} %get-tuple-element.230), channel_id=1, source_target_pairs={{0,4},{4,0},{8,12},{12,8},{16,20},{20,16},{24,28},{28,24},{1,5},{5... | collective-permute-start | bytes 884744 | tf_op jit(solution)/shard_map/ppermute | solution.py:769
  52.8 9.6 %collective-permute-start.25 = (bf16[144,768]{1,0:T(8,128)(2,1)S(1)}, bf16[144,768]{1,0:T(8,128)(2,1)S(1)}, u32[]{:S(2)}, u32[]{:S(2)}) collective-permute-start(bf16[144,768]{1,0:T(8,128)(2,1)S(1)} %input_sum.1.refs_4_.refs_0_), channel_id=1, source_target_pairs={{0,2},{1,3},{2,0},{3,1},{4,6},{5,7},{6,4},{7,5},{8,10},{9,11},{10,... | collective-permute-start | bytes 663560 | tf_op jit(solution)/shard_map/ppermute | solution.py:765
  53.7 17.8 %collective-permute-start.30 = (bf16[1376,128]{1,0:T(8,128)(2,1)S(1)}, bf16[1376,128]{1,0:T(8,128)(2,1)S(1)}, u32[]{:S(2)}, u32[]{:S(2)}) collective-permute-start(bf16[1376,128]{1,0:T(8,128)(2,1)S(1)} %get-tuple-element.234), channel_id=1, source_target_pairs={{0,8},{4,12},{8,0},{12,4},{16,24},{20,28},{24,16},{28,20},{1,9},{5... | collective-permute-start | bytes 1056776 | tf_op jit(solution)/shard_map/ppermute | solution.py:769
  55.0 16.5 %collective-permute-start.29 = (bf16[2112,128]{1,0:T(8,128)(2,1)S(1)}, bf16[2112,128]{1,0:T(8,128)(2,1)S(1)}, u32[]{:S(2)}, u32[]{:S(2)}) collective-permute-start(bf16[2112,128]{1,0:T(8,128)(2,1)S(1)} %get-tuple-element.233), channel_id=1, source_target_pairs={{0,4},{4,0},{8,12},{12,8},{16,20},{20,16},{24,28},{28,24},{1,5},{5... | collective-permute-start | bytes 1622024 | tf_op jit(solution)/shard_map/ppermute | solution.py:769
  59.8 16.4 %collective-permute-start.39 = (bf16[192,768]{1,0:T(8,128)(2,1)S(1)}, bf16[192,768]{1,0:T(8,128)(2,1)S(1)}, u32[]{:S(2)}, u32[]{:S(2)}) collective-permute-start(bf16[192,768]{1,0:T(8,128)(2,1)S(1)} %get-tuple-element.231.refs_2_), channel_id=1, source_target_pairs={{0,16},{4,20},{8,24},{12,28},{16,0},{20,4},{24,8},{28,12},{1,17},{... | collective-permute-start | bytes 884744 | tf_op jit(solution)/shard_map/ppermute | solution.py:769
  62.4 10.1 %collective-permute-start.28 = (bf16[128,768]{1,0:T(8,128)(2,1)S(1)}, bf16[128,768]{1,0:T(8,128)(2,1)S(1)}, u32[]{:S(2)}, u32[]{:S(2)}) collective-permute-start(bf16[128,768]{1,0:T(8,128)(2,1)S(1)} %ffn_out.1.refs_6_), channel_id=1, source_target_pairs={{0,2},{1,3},{2,0},{3,1},{4,6},{5,7},{6,4},{7,5},{8,10},{9,11},{10,... | collective-permute-start | bytes 589832 | tf_op jit(solution)/shard_map/ppermute | solution.py:765
  63.8 7.7 %collective-permute-start.31 = (bf16[16,128]{1,0:T(8,128)(2,1)S(1)}, bf16[16,128]{1,0:T(8,128)(2,1)S(1)}, u32[]{:S(2)}, u32[]{:S(2)}) collective-permute-start(bf16[16,128]{1,0:T(8,128)(2,1)S(1)} %gain.1.gains), channel_id=1, source_target_pairs={{0,4},{4,0},{8,12},{12,8},{16,20},{20,16},{24,28},{28,24},{1,5},{5... | collective-permute-start | bytes 12296 | tf_op jit(solution)/shard_map/ppermute | solution.py:769
  71.7 6.4 %collective-permute-start.34 = (bf16[208,256]{1,0:T(8,128)(2,1)S(1)}, bf16[208,256]{1,0:T(8,128)(2,1)S(1)}, u32[]{:S(2)}, u32[]{:S(2)}) collective-permute-start(bf16[208,256]{1,0:T(8,128)(2,1)S(1)} %get-tuple-element.238.refs_8_), channel_id=1, source_target_pairs={{0,4},{4,0},{8,12},{12,8},{16,20},{20,16},{24,28},{28,24},{1,5},{5... | collective-permute-start | bytes 319496 | tf_op jit(solution)/shard_map/ppermute | solution.py:769
  72.0 9.8 %collective-permute-start.33 = (bf16[784,128]{1,0:T(8,128)(2,1)S(1)}, bf16[784,128]{1,0:T(8,128)(2,1)S(1)}, u32[]{:S(2)}, u32[]{:S(2)}) collective-permute-start(bf16[784,128]{1,0:T(8,128)(2,1)S(1)} %get-tuple-element.240), channel_id=1, source_target_pairs={{0,8},{4,12},{8,0},{12,4},{16,24},{20,28},{24,16},{28,20},{1,9},{5... | collective-permute-start | bytes 602120 | tf_op jit(solution)/shard_map/ppermute | solution.py:769
  72.8 13.1 %collective-permute-start.32 = (bf16[256,768]{1,0:T(8,128)(2,1)S(1)}, bf16[256,768]{1,0:T(8,128)(2,1)S(1)}, u32[]{:S(2)}, u32[]{:S(2)}) collective-permute-start(bf16[256,768]{1,0:T(8,128)(2,1)S(1)} %input_grad.1.refs_3_.refs_0_), channel_id=1, source_target_pairs={{0,1},{1,0},{2,3},{3,2},{4,5},{5,4},{6,7},{7,6},{8,9},{9,8},{10,11... | collective-permute-start | bytes 1179656 | tf_op jit(solution)/shard_map/ppermute | solution.py:761
  72.9 12.2 %collective-permute-start.38 = (bf16[576,128]{1,0:T(8,128)(2,1)S(1)}, bf16[576,128]{1,0:T(8,128)(2,1)S(1)}, u32[]{:S(2)}, u32[]{:S(2)}) collective-permute-start(bf16[576,128]{1,0:T(8,128)(2,1)S(1)} %get-tuple-element.262), channel_id=1, source_target_pairs={{0,16},{4,20},{8,24},{12,28},{16,0},{20,4},{24,8},{28,12},{1,17},{... | collective-permute-start | bytes 442376 | tf_op jit(solution)/shard_map/ppermute | solution.py:769
  76.2 1.8 %collective-permute-start.35 = (bf16[256,768]{1,0:T(8,128)(2,1)S(1)}, bf16[256,768]{1,0:T(8,128)(2,1)S(1)}, u32[]{:S(2)}, u32[]{:S(2)}) collective-permute-start(bf16[256,768]{1,0:T(8,128)(2,1)S(1)} %get-tuple-element.244), channel_id=1, source_target_pairs={{0,1},{1,0},{2,3},{3,2},{4,5},{5,4},{6,7},{7,6},{8,9},{9,8},{10,11... | collective-permute-start | bytes 1179656 | tf_op jit(solution)/shard_map/ppermute | solution.py:761
  81.9 8.0 %collective-permute-start.36 = (bf16[608,128]{1,0:T(8,128)(2,1)S(1)}, bf16[608,128]{1,0:T(8,128)(2,1)S(1)}, u32[]{:S(2)}, u32[]{:S(2)}) collective-permute-start(bf16[608,128]{1,0:T(8,128)(2,1)S(1)} %get-tuple-element.246.refs_2_), channel_id=1, source_target_pairs={{0,16},{4,20},{8,24},{12,28},{16,0},{20,4},{24,8},{28,12},{1,17},{... | collective-permute-start | bytes 466952 | tf_op jit(solution)/shard_map/ppermute | solution.py:769
  82.2 7.7 %collective-permute-start.37 = (bf16[128,768]{1,0:T(8,128)(2,1)S(1)}, bf16[128,768]{1,0:T(8,128)(2,1)S(1)}, u32[]{:S(2)}, u32[]{:S(2)}) collective-permute-start(bf16[128,768]{1,0:T(8,128)(2,1)S(1)} %get-tuple-element.250), channel_id=1, source_target_pairs={{0,2},{1,3},{2,0},{3,1},{4,6},{5,7},{6,4},{7,5},{8,10},{9,11},{10,... | collective-permute-start | bytes 589832 | tf_op jit(solution)/shard_map/ppermute | solution.py:765

commit v8 on v7

--- a/solution.py
+++ b/solution.py
@@ -695,11 +695,14 @@
     output[...] = total[:, 3 * count :].T
 
 
+def encoded_out_kernel(own, other, out, token):
+    out[...] = low_sum(own[...], other[...])
+    token[...] = own[: token.shape[0], : token.shape[1]]
+
+
 def self_final_kernel(
-    large, keep, got, encoded_own, encoded_other,
-    encoded_grad, query, key, value, output, table, gain_two, gain_three, gain_one,
+    large, keep, got, query, key, value, output, table, gain_two, gain_three, gain_one
 ):
-    encoded_grad[...] = low_sum(encoded_own[...], encoded_other[...])
     size, count = key.shape
     small = 4 * count - large
     start = size * (large // PIECE)
@@ -1049,11 +1052,14 @@
         def self_final(*refs):
             self_final_kernel(large, *refs)
 
-        (encoded_grad, grad_self_query, grad_self_key, grad_self_value, grad_self_output, grad_table, grad_gain_two,
+        encoded_grad, _ = go(
+            encoded_out_kernel, "encoded_out", [((span_part, width), BF16), ((16, 128), BF16)],
+            [encoded_part, encoded_other],
+        )
+        (grad_self_query, grad_self_key, grad_self_value, grad_self_output, grad_table, grad_gain_two,
          grad_gain_three, grad_gain_one) = go(
             self_final, "self_final",
-            [((span_part, width), BF16)] + [square] * 3 + [turned, (table.shape, F32)] + [((1, size), F32)] * 3,
-            [self_keep, self_got, encoded_part, encoded_other], last=True,
+            [square] * 3 + [turned, (table.shape, F32)] + [((1, size), F32)] * 3, [self_keep, self_got], last=True,
         )
         grad_gain_one, grad_gain_two, grad_gain_three = (
             item.reshape(size) for item in (grad_gain_one, grad_gain_two, grad_gain_three)

time: 91.1 us -> 91 us (level)
    ppermute x14, waiting for transfers between devices: 20.8 us -> 19 us  [to_peer(): lax.ppermute(value, 'dp', [(i, i ^ 1 << bit) for i in range(lax.axis_size...]
    ppermute x8, waiting for transfers between devices: 7.18 us -> 8.2 us  [to_chip(): lax.ppermute(value, 'tensor', [(i, i ^ 2) for i in range(lax.axis_size('t...]
    pallas_call x34 -> x35, Pallas kernels: 25.4 us -> 26 us  [run(): pl.pallas_call(body, out_shape=shapes, in_specs=place, out_specs=[vmem] *...]
  transfers between devices with their start and end apart: 40 -> 40, of which waited for: 12 -> 13; matrix products, arithmetic and copies ran while one was open for 0% -> 0% of each run, Pallas kernels for 26% -> 27%
where the time goes in v8:
time: 91 us; the launch traced here: 90.8 us
  starting transfers between devices  31.7 us (35%)
  waiting for transfers between devices  29.3 us (32%)
  Pallas kernels  26 us (29%)
  between operations  3.82 us (4%)
    pallas_call x35, Pallas kernels, run(): pl.pallas_call(body, out_shape=shapes, in_specs=place, out_specs=[vmem] *...  26 us
    ppermute x14, waiting for transfers between devices, to_peer(): lax.ppermute(value, 'dp', [(i, i ^ 1 << bit) for i in range(lax.axis_size...  19 us
    ppermute x14, starting transfers between devices, to_peer(): lax.ppermute(value, 'dp', [(i, i ^ 1 << bit) for i in range(lax.axis_size...  18 us
    ppermute x8, starting transfers between devices, to_chip(): lax.ppermute(value, 'tensor', [(i, i ^ 2) for i in range(lax.axis_size('t...  9.82 us
    ppermute x8, waiting for transfers between devices, to_chip(): lax.ppermute(value, 'tensor', [(i, i ^ 2) for i in range(lax.axis_size('t...  8.2 us
    ppermute x18, starting transfers between devices, to_core(): lax.ppermute(value, 'tensor', [(i, i ^ 1) for i in range(lax.axis_size('t...  3.88 us
    ppermute x18, waiting for transfers between devices, to_core(): lax.ppermute(value, 'tensor', [(i, i ^ 1) for i in range(lax.axis_size('t...  2.02 us
  transfers between devices with their start and end apart: 40, of which 13 were waited for; matrix products, arithmetic and copies ran while one was open for 0% of the time, Pallas kernels for 27%

profile of v8, /device:TPU:0, one launch (start us, length us, event | category | flops | bytes accessed | tf_op | source)
XLA Modules:
  0.0 90.8 jit_solution(1691324347848245834)
XLA Ops:
  0.8 3.0 %collective-permute-start.1 = (bf16[128,768]{1,0:T(8,128)(2,1)}, bf16[128,768]{1,0:T(8,128)(2,1)S(1)}, u32[]{:S(2)}, u32[]{:S(2)}) collective-permute-start(bf16[128,768]{1,0:T(8,128)(2,1)} %bitcast.33), channel_id=1, source_target_pairs={{0,2},{1,3},{2,0},{3,1},{4,6},{5,7},{6,4},{7,5},{8,10},{9,11},{10,... | collective-permute-start | bytes 589832 | tf_op jit(solution)/shard_map/ppermute | solution.py:768
  3.8 0.5 collective-permute-start.4
  5.1 1.6 %self_forward.1 = (bf16[128,768]{1,0:T(8,128)(2,1)S(1)}, bf16[64,768]{1,0:T(8,128)(2,1)S(1)}, bf16[64,768]{1,0:T(8,128)(2,1)S(1)}, bf16[256,768]{1,0:T(8,128)(2,...) custom-call(s32[1]{0:T(128)S(6)} %copy.40.refs_0_, ...), custom_call_target="tpu_custom_call" | custom-call | flops 4024999936 | tf_op jit(solution)/shard_map/self_forward/pallas_call | solution.py:745
  6.8 0.4 collective-permute-start.6
  7.3 0.4 collective-permute-start.9
  7.7 0.5 source_first.1
  8.3 0.9 collective-permute-start.7
  9.2 0.5 collective-permute-start.2
  11.7 1.2 %source_second.1 = (bf16[512,192]{1,0:T(8,128)(2,1)S(1)}, bf16[192,512]{1,0:T(8,128)(2,1)S(1)}, bf16[512,192]{1,0:T(8,128)(2,1)S(1)}, bf16[192,512]{1,0:T(8,128)(2,1)S(1)}) custom-call(bf16[128,768]{1,0:T(8,128)(2,1)S(1)} %collective-permute-done.refs_0_.refs_5_.refs_7_, bf16[128,768]{1,0:T(8,128)(2,1)S(1)} %collective-permute-done.1.refs_1_.refs_4_.refs_6_, ...), custom_call_target="tpu_custom_call" | custom-call | tf_op jit(solution)/shard_map/source_second/pallas_call | solution.py:745
  13.0 0.5 collective-permute-start.12
  13.5 2.4 %collective-permute-done.7.refs_2_ = bf16[144,768]{1,0:T(8,128)(2,1)S(1)} collective-permute-done((bf16[144,768]{1,0:T(8,128)(2,1)S(1)}, bf16[144,768]{1,0:T(8,128)(2,1)S(1)}, u32[]{:S(2)}, u32[]{:S(2)}) %collective-permute-start.7) | collective-permute-done | bytes 221216 | tf_op jit(solution)/shard_map/ppermute | solution.py:768
  16.0 2.5 %cross_forward.1 = (bf16[128,768]{1,0:T(8,128)(2,1)S(1)}, f32[128,768]{1,0:T(8,128)S(1)}, bf16[128,768]{1,0:T(8,128)(2,1)S(1)}, bf16[128,192]{1,0:T(8,128)(2,1)S...) custom-call(f32[512,128]{1,0:T(8,128)S(1)} %get-tuple-element.159.re, ...), custom_call_target="tpu_custom_call" | custom-call | tf_op jit(solution)/shard_map/cross_forward/pallas_call | solution.py:745
  18.4 0.9 collective-permute-start.10
  19.5 0.9 act_grad.1
  20.5 1.6 %source_back.1 = (bf16[192,256]{1,0:T(8,128)(2,1)S(1)}, bf16[256,192]{1,0:T(8,128)(2,1)S(1)}, bf16[192,512]{1,0:T(8,128)(2,1)S(1)}, bf16[512,192]{1,0:T(8,128)(2...) custom-call(bf16[256,768]{1,0:T(8,128)(2,1)S(1)} %get-tuple-element.171.refs_0_, ...), custom_call_target="tpu_custom_call" | custom-call | tf_op jit(solution)/shard_map/source_back/pallas_call | solution.py:745
  22.1 2.7 %collective-permute-done.10.refs_1_ = bf16[128,768]{1,0:T(8,128)(2,1)S(1)} collective-permute-done((bf16[128,768]{1,0:T(8,128)(2,1)S(1)}, bf16[128,768]{1,0:T(8,128)(2,1)S(1)}, u32[]{:S(2)}, u32[]{:S(2)}) %collective-permute-start.10) | collective-permute-done | bytes 196640 | tf_op jit(solution)/shard_map/ppermute | solution.py:768
  24.7 1.0 %ffn_peer.1 = (f32[128,768]{1,0:T(8,128)S(1)}, bf16[128,768]{1,0:T(8,128)(2,1)S(1)}, f32[128,768]{1,0:T(8,128)S(1)}, bf16[128,2304]{1,0:T(8,128)(2,1)S(1)}) custom-call(bf16[128,768]{1,0:T(8,128)(2,1)S(1)} %get-tuple-element.164.refs_0_, bf16[128,768]{1,0:T(8,128)(2,1)S(1)} %collective-permute-done.10.refs_1_, f32[128,768]{1,0:T(8,128)S(1)} %get-tuple-element.165.refs_2_, ...), custom_call_target="tpu_custom_call" | custom-call | tf_op jit(solution)/shard_map/ffn_peer/pallas_call | solution.py:745
  25.8 0.9 ffn_own.1
  26.6 0.9 collective-permute-start.14
  27.5 0.3 collective-permute-done.15.refs_1_
  27.8 1.0 %ffn_weights.1 = (bf16[4,96,768]{2,1,0:T(8,128)(2,1)S(1)}, bf16[4,96,768]{2,1,0:T(8,128)(2,1)S(1)}, bf16[4,96,768]{2,1,0:T(8,128)(2,1)S(1)}, bf16[4,96,768]{2,1,0:T(8,128)(2,1)S(1)}) custom-call(bf16[128,768]{1,0:T(8,128)(2,1)S(1)} %get-tuple-element.175.normed.refs_0_, bf16[128,2304]{1,0:T(8,128)(2,1)S(1)} %collective-permute-done.15.refs_1_, ...), custom_call_target="tpu_custom_call" | custom-call | flops 5750000128 | tf_op jit(solution)/shard_map/ffn_weights/pallas_call | solution.py:745
  28.8 1.6 %collective-permute-start.20 = (bf16[4,96,768]{2,1,0:T(8,128)(2,1)S(1)}, bf16[4,96,768]{2,1,0:T(8,128)(2,1)S(1)}, u32[]{:S(2)}, u32[]{:S(2)}) collective-permute-start(bf16[4,96,768]{2,1,0:T(8,128)(2,1)S(1)} %get-tuple-element.209), channel_id=1, source_target_pairs={{0,4},{4,0},{8,12},{12,8},{16,20},{20,16},{24,28},{28,24},{1,5},{5... | collective-permute-start | bytes 1769480 | tf_op jit(solution)/shard_map/ppermute | solution.py:772
  30.4 1.6 %collective-permute-start.21 = (bf16[4,96,768]{2,1,0:T(8,128)(2,1)S(1)}, bf16[4,96,768]{2,1,0:T(8,128)(2,1)S(1)}, u32[]{:S(2)}, u32[]{:S(2)}) collective-permute-start(bf16[4,96,768]{2,1,0:T(8,128)(2,1)S(1)} %get-tuple-element.211), channel_id=1, source_target_pairs={{0,8},{4,12},{8,0},{12,4},{16,24},{20,28},{24,16},{28,20},{1,9},{5... | collective-permute-start | bytes 1769480 | tf_op jit(solution)/shard_map/ppermute | solution.py:772
  31.9 2.1 %collective-permute-done.14.refs_1_ = bf16[128,768]{1,0:T(8,128)(2,1)S(1)} collective-permute-done((bf16[128,768]{1,0:T(8,128)(2,1)S(1)}, bf16[128,768]{1,0:T(8,128)(2,1)S(1)}, u32[]{:S(2)}, u32[]{:S(2)}) %collective-permute-start.14) | collective-permute-done | bytes 196640 | tf_op jit(solution)/shard_map/ppermute | solution.py:768
  34.0 2.3 %cross_backward.1 = (bf16[128,768]{1,0:T(8,128)(2,1)S(1)}, f32[128,768]{1,0:T(8,128)S(1)}, f32[8,768]{1,0:T(8,128)S(1)}, bf16[512,384]{1,0:T(8,128)(2,1)S(1)}, b...) custom-call(bf16[128,768]{1,0:T(8,128)(2,1)S(1)} %get-tuple-element., ...), custom_call_target="tpu_custom_call" | custom-call | tf_op jit(solution)/shard_map/cross_backward/pallas_call | solution.py:745
  36.4 0.4 source_grad.1.refs_15_
  36.8 0.5 collective-permute-start.18
  37.3 0.8 collective-permute-start.16
  38.1 1.0 %collective-permute-done.18.refs_12_ = bf16[128,960]{1,0:T(8,128)(2,1)S(1)} collective-permute-done((bf16[128,960]{1,0:T(8,128)(2,1)S(1)}, bf16[128,960]{1,0:T(8,128)(2,1)S(1)}, u32[]{:S(2)}, u32[]{:S(2)}) %collective-permute-start.18) | collective-permute-done | bytes 245792 | tf_op jit(solution)/shard_map/ppermute | solution.py:764
  39.1 1.8 %cross_weights.1 = (bf16[4,96,384]{2,1,0:T(8,128)(2,1)S(1)}, bf16[4,96,384]{2,1,0:T(8,128)(2,1)S(1)}, bf16[4,96,384]{2,1,0:T(8,128)(2,1)S(1)}, bf16[4,96,384]{2,1,0:T(8,128)(2,1)S(1)}, bf16[512,384]{1,0:T(8,128)(2,1)S(1)}) custom-call(bf16[512,384]{1,0:T(8,128)(2,1)S(1)} %get-tuple-element.194.refs_0_, ...), custom_call_target="tpu_custom_call" | custom-call | tf_op jit(solution)/shard_map/cross_weights/pallas_call | solution.py:745
  40.8 1.6 %collective-permute-start.23 = (bf16[4,96,384]{2,1,0:T(8,128)(2,1)S(1)}, bf16[4,96,384]{2,1,0:T(8,128)(2,1)S(1)}, u32[]{:S(2)}, u32[]{:S(2)}) collective-permute-start(bf16[4,96,384]{2,1,0:T(8,128)(2,1)S(1)} %get-tuple-element.215), channel_id=1, source_target_pairs={{0,4},{4,0},{8,12},{12,8},{16,20},{20,16},{24,28},{28,24},{1,5},{5... | collective-permute-start | bytes 884744 | tf_op jit(solution)/shard_map/ppermute | solution.py:772
  42.4 1.6 %collective-permute-start.24 = (bf16[4,96,384]{2,1,0:T(8,128)(2,1)S(1)}, bf16[4,96,384]{2,1,0:T(8,128)(2,1)S(1)}, u32[]{:S(2)}, u32[]{:S(2)}) collective-permute-start(bf16[4,96,384]{2,1,0:T(8,128)(2,1)S(1)} %get-tuple-element.217), channel_id=1, source_target_pairs={{0,8},{4,12},{8,0},{12,4},{16,24},{20,28},{24,16},{28,20},{1,9},{5... | collective-permute-start | bytes 884744 | tf_op jit(solution)/shard_map/ppermute | solution.py:772
  44.0 0.5 ffn_out.1.refs_6_
  44.8 1.2 %collective-permute-done.21.refs_3_ = bf16[4,96,768]{2,1,0:T(8,128)(2,1)S(1)} collective-permute-done((bf16[4,96,768]{2,1,0:T(8,128)(2,1)S(1)}, bf16[4,96,768]{2,1,0:T(8,128)(2,1)S(1)}, u32[]{:S(2)}, u32[]{:S(2)}) %collective-permute-start.21) | collective-permute-done | bytes 589856 | tf_op jit(solution)/shard_map/ppermute | solution.py:772
  46.0 0.3 ffn_second.1
  46.3 1.8 %self_backward.1 = (bf16[144,768]{1,0:T(8,128)(2,1)S(1)}, bf16[144,768]{1,0:T(8,128)(2,1)S(1)}, bf16[256,768]{1,0:T(8,128)(2,1)S(1)}, bf16[256,192]{1,0:T(8,128)...) custom-call(bf16[144,768]{1,0:T(8,128)(2,1)S(1)} %get-tuple-element.205.refs_4_., ...), custom_call_target="tpu_custom_call" | custom-call | tf_op jit(solution)/shard_map/self_backward/pallas_call | solution.py:745
  48.3 1.5 %collective-permute-start.26 = (bf16[2,96,768]{2,1,0:T(8,128)(2,1)S(1)}, bf16[2,96,768]{2,1,0:T(8,128)(2,1)S(1)}, u32[]{:S(2)}, u32[]{:S(2)}) collective-permute-start(bf16[2,96,768]{2,1,0:T(8,128)(2,1)S(1)} %get-tuple-element.212.refs_11_), channel_id=1, source_target_pairs={{0,8},{4,12},{8,0},{12,4},{16,24},{20,28},{24,16},{28,20},{1,9},{5... | collective-permute-start | bytes 884744 | tf_op jit(solution)/shard_map/ppermute | solution.py:772
  49.8 1.3 %collective-permute-start.27 = (bf16[2,96,768]{2,1,0:T(8,128)(2,1)S(1)}, bf16[2,96,768]{2,1,0:T(8,128)(2,1)S(1)}, u32[]{:S(2)}, u32[]{:S(2)}) collective-permute-start(bf16[2,96,768]{2,1,0:T(8,128)(2,1)S(1)} %get-tuple-element.231), channel_id=1, source_target_pairs={{0,4},{4,0},{8,12},{12,8},{16,20},{20,16},{24,28},{28,24},{1,5},{5... | collective-permute-start | bytes 884744 | tf_op jit(solution)/shard_map/ppermute | solution.py:772
  51.1 1.4 %self_weights.1 = (bf16[4,96,512]{2,1,0:T(8,128)(2,1)S(1)}, bf16[4,96,512]{2,1,0:T(8,128)(2,1)S(1)}, bf16[4,96,256]{2,1,0:T(8,128)(2,1)S(1)}, bf16[4,96,256]{2,1,0:T(8,128)(2,1)S(1)}, bf16[16,256]{1,0:T(8,128)(2,1)S(1)}) custom-call(bf16[256,768]{1,0:T(8,128)(2,1)S(1)} %get-tuple-element.171.refs_0_, bf16[256,768]{1,0:T(8,128)(2,1)S(1)} %get-tuple-element.218.refs_1_, ...), custom_call_target="tpu_custom_call" | custom-call | tf_op jit(solution)/shard_map/self_weights/pallas_call | solution.py:745
  52.8 0.9 collective-permute-start.25
  53.7 1.3 %collective-permute-start.30 = (bf16[1376,128]{1,0:T(8,128)(2,1)S(1)}, bf16[1376,128]{1,0:T(8,128)(2,1)S(1)}, u32[]{:S(2)}, u32[]{:S(2)}) collective-permute-start(bf16[1376,128]{1,0:T(8,128)(2,1)S(1)} %get-tuple-element.235), channel_id=1, source_target_pairs={{0,8},{4,12},{8,0},{12,4},{16,24},{20,28},{24,16},{28,20},{1,9},{5... | collective-permute-start | bytes 1056776 | tf_op jit(solution)/shard_map/ppermute | solution.py:772
  55.0 0.4 collective-permute-start.29
  55.4 4.3 %collective-permute-done.27.refs_3_ = bf16[2,96,768]{2,1,0:T(8,128)(2,1)S(1)} collective-permute-done((bf16[2,96,768]{2,1,0:T(8,128)(2,1)S(1)}, bf16[2,96,768]{2,1,0:T(8,128)(2,1)S(1)}, u32[]{:S(2)}, u32[]{:S(2)}) %collective-permute-start.27) | collective-permute-done | bytes 294944 | tf_op jit(solution)/shard_map/ppermute | solution.py:772
  59.8 2.7 %collective-permute-start.39 = (bf16[192,768]{1,0:T(8,128)(2,1)S(1)}, bf16[192,768]{1,0:T(8,128)(2,1)S(1)}, u32[]{:S(2)}, u32[]{:S(2)}) collective-permute-start(bf16[192,768]{1,0:T(8,128)(2,1)S(1)} %get-tuple-element.232.refs_2_), channel_id=1, source_target_pairs={{0,16},{4,20},{8,24},{12,28},{16,0},{20,4},{24,8},{28,12},{1,17},{... | collective-permute-start | bytes 884744 | tf_op jit(solution)/shard_map/ppermute | solution.py:772
  62.4 1.4 %collective-permute-start.28 = (bf16[128,768]{1,0:T(8,128)(2,1)S(1)}, bf16[128,768]{1,0:T(8,128)(2,1)S(1)}, u32[]{:S(2)}, u32[]{:S(2)}) collective-permute-start(bf16[128,768]{1,0:T(8,128)(2,1)S(1)} %ffn_out.1.refs_6_), channel_id=1, source_target_pairs={{0,2},{1,3},{2,0},{3,1},{4,6},{5,7},{6,4},{7,5},{8,10},{9,11},{10,... | collective-permute-start | bytes 589832 | tf_op jit(solution)/shard_map/ppermute | solution.py:768
  63.8 0.8 collective-permute-start.31
  64.6 6.8 %collective-permute-done.30.zo_got = bf16[1376,128]{1,0:T(8,128)(2,1)S(1)} collective-permute-done((bf16[1376,128]{1,0:T(8,128)(2,1)S(1)}, bf16[1376,128]{1,0:T(8,128)(2,1)S(1)}, u32[]{:S(2)}, u32[]{:S(2)}) %collective-permute-start.30) | collective-permute-done | bytes 352288 | tf_op jit(solution)/shard_map/ppermute | solution.py:772
  71.7 0.3 collective-permute-start.34
  72.0 0.5 collective-permute-start.33
  72.5 0.3 input_grad.1.refs_3_.refs_0_
  72.9 2.6 %collective-permute-start.38 = (bf16[576,128]{1,0:T(8,128)(2,1)S(1)}, bf16[576,128]{1,0:T(8,128)(2,1)S(1)}, u32[]{:S(2)}, u32[]{:S(2)}) collective-permute-start(bf16[576,128]{1,0:T(8,128)(2,1)S(1)} %get-tuple-element.264), channel_id=1, source_target_pairs={{0,16},{4,20},{8,24},{12,28},{16,0},{20,4},{24,8},{28,12},{1,17},{... | collective-permute-start | bytes 442376 | tf_op jit(solution)/shard_map/ppermute | solution.py:772
  75.5 0.6 encoded.1
  76.4 0.8 ffn_final.1
  77.3 0.7 collective-permute-done.35.other
  78.1 3.8 %collective-permute-done.33.refs_1_ = bf16[784,128]{1,0:T(8,128)(2,1)S(1)} collective-permute-done((bf16[784,128]{1,0:T(8,128)(2,1)S(1)}, bf16[784,128]{1,0:T(8,128)(2,1)S(1)}, u32[]{:S(2)}, u32[]{:S(2)}) %collective-permute-start.33) | collective-permute-done | bytes 200736 | tf_op jit(solution)/shard_map/ppermute | solution.py:772
  81.9 0.3 collective-permute-start.37
  82.2 1.2 %collective-permute-start.36 = (bf16[128,768]{1,0:T(8,128)(2,1)S(1)}, bf16[128,768]{1,0:T(8,128)(2,1)S(1)}, u32[]{:S(2)}, u32[]{:S(2)}) collective-permute-start(bf16[128,768]{1,0:T(8,128)(2,1)S(1)} %get-tuple-element.250), channel_id=1, source_target_pairs={{0,2},{1,3},{2,0},{3,1},{4,6},{5,7},{6,4},{7,5},{8,10},{9,11},{10,... | collective-permute-start | bytes 589832 | tf_op jit(solution)/shard_map/ppermute | solution.py:768
  83.4 1.7 %collective-permute-done.38.refs_1_ = bf16[576,128]{1,0:T(8,128)(2,1)S(1)} collective-permute-done((bf16[576,128]{1,0:T(8,128)(2,1)S(1)}, bf16[576,128]{1,0:T(8,128)(2,1)S(1)}, u32[]{:S(2)}, u32[]{:S(2)}) %collective-permute-start.38) | collective-permute-done | bytes 147488 | tf_op jit(solution)/shard_map/ppermute | solution.py:772
  85.1 0.8 cross_final.1
  85.9 0.9 %rows.1 = (bf16[256,768]{1,0:T(8,128)(2,1)}, bf16[256,768]{1,0:T(8,128)(2,1)}, bf16[16,128]{1,0:T(8,128)(2,1)S(1)}) custom-call(bf16[256,768]{1,0:T(8,128)(2,1)S(1)} %input_grad.1.refs_3_.refs_0_, bf16[256,768]{1,0:T(8,128)(2,1)S(1)} %collective-permute-done.32.refs_1_, bf16[608,128]{1,0:T(8,128)(2,1)S(1)} %get-tuple-element.247.refs_2_), custom_call_target="tpu_custom_call" | custom-call | tf_op jit(solution)/shard_map/rows/pallas_call | solution.py:745
  86.9 1.0 %collective-permute-done.36.refs_1_ = bf16[128,768]{1,0:T(8,128)(2,1)S(1)} collective-permute-done((bf16[128,768]{1,0:T(8,128)(2,1)S(1)}, bf16[128,768]{1,0:T(8,128)(2,1)S(1)}, u32[]{:S(2)}, u32[]{:S(2)}) %collective-permute-start.36) | collective-permute-done | bytes 196640 | tf_op jit(solution)/shard_map/ppermute | solution.py:768
  87.9 0.7 encoded_out.1
  88.6 1.3 %collective-permute-done.37.refs_1_ = bf16[608,128]{1,0:T(8,128)(2,1)S(1)} collective-permute-done((bf16[608,128]{1,0:T(8,128)(2,1)S(1)}, bf16[608,128]{1,0:T(8,128)(2,1)S(1)}, u32[]{:S(2)}, u32[]{:S(2)}) %collective-permute-start.37) | collective-permute-done | bytes 155680 | tf_op jit(solution)/shard_map/ppermute | solution.py:772
  89.9 0.9 self_final.1
  (89 shorter events, 2.6 us)
Async XLA Ops:
  0.7 3.1 %copy-start = (bf16[768,192]{0,1:T(8,128)(2,1)S(1)}, bf16[768,192]{0,1:T(8,128)(2,1)}, u32[]{:S(2)}) copy-start(bf16[768,192]{0,1:T(8,128)(2,1)} %param.40) | copy-start | bytes 884740
  0.7 3.1 %copy-start.1 = (bf16[768,192]{0,1:T(8,128)(2,1)S(1)}, bf16[768,192]{0,1:T(8,128)(2,1)}, u32[]{:S(2)}) copy-start(bf16[768,192]{0,1:T(8,128)(2,1)} %param.41) | copy-start | bytes 884740
  0.7 4.3 %copy-start.3 = (bf16[1,256,768]{2,1,0:T(8,128)(2,1)S(1)}, bf16[1,256,768]{2,1,0:T(8,128)(2,1)}, u32[]{:S(2)}) copy-start(bf16[1,256,768]{2,1,0:T(8,128)(2,1)} %param.23) | copy-start | bytes 1179652
  0.7 4.3 %copy-start.5 = (bf16[768,192]{0,1:T(8,128)(2,1)S(1)}, bf16[768,192]{0,1:T(8,128)(2,1)}, u32[]{:S(2)}) copy-start(bf16[768,192]{0,1:T(8,128)(2,1)} %param.34) | copy-start | bytes 884740
  0.7 4.3 %copy-start.6 = (bf16[768,192]{0,1:T(8,128)(2,1)S(1)}, bf16[768,192]{0,1:T(8,128)(2,1)}, u32[]{:S(2)}) copy-start(bf16[768,192]{0,1:T(8,128)(2,1)} %param.35) | copy-start | bytes 884740
  0.7 4.3 %copy-start.10 = (bf16[768,192]{0,1:T(8,128)(2,1)S(1)}, bf16[768,192]{0,1:T(8,128)(2,1)}, u32[]{:S(2)}) copy-start(bf16[768,192]{0,1:T(8,128)(2,1)} %param.33) | copy-start | bytes 884740
  0.7 4.3 %copy-start.11 = (bf16[192,768]{1,0:T(8,128)(2,1)S(1)}, bf16[192,768]{1,0:T(8,128)(2,1)}, u32[]{:S(2)}) copy-start(bf16[192,768]{1,0:T(8,128)(2,1)} %refs_2_.5) | copy-start | bytes 884740
  0.7 4.3 %copy-start.14 = (f32[768]{0:T(1024)S(1)}, f32[768]{0:T(1024)}, u32[]{:S(2)}) copy-start(f32[768]{0:T(1024)} %refs_3_.7) | copy-start | bytes 9220
  0.7 4.3 %copy-start.15 = (s32[256]{0:T(256)S(1)}, s32[256]{0:T(256)}, u32[]{:S(2)}) copy-start(s32[256]{0:T(256)} %param.29) | copy-start | bytes 3076
  0.7 4.3 %copy-start.18 = (f32[32,3]{0,1:T(4,128)S(1)}, f32[32,3]{0,1:T(4,128)}, u32[]{:S(2)}) copy-start(f32[32,3]{0,1:T(4,128)} %param.37) | copy-start | bytes 1156
  0.8 8.5 %collective-permute-start.1 = (bf16[128,768]{1,0:T(8,128)(2,1)}, bf16[128,768]{1,0:T(8,128)(2,1)S(1)}, u32[]{:S(2)}, u32[]{:S(2)}) collective-permute-start(bf16[128,768]{1,0:T(8,128)(2,1)} %bitcast.33), channel_id=1, source_target_pairs={{0,2},{1,3},{2,0},{3,1},{4,6},{5,7},{6,4},{7,5},{8,10},{9,11},{10,... | collective-permute-start | bytes 589832 | tf_op jit(solution)/shard_map/ppermute | solution.py:768
  3.8 3.4 %collective-permute-start.3 = (bf16[192,768]{1,0:T(8,128)(2,1)S(1)}, bf16[192,768]{1,0:T(8,128)(2,1)S(1)}, u32[]{:S(2)}, u32[]{:S(2)}) collective-permute-start(bf16[192,768]{1,0:T(8,128)(2,1)S(1)} %bitcast.19), channel_id=1, source_target_pairs={{0,1},{1,0},{2,3},{3,2},{4,5},{5,4},{6,7},{7,6},{8,9},{9,8},{10,11... | collective-permute-start | bytes 884744 | tf_op jit(solution)/shard_map/ppermute | solution.py:764
  3.8 3.5 %collective-permute-start.4 = (bf16[192,768]{1,0:T(8,128)(2,1)S(1)}, bf16[192,768]{1,0:T(8,128)(2,1)S(1)}, u32[]{:S(2)}, u32[]{:S(2)}) collective-permute-start(bf16[192,768]{1,0:T(8,128)(2,1)S(1)} %bitcast.24), channel_id=1, source_target_pairs={{0,1},{1,0},{2,3},{3,2},{4,5},{5,4},{6,7},{7,6},{8,9},{9,8},{10,11... | collective-permute-start | bytes 884744 | tf_op jit(solution)/shard_map/ppermute | solution.py:764
  5.0 2.2 %copy-start.8 = (bf16[768,192]{0,1:T(8,128)(2,1)S(1)}, bf16[768,192]{0,1:T(8,128)(2,1)}, u32[]{:S(2)}) copy-start(bf16[768,192]{0,1:T(8,128)(2,1)} %param.39) | copy-start | bytes 884740
  5.1 2.2 %copy-start.9 = (bf16[192,768]{1,0:T(8,128)(2,1)S(1)}, bf16[192,768]{1,0:T(8,128)(2,1)}, u32[]{:S(2)}) copy-start(bf16[192,768]{1,0:T(8,128)(2,1)} %refs_5_.1) | copy-start | bytes 884740
  5.1 2.7 %copy-start.4 = (bf16[1,128,768]{2,1,0:T(8,128)(2,1)S(1)}, bf16[1,128,768]{2,1,0:T(8,128)(2,1)}, u32[]{:S(2)}) copy-start(bf16[1,128,768]{2,1,0:T(8,128)(2,1)} %param.24) | copy-start | bytes 589828
  6.6 1.6 %collective-permute-start.5 = (bf16[64,768]{1,0:T(8,128)(2,1)S(1)}, bf16[64,768]{1,0:T(8,128)(2,1)S(1)}, u32[]{:S(2)}, u32[]{:S(2)}) collective-permute-start(bf16[64,768]{1,0:T(8,128)(2,1)S(1)} %get-tuple-element.153), channel_id=1, source_target_pairs={{0,1},{1,0},{2,3},{3,2},{4,5},{5,4},{6,7},{7,6},{8,9},{9,8},{10,11... | collective-permute-start | bytes 294920 | tf_op jit(solution)/shard_map/ppermute | solution.py:764
  6.8 1.5 %collective-permute-start.6 = (bf16[64,768]{1,0:T(8,128)(2,1)S(1)}, bf16[64,768]{1,0:T(8,128)(2,1)S(1)}, u32[]{:S(2)}, u32[]{:S(2)}) collective-permute-start(bf16[64,768]{1,0:T(8,128)(2,1)S(1)} %get-tuple-element.154), channel_id=1, source_target_pairs={{0,1},{1,0},{2,3},{3,2},{4,5},{5,4},{6,7},{7,6},{8,9},{9,8},{10,11... | collective-permute-start | bytes 294920 | tf_op jit(solution)/shard_map/ppermute | solution.py:764
  7.2 6.3 %collective-permute-start.8 = (bf16[192,768]{1,0:T(8,128)(2,1)S(1)}, bf16[192,768]{1,0:T(8,128)(2,1)S(1)}, u32[]{:S(2)}, u32[]{:S(2)}) collective-permute-start(bf16[192,768]{1,0:T(8,128)(2,1)S(1)} %bitcast.44), channel_id=1, source_target_pairs={{0,1},{1,0},{2,3},{3,2},{4,5},{5,4},{6,7},{7,6},{8,9},{9,8},{10,11... | collective-permute-start | bytes 884744 | tf_op jit(solution)/shard_map/ppermute | solution.py:764
  7.3 6.2 %collective-permute-start.9 = (bf16[192,768]{1,0:T(8,128)(2,1)S(1)}, bf16[192,768]{1,0:T(8,128)(2,1)S(1)}, u32[]{:S(2)}, u32[]{:S(2)}) collective-permute-start(bf16[192,768]{1,0:T(8,128)(2,1)S(1)} %copy-done.9), channel_id=1, source_target_pairs={{0,1},{1,0},{2,3},{3,2},{4,5},{5,4},{6,7},{7,6},{8,9},{9,8},{10,11... | collective-permute-start | bytes 884744 | tf_op jit(solution)/shard_map/ppermute | solution.py:764
  8.3 4.6 %copy-start.7 = (bf16[768,768]{1,0:T(8,128)(2,1)S(1)}, bf16[768,768]{1,0:T(8,128)(2,1)}, u32[]{:S(2)}) copy-start(bf16[768,768]{1,0:T(8,128)(2,1)} %up_own.1) | copy-start | bytes 3538948
  8.3 4.6 %copy-start.2 = (bf16[768,768]{1,0:T(8,128)(2,1)S(1)}, bf16[768,768]{1,0:T(8,128)(2,1)}, u32[]{:S(2)}) copy-start(bf16[768,768]{1,0:T(8,128)(2,1)} %refs_2_.4) | copy-start | bytes 3538948
  8.3 7.6 %collective-permute-start.7 = (bf16[144,768]{1,0:T(8,128)(2,1)S(1)}, bf16[144,768]{1,0:T(8,128)(2,1)S(1)}, u32[]{:S(2)}, u32[]{:S(2)}) collective-permute-start(bf16[144,768]{1,0:T(8,128)(2,1)S(1)} %self_sum.1.refs_11_.refs_1_), channel_id=1, source_target_pairs={{0,2},{1,3},{2,0},{3,1},{4,6},{5,7},{6,4},{7,5},{8,10},{9,11},{10,... | collective-permute-start | bytes 663560 | tf_op jit(solution)/shard_map/ppermute | solution.py:768
  9.2 2.5 %collective-permute-start = (bf16[128,768]{1,0:T(8,128)(2,1)S(1)}, bf16[128,768]{1,0:T(8,128)(2,1)S(1)}, u32[]{:S(2)}, u32[]{:S(2)}) collective-permute-start(bf16[128,768]{1,0:T(8,128)(2,1)S(1)} %bitcast.35), channel_id=1, source_target_pairs={{0,1},{1,0},{2,3},{3,2},{4,5},{5,4},{6,7},{7,6},{8,9},{9,8},{10,11... | collective-permute-start | bytes 589832 | tf_op jit(solution)/shard_map/ppermute | solution.py:764
  9.2 2.5 %collective-permute-start.2 = (bf16[128,768]{1,0:T(8,128)(2,1)S(1)}, bf16[128,768]{1,0:T(8,128)(2,1)S(1)}, u32[]{:S(2)}, u32[]{:S(2)}) collective-permute-start(bf16[128,768]{1,0:T(8,128)(2,1)S(1)} %collective-permute-done.1.refs_1_.refs_4_.refs_6_), channel_id=1, source_target_pairs={{0,1},{1,0},{2,3},{3,2},{4,5},{5,4},{6,7},{7,6},{8,9},{9,8},{10,11... | collective-permute-start | bytes 589832 | tf_op jit(solution)/shard_map/ppermute | solution.py:764
  11.7 4.3 %copy-start.12 = (f32[768]{0:T(1024)S(1)}, f32[768]{0:T(1024)}, u32[]{:S(2)}) copy-start(f32[768]{0:T(1024)} %refs_3_.6) | copy-start | bytes 9220
  12.9 11.8 %collective-permute-start.11 = (bf16[768,768]{1,0:T(8,128)(2,1)S(1)}, bf16[768,768]{1,0:T(8,128)(2,1)S(1)}, u32[]{:S(2)}, u32[]{:S(2)}) collective-permute-start(bf16[768,768]{1,0:T(8,128)(2,1)S(1)} %copy-done.7), channel_id=1, source_target_pairs={{0,1},{1,0},{2,3},{3,2},{4,5},{5,4},{6,7},{7,6},{8,9},{9,8},{10,11... | collective-permute-start | bytes 3538952 | tf_op jit(solution)/shard_map/ppermute | solution.py:764
  13.0 6.6 %collective-permute-start.12 = (bf16[768,768]{1,0:T(8,128)(2,1)S(1)}, bf16[768,768]{1,0:T(8,128)(2,1)S(1)}, u32[]{:S(2)}, u32[]{:S(2)}) collective-permute-start(bf16[768,768]{1,0:T(8,128)(2,1)S(1)} %copy-done.2), channel_id=1, source_target_pairs={{0,1},{1,0},{2,3},{3,2},{4,5},{5,4},{6,7},{7,6},{8,9},{9,8},{10,11... | collective-permute-start | bytes 3538952 | tf_op jit(solution)/shard_map/ppermute | solution.py:764
  16.0 3.3 %copy-start.16 = (bf16[1,256,768]{2,1,0:T(8,128)(2,1)S(1)}, bf16[1,256,768]{2,1,0:T(8,128)(2,1)}, u32[]{:S(2)}) copy-start(bf16[1,256,768]{2,1,0:T(8,128)(2,1)} %param.31) | copy-start | bytes 1179652
  16.0 3.3 %copy-start.17 = (f32[16,256]{1,0:T(8,128)S(1)}, f32[16,256]{1,0:T(8,128)}, u32[]{:S(2)}) copy-start(f32[16,256]{1,0:T(8,128)} %refs_2_.3) | copy-start | bytes 49156
  18.4 6.3 %collective-permute-start.10 = (bf16[128,768]{1,0:T(8,128)(2,1)S(1)}, bf16[128,768]{1,0:T(8,128)(2,1)S(1)}, u32[]{:S(2)}, u32[]{:S(2)}) collective-permute-start(bf16[128,768]{1,0:T(8,128)(2,1)S(1)} %get-tuple-element.164.refs_0_), channel_id=1, source_target_pairs={{0,2},{1,3},{2,0},{3,1},{4,6},{5,7},{6,4},{7,5},{8,10},{9,11},{10,... | collective-permute-start | bytes 589832 | tf_op jit(solution)/shard_map/ppermute | solution.py:768
  19.3 5.4 %collective-permute-start.13 = (bf16[128,960]{1,0:T(8,128)(2,1)S(1)}, bf16[128,960]{1,0:T(8,128)(2,1)S(1)}, u32[]{:S(2)}, u32[]{:S(2)}) collective-permute-start(bf16[128,960]{1,0:T(8,128)(2,1)S(1)} %get-tuple-element.174), channel_id=1, source_target_pairs={{0,1},{1,0},{2,3},{3,2},{4,5},{5,4},{6,7},{7,6},{8,9},{9,8},{10,11... | collective-permute-start | bytes 737288 | tf_op jit(solution)/shard_map/ppermute | solution.py:764
  20.4 4.3 %copy-start.13 = (f32[768]{0:T(1024)S(1)}, f32[768]{0:T(1024)}, u32[]{:S(2)}) copy-start(f32[768]{0:T(1024)} %refs_3_.5) | copy-start | bytes 9220
  25.7 2.1 %collective-permute-start.15 = (bf16[128,2304]{1,0:T(8,128)(2,1)S(1)}, bf16[128,2304]{1,0:T(8,128)(2,1)S(1)}, u32[]{:S(2)}, u32[]{:S(2)}) collective-permute-start(bf16[128,2304]{1,0:T(8,128)(2,1)S(1)} %get-tuple-element.186.refs_1_), channel_id=1, source_target_pairs={{0,1},{1,0},{2,3},{3,2},{4,5},{5,4},{6,7},{7,6},{8,9},{9,8},{10,11... | collective-permute-start | bytes 1769480 | tf_op jit(solution)/shard_map/ppermute | solution.py:764
  26.6 7.4 %collective-permute-start.14 = (bf16[128,768]{1,0:T(8,128)(2,1)S(1)}, bf16[128,768]{1,0:T(8,128)(2,1)S(1)}, u32[]{:S(2)}, u32[]{:S(2)}) collective-permute-start(bf16[128,768]{1,0:T(8,128)(2,1)S(1)} %get-tuple-element.177.refs_6_.refs_0_), channel_id=1, source_target_pairs={{0,2},{1,3},{2,0},{3,1},{4,6},{5,7},{6,4},{7,5},{8,10},{9,11},{10,... | collective-permute-start | bytes 589832 | tf_op jit(solution)/shard_map/ppermute | solution.py:768
  28.8 16.0 %collective-permute-start.20 = (bf16[4,96,768]{2,1,0:T(8,128)(2,1)S(1)}, bf16[4,96,768]{2,1,0:T(8,128)(2,1)S(1)}, u32[]{:S(2)}, u32[]{:S(2)}) collective-permute-start(bf16[4,96,768]{2,1,0:T(8,128)(2,1)S(1)} %get-tuple-element.209), channel_id=1, source_target_pairs={{0,4},{4,0},{8,12},{12,8},{16,20},{20,16},{24,28},{28,24},{1,5},{5... | collective-permute-start | bytes 1769480 | tf_op jit(solution)/shard_map/ppermute | solution.py:772
  30.4 15.6 %collective-permute-start.21 = (bf16[4,96,768]{2,1,0:T(8,128)(2,1)S(1)}, bf16[4,96,768]{2,1,0:T(8,128)(2,1)S(1)}, u32[]{:S(2)}, u32[]{:S(2)}) collective-permute-start(bf16[4,96,768]{2,1,0:T(8,128)(2,1)S(1)} %get-tuple-element.211), channel_id=1, source_target_pairs={{0,8},{4,12},{8,0},{12,4},{16,24},{20,28},{24,16},{28,20},{1,9},{5... | collective-permute-start | bytes 1769480 | tf_op jit(solution)/shard_map/ppermute | solution.py:772
  36.7 2.4 %collective-permute-start.17 = (bf16[1024,192]{1,0:T(8,128)(2,1)S(1)}, bf16[1024,192]{1,0:T(8,128)(2,1)S(1)}, u32[]{:S(2)}, u32[]{:S(2)}) collective-permute-start(bf16[1024,192]{1,0:T(8,128)(2,1)S(1)} %source_grad.1.refs_15_), channel_id=1, source_target_pairs={{0,1},{1,0},{2,3},{3,2},{4,5},{5,4},{6,7},{7,6},{8,9},{9,8},{10,11... | collective-permute-start | bytes 1179656 | tf_op jit(solution)/shard_map/ppermute | solution.py:764
  36.8 2.3 %collective-permute-start.18 = (bf16[128,960]{1,0:T(8,128)(2,1)S(1)}, bf16[128,960]{1,0:T(8,128)(2,1)S(1)}, u32[]{:S(2)}, u32[]{:S(2)}) collective-permute-start(bf16[128,960]{1,0:T(8,128)(2,1)S(1)} %get-tuple-element.201), channel_id=1, source_target_pairs={{0,1},{1,0},{2,3},{3,2},{4,5},{5,4},{6,7},{7,6},{8,9},{9,8},{10,11... | collective-permute-start | bytes 737288 | tf_op jit(solution)/shard_map/ppermute | solution.py:764
  37.3 7.2 %collective-permute-start.16 = (bf16[128,768]{1,0:T(8,128)(2,1)S(1)}, bf16[128,768]{1,0:T(8,128)(2,1)S(1)}, u32[]{:S(2)}, u32[]{:S(2)}) collective-permute-start(bf16[128,768]{1,0:T(8,128)(2,1)S(1)} %get-tuple-element.191.refs_0_), channel_id=1, source_target_pairs={{0,2},{1,3},{2,0},{3,1},{4,6},{5,7},{6,4},{7,5},{8,10},{9,11},{10,... | collective-permute-start | bytes 589832 | tf_op jit(solution)/shard_map/ppermute | solution.py:768
  40.8 11.6 %collective-permute-start.23 = (bf16[4,96,384]{2,1,0:T(8,128)(2,1)S(1)}, bf16[4,96,384]{2,1,0:T(8,128)(2,1)S(1)}, u32[]{:S(2)}, u32[]{:S(2)}) collective-permute-start(bf16[4,96,384]{2,1,0:T(8,128)(2,1)S(1)} %get-tuple-element.215), channel_id=1, source_target_pairs={{0,4},{4,0},{8,12},{12,8},{16,20},{20,16},{24,28},{28,24},{1,5},{5... | collective-permute-start | bytes 884744 | tf_op jit(solution)/shard_map/ppermute | solution.py:772
  42.4 10.1 %collective-permute-start.24 = (bf16[4,96,384]{2,1,0:T(8,128)(2,1)S(1)}, bf16[4,96,384]{2,1,0:T(8,128)(2,1)S(1)}, u32[]{:S(2)}, u32[]{:S(2)}) collective-permute-start(bf16[4,96,384]{2,1,0:T(8,128)(2,1)S(1)} %get-tuple-element.217), channel_id=1, source_target_pairs={{0,8},{4,12},{8,0},{12,4},{16,24},{20,28},{24,16},{28,20},{1,9},{5... | collective-permute-start | bytes 884744 | tf_op jit(solution)/shard_map/ppermute | solution.py:772
  44.7 1.5 %collective-permute-start.19 = (bf16[144,768]{1,0:T(8,128)(2,1)S(1)}, bf16[144,768]{1,0:T(8,128)(2,1)S(1)}, u32[]{:S(2)}, u32[]{:S(2)}) collective-permute-start(bf16[144,768]{1,0:T(8,128)(2,1)S(1)} %get-tuple-element.205.refs_4_.refs_0_.refs_8_), channel_id=1, source_target_pairs={{0,1},{1,0},{2,3},{3,2},{4,5},{5,4},{6,7},{7,6},{8,9},{9,8},{10,11... | collective-permute-start | bytes 663560 | tf_op jit(solution)/shard_map/ppermute | solution.py:764
  48.1 4.7 %collective-permute-start.22 = (bf16[144,768]{1,0:T(8,128)(2,1)S(1)}, bf16[144,768]{1,0:T(8,128)(2,1)S(1)}, u32[]{:S(2)}, u32[]{:S(2)}) collective-permute-start(bf16[144,768]{1,0:T(8,128)(2,1)S(1)} %get-tuple-element.214), channel_id=1, source_target_pairs={{0,1},{1,0},{2,3},{3,2},{4,5},{5,4},{6,7},{7,6},{8,9},{9,8},{10,11... | collective-permute-start | bytes 663560 | tf_op jit(solution)/shard_map/ppermute | solution.py:764
  48.3 11.4 %collective-permute-start.26 = (bf16[2,96,768]{2,1,0:T(8,128)(2,1)S(1)}, bf16[2,96,768]{2,1,0:T(8,128)(2,1)S(1)}, u32[]{:S(2)}, u32[]{:S(2)}) collective-permute-start(bf16[2,96,768]{2,1,0:T(8,128)(2,1)S(1)} %get-tuple-element.212.refs_11_), channel_id=1, source_target_pairs={{0,8},{4,12},{8,0},{12,4},{16,24},{20,28},{24,16},{28,20},{1,9},{5... | collective-permute-start | bytes 884744 | tf_op jit(solution)/shard_map/ppermute | solution.py:772
  49.8 9.9 %collective-permute-start.27 = (bf16[2,96,768]{2,1,0:T(8,128)(2,1)S(1)}, bf16[2,96,768]{2,1,0:T(8,128)(2,1)S(1)}, u32[]{:S(2)}, u32[]{:S(2)}) collective-permute-start(bf16[2,96,768]{2,1,0:T(8,128)(2,1)S(1)} %get-tuple-element.231), channel_id=1, source_target_pairs={{0,4},{4,0},{8,12},{12,8},{16,20},{20,16},{24,28},{28,24},{1,5},{5... | collective-permute-start | bytes 884744 | tf_op jit(solution)/shard_map/ppermute | solution.py:772
  52.8 9.6 %collective-permute-start.25 = (bf16[144,768]{1,0:T(8,128)(2,1)S(1)}, bf16[144,768]{1,0:T(8,128)(2,1)S(1)}, u32[]{:S(2)}, u32[]{:S(2)}) collective-permute-start(bf16[144,768]{1,0:T(8,128)(2,1)S(1)} %input_sum.1.refs_4_.refs_0_), channel_id=1, source_target_pairs={{0,2},{1,3},{2,0},{3,1},{4,6},{5,7},{6,4},{7,5},{8,10},{9,11},{10,... | collective-permute-start | bytes 663560 | tf_op jit(solution)/shard_map/ppermute | solution.py:768
  53.7 17.8 %collective-permute-start.30 = (bf16[1376,128]{1,0:T(8,128)(2,1)S(1)}, bf16[1376,128]{1,0:T(8,128)(2,1)S(1)}, u32[]{:S(2)}, u32[]{:S(2)}) collective-permute-start(bf16[1376,128]{1,0:T(8,128)(2,1)S(1)} %get-tuple-element.235), channel_id=1, source_target_pairs={{0,8},{4,12},{8,0},{12,4},{16,24},{20,28},{24,16},{28,20},{1,9},{5... | collective-permute-start | bytes 1056776 | tf_op jit(solution)/shard_map/ppermute | solution.py:772
  55.0 16.5 %collective-permute-start.29 = (bf16[2112,128]{1,0:T(8,128)(2,1)S(1)}, bf16[2112,128]{1,0:T(8,128)(2,1)S(1)}, u32[]{:S(2)}, u32[]{:S(2)}) collective-permute-start(bf16[2112,128]{1,0:T(8,128)(2,1)S(1)} %get-tuple-element.234), channel_id=1, source_target_pairs={{0,4},{4,0},{8,12},{12,8},{16,20},{20,16},{24,28},{28,24},{1,5},{5... | collective-permute-start | bytes 1622024 | tf_op jit(solution)/shard_map/ppermute | solution.py:772
  59.8 16.4 %collective-permute-start.39 = (bf16[192,768]{1,0:T(8,128)(2,1)S(1)}, bf16[192,768]{1,0:T(8,128)(2,1)S(1)}, u32[]{:S(2)}, u32[]{:S(2)}) collective-permute-start(bf16[192,768]{1,0:T(8,128)(2,1)S(1)} %get-tuple-element.232.refs_2_), channel_id=1, source_target_pairs={{0,16},{4,20},{8,24},{12,28},{16,0},{20,4},{24,8},{28,12},{1,17},{... | collective-permute-start | bytes 884744 | tf_op jit(solution)/shard_map/ppermute | solution.py:772
  62.4 10.1 %collective-permute-start.28 = (bf16[128,768]{1,0:T(8,128)(2,1)S(1)}, bf16[128,768]{1,0:T(8,128)(2,1)S(1)}, u32[]{:S(2)}, u32[]{:S(2)}) collective-permute-start(bf16[128,768]{1,0:T(8,128)(2,1)S(1)} %ffn_out.1.refs_6_), channel_id=1, source_target_pairs={{0,2},{1,3},{2,0},{3,1},{4,6},{5,7},{6,4},{7,5},{8,10},{9,11},{10,... | collective-permute-start | bytes 589832 | tf_op jit(solution)/shard_map/ppermute | solution.py:768
  63.8 7.7 %collective-permute-start.31 = (bf16[16,128]{1,0:T(8,128)(2,1)S(1)}, bf16[16,128]{1,0:T(8,128)(2,1)S(1)}, u32[]{:S(2)}, u32[]{:S(2)}) collective-permute-start(bf16[16,128]{1,0:T(8,128)(2,1)S(1)} %gain.1.gains), channel_id=1, source_target_pairs={{0,4},{4,0},{8,12},{12,8},{16,20},{20,16},{24,28},{28,24},{1,5},{5... | collective-permute-start | bytes 12296 | tf_op jit(solution)/shard_map/ppermute | solution.py:772
  71.7 6.4 %collective-permute-start.34 = (bf16[208,256]{1,0:T(8,128)(2,1)S(1)}, bf16[208,256]{1,0:T(8,128)(2,1)S(1)}, u32[]{:S(2)}, u32[]{:S(2)}) collective-permute-start(bf16[208,256]{1,0:T(8,128)(2,1)S(1)} %get-tuple-element.239.refs_8_), channel_id=1, source_target_pairs={{0,4},{4,0},{8,12},{12,8},{16,20},{20,16},{24,28},{28,24},{1,5},{5... | collective-permute-start | bytes 319496 | tf_op jit(solution)/shard_map/ppermute | solution.py:772
  72.0 9.8 %collective-permute-start.33 = (bf16[784,128]{1,0:T(8,128)(2,1)S(1)}, bf16[784,128]{1,0:T(8,128)(2,1)S(1)}, u32[]{:S(2)}, u32[]{:S(2)}) collective-permute-start(bf16[784,128]{1,0:T(8,128)(2,1)S(1)} %get-tuple-element.241), channel_id=1, source_target_pairs={{0,8},{4,12},{8,0},{12,4},{16,24},{20,28},{24,16},{28,20},{1,9},{5... | collective-permute-start | bytes 602120 | tf_op jit(solution)/shard_map/ppermute | solution.py:772
  72.8 13.1 %collective-permute-start.32 = (bf16[256,768]{1,0:T(8,128)(2,1)S(1)}, bf16[256,768]{1,0:T(8,128)(2,1)S(1)}, u32[]{:S(2)}, u32[]{:S(2)}) collective-permute-start(bf16[256,768]{1,0:T(8,128)(2,1)S(1)} %input_grad.1.refs_3_.refs_0_), channel_id=1, source_target_pairs={{0,1},{1,0},{2,3},{3,2},{4,5},{5,4},{6,7},{7,6},{8,9},{9,8},{10,11... | collective-permute-start | bytes 1179656 | tf_op jit(solution)/shard_map/ppermute | solution.py:764
  72.9 12.2 %collective-permute-start.38 = (bf16[576,128]{1,0:T(8,128)(2,1)S(1)}, bf16[576,128]{1,0:T(8,128)(2,1)S(1)}, u32[]{:S(2)}, u32[]{:S(2)}) collective-permute-start(bf16[576,128]{1,0:T(8,128)(2,1)S(1)} %get-tuple-element.264), channel_id=1, source_target_pairs={{0,16},{4,20},{8,24},{12,28},{16,0},{20,4},{24,8},{28,12},{1,17},{... | collective-permute-start | bytes 442376 | tf_op jit(solution)/shard_map/ppermute | solution.py:772
  76.2 1.8 %collective-permute-start.35 = (bf16[256,768]{1,0:T(8,128)(2,1)S(1)}, bf16[256,768]{1,0:T(8,128)(2,1)S(1)}, u32[]{:S(2)}, u32[]{:S(2)}) collective-permute-start(bf16[256,768]{1,0:T(8,128)(2,1)S(1)} %get-tuple-element.245), channel_id=1, source_target_pairs={{0,1},{1,0},{2,3},{3,2},{4,5},{5,4},{6,7},{7,6},{8,9},{9,8},{10,11... | collective-permute-start | bytes 1179656 | tf_op jit(solution)/shard_map/ppermute | solution.py:764
  81.9 8.0 %collective-permute-start.37 = (bf16[608,128]{1,0:T(8,128)(2,1)S(1)}, bf16[608,128]{1,0:T(8,128)(2,1)S(1)}, u32[]{:S(2)}, u32[]{:S(2)}) collective-permute-start(bf16[608,128]{1,0:T(8,128)(2,1)S(1)} %get-tuple-element.247.refs_2_), channel_id=1, source_target_pairs={{0,16},{4,20},{8,24},{12,28},{16,0},{20,4},{24,8},{28,12},{1,17},{... | collective-permute-start | bytes 466952 | tf_op jit(solution)/shard_map/ppermute | solution.py:772
  82.2 5.7 %collective-permute-start.36 = (bf16[128,768]{1,0:T(8,128)(2,1)S(1)}, bf16[128,768]{1,0:T(8,128)(2,1)S(1)}, u32[]{:S(2)}, u32[]{:S(2)}) collective-permute-start(bf16[128,768]{1,0:T(8,128)(2,1)S(1)} %get-tuple-element.250), channel_id=1, source_target_pairs={{0,2},{1,3},{2,0},{3,1},{4,6},{5,7},{6,4},{7,5},{8,10},{9,11},{10,... | collective-permute-start | bytes 589832 | tf_op jit(solution)/shard_map/ppermute | solution.py:768
